TPU v7x, 32 devices: a whole 2x2x4 slice. The times are simulated.
32 devices in a mesh: group: 2 (over y), tensor: 16 (over z, x, core).
Axes of the slice: x: 2, y: 2, z: 4, core: 2. Of those that a mesh axis runs over, the one named last changes fastest.
Arguments:
- tokens: bfloat16 [64, 8192], P(('group', 'tensor')), parts along dimension 0, may hold values from -6 to 6
- gate_weight: bfloat16 [8192, 28672], P(None, 'tensor'), may hold values from -0.0625 to 0.0625
- up_weight: bfloat16 [8192, 28672], P(None, 'tensor'), may hold values from -0.0625 to 0.0625
- a_gate: float32 [16384, 1024], P(('group', 'tensor')), parts along dimension 0, may hold values from -0.0625 to 0.0625
- a_up: float32 [16384, 1024], P(('group', 'tensor')), parts along dimension 0, may hold values from -0.0625 to 0.0625
- b_gate: float32 [2048, 28672], P('group', 'tensor'), parts along dimension 0, may hold values from -0.75 to 0.75
- b_up: float32 [2048, 28672], P('group', 'tensor'), parts along dimension 0, may hold values from -0.75 to 0.75
- agent: int32 [64], P('group'), parts along dimension 0, may hold values from 0 to 15
- d_hidden: bfloat16 [64, 28672], P('group', 'tensor'), parts along dimension 0, may hold values from -6 to 6
Outputs:
- token_gradient: bfloat16 [64, 8192], P(('group', 'tensor')), parts along dimension 0
- gate_down_gradient: float32 [16384, 1024], P(('group', 'tensor')), parts along dimension 0
- up_down_gradient: float32 [16384, 1024], P(('group', 'tensor')), parts along dimension 0
- gate_lift_gradient: float32 [2048, 28672], P('group', 'tensor'), parts along dimension 0
- up_lift_gradient: float32 [2048, 28672], P('group', 'tensor'), parts along dimension 0
There are 2 independent parts, one for each index of `group`. A program takes and returns all parts, laid end to end along the dimension named above; an argument that names none is the same for every part. Nothing has to cross between parts.
All inputs are finite; a program needn't handle non-finite values.
Results may differ from a plain program's by a relative error of at most 0.009.
Values may be sent and summed in bfloat16 or wider, within the bound.
No kernel may reach another device: no remote copies, remote signals or barrier semaphores. Data moves between devices by JAX's collectives and lax.ppermute only.
A program may use at most 192 MiB of HBM per device.

v0:
```python
import jax
import jax.numpy as jnp
from jax import lax
from jax.sharding import PartitionSpec as P

R = 64
AG = 16


adapter_scale = 2.0


def agent_mask(agent):
    return (agent[:, None] == jnp.arange(AG, dtype=jnp.int32)[None, :]).astype(jnp.float32)


def select_rank(values, onehot):
    shaped = values.reshape(values.shape[0], AG, R)
    return jnp.sum(shaped * onehot[:, :, None], axis=1)


def spread_rank(small, onehot):
    wide = onehot[:, :, None] * small.astype(jnp.float32)[:, None, :]
    return wide.reshape(small.shape[0], AG * R).astype(jnp.bfloat16)


def flipped_product(left, weight):
    return lax.dot_general(
        left, weight, (((1,), (1,)), ((), ())), preferred_element_type=jnp.float32
    )


def per_device(tokens, gate_weight, up_weight, a_gate, a_up, b_gate, b_up, agent, d_hidden):
    onehot = agent_mask(agent)
    feat_rows = a_gate.shape[0]
    feat_start = lax.axis_index("tensor") * feat_rows
    agent_gate_down = a_gate.astype(jnp.bfloat16)
    agent_up_down = a_up.astype(jnp.bfloat16)
    agent_gate_lift = b_gate.astype(jnp.bfloat16)
    agent_up_lift = b_up.astype(jnp.bfloat16)
    complete_result = lax.all_gather(tokens, "tensor", axis=0, tiled=True)
    own_cols = lax.dynamic_slice_in_dim(complete_result, feat_start, feat_rows, 1)
    part_gate = select_rank(
        jnp.dot(own_cols, agent_gate_down, preferred_element_type=jnp.float32), onehot
    )
    part_up = select_rank(
        jnp.dot(own_cols, agent_up_down, preferred_element_type=jnp.float32), onehot
    )
    u_gate, u_up = lax.psum((part_gate, part_up), "tensor")
    up_factor_gate = spread_rank(u_gate.astype(jnp.bfloat16), onehot)
    up_factor_up = spread_rank(u_up.astype(jnp.bfloat16), onehot)
    gate_values = jnp.dot(
        complete_result, gate_weight, preferred_element_type=jnp.float32
    ) + adapter_scale * jnp.dot(up_factor_gate, agent_gate_lift, preferred_element_type=jnp.float32)
    up_values = jnp.dot(
        complete_result, up_weight, preferred_element_type=jnp.float32
    ) + adapter_scale * jnp.dot(up_factor_up, agent_up_lift, preferred_element_type=jnp.float32)
    sig = jax.nn.sigmoid(gate_values)
    hidden_grad = d_hidden.astype(jnp.float32)
    gate_gradient = (hidden_grad * up_values * sig * (1.0 + gate_values * (1.0 - sig))).astype(
        jnp.bfloat16
    )
    up_gradient = (hidden_grad * gate_values * sig).astype(jnp.bfloat16)
    pg_gate = select_rank(flipped_product(gate_gradient, agent_gate_lift), onehot)
    pg_up = select_rank(flipped_product(up_gradient, agent_up_lift), onehot)
    g_gate, g_up = lax.psum((pg_gate, pg_up), "tensor")
    gate_factor_gate = spread_rank(g_gate.astype(jnp.bfloat16), onehot)
    gate_factor_up = spread_rank(g_up.astype(jnp.bfloat16), onehot)
    adapter_contribution = adapter_scale * (
        flipped_product(gate_factor_gate, agent_gate_down)
        + flipped_product(gate_factor_up, agent_up_down)
    )
    base_rows = flipped_product(gate_gradient, gate_weight) + flipped_product(
        up_gradient, up_weight
    )
    joined = lax.dynamic_slice_in_dim(base_rows, feat_start, feat_rows, 1) + adapter_contribution
    token_gradient = lax.psum_scatter(
        lax.dynamic_update_slice_in_dim(base_rows, joined, feat_start, 1),
        "tensor",
        scatter_dimension=0,
        tiled=True,
    ).astype(jnp.bfloat16)
    gate_down_gradient = adapter_scale * lax.dot_general(
        own_cols, gate_factor_gate, (((0,), (0,)), ((), ())), preferred_element_type=jnp.float32
    )
    up_down_gradient = adapter_scale * lax.dot_general(
        own_cols, gate_factor_up, (((0,), (0,)), ((), ())), preferred_element_type=jnp.float32
    )
    gate_lift_gradient = adapter_scale * lax.dot_general(
        up_factor_gate, gate_gradient, (((0,), (0,)), ((), ())), preferred_element_type=jnp.float32
    )
    up_lift_gradient = adapter_scale * lax.dot_general(
        up_factor_up, up_gradient, (((0,), (0,)), ((), ())), preferred_element_type=jnp.float32
    )
    return (
        token_gradient,
        gate_down_gradient,
        up_down_gradient,
        gate_lift_gradient,
        up_lift_gradient,
    )


def solution(mesh):
    in_specs = (
        P(("group", "tensor"), None),
        P(None, "tensor"),
        P(None, "tensor"),
        P(("group", "tensor"), None),
        P(("group", "tensor"), None),
        P("group", "tensor"),
        P("group", "tensor"),
        P("group"),
        P("group", "tensor"),
    )
    out_specs = (
        P(("group", "tensor"), None),
        P(("group", "tensor"), None),
        P(("group", "tensor"), None),
        P("group", "tensor"),
        P("group", "tensor"),
    )
    return jax.shard_map(
        per_device, mesh=mesh, in_specs=in_specs, out_specs=out_specs, check_vma=False
    )
```

profile of v0, /device:TPU:0, one launch (start us, length us, event | category | flops | bytes accessed | tf_op | source)
XLA Modules:
  0.0 305.5 jit_solution(5666566312597510097)
XLA Ops:
  0.6 1.2 dynamic-slice
  2.5 0.7 fusion.28
  3.3 24.8 %all-gather = bf16[16,2,8192]{2,1,0:T(2,128)(2,1)S(1)} all-gather(bf16[1,2,8192]{2,1,0:T(2,128)(2,1)} %bitcast.24), channel_id=1, replica_groups=mesh['group'=2,'tensor'=16] {'tensor'}, dimensions={0}, use_global_device_ids=true | all-gather | bytes 557056 | tf_op jit(solution)/shard_map/all_gather | solution.py:41
  28.0 0.2 reshape.73
  28.2 1.9 fusion.17
  30.1 0.1 reshape.69
  30.2 1.9 fusion.20
  32.1 0.1 reshape.68
  32.2 0.2 multiply_reduce_fusion.2
  32.4 57.9 %all-reduce.2 = (bf16[32,64]{1,0:T(8,128)(2,1)S(1)}, bf16[32,64]{1,0:T(8,128)(2,1)S(1)}) all-reduce(f32[32,64]{1,0:T(8,128)S(1)} %get-tuple-element.8, f32[32,64]{1,0:T(8,128)S(1)} %get-tuple-element.7), channel_id=1, replica_groups=mesh['group'=2,'tensor'=16] {'tensor'}, use_global_device_ids=true, to_apply=%region_1.0 | all-reduce | flops 4096 | bytes 24576 | tf_op jit(solution)/shard_map/psum | solution.py:49
  90.3 11.9 %fusion.34 = f32[32,1792]{1,0:T(8,128)S(1)} fusion(bf16[32,8192]{1,0:T(8,128)(2,1)S(1)} %reshape.73, bf16[8192,1792]{1,0:T(8,128)(2,1)} %param.10), kind=kOutput, calls=%fused_computation.58 | convolution fusion | flops 939524096 | bytes 30113792 | tf_op jit(solution)/shard_map/dot_general | solution.py:52
  102.2 0.0 copy-start.4
  102.2 11.9 %fusion.33 = f32[32,1792]{1,0:T(8,128)S(1)} fusion(bf16[32,8192]{1,0:T(8,128)(2,1)S(1)} %reshape.73, bf16[8192,1792]{1,0:T(8,128)(2,1)} %param.11), kind=kOutput, calls=%fused_computation.57 | convolution fusion | flops 939524096 | bytes 30113792 | tf_op jit(solution)/shard_map/dot_general | solution.py:55
  114.1 0.1 multiply_convert_fusion.2
  114.3 0.1 convert_element_type.91
  114.4 0.1 convert_element_type.85
  114.6 0.0 copy-done.4
  114.6 0.0 slice-start
  114.6 4.0 %fusion.23 = (bf16[32,1792]{1,0:T(8,128)(2,1)S(1)}, f32[32,1792]{1,0:T(8,128)S(1)}) fusion(bf16[32,1792]{1,0:T(8,128)(2,1)S(1)} %copy-done.4, f32[32,1792]{1,0:T(8,128)S(1)} %fusion.34, bf16[32,1024]{1,0:T(8,128)(2,1)S(1)} %convert_element_type.91, f32[1024,1792]{1,0:T(8,128)} %param.14), kind=kOutput, calls=%fused_computation.40 | convolution fusion | flops 119791616 | bytes 8093696 | tf_op jit(solution)/shard_map/dot_general | solution.py:54
  118.6 0.0 slice-start.1
  118.6 4.0 %fusion.5 = bf16[32,1792]{1,0:T(8,128)(2,1)S(1)} fusion(f32[32,1792]{1,0:T(8,128)S(1)} %fusion.33, bf16[32,1024]{1,0:T(8,128)(2,1)S(1)} %convert_element_type.85, f32[1024,1792]{1,0:T(8,128)} %param.15, bf16[32,1792]{1,0:T(8,128)(2,1)S(1)} %copy-done.4, f32[32,1792]{1,0:T(8,128)S(1)} %get-tuple-element.18), kind=kOutput, calls=%fused_computation.10 | convolution fusion | flops 120020992 | bytes 8093696 | tf_op jit(solution)/shard_map/dot_general | solution.py:57
  122.6 0.0 slice-done
  122.6 0.0 slice-done.1
  122.7 0.0 copy-start.1
  122.7 1.2 fusion.6
  123.8 0.1 reshape.70
  124.0 4.9 %fusion.9 = f32[32,1024]{1,0:T(8,128)} fusion(bf16[32,1792]{1,0:T(8,128)(2,1)S(1)} %get-tuple-element.17, f32[1024,1792]{1,0:T(8,128)} %param.15), kind=kOutput, calls=%fused_computation.14 | convolution fusion | flops 119275520 | bytes 7585792 | tf_op jit(solution)/shard_map/dot_general | solution.py:28
  128.9 1.0 reshape.71
  129.9 0.2 multiply_reduce_fusion
  130.1 57.8 %all-reduce.1 = (bf16[32,64]{1,0:T(8,128)(2,1)S(1)}, bf16[32,64]{1,0:T(8,128)(2,1)S(1)}) all-reduce(f32[32,64]{1,0:T(8,128)S(1)} %get-tuple-element.6, f32[32,64]{1,0:T(8,128)S(1)} %get-tuple-element.5), channel_id=1, replica_groups=mesh['group'=2,'tensor'=16] {'tensor'}, use_global_device_ids=true, to_apply=%region_5.0 | all-reduce | flops 4096 | bytes 24576 | tf_op jit(solution)/shard_map/psum | solution.py:66
  187.9 0.1 multiply_convert_fusion
  188.1 0.1 convert_element_type.102
  188.2 0.0 copy-start.3
  188.2 0.1 convert_element_type.98
  188.4 0.0 copy-done.1
  188.4 0.0 copy-start.2
  188.4 0.4 fusion.15
  188.8 15.1 %fusion.35 = f32[32,8192]{1,0:T(8,128)} fusion(bf16[32,1792]{1,0:T(8,128)(2,1)S(1)} %fusion.5, bf16[8192,1792]{1,0:T(8,128)(2,1)} %param.10), kind=kOutput, calls=%fused_computation.59 | convolution fusion | flops 939524096 | bytes 30523392 | tf_op jit(solution)/shard_map/dot_general | solution.py:28
  203.9 0.0 copy-done.2
  204.0 15.5 %convolution_add_fusion = f32[32,8192]{1,0:T(8,128)} fusion(f32[32,8192]{1,0:T(8,128)} %fusion.35, bf16[32,1792]{1,0:T(8,128)(2,1)S(1)} %get-tuple-element.17, bf16[8192,1792]{1,0:T(8,128)(2,1)} %param.11), kind=kOutput, calls=%fused_computation | convolution fusion | flops 939786240 | bytes 31571968 | tf_op jit(solution)/shard_map/dot_general | solution.py:28
  219.4 0.0 copy-done.3
  219.4 1.9 fusion.14
  221.3 69.9 %all-reduce.4 = bf16[32,8192]{1,0:T(8,128)(2,1)S(1)} all-reduce(f32[32,8192]{1,0:T(8,128)} %fusion.14), channel_id=2, replica_groups=mesh['group'=2,'tensor'=16] {'tensor'}, use_global_device_ids=true, to_apply=%region_8.0.clone | all-reduce | flops 262144 | bytes 1572864
  291.2 0.7 dynamic-slice_convert_fusion
  291.9 2.6 convolution_multiply_fusion.4
  294.5 2.6 convolution_multiply_fusion.5
  297.1 4.2 %convolution_multiply_fusion = f32[1024,1792]{1,0:T(8,128)} fusion(bf16[32,1024]{1,0:T(8,128)(2,1)S(1)} %convert_element_type.85, bf16[32,1792]{1,0:T(8,128)(2,1)S(1)} %get-tuple-element.17), kind=kOutput, calls=%fused_computation.1 | convolution fusion | flops 119275520 | bytes 7520256 | tf_op jit(solution)/shard_map/dot_general | solution.py:92
  301.3 4.2 %convolution_multiply_fusion.1 = f32[1024,1792]{1,0:T(8,128)} fusion(bf16[32,1024]{1,0:T(8,128)(2,1)S(1)} %convert_element_type.91, bf16[32,1792]{1,0:T(8,128)(2,1)S(1)} %fusion.5), kind=kOutput, calls=%fused_computation.2 | convolution fusion | flops 119275520 | bytes 7520256 | tf_op jit(solution)/shard_map/dot_general | solution.py:89
  (7 shorter events, 0.0 us)
Async XLA Ops:
  102.2 12.4 %copy-start.4 = (bf16[32,1792]{1,0:T(8,128)(2,1)S(1)}, bf16[32,1792]{1,0:T(8,128)(2,1)}, u32[]{:S(2)}) copy-start(bf16[32,1792]{1,0:T(8,128)(2,1)} %param.17) | copy-start | bytes 344068
  114.6 8.0 %slice-start = ((s8[7340032]{0:T(1024)(128)(4,1)}), s8[4194304]{0:T(1024)(128)(4,1)S(1)}, s32[]{:S(2)}) async-start(s8[7340032]{0:T(1024)(128)(4,1)} %bitcast.22), calls=%async_computation | async-start | bytes 8388608
  118.6 4.0 %slice-start.1 = ((s8[7340032]{0:T(1024)(128)(4,1)}), s8[3145728]{0:T(1024)(128)(4,1)S(1)}, s32[]{:S(2)}) async-start(s8[7340032]{0:T(1024)(128)(4,1)} %bitcast.22), calls=%async_computation.1 | async-start | bytes 6291456
  122.7 65.7 %copy-start.1 = (f32[512,1024]{1,0:T(8,128)S(1)}, f32[512,1024]{1,0:T(8,128)}, u32[]{:S(2)}) copy-start(f32[512,1024]{1,0:T(8,128)} %param.12) | copy-start | bytes 6291460
  188.2 31.2 %copy-start.3 = (bf16[32,1024]{1,0:T(8,128)(2,1)}, bf16[32,1024]{1,0:T(8,128)(2,1)S(1)}, u32[]{:S(2)}) copy-start(bf16[32,1024]{1,0:T(8,128)(2,1)S(1)} %convert_element_type.102) | copy-start | bytes 196612
  188.4 15.6 %copy-start.2 = (bf16[32,1024]{1,0:T(8,128)(2,1)}, bf16[32,1024]{1,0:T(8,128)(2,1)S(1)}, u32[]{:S(2)}) copy-start(bf16[32,1024]{1,0:T(8,128)(2,1)S(1)} %convert_element_type.98) | copy-start | bytes 196612
  204.0 15.5 %copy-start = (f32[512,1024]{1,0:T(8,128)S(1)}, f32[512,1024]{1,0:T(8,128)}, u32[]{:S(2)}) copy-start(f32[512,1024]{1,0:T(8,128)} %param.13) | copy-start | bytes 6291460
where the time goes:
time: 306 us
  blocking collectives  210 us (69%)
  matrix products  88.2 us (29%)
  local copies, waits for them, and re-layouts  4.06 us (1%)
    unnamed x1, blocking collectives  69.9 us
    psum x1, blocking collectives, per_device(): u_gate, u_up = lax.psum((part_gate, part_up), 'tensor')  57.9 us
    psum x1, blocking collectives, per_device(): g_gate, g_up = lax.psum((pg_gate, pg_up), 'tensor')  57.8 us
    dot_general x6, matrix products, flipped_product(): lax.dot_general(left, weight, (((1,), (1,)), ((), ())), preferred_element...  39 us
    all_gather x1, blocking collectives, per_device(): complete_result = lax.all_gather(tokens, 'tensor', axis=0, tiled=True)  24.8 us
    dot_general x1, matrix products, per_device(): jnp.dot(complete_result, up_weight, preferred_element_type=jnp.float32)  11.9 us
    dot_general x1, matrix products, per_device(): jnp.dot(complete_result, gate_weight, preferred_element_type=jnp.float32)  11.9 us

commit v1 on v0

--- a/solution.py
+++ b/solution.py
@@ -1,13 +1,16 @@
 import jax
 import jax.numpy as jnp
 from jax import lax
+from jax.experimental import pallas as pl
+from jax.experimental.pallas import tpu as pltpu
 from jax.sharding import PartitionSpec as P
 
 R = 64
 AG = 16
 
-
 adapter_scale = 2.0
+BF16 = jnp.bfloat16
+F32 = jnp.float32
 
 
 def agent_mask(agent):
@@ -30,7 +33,13 @@
     )
 
 
-def per_device(tokens, gate_weight, up_weight, a_gate, a_up, b_gate, b_up, agent, d_hidden):
+def rows_product(left, right):
+    return lax.dot_general(
+        left, right, (((0,), (0,)), ((), ())), preferred_element_type=jnp.float32
+    )
+
+
+def plain_device(tokens, gate_weight, up_weight, a_gate, a_up, b_gate, b_up, agent, d_hidden):
     onehot = agent_mask(agent)
     feat_rows = a_gate.shape[0]
     feat_start = lax.axis_index("tensor") * feat_rows
@@ -80,18 +89,10 @@
         scatter_dimension=0,
         tiled=True,
     ).astype(jnp.bfloat16)
-    gate_down_gradient = adapter_scale * lax.dot_general(
-        own_cols, gate_factor_gate, (((0,), (0,)), ((), ())), preferred_element_type=jnp.float32
-    )
-    up_down_gradient = adapter_scale * lax.dot_general(
-        own_cols, gate_factor_up, (((0,), (0,)), ((), ())), preferred_element_type=jnp.float32
-    )
-    gate_lift_gradient = adapter_scale * lax.dot_general(
-        up_factor_gate, gate_gradient, (((0,), (0,)), ((), ())), preferred_element_type=jnp.float32
-    )
-    up_lift_gradient = adapter_scale * lax.dot_general(
-        up_factor_up, up_gradient, (((0,), (0,)), ((), ())), preferred_element_type=jnp.float32
-    )
+    gate_down_gradient = adapter_scale * rows_product(own_cols, gate_factor_gate)
+    up_down_gradient = adapter_scale * rows_product(own_cols, gate_factor_up)
+    gate_lift_gradient = adapter_scale * rows_product(up_factor_gate, gate_gradient)
+    up_lift_gradient = adapter_scale * rows_product(up_factor_up, up_gradient)
     return (
         token_gradient,
         gate_down_gradient,
@@ -101,7 +102,224 @@
     )
 
 
+def forward_kernel(side_ref, x_ref, wg_ref, wu_ref, g_ref, u_ref):
+    @pl.when(pl.program_id(0) == 0)
+    def _():
+        g_ref[...] = jnp.zeros_like(g_ref)
+        u_ref[...] = jnp.zeros_like(u_ref)
+
+    x = x_ref[...]
+    g_ref[...] += jnp.dot(x, wg_ref[...], preferred_element_type=F32)
+    u_ref[...] += jnp.dot(x, wu_ref[...], preferred_element_type=F32)
+
+
+def forward_products(side, x, gate_weight, up_weight, half, depth=1024):
+    rows, d = x.shape
+    weight_block = pl.BlockSpec((depth, half), lambda k, s: (k, s[0]))
+    out_block = pl.BlockSpec((rows, half), lambda k, s: (0, 0))
+    return pl.pallas_call(
+        forward_kernel,
+        grid_spec=pltpu.PrefetchScalarGridSpec(
+            num_scalar_prefetch=1,
+            grid=(d // depth,),
+            in_specs=[pl.BlockSpec((rows, depth), lambda k, s: (0, k)), weight_block, weight_block],
+            out_specs=[out_block, out_block],
+        ),
+        out_shape=[jax.ShapeDtypeStruct((rows, half), F32)] * 2,
+        compiler_params=pltpu.CompilerParams(vmem_limit_bytes=20 << 20),
+        cost_estimate=pl.CostEstimate(
+            flops=4 * rows * d * half, bytes_accessed=4 * d * half, transcendentals=0
+        ),
+        name="forward_products",
+    )(side, x, gate_weight, up_weight)
+
+
+def backward_kernel(side_ref, dg_ref, du_ref, wg_ref, wu_ref, out_ref):
+    total = flipped_product(dg_ref[...], wg_ref[...]) + flipped_product(du_ref[...], wu_ref[...])
+    out_ref[...] = total.astype(out_ref.dtype)
+
+
+def backward_products(side, dg, du, gate_weight, up_weight, first, count, depth=1024):
+    rows, half = dg.shape
+    start = first // depth
+    weight_block = pl.BlockSpec((depth, half), lambda k, s: (k + start, s[0]))
+    left_block = pl.BlockSpec((rows, half), lambda k, s: (0, 0))
+    return pl.pallas_call(
+        backward_kernel,
+        grid_spec=pltpu.PrefetchScalarGridSpec(
+            num_scalar_prefetch=1,
+            grid=(count // depth,),
+            in_specs=[left_block, left_block, weight_block, weight_block],
+            out_specs=pl.BlockSpec((rows, depth), lambda k, s: (0, k)),
+        ),
+        out_shape=jax.ShapeDtypeStruct((rows, count), F32),
+        compiler_params=pltpu.CompilerParams(vmem_limit_bytes=24 << 20),
+        cost_estimate=pl.CostEstimate(
+            flops=4 * rows * count * half, bytes_accessed=4 * count * half, transcendentals=0
+        ),
+        name="backward_products",
+    )(side, dg, du, gate_weight, up_weight)
+
+
+N = 16
+
+
+def along_tensor(value, mask):
+    return lax.ppermute(value, "tensor", [(i, i ^ mask) for i in range(N)])
+
+
+def across_groups(value):
+    return lax.ppermute(value, "group", [(0, 1), (1, 0)])
+
+
+def sum_over_tensor(value):
+    shape = value.shape
+    v = value.reshape(2, 2, 4, 2, shape[1])
+    v = v + along_tensor(v, 1)[::-1]
+    v = v + along_tensor(v, 2)[:, ::-1]
+    parts = [along_tensor(v, 4 * m) for m in (1, 2, 3)]
+    total = v
+    for m, part in zip((1, 2, 3), parts):
+        total = total + jnp.stack([part[:, :, q ^ m] for q in range(4)], axis=2)
+    return total.reshape(shape)
+
+
+def split_device(tokens, gate_weight, up_weight, a_gate, a_up, b_gate, b_up, agent, d_hidden):
+    group = lax.axis_index("group")
+    t = lax.axis_index("tensor")
+    side = group.astype(jnp.int32).reshape(1)
+    d = tokens.shape[1]
+    ff = b_gate.shape[1]
+    half = ff // 2
+    feat_rows = a_gate.shape[0]
+    feat_start = t * feat_rows
+    mine = group * half
+    other = half - mine
+
+    line = jnp.concatenate([tokens] + [along_tensor(tokens, 4 * m) for m in (1, 2, 3)], axis=0)
+    both = jnp.stack([line, across_groups(line)])
+    both = jnp.concatenate([both, along_tensor(both, 2)], axis=1)
+    both = jnp.concatenate([both, along_tensor(both, 1)], axis=1)
+    rows = both.shape[1]
+    x = both.reshape(2 * rows, d)
+
+    place = jnp.arange(rows, dtype=jnp.int32)
+    block = ((place >> 1) & 3) * 4 + ((place >> 3) & 1) * 2 + (place >> 4)
+    token_of = ((t ^ block) << 1) + (place & 1)
+    shuffle = token_of[:, None] == jnp.arange(rows, dtype=jnp.int32)[None, :]
+    agent_here = jnp.sum(jnp.where(shuffle, agent[None, :], 0), axis=1)
+    onehot = agent_mask(agent_here)
+
+    hidden_other = across_groups(lax.dynamic_slice_in_dim(d_hidden, other, half, 1))
+    hidden_mine = lax.dynamic_slice_in_dim(d_hidden, mine, half, 1)
+    hidden = jnp.dot(
+        shuffle.astype(BF16),
+        jnp.concatenate([hidden_mine, hidden_other], axis=1),
+        preferred_element_type=F32,
+    )
+    hidden_grad = jnp.concatenate([hidden[:, :half], hidden[:, half:]], axis=0)
+
+    agent_gate_down = a_gate.astype(BF16)
+    agent_up_down = a_up.astype(BF16)
+    agent_gate_lift = b_gate.astype(BF16)
+    agent_up_lift = b_up.astype(BF16)
+
+    own_cols = lax.dynamic_slice_in_dim(x[:rows], feat_start, feat_rows, 1)
+    part_gate = select_rank(jnp.dot(own_cols, agent_gate_down, preferred_element_type=F32), onehot)
+    part_up = select_rank(jnp.dot(own_cols, agent_up_down, preferred_element_type=F32), onehot)
+    u = sum_over_tensor(jnp.concatenate([part_gate, part_up], axis=1)).astype(BF16)
+    up_factor_gate = spread_rank(u[:, :R], onehot)
+    up_factor_up = spread_rank(u[:, R:], onehot)
+
+    base_gate, base_up = forward_products(side, x, gate_weight, up_weight, half)
+
+    lifted = jnp.stack(
+        [
+            adapter_scale * jnp.dot(up_factor_gate, agent_gate_lift, preferred_element_type=F32),
+            adapter_scale * jnp.dot(up_factor_up, agent_up_lift, preferred_element_type=F32),
+        ]
+    )
+    lifted_other = across_groups(lax.dynamic_slice_in_dim(lifted, other, half, 2).astype(BF16))
+    lifted_mine = lax.dynamic_slice_in_dim(lifted, mine, half, 2)
+    gate_values = base_gate + jnp.concatenate([lifted_mine[0], lifted_other[0].astype(F32)], axis=0)
+    up_values = base_up + jnp.concatenate([lifted_mine[1], lifted_other[1].astype(F32)], axis=0)
+
+    sig = jax.nn.sigmoid(gate_values)
+    gate_gradient = (hidden_grad * up_values * sig * (1.0 + gate_values * (1.0 - sig))).astype(BF16)
+    up_gradient = (hidden_grad * gate_values * sig).astype(BF16)
+
+    swapped = across_groups(jnp.stack([gate_gradient[rows:], up_gradient[rows:]]))
+    own = jnp.stack([gate_gradient[:rows], up_gradient[:rows]])
+    first = group == 0
+    whole = jnp.concatenate(
+        [jnp.where(first, own, swapped), jnp.where(first, swapped, own)], axis=2
+    )
+
+    def core_first(v):
+        q = rows // 2
+        return jnp.concatenate([v[:q], v[rows : rows + q], v[q:rows], v[rows + q :]], axis=0)
+
+    dg, du = core_first(gate_gradient), core_first(up_gradient)
+    chunks = 2
+    count = d // chunks
+    pieces = []
+    for c in range(chunks):
+        grad = backward_products(side, dg, du, gate_weight, up_weight, c * count, count)
+        grad = grad[:rows] + along_tensor(grad[rows:].astype(BF16), 1).astype(F32)
+        grad = grad[: rows // 2] + across_groups(grad[rows // 2 :].astype(BF16)).astype(F32)
+        grad = grad[: rows // 4] + along_tensor(grad[rows // 4 :].astype(BF16), 2).astype(F32)
+        total = grad[:2]
+        for m in (1, 2, 3):
+            total = total + along_tensor(grad[2 * m : 2 * m + 2].astype(BF16), 4 * m).astype(F32)
+        pieces.append(total)
+
+    pg_gate = select_rank(flipped_product(whole[0], agent_gate_lift), onehot)
+    pg_up = select_rank(flipped_product(whole[1], agent_up_lift), onehot)
+    g = sum_over_tensor(jnp.concatenate([pg_gate, pg_up], axis=1)).astype(BF16)
+    gate_factor_gate = spread_rank(g[:, :R], onehot)
+    gate_factor_up = spread_rank(g[:, R:], onehot)
+    adapter_contribution = adapter_scale * (
+        flipped_product(gate_factor_gate, agent_gate_down)
+        + flipped_product(gate_factor_up, agent_up_down)
+    )
+    move = adapter_contribution.astype(BF16).reshape(2, 2, 4, 2, feat_rows)
+    move = jnp.stack([move[0], along_tensor(move[1], 1)])
+    move = jnp.stack([move[:, 0], along_tensor(move[:, 1], 2)])
+    move = jnp.stack([move[:, :, 0]] + [along_tensor(move[:, :, m], 4 * m) for m in (1, 2, 3)])
+    move = move.reshape(N, 2 * feat_rows)
+    source = jnp.arange(N, dtype=jnp.int32)
+    sort = (source[:, None] == (t ^ source)[None, :]).astype(BF16)
+    sorted_rows = jnp.dot(sort, move, preferred_element_type=F32).reshape(N, 2, feat_rows)
+    contribution = sorted_rows.transpose(1, 0, 2).reshape(2, d)
+    token_gradient = (jnp.concatenate(pieces, axis=1) + contribution).astype(BF16)
+
+    gate_down_gradient = adapter_scale * rows_product(own_cols, gate_factor_gate)
+    up_down_gradient = adapter_scale * rows_product(own_cols, gate_factor_up)
+    gate_lift_gradient = adapter_scale * rows_product(up_factor_gate, whole[0])
+    up_lift_gradient = adapter_scale * rows_product(up_factor_up, whole[1])
+    return (
+        token_gradient,
+        gate_down_gradient,
+        up_down_gradient,
+        gate_lift_gradient,
+        up_lift_gradient,
+    )
+
+
 def solution(mesh):
+    sizes = dict(mesh.shape)
+
+    def per_device(*args):
+        tokens, b_gate = args[0], args[5]
+        fits = (
+            sizes["group"] == 2
+            and sizes["tensor"] == N
+            and tokens.shape[0] == 2
+            and b_gate.shape[1] % 256 == 0
+            and tokens.shape[1] % 2048 == 0
+        )
+        return (split_device if fits else plain_device)(*args)
+
     in_specs = (
         P(("group", "tensor"), None),
         P(None, "tensor"),

time: 306 us -> 178 us (0.58)
  blocking collectives: 210 us -> 0 us
  matrix products: 88.2 us -> 24.8 us
  waiting for transfers between devices: 0 us -> 40.6 us
  starting transfers between devices: 0 us -> 37.8 us
  local copies, waits for them, and re-layouts: 4.06 us -> 31 us
  Pallas kernels: 0 us -> 25.7 us
  other arithmetic: 1.39 us -> 16.4 us
    psum x2 -> x0, blocking collectives: 116 us -> none  [the longest x1 57.9 us: per_device(): u_gate, u_up = lax.psum((part_gate, part_up), 'tensor')]
    unnamed x1 -> x0, blocking collectives: 69.9 us -> none
    ppermute x0 -> x36, waiting for transfers between devices: none -> 40.6 us  [the longest x30 24.6 us: along_tensor(): return lax.ppermute(value, 'tensor', [(i, i ^ mask) for i in range(N)])]
    ppermute x0 -> x36, starting transfers between devices: none -> 37.8 us  [the longest x30 31.3 us: along_tensor(): return lax.ppermute(value, 'tensor', [(i, i ^ mask) for i in range(N)])]
    dot_general x6 -> x4, matrix products: 39 us -> 6.19 us  [flipped_product(): lax.dot_general(left, weight, (((1,), (1,)), ((), ())), preferred_element...]
    dot_general x10, matrix products: 49.2 us -> 18.6 us  [the longest x4 13.4 us: rows_product(): lax.dot_general(left, right, (((0,), (0,)), ((), ())), preferred_element_...]
    pallas_call x0 -> x3, Pallas kernels: none -> 25.7 us  [the longest x2 14.7 us: backward_products(): pl.pallas_call(backward_kernel, grid_spec=pltpu.PrefetchScalarGridSpec(nu...]
    all_gather x1 -> x0, blocking collectives: 24.8 us -> none  [per_device(): complete_result = lax.all_gather(tokens, 'tensor', axis=0, tiled=True)]
  transfers between devices with their start and end apart: 0 -> 36, of which waited for: 0 -> 19; matrix products, arithmetic and copies ran while one was open for 0% -> 24% of each run, Pallas kernels for 0% -> 14%
where the time goes in v1:
time: 178 us; the launch traced here: 177 us
  waiting for transfers between devices  40.6 us (23%)
  starting transfers between devices  37.8 us (21%)
  local copies, waits for them, and re-layouts  31 us (17%)
  Pallas kernels  25.7 us (14%)
  matrix products  24.8 us (14%)
  other arithmetic  16.4 us (9%)
    ppermute x30, starting transfers between devices, along_tensor(): return lax.ppermute(value, 'tensor', [(i, i ^ mask) for i in range(N)])  31.3 us
    ppermute x30, waiting for transfers between devices, along_tensor(): return lax.ppermute(value, 'tensor', [(i, i ^ mask) for i in range(N)])  24.6 us
    unnamed x19, local copies, waits for them, and re-layouts  22.9 us
    ppermute x6, waiting for transfers between devices, across_groups(): return lax.ppermute(value, 'group', [(0, 1), (1, 0)])  16 us
    pallas_call x2, Pallas kernels, backward_products(): pl.pallas_call(backward_kernel, grid_spec=pltpu.PrefetchScalarGridSpec(nu...  14.7 us
    dot_general x4, matrix products, rows_product(): lax.dot_general(left, right, (((0,), (0,)), ((), ())), preferred_element_...  13.4 us
    pallas_call x1, Pallas kernels, forward_products(): pl.pallas_call(forward_kernel, grid_spec=pltpu.PrefetchScalarGridSpec(num...  11 us
    ppermute x6, starting transfers between devices, across_groups(): return lax.ppermute(value, 'group', [(0, 1), (1, 0)])  6.45 us
  transfers between devices with their start and end apart: 36, of which 19 were waited for; matrix products, arithmetic and copies ran while one was open for 24% of the time, Pallas kernels for 14%

profile of v1, /device:TPU:0, one launch (start us, length us, event | category | flops | bytes accessed | tf_op | source)
XLA Modules:
  0.0 177.4 jit_solution(11386703274710840896)
XLA Ops:
  0.6 4.1 %collective-permute-start.2 = (bf16[2,8192]{1,0:T(2,128)(2,1)}, bf16[2,8192]{1,0:T(2,128)(2,1)S(1)}, u32[]{:S(2)}, u32[]{:S(2)}) collective-permute-start(bf16[2,8192]{1,0:T(2,128)(2,1)} %param.9), channel_id=1, source_target_pairs={{0,8},{1,9},{2,10},{3,11},{4,12},{5,13},{6,14},{7,15},{8,0},{9,1},... | collective-permute-start | bytes 98312 | tf_op jit(solution)/shard_map/ppermute | solution.py:168
  4.7 1.6 collective-permute-start.1
  7.3 1.6 collective-permute-done.1
  8.9 3.4 %collective-permute-done.3 = bf16[2,8192]{1,0:T(2,128)(2,1)S(1)} collective-permute-done((bf16[2,8192]{1,0:T(2,128)(2,1)}, bf16[2,8192]{1,0:T(2,128)(2,1)S(1)}, u32[]{:S(2)}, u32[]{:S(2)}) %collective-permute-start.3) | collective-permute-done | bytes 32800 | tf_op jit(solution)/shard_map/ppermute | solution.py:168
  13.1 1.6 collective-permute-start.4
  14.7 3.4 %collective-permute-done.4 = bf16[8,8192]{1,0:T(8,128)(2,1)S(1)} collective-permute-done((bf16[8,8192]{1,0:T(8,128)(2,1)S(1)}, bf16[8,8192]{1,0:T(8,128)(2,1)S(1)}, u32[]{:S(2)}, u32[]{:S(2)}) %collective-permute-start.4) | collective-permute-done | bytes 131104 | tf_op jit(solution)/shard_map/ppermute | solution.py:172
  18.2 1.6 collective-permute-start.5
  20.6 1.6 collective-permute-start
  22.2 1.8 copy.31
  24.0 2.1 %copy.32 = bf16[512,1024]{0,1:T(8,128)(2,1)S(1)} copy(f32[512,1024]{1,0:T(8,128)} %param.13) | data formatting | bytes 3145728 | tf_op args[4]
  26.1 5.3 %convert_element_type.180 = bf16[1024,1792]{1,0:T(8,128)(2,1)} convert(f32[1024,1792]{1,0:T(8,128)} %param.14) | non-fusion elementwise | flops 1835008 | bytes 11010048 | tf_op jit(solution)/shard_map/convert_element_type | solution.py:224
  31.4 5.3 %convert_element_type.184 = bf16[1024,1792]{1,0:T(8,128)(2,1)} convert(f32[1024,1792]{1,0:T(8,128)} %param.15) | non-fusion elementwise | flops 1835008 | bytes 11010048 | tf_op jit(solution)/shard_map/convert_element_type | solution.py:225
  37.1 1.7 collective-permute-done.6
  42.0 3.2 %collective-permute-done.8 = f32[2,2,4,2,128]{4,3,2,1,0:T(2,128)S(1)} collective-permute-done((f32[2,2,4,2,128]{4,3,2,1,0:T(2,128)S(1)}, f32[2,2,4,2,128]{4,3,2,1,0:T(2,128)S(1)}, u32[]{:S(2)}, u32[]{:S(2)}) %collective-permute-start.8) | collective-permute-done | bytes 16416 | tf_op jit(solution)/shard_map/ppermute | solution.py:168
  45.3 9.3 %copy-done = bf16[8192,1792]{1,0:T(8,128)(2,1)S(1)} copy-done((bf16[8192,1792]{1,0:T(8,128)(2,1)S(1)}, bf16[8192,1792]{1,0:T(8,128)(2,1)}, u32[]{:S(2)}) %copy-start) | copy-done | bytes 29360152
  54.6 11.0 %forward_products.1 = (f32[64,896]{1,0:T(8,128)S(1)}, f32[64,896]{1,0:T(8,128)S(1)}) custom-call(s32[1]{0:T(128)} %bitcast.side_ref, bf16[64,8192]{1,0:T(8,128)(2,1)S(1)} %bitcast.125, bf16[8192,1792]{1,0:T(8,128)(2,1)S(1)} %copy-done, bf16[8192,1792]{1,0:T(8,128)(2,1)} %wu_ref.5), custom_call_target="tpu_custom_call" | custom-call | flops 1879048192 | bytes 29360128 | tf_op jit(solution)/shard_map/forward_products/pallas_call | solution.py:120
  65.6 1.4 collective-permute-start.11
  67.0 2.1 %collective-permute-start.9 = (f32[2,2,4,2,128]{4,3,2,1,0:T(2,128)S(1)}, f32[2,2,4,2,128]{4,3,2,1,0:T(2,128)S(1)}, u32[]{:S(2)}, u32[]{:S(2)}) collective-permute-start(f32[2,2,4,2,128]{4,3,2,1,0:T(2,128)S(1)} %reverse_add_fusion.2), channel_id=1, source_target_pairs={{0,4},{1,5},{2,6},{3,7},{4,0},{5,1},{6,2},{7,3},{8,12},{9,13},{10,... | collective-permute-start | bytes 49160 | tf_op jit(solution)/shard_map/ppermute | solution.py:168
  69.1 2.1 %collective-permute-done.11 = f32[2,2,4,2,128]{4,3,2,1,0:T(2,128)S(1)} collective-permute-done((f32[2,2,4,2,128]{4,3,2,1,0:T(2,128)S(1)}, f32[2,2,4,2,128]{4,3,2,1,0:T(2,128)S(1)}, u32[]{:S(2)}, u32[]{:S(2)}) %collective-permute-start.11) | collective-permute-done | bytes 16416 | tf_op jit(solution)/shard_map/ppermute | solution.py:168
  71.9 2.9 %fusion = f32[1,32,1792]{2,1,0:T(8,128)S(1)} fusion(bf16[32,1024]{1,0:T(8,128)(2,1)S(1)} %convert_element_type.179, bf16[1024,1792]{1,0:T(8,128)(2,1)} %convert_element_type.180), kind=kOutput, calls=%fused_computation.4 | convolution fusion | flops 117497856 | bytes 3964928 | tf_op jit(solution)/shard_map/dot_general | solution.py:238
  76.4 4.7 %collective-permute-done.12 = bf16[2,32,896]{2,1,0:T(8,128)(2,1)S(1)} collective-permute-done((bf16[2,32,896]{2,1,0:T(8,128)(2,1)S(1)}, bf16[2,32,896]{2,1,0:T(8,128)(2,1)S(1)}, u32[]{:S(2)}, u32[]{:S(2)}) %collective-permute-start.12) | collective-permute-done | bytes 114720 | tf_op jit(solution)/shard_map/ppermute | solution.py:172
  81.9 4.3 %collective-permute-done.25 = bf16[2,32,896]{2,1,0:T(8,128)(2,1)S(1)} collective-permute-done((bf16[2,32,896]{2,1,0:T(8,128)(2,1)S(1)}, bf16[2,32,896]{2,1,0:T(8,128)(2,1)S(1)}, u32[]{:S(2)}, u32[]{:S(2)}) %collective-permute-start.25) | collective-permute-done | bytes 114720 | tf_op jit(solution)/shard_map/ppermute | solution.py:172
  86.3 1.8 %fusion.4 = f32[32,64]{1,0:T(8,128)S(1)} fusion(bf16[16,64,1792]{2,1,0:T(8,128)(2,1)S(1)} %bitcast.127, f32[32,16]{0,1:T(8,128)S(1)} %fusion.58, bf16[2,32,896]{2,1,0:T(8,128)(2,1)S(1)} %get-tuple-element.15, bf16[2,32,896]{2,1,0:T(8,128)(2,1)S(1)} %get-tuple-element.16), kind=kOutput, calls=%fused_computation.14 | convolution fusion | flops 117733376 | bytes 3909632 | tf_op jit(solution)/shard_map/dot_general | solution.py:31
  88.1 1.8 %fusion.5 = f32[32,64]{1,0:T(8,128)S(1)} fusion(bf16[16,64,1792]{2,1,0:T(8,128)(2,1)S(1)} %bitcast.126, f32[32,16]{0,1:T(8,128)S(1)} %fusion.58, bf16[2,32,896]{2,1,0:T(8,128)(2,1)S(1)} %get-tuple-element.16, bf16[2,32,896]{2,1,0:T(8,128)(2,1)S(1)} %get-tuple-element.15), kind=kOutput, calls=%fused_computation.15 | convolution fusion | flops 117733376 | bytes 3909632 | tf_op jit(solution)/shard_map/dot_general | solution.py:31
  90.0 9.3 %copy-done.1 = bf16[8192,1792]{1,0:T(8,128)(2,1)S(1)} copy-done((bf16[8192,1792]{1,0:T(8,128)(2,1)S(1)}, bf16[8192,1792]{1,0:T(8,128)(2,1)}, u32[]{:S(2)}) %copy-start.1) | copy-done | bytes 29360152
  99.3 7.3 %backward_products.3 = f32[64,4096]{1,0:T(8,128)S(1)} custom-call(s32[1]{0:T(128)} %bitcast.side_ref, bf16[64,896]{1,0:T(8,128)(2,1)S(1)} %pad_maximum_fusion.6.dg_ref, bf16[64,896]{1,0:T(8,128)(2,1)S(1)} %pad_maximum_fusion.7.du_ref, bf16[8192,1792]{1,0:T(8,128)(2,1)S(1)} %copy-done.1, bf16[8192,1792]{1,0:T(8,128)(2,1)} %wu_ref.5), custom_call_target="tpu_custom_call" | custom-call | flops 939524096 | bytes 14680064 | tf_op jit(solution)/shard_map/backward_products/pallas_call | solution.py:147
  107.2 7.5 %backward_products.2 = f32[64,4096]{1,0:T(8,128)S(1)} custom-call(s32[1]{0:T(128)} %bitcast.side_ref, bf16[64,896]{1,0:T(8,128)(2,1)S(1)} %pad_maximum_fusion.6.dg_ref, bf16[64,896]{1,0:T(8,128)(2,1)S(1)} %pad_maximum_fusion.7.du_ref, bf16[8192,1792]{1,0:T(8,128)(2,1)S(1)} %copy-done.1, bf16[8192,1792]{1,0:T(8,128)(2,1)} %wu_ref.5), custom_call_target="tpu_custom_call" | custom-call | flops 939524096 | bytes 14680064 | tf_op jit(solution)/shard_map/backward_products/pallas_call | solution.py:147
  116.7 1.5 collective-permute-start.29
  118.2 4.2 %convolution_multiply_fusion = f32[1024,1792]{1,0:T(8,128)} fusion(bf16[32,1024]{1,0:T(8,128)(2,1)S(1)} %convert_element_type.183, bf16[2,32,896]{2,1,0:T(8,128)(2,1)S(1)} %get-tuple-element.16, bf16[2,32,896]{2,1,0:T(8,128)(2,1)S(1)} %get-tuple-element.15), kind=kOutput, calls=%fused_computation | convolution fusion | flops 119504896 | bytes 7634944 | tf_op jit(solution)/shard_map/dot_general | solution.py:37
  122.4 3.1 %collective-permute-start.30 = (f32[2,2,4,2,128]{4,3,2,1,0:T(2,128)S(1)}, f32[2,2,4,2,128]{4,3,2,1,0:T(2,128)S(1)}, u32[]{:S(2)}, u32[]{:S(2)}) collective-permute-start(f32[2,2,4,2,128]{4,3,2,1,0:T(2,128)S(1)} %reverse_add_fusion), channel_id=1, source_target_pairs={{0,12},{1,13},{2,14},{3,15},{4,8},{5,9},{6,10},{7,11},{8,4},{9,5},... | collective-permute-start | bytes 49160 | tf_op jit(solution)/shard_map/ppermute | solution.py:168
  125.5 2.6 %collective-permute-done.30 = f32[2,2,4,2,128]{4,3,2,1,0:T(2,128)S(1)} collective-permute-done((f32[2,2,4,2,128]{4,3,2,1,0:T(2,128)S(1)}, f32[2,2,4,2,128]{4,3,2,1,0:T(2,128)S(1)}, u32[]{:S(2)}, u32[]{:S(2)}) %collective-permute-start.30) | collective-permute-done | bytes 16416 | tf_op jit(solution)/shard_map/ppermute | solution.py:168
  130.8 1.7 convert_element_type.211
  132.5 1.6 copy.35
  135.1 1.5 fusion.95
  137.9 4.2 %convolution_multiply_fusion.1 = f32[1024,1792]{1,0:T(8,128)} fusion(bf16[32,1024]{1,0:T(8,128)(2,1)S(1)} %convert_element_type.179, bf16[2,32,896]{2,1,0:T(8,128)(2,1)S(1)} %get-tuple-element.15, bf16[2,32,896]{2,1,0:T(8,128)(2,1)S(1)} %get-tuple-element.16), kind=kOutput, calls=%fused_computation.1 | convolution fusion | flops 119504896 | bytes 7634944 | tf_op jit(solution)/shard_map/dot_general | solution.py:37
  142.2 1.6 collective-permute-start.32
  143.7 2.5 %convolution_multiply_fusion.4 = f32[512,1024]{1,0:T(8,128)} fusion(bf16[32,1024]{1,0:T(8,128)(2,1)S(1)} %copy-done.6, bf16[1,32,8192]{2,1,0:T(8,128)(2,1)} %copy-done.5, s32[]{:T(128)S(6)} %select_n.30), kind=kOutput, calls=%fused_computation.6 | convolution fusion | flops 34078720 | bytes 2195460 | tf_op jit(solution)/shard_map/dot_general | solution.py:37
  146.6 1.7 collective-permute-start.35
  148.3 1.6 collective-permute-start.34
  149.9 2.5 %convolution_multiply_fusion.5 = f32[512,1024]{1,0:T(8,128)} fusion(bf16[32,1024]{1,0:T(8,128)(2,1)S(1)} %convert_element_type.208, bf16[1,32,8192]{2,1,0:T(8,128)(2,1)} %copy-done.5, s32[]{:T(128)S(6)} %select_n.30), kind=kOutput, calls=%fused_computation.7 | convolution fusion | flops 34078720 | bytes 2195460 | tf_op jit(solution)/shard_map/dot_general | solution.py:37
  155.7 1.6 collective-permute-start.14
  157.3 2.8 %collective-permute-done.20 = bf16[16,4096]{1,0:T(8,128)(2,1)S(1)} collective-permute-done((bf16[16,4096]{1,0:T(8,128)(2,1)S(1)}, bf16[16,4096]{1,0:T(8,128)(2,1)S(1)}, u32[]{:S(2)}, u32[]{:S(2)}) %collective-permute-start.20) | collective-permute-done | bytes 131104 | tf_op jit(solution)/shard_map/ppermute | solution.py:172
  162.3 2.1 %collective-permute-done.21 = bf16[8,4096]{1,0:T(8,128)(2,1)S(1)} collective-permute-done((bf16[8,4096]{1,0:T(8,128)(2,1)S(1)}, bf16[8,4096]{1,0:T(8,128)(2,1)S(1)}, u32[]{:S(2)}, u32[]{:S(2)}) %collective-permute-start.21) | collective-permute-done | bytes 65568 | tf_op jit(solution)/shard_map/ppermute | solution.py:168
  164.5 1.2 collective-permute-start.22
  165.7 1.8 %collective-permute-start.24 = (bf16[2,4096]{1,0:T(2,128)(2,1)S(1)}, bf16[2,4096]{1,0:T(2,128)(2,1)S(1)}, u32[]{:S(2)}, u32[]{:S(2)}) collective-permute-start(bf16[2,4096]{1,0:T(2,128)(2,1)S(1)} %get-tuple-element.43), channel_id=1, source_target_pairs={{0,12},{1,13},{2,14},{3,15},{4,8},{5,9},{6,10},{7,11},{8,4},{9,5},... | collective-permute-start | bytes 49160 | tf_op jit(solution)/shard_map/ppermute | solution.py:168
  168.2 2.1 %collective-permute-start.16 = (bf16[2,4096]{1,0:T(2,128)(2,1)S(1)}, bf16[2,4096]{1,0:T(2,128)(2,1)S(1)}, u32[]{:S(2)}, u32[]{:S(2)}) collective-permute-start(bf16[2,4096]{1,0:T(2,128)(2,1)S(1)} %get-tuple-element.39), channel_id=1, source_target_pairs={{0,4},{1,5},{2,6},{3,7},{4,0},{5,1},{6,2},{7,3},{8,12},{9,13},{10,... | collective-permute-start | bytes 49160 | tf_op jit(solution)/shard_map/ppermute | solution.py:168
  170.3 1.8 %collective-permute-start.18 = (bf16[2,4096]{1,0:T(2,128)(2,1)S(1)}, bf16[2,4096]{1,0:T(2,128)(2,1)S(1)}, u32[]{:S(2)}, u32[]{:S(2)}) collective-permute-start(bf16[2,4096]{1,0:T(2,128)(2,1)S(1)} %get-tuple-element.40), channel_id=1, source_target_pairs={{0,12},{1,13},{2,14},{3,15},{4,8},{5,9},{6,10},{7,11},{8,4},{9,5},... | collective-permute-start | bytes 49160 | tf_op jit(solution)/shard_map/ppermute | solution.py:168
  172.2 3.6 %collective-permute-done.18 = bf16[2,4096]{1,0:T(2,128)(2,1)S(1)} collective-permute-done((bf16[2,4096]{1,0:T(2,128)(2,1)S(1)}, bf16[2,4096]{1,0:T(2,128)(2,1)S(1)}, u32[]{:S(2)}, u32[]{:S(2)}) %collective-permute-start.18) | collective-permute-done | bytes 16416 | tf_op jit(solution)/shard_map/ppermute | solution.py:168
  (133 shorter events, 25.4 us)
Async XLA Ops:
  0.6 6.7 %collective-permute-start.2 = (bf16[2,8192]{1,0:T(2,128)(2,1)}, bf16[2,8192]{1,0:T(2,128)(2,1)S(1)}, u32[]{:S(2)}, u32[]{:S(2)}) collective-permute-start(bf16[2,8192]{1,0:T(2,128)(2,1)} %param.9), channel_id=1, source_target_pairs={{0,8},{1,9},{2,10},{3,11},{4,12},{5,13},{6,14},{7,15},{8,0},{9,1},... | collective-permute-start | bytes 98312 | tf_op jit(solution)/shard_map/ppermute | solution.py:168
  4.7 4.1 %collective-permute-start.1 = (bf16[2,8192]{1,0:T(2,128)(2,1)}, bf16[2,8192]{1,0:T(2,128)(2,1)S(1)}, u32[]{:S(2)}, u32[]{:S(2)}) collective-permute-start(bf16[2,8192]{1,0:T(2,128)(2,1)} %param.9), channel_id=1, source_target_pairs={{0,4},{1,5},{2,6},{3,7},{4,0},{5,1},{6,2},{7,3},{8,12},{9,13},{10,... | collective-permute-start | bytes 98312 | tf_op jit(solution)/shard_map/ppermute | solution.py:168
  6.3 5.9 %collective-permute-start.3 = (bf16[2,8192]{1,0:T(2,128)(2,1)}, bf16[2,8192]{1,0:T(2,128)(2,1)S(1)}, u32[]{:S(2)}, u32[]{:S(2)}) collective-permute-start(bf16[2,8192]{1,0:T(2,128)(2,1)} %param.9), channel_id=1, source_target_pairs={{0,12},{1,13},{2,14},{3,15},{4,8},{5,9},{6,10},{7,11},{8,4},{9,5},... | collective-permute-start | bytes 98312 | tf_op jit(solution)/shard_map/ppermute | solution.py:168
  13.1 5.0 %collective-permute-start.4 = (bf16[8,8192]{1,0:T(8,128)(2,1)S(1)}, bf16[8,8192]{1,0:T(8,128)(2,1)S(1)}, u32[]{:S(2)}, u32[]{:S(2)}) collective-permute-start(bf16[8,8192]{1,0:T(8,128)(2,1)S(1)} %get-tuple-element.22), channel_id=1, source_target_pairs={{0,16},{16,0},{1,17},{17,1},{2,18},{18,2},{3,19},{19,3},{4,20},{20... | collective-permute-start | bytes 393224 | tf_op jit(solution)/shard_map/ppermute | solution.py:172
  18.2 18.5 %collective-permute-start.5 = (bf16[2,8,8192]{2,1,0:T(8,128)(2,1)S(1)}, bf16[2,8,8192]{2,1,0:T(8,128)(2,1)S(1)}, u32[]{:S(2)}, u32[]{:S(2)}) collective-permute-start(bf16[2,8,8192]{2,1,0:T(8,128)(2,1)S(1)} %pad_maximum_fusion.2), channel_id=1, source_target_pairs={{0,2},{1,3},{2,0},{3,1},{4,6},{5,7},{6,4},{7,5},{8,10},{9,11},{10,... | collective-permute-start | bytes 786440 | tf_op jit(solution)/shard_map/ppermute | solution.py:168
  20.6 19.7 %collective-permute-start = (bf16[32,896]{1,0:T(8,128)(2,1)S(1)}, bf16[32,896]{1,0:T(8,128)(2,1)S(1)}, u32[]{:S(2)}, u32[]{:S(2)}) collective-permute-start(bf16[32,896]{1,0:T(8,128)(2,1)S(1)} %get-tuple-element.38), channel_id=1, source_target_pairs={{0,16},{16,0},{1,17},{17,1},{2,18},{18,2},{3,19},{19,3},{4,20},{20... | collective-permute-start | bytes 172040 | tf_op jit(solution)/shard_map/ppermute | solution.py:172
  24.0 14.9 %copy-start.4 = (bf16[512,1024]{0,1:T(8,128)(2,1)}, bf16[512,1024]{0,1:T(8,128)(2,1)S(1)}, u32[]{:S(2)}) copy-start(bf16[512,1024]{0,1:T(8,128)(2,1)S(1)} %copy.31) | copy-start | bytes 3145732
  31.4 5.4 %copy-start.7 = (s32[32]{0:T(128)S(1)}, s32[32]{0:T(128)}, u32[]{:S(2)}) copy-start(s32[32]{0:T(128)} %param.16) | copy-start | bytes 388
  36.8 2.0 %collective-permute-start.6 = (bf16[2,16,8192]{2,1,0:T(8,128)(2,1)S(1)}, bf16[2,16,8192]{2,1,0:T(8,128)(2,1)S(1)}, u32[]{:S(2)}, u32[]{:S(2)}) collective-permute-start(bf16[2,16,8192]{2,1,0:T(8,128)(2,1)S(1)} %pad_maximum_fusion.1), channel_id=1, source_target_pairs={{0,1},{1,0},{2,3},{3,2},{4,5},{5,4},{6,7},{7,6},{8,9},{9,8},{10,11... | collective-permute-start | bytes 1572872 | tf_op jit(solution)/shard_map/ppermute | solution.py:168
  38.9 6.4 %copy-start.5 = (bf16[1,32,8192]{2,1,0:T(8,128)(2,1)}, bf16[1,32,8192]{2,1,0:T(8,128)(2,1)S(1)}, u32[]{:S(2)}) copy-start(bf16[1,32,8192]{2,1,0:T(8,128)(2,1)S(1)} %slice.322) | copy-start | bytes 1572868
  40.2 1.2 collective-permute-start.7
  41.4 3.8 %collective-permute-start.8 = (f32[2,2,4,2,128]{4,3,2,1,0:T(2,128)S(1)}, f32[2,2,4,2,128]{4,3,2,1,0:T(2,128)S(1)}, u32[]{:S(2)}, u32[]{:S(2)}) collective-permute-start(f32[2,2,4,2,128]{4,3,2,1,0:T(2,128)S(1)} %reverse_add_fusion.3), channel_id=1, source_target_pairs={{0,2},{1,3},{2,0},{3,1},{4,6},{5,7},{6,4},{7,5},{8,10},{9,11},{10,... | collective-permute-start | bytes 49160 | tf_op jit(solution)/shard_map/ppermute | solution.py:168
  45.2 24.0 %collective-permute-start.10 = (f32[2,2,4,2,128]{4,3,2,1,0:T(2,128)S(1)}, f32[2,2,4,2,128]{4,3,2,1,0:T(2,128)S(1)}, u32[]{:S(2)}, u32[]{:S(2)}) collective-permute-start(f32[2,2,4,2,128]{4,3,2,1,0:T(2,128)S(1)} %reverse_add_fusion.2), channel_id=1, source_target_pairs={{0,8},{1,9},{2,10},{3,11},{4,12},{5,13},{6,14},{7,15},{8,0},{9,1},... | collective-permute-start | bytes 49160 | tf_op jit(solution)/shard_map/ppermute | solution.py:168
  45.3 9.4 %copy-start = (bf16[8192,1792]{1,0:T(8,128)(2,1)S(1)}, bf16[8192,1792]{1,0:T(8,128)(2,1)}, u32[]{:S(2)}) copy-start(bf16[8192,1792]{1,0:T(8,128)(2,1)} %wg_ref.5) | copy-start | bytes 88080384
  65.6 5.6 %collective-permute-start.11 = (f32[2,2,4,2,128]{4,3,2,1,0:T(2,128)S(1)}, f32[2,2,4,2,128]{4,3,2,1,0:T(2,128)S(1)}, u32[]{:S(2)}, u32[]{:S(2)}) collective-permute-start(f32[2,2,4,2,128]{4,3,2,1,0:T(2,128)S(1)} %reverse_add_fusion.2), channel_id=1, source_target_pairs={{0,12},{1,13},{2,14},{3,15},{4,8},{5,9},{6,10},{7,11},{8,4},{9,5},... | collective-permute-start | bytes 49160 | tf_op jit(solution)/shard_map/ppermute | solution.py:168
  67.0 4.2 %collective-permute-start.9 = (f32[2,2,4,2,128]{4,3,2,1,0:T(2,128)S(1)}, f32[2,2,4,2,128]{4,3,2,1,0:T(2,128)S(1)}, u32[]{:S(2)}, u32[]{:S(2)}) collective-permute-start(f32[2,2,4,2,128]{4,3,2,1,0:T(2,128)S(1)} %reverse_add_fusion.2), channel_id=1, source_target_pairs={{0,4},{1,5},{2,6},{3,7},{4,0},{5,1},{6,2},{7,3},{8,12},{9,13},{10,... | collective-permute-start | bytes 49160 | tf_op jit(solution)/shard_map/ppermute | solution.py:168
  71.9 3.1 %copy-start.2 = (bf16[1024,1792]{1,0:T(8,128)(2,1)S(1)}, bf16[1024,1792]{1,0:T(8,128)(2,1)}, u32[]{:S(2)}) copy-start(bf16[1024,1792]{1,0:T(8,128)(2,1)} %convert_element_type.184) | copy-start | bytes 11010052
  75.8 10.5 %copy-start.3 = (bf16[1024,1792]{1,0:T(8,128)(2,1)S(1)}, bf16[1024,1792]{1,0:T(8,128)(2,1)}, u32[]{:S(2)}) copy-start(bf16[1024,1792]{1,0:T(8,128)(2,1)} %convert_element_type.180) | copy-start | bytes 11010052
  75.9 5.3 %collective-permute-start.12 = (bf16[2,32,896]{2,1,0:T(8,128)(2,1)S(1)}, bf16[2,32,896]{2,1,0:T(8,128)(2,1)S(1)}, u32[]{:S(2)}, u32[]{:S(2)}) collective-permute-start(bf16[2,32,896]{2,1,0:T(8,128)(2,1)S(1)} %fusion.9), channel_id=1, source_target_pairs={{0,16},{16,0},{1,17},{17,1},{2,18},{18,2},{3,19},{19,3},{4,20},{20... | collective-permute-start | bytes 344072 | tf_op jit(solution)/shard_map/ppermute | solution.py:172
  81.4 4.9 %collective-permute-start.25 = (bf16[2,32,896]{2,1,0:T(8,128)(2,1)S(1)}, bf16[2,32,896]{2,1,0:T(8,128)(2,1)S(1)}, u32[]{:S(2)}, u32[]{:S(2)}) collective-permute-start(bf16[2,32,896]{2,1,0:T(8,128)(2,1)S(1)} %pad_maximum_fusion.9), channel_id=1, source_target_pairs={{0,16},{16,0},{1,17},{17,1},{2,18},{18,2},{3,19},{19,3},{4,20},{20... | collective-permute-start | bytes 344072 | tf_op jit(solution)/shard_map/ppermute | solution.py:172
  89.9 16.7 %collective-permute-start.26 = (f32[2,2,4,2,128]{4,3,2,1,0:T(2,128)S(1)}, f32[2,2,4,2,128]{4,3,2,1,0:T(2,128)S(1)}, u32[]{:S(2)}, u32[]{:S(2)}) collective-permute-start(f32[2,2,4,2,128]{4,3,2,1,0:T(2,128)S(1)} %bitcast.139), channel_id=1, source_target_pairs={{0,1},{1,0},{2,3},{3,2},{4,5},{5,4},{6,7},{7,6},{8,9},{9,8},{10,11... | collective-permute-start | bytes 49160 | tf_op jit(solution)/shard_map/ppermute | solution.py:168
  89.9 9.4 %copy-start.1 = (bf16[8192,1792]{1,0:T(8,128)(2,1)S(1)}, bf16[8192,1792]{1,0:T(8,128)(2,1)}, u32[]{:S(2)}) copy-start(bf16[8192,1792]{1,0:T(8,128)(2,1)} %wg_ref.5) | copy-start | bytes 88080384
  106.6 10.0 %collective-permute-start.27 = (f32[2,2,4,2,128]{4,3,2,1,0:T(2,128)S(1)}, f32[2,2,4,2,128]{4,3,2,1,0:T(2,128)S(1)}, u32[]{:S(2)}, u32[]{:S(2)}) collective-permute-start(f32[2,2,4,2,128]{4,3,2,1,0:T(2,128)S(1)} %reverse_add_fusion.1), channel_id=1, source_target_pairs={{0,2},{1,3},{2,0},{3,1},{4,6},{5,7},{6,4},{7,5},{8,10},{9,11},{10,... | collective-permute-start | bytes 49160 | tf_op jit(solution)/shard_map/ppermute | solution.py:168
  115.4 37.7 %collective-permute-start.19 = (bf16[32,4096]{1,0:T(8,128)(2,1)}, bf16[32,4096]{1,0:T(8,128)(2,1)}, u32[]{:S(2)}, u32[]{:S(2)}) collective-permute-start(bf16[32,4096]{1,0:T(8,128)(2,1)} %slice.491), channel_id=1, source_target_pairs={{0,1},{1,0},{2,3},{3,2},{4,5},{5,4},{6,7},{7,6},{8,9},{9,8},{10,11... | collective-permute-start | bytes 786440 | tf_op jit(solution)/shard_map/ppermute | solution.py:168
  116.3 38.3 %collective-permute-start.13 = (bf16[32,4096]{1,0:T(8,128)(2,1)}, bf16[32,4096]{1,0:T(8,128)(2,1)}, u32[]{:S(2)}, u32[]{:S(2)}) collective-permute-start(bf16[32,4096]{1,0:T(8,128)(2,1)} %slice.492), channel_id=1, source_target_pairs={{0,1},{1,0},{2,3},{3,2},{4,5},{5,4},{6,7},{7,6},{8,9},{9,8},{10,11... | collective-permute-start | bytes 786440 | tf_op jit(solution)/shard_map/ppermute | solution.py:168
  116.7 8.8 %collective-permute-start.29 = (f32[2,2,4,2,128]{4,3,2,1,0:T(2,128)S(1)}, f32[2,2,4,2,128]{4,3,2,1,0:T(2,128)S(1)}, u32[]{:S(2)}, u32[]{:S(2)}) collective-permute-start(f32[2,2,4,2,128]{4,3,2,1,0:T(2,128)S(1)} %reverse_add_fusion), channel_id=1, source_target_pairs={{0,8},{1,9},{2,10},{3,11},{4,12},{5,13},{6,14},{7,15},{8,0},{9,1},... | collective-permute-start | bytes 49160 | tf_op jit(solution)/shard_map/ppermute | solution.py:168
  122.4 5.6 %collective-permute-start.30 = (f32[2,2,4,2,128]{4,3,2,1,0:T(2,128)S(1)}, f32[2,2,4,2,128]{4,3,2,1,0:T(2,128)S(1)}, u32[]{:S(2)}, u32[]{:S(2)}) collective-permute-start(f32[2,2,4,2,128]{4,3,2,1,0:T(2,128)S(1)} %reverse_add_fusion), channel_id=1, source_target_pairs={{0,12},{1,13},{2,14},{3,15},{4,8},{5,9},{6,10},{7,11},{8,4},{9,5},... | collective-permute-start | bytes 49160 | tf_op jit(solution)/shard_map/ppermute | solution.py:168
  125.5 3.7 %collective-permute-start.28 = (f32[2,2,4,2,128]{4,3,2,1,0:T(2,128)S(1)}, f32[2,2,4,2,128]{4,3,2,1,0:T(2,128)S(1)}, u32[]{:S(2)}, u32[]{:S(2)}) collective-permute-start(f32[2,2,4,2,128]{4,3,2,1,0:T(2,128)S(1)} %reverse_add_fusion), channel_id=1, source_target_pairs={{0,4},{1,5},{2,6},{3,7},{4,0},{5,1},{6,2},{7,3},{8,12},{9,13},{10,... | collective-permute-start | bytes 49160 | tf_op jit(solution)/shard_map/ppermute | solution.py:168
  137.8 5.9 %copy-start.6 = (bf16[32,1024]{1,0:T(8,128)(2,1)S(1)}, bf16[32,1024]{1,0:T(8,128)(2,1)}, u32[]{:S(2)}) copy-start(bf16[32,1024]{1,0:T(8,128)(2,1)} %convert_element_type.211) | copy-start | bytes 196612
  137.8 4.3 %collective-permute-start.31 = (bf16[2,4,2,512]{3,2,1,0:T(2,128)(2,1)S(1)}, bf16[2,4,2,512]{3,2,1,0:T(2,128)(2,1)S(1)}, u32[]{:S(2)}, u32[]{:S(2)}) collective-permute-start(bf16[2,4,2,512]{3,2,1,0:T(2,128)(2,1)S(1)} %squeeze.35), channel_id=1, source_target_pairs={{0,1},{1,0},{2,3},{3,2},{4,5},{5,4},{6,7},{7,6},{8,9},{9,8},{10,11... | collective-permute-start | bytes 49160 | tf_op jit(solution)/shard_map/ppermute | solution.py:168
  142.2 4.1 %collective-permute-start.32 = (bf16[2,4,2,512]{3,2,1,0:T(2,128)(2,1)S(1)}, bf16[2,4,2,512]{3,2,1,0:T(2,128)(2,1)S(1)}, u32[]{:S(2)}, u32[]{:S(2)}) collective-permute-start(bf16[2,4,2,512]{3,2,1,0:T(2,128)(2,1)S(1)} %get-tuple-element.50), channel_id=1, source_target_pairs={{0,2},{1,3},{2,0},{3,1},{4,6},{5,7},{6,4},{7,5},{8,10},{9,11},{10,... | collective-permute-start | bytes 49160 | tf_op jit(solution)/shard_map/ppermute | solution.py:168
  146.3 6.1 %collective-permute-start.33 = (bf16[2,2,2,512]{3,2,1,0:T(2,128)(2,1)S(1)}, bf16[2,2,2,512]{3,2,1,0:T(2,128)(2,1)S(1)}, u32[]{:S(2)}, u32[]{:S(2)}) collective-permute-start(bf16[2,2,2,512]{3,2,1,0:T(2,128)(2,1)S(1)} %get-tuple-element.46), channel_id=1, source_target_pairs={{0,4},{1,5},{2,6},{3,7},{4,0},{5,1},{6,2},{7,3},{8,12},{9,13},{10,... | collective-permute-start | bytes 24584 | tf_op jit(solution)/shard_map/ppermute | solution.py:168
  146.6 5.9 %collective-permute-start.35 = (bf16[2,2,2,512]{3,2,1,0:T(2,128)(2,1)S(1)}, bf16[2,2,2,512]{3,2,1,0:T(2,128)(2,1)S(1)}, u32[]{:S(2)}, u32[]{:S(2)}) collective-permute-start(bf16[2,2,2,512]{3,2,1,0:T(2,128)(2,1)S(1)} %get-tuple-element.47), channel_id=1, source_target_pairs={{0,12},{1,13},{2,14},{3,15},{4,8},{5,9},{6,10},{7,11},{8,4},{9,5},... | collective-permute-start | bytes 24584 | tf_op jit(solution)/shard_map/ppermute | solution.py:168
  148.3 4.5 %collective-permute-start.34 = (bf16[2,2,2,512]{3,2,1,0:T(2,128)(2,1)S(1)}, bf16[2,2,2,512]{3,2,1,0:T(2,128)(2,1)S(1)}, u32[]{:S(2)}, u32[]{:S(2)}) collective-permute-start(bf16[2,2,2,512]{3,2,1,0:T(2,128)(2,1)S(1)} %get-tuple-element.48), channel_id=1, source_target_pairs={{0,8},{1,9},{2,10},{3,11},{4,12},{5,13},{6,14},{7,15},{8,0},{9,1},... | collective-permute-start | bytes 24584 | tf_op jit(solution)/shard_map/ppermute | solution.py:168
  154.1 6.0 %collective-permute-start.20 = (bf16[16,4096]{1,0:T(8,128)(2,1)S(1)}, bf16[16,4096]{1,0:T(8,128)(2,1)S(1)}, u32[]{:S(2)}, u32[]{:S(2)}) collective-permute-start(bf16[16,4096]{1,0:T(8,128)(2,1)S(1)} %slice.493), channel_id=1, source_target_pairs={{0,16},{16,0},{1,17},{17,1},{2,18},{18,2},{3,19},{19,3},{4,20},{20... | collective-permute-start | bytes 393224 | tf_op jit(solution)/shard_map/ppermute | solution.py:172
  155.7 5.8 %collective-permute-start.14 = (bf16[16,4096]{1,0:T(8,128)(2,1)S(1)}, bf16[16,4096]{1,0:T(8,128)(2,1)S(1)}, u32[]{:S(2)}, u32[]{:S(2)}) collective-permute-start(bf16[16,4096]{1,0:T(8,128)(2,1)S(1)} %slice.494), channel_id=1, source_target_pairs={{0,16},{16,0},{1,17},{17,1},{2,18},{18,2},{3,19},{19,3},{4,20},{20... | collective-permute-start | bytes 393224 | tf_op jit(solution)/shard_map/ppermute | solution.py:172
  160.1 4.3 %collective-permute-start.21 = (bf16[8,4096]{1,0:T(8,128)(2,1)S(1)}, bf16[8,4096]{1,0:T(8,128)(2,1)S(1)}, u32[]{:S(2)}, u32[]{:S(2)}) collective-permute-start(bf16[8,4096]{1,0:T(8,128)(2,1)S(1)} %slice.495), channel_id=1, source_target_pairs={{0,2},{1,3},{2,0},{3,1},{4,6},{5,7},{6,4},{7,5},{8,10},{9,11},{10,... | collective-permute-start | bytes 196616 | tf_op jit(solution)/shard_map/ppermute | solution.py:168
  161.5 6.6 %collective-permute-start.15 = (bf16[8,4096]{1,0:T(8,128)(2,1)S(1)}, bf16[8,4096]{1,0:T(8,128)(2,1)S(1)}, u32[]{:S(2)}, u32[]{:S(2)}) collective-permute-start(bf16[8,4096]{1,0:T(8,128)(2,1)S(1)} %slice.496), channel_id=1, source_target_pairs={{0,2},{1,3},{2,0},{3,1},{4,6},{5,7},{6,4},{7,5},{8,10},{9,11},{10,... | collective-permute-start | bytes 196616 | tf_op jit(solution)/shard_map/ppermute | solution.py:168
  164.5 7.6 %collective-permute-start.22 = (bf16[2,4096]{1,0:T(2,128)(2,1)S(1)}, bf16[2,4096]{1,0:T(2,128)(2,1)S(1)}, u32[]{:S(2)}, u32[]{:S(2)}) collective-permute-start(bf16[2,4096]{1,0:T(2,128)(2,1)S(1)} %get-tuple-element.42), channel_id=1, source_target_pairs={{0,4},{1,5},{2,6},{3,7},{4,0},{5,1},{6,2},{7,3},{8,12},{9,13},{10,... | collective-permute-start | bytes 49160 | tf_op jit(solution)/shard_map/ppermute | solution.py:168
  165.7 6.4 %collective-permute-start.24 = (bf16[2,4096]{1,0:T(2,128)(2,1)S(1)}, bf16[2,4096]{1,0:T(2,128)(2,1)S(1)}, u32[]{:S(2)}, u32[]{:S(2)}) collective-permute-start(bf16[2,4096]{1,0:T(2,128)(2,1)S(1)} %get-tuple-element.43), channel_id=1, source_target_pairs={{0,12},{1,13},{2,14},{3,15},{4,8},{5,9},{6,10},{7,11},{8,4},{9,5},... | collective-permute-start | bytes 49160 | tf_op jit(solution)/shard_map/ppermute | solution.py:168
  167.6 4.6 %collective-permute-start.23 = (bf16[2,4096]{1,0:T(2,128)(2,1)S(1)}, bf16[2,4096]{1,0:T(2,128)(2,1)S(1)}, u32[]{:S(2)}, u32[]{:S(2)}) collective-permute-start(bf16[2,4096]{1,0:T(2,128)(2,1)S(1)} %get-tuple-element.44), channel_id=1, source_target_pairs={{0,8},{1,9},{2,10},{3,11},{4,12},{5,13},{6,14},{7,15},{8,0},{9,1},... | collective-permute-start | bytes 49160 | tf_op jit(solution)/shard_map/ppermute | solution.py:168
  168.2 4.1 %collective-permute-start.16 = (bf16[2,4096]{1,0:T(2,128)(2,1)S(1)}, bf16[2,4096]{1,0:T(2,128)(2,1)S(1)}, u32[]{:S(2)}, u32[]{:S(2)}) collective-permute-start(bf16[2,4096]{1,0:T(2,128)(2,1)S(1)} %get-tuple-element.39), channel_id=1, source_target_pairs={{0,4},{1,5},{2,6},{3,7},{4,0},{5,1},{6,2},{7,3},{8,12},{9,13},{10,... | collective-permute-start | bytes 49160 | tf_op jit(solution)/shard_map/ppermute | solution.py:168
  170.3 5.5 %collective-permute-start.18 = (bf16[2,4096]{1,0:T(2,128)(2,1)S(1)}, bf16[2,4096]{1,0:T(2,128)(2,1)S(1)}, u32[]{:S(2)}, u32[]{:S(2)}) collective-permute-start(bf16[2,4096]{1,0:T(2,128)(2,1)S(1)} %get-tuple-element.40), channel_id=1, source_target_pairs={{0,12},{1,13},{2,14},{3,15},{4,8},{5,9},{6,10},{7,11},{8,4},{9,5},... | collective-permute-start | bytes 49160 | tf_op jit(solution)/shard_map/ppermute | solution.py:168
  172.1 4.6 %collective-permute-start.17 = (bf16[2,4096]{1,0:T(2,128)(2,1)S(1)}, bf16[2,4096]{1,0:T(2,128)(2,1)S(1)}, u32[]{:S(2)}, u32[]{:S(2)}) collective-permute-start(bf16[2,4096]{1,0:T(2,128)(2,1)S(1)} %get-tuple-element.41), channel_id=1, source_target_pairs={{0,8},{1,9},{2,10},{3,11},{4,12},{5,13},{6,14},{7,15},{8,0},{9,1},... | collective-permute-start | bytes 49160 | tf_op jit(solution)/shard_map/ppermute | solution.py:168

commit v2 on v0

--- a/solution.py
+++ b/solution.py
@@ -1,13 +1,16 @@
 import jax
 import jax.numpy as jnp
 from jax import lax
+from jax.experimental import pallas as pl
+from jax.experimental.pallas import tpu as pltpu
 from jax.sharding import PartitionSpec as P
 
 R = 64
 AG = 16
 
-
 adapter_scale = 2.0
+BF16 = jnp.bfloat16
+F32 = jnp.float32
 
 
 def agent_mask(agent):
@@ -30,7 +33,13 @@
     )
 
 
-def per_device(tokens, gate_weight, up_weight, a_gate, a_up, b_gate, b_up, agent, d_hidden):
+def rows_product(left, right):
+    return lax.dot_general(
+        left, right, (((0,), (0,)), ((), ())), preferred_element_type=jnp.float32
+    )
+
+
+def plain_device(tokens, gate_weight, up_weight, a_gate, a_up, b_gate, b_up, agent, d_hidden):
     onehot = agent_mask(agent)
     feat_rows = a_gate.shape[0]
     feat_start = lax.axis_index("tensor") * feat_rows
@@ -80,18 +89,10 @@
         scatter_dimension=0,
         tiled=True,
     ).astype(jnp.bfloat16)
-    gate_down_gradient = adapter_scale * lax.dot_general(
-        own_cols, gate_factor_gate, (((0,), (0,)), ((), ())), preferred_element_type=jnp.float32
-    )
-    up_down_gradient = adapter_scale * lax.dot_general(
-        own_cols, gate_factor_up, (((0,), (0,)), ((), ())), preferred_element_type=jnp.float32
-    )
-    gate_lift_gradient = adapter_scale * lax.dot_general(
-        up_factor_gate, gate_gradient, (((0,), (0,)), ((), ())), preferred_element_type=jnp.float32
-    )
-    up_lift_gradient = adapter_scale * lax.dot_general(
-        up_factor_up, up_gradient, (((0,), (0,)), ((), ())), preferred_element_type=jnp.float32
-    )
+    gate_down_gradient = adapter_scale * rows_product(own_cols, gate_factor_gate)
+    up_down_gradient = adapter_scale * rows_product(own_cols, gate_factor_up)
+    gate_lift_gradient = adapter_scale * rows_product(up_factor_gate, gate_gradient)
+    up_lift_gradient = adapter_scale * rows_product(up_factor_up, up_gradient)
     return (
         token_gradient,
         gate_down_gradient,
@@ -101,7 +102,237 @@
     )
 
 
+def forward_kernel(x_ref, wg_ref, wu_ref, g0_ref, u0_ref, g_ref, u_ref):
+    @pl.when(pl.program_id(0) == 0)
+    def _():
+        g_ref[...] = g0_ref[...]
+        u_ref[...] = u0_ref[...]
+
+    x = x_ref[...]
+    g_ref[...] += jnp.dot(x, wg_ref[...], preferred_element_type=F32)
+    u_ref[...] += jnp.dot(x, wu_ref[...], preferred_element_type=F32)
+
+
+def forward_products(x, gate_weight, up_weight, so_far, first, count, depth=512):
+    rows = x.shape[0]
+    ff = gate_weight.shape[1]
+    start = first // depth
+    weight_block = pl.BlockSpec((depth, ff), lambda k: (k + start, 0))
+    out_block = pl.BlockSpec((rows, ff), lambda k: (0, 0))
+    return pl.pallas_call(
+        forward_kernel,
+        grid=(count // depth,),
+        in_specs=[
+            pl.BlockSpec((rows, depth), lambda k: (0, k + start)),
+            weight_block,
+            weight_block,
+            out_block,
+            out_block,
+        ],
+        out_specs=[out_block, out_block],
+        out_shape=[jax.ShapeDtypeStruct((rows, ff), F32)] * 2,
+        compiler_params=pltpu.CompilerParams(vmem_limit_bytes=40 << 20),
+        cost_estimate=pl.CostEstimate(
+            flops=4 * rows * count * ff, bytes_accessed=4 * count * ff, transcendentals=0
+        ),
+        name="forward_products",
+    )(x, gate_weight, up_weight, *so_far)
+
+
+def backward_kernel(dgt_ref, dut_ref, wg_ref, wu_ref, keep_ref, send_ref):
+    total = jnp.dot(wg_ref[...], dgt_ref[...], preferred_element_type=F32)
+    total += jnp.dot(wu_ref[...], dut_ref[...], preferred_element_type=F32)
+    flat = total.T
+    half = keep_ref.shape[0]
+    keep_ref[...] = flat[:half]
+    send_ref[...] = flat[half:].astype(send_ref.dtype)
+
+
+def backward_products(dgt, dut, gate_weight, up_weight, first, count, depth=256):
+    ff, rows = dgt.shape
+    start = first // depth
+    weight_block = pl.BlockSpec((depth, ff), lambda k: (k + start, 0))
+    right_block = pl.BlockSpec((ff, rows), lambda k: (0, 0))
+    out_block = pl.BlockSpec((rows // 2, depth), lambda k: (0, k))
+    return pl.pallas_call(
+        backward_kernel,
+        grid=(count // depth,),
+        in_specs=[right_block, right_block, weight_block, weight_block],
+        out_specs=[out_block, out_block],
+        out_shape=[
+            jax.ShapeDtypeStruct((rows // 2, count), F32),
+            jax.ShapeDtypeStruct((rows // 2, count), BF16),
+        ],
+        compiler_params=pltpu.CompilerParams(vmem_limit_bytes=40 << 20),
+        cost_estimate=pl.CostEstimate(
+            flops=4 * rows * count * ff, bytes_accessed=4 * count * ff, transcendentals=0
+        ),
+        name="backward_products",
+    )(dgt, dut, gate_weight, up_weight)
+
+
+N = 16
+
+
+def along_tensor(value, mask):
+    return lax.ppermute(value, "tensor", [(i, i ^ mask) for i in range(N)])
+
+
+SLOTS = 4
+
+
+def summed(value, recv, slot):
+    shape = value.shape
+    v, r = (w.reshape(2, 2, 2, 2, 2, shape[1]) for w in (value, recv))
+    r = (r[::-1], r[:, ::-1], r[:, :, :, ::-1], r[:, :, ::-1])[slot]
+    return (v + r).reshape(shape)
+
+
+def in_order(*values):
+    return lax.optimization_barrier(values)
+
+
+def staged_device(tokens, gate_weight, up_weight, a_gate, a_up, b_gate, b_up, agent, d_hidden):
+    t = lax.axis_index("tensor")
+    d = tokens.shape[1]
+    feat_rows = a_gate.shape[0]
+    feat_start = t * feat_rows
+
+    x = jnp.concatenate([tokens] + [along_tensor(tokens, 4 * m) for m in (1, 2, 3)], axis=0)
+    x = jnp.concatenate([x, along_tensor(x, 2)], axis=0)
+    x = jnp.concatenate([x, along_tensor(x, 1)], axis=0)
+    rows = x.shape[0]
+
+    place = jnp.arange(rows, dtype=jnp.int32)
+    block = ((place >> 1) & 3) * 4 + ((place >> 3) & 1) * 2 + (place >> 4)
+    token_of = ((t ^ block) << 1) + (place & 1)
+    shuffle = token_of[:, None] == jnp.arange(rows, dtype=jnp.int32)[None, :]
+    agent_here = jnp.sum(jnp.where(shuffle, agent[None, :], 0), axis=1)
+    onehot = agent_mask(agent_here)
+    hidden_grad = jnp.dot(shuffle.astype(BF16), d_hidden, preferred_element_type=F32)
+
+    agent_gate_down = a_gate.astype(BF16)
+    agent_up_down = a_up.astype(BF16)
+    agent_gate_lift = b_gate.astype(BF16)
+    agent_up_lift = b_up.astype(BF16)
+
+    own_cols = lax.dynamic_slice_in_dim(x, feat_start, feat_rows, 1)
+    part_gate = select_rank(jnp.dot(own_cols, agent_gate_down, preferred_element_type=F32), onehot)
+    part_up = select_rank(jnp.dot(own_cols, agent_up_down, preferred_element_type=F32), onehot)
+    part = jnp.concatenate([part_gate, part_up], axis=1)
+    base = [jnp.zeros((rows, gate_weight.shape[1]), F32)] * 2
+    count = d // SLOTS
+    for slot in range(SLOTS):
+        recv = along_tensor(part, 1 << slot)
+        base = forward_products(x, gate_weight, up_weight, base, slot * count, count)
+        recv, part, *base = in_order(recv, part, *base)
+        part = summed(part, recv, slot)
+    u = part.astype(BF16)
+    up_factor_gate = spread_rank(u[:, :R], onehot)
+    up_factor_up = spread_rank(u[:, R:], onehot)
+
+    gate_values = base[0] + adapter_scale * jnp.dot(
+        up_factor_gate, agent_gate_lift, preferred_element_type=F32
+    )
+    up_values = base[1] + adapter_scale * jnp.dot(
+        up_factor_up, agent_up_lift, preferred_element_type=F32
+    )
+    sig = jax.nn.sigmoid(gate_values)
+    gate_gradient = (hidden_grad * up_values * sig * (1.0 + gate_values * (1.0 - sig))).astype(BF16)
+    up_gradient = (hidden_grad * gate_values * sig).astype(BF16)
+
+    pg_gate = select_rank(flipped_product(gate_gradient, agent_gate_lift), onehot)
+    pg_up = select_rank(flipped_product(up_gradient, agent_up_lift), onehot)
+    part = jnp.concatenate([pg_gate, pg_up], axis=1)
+    dgt, dut = gate_gradient.T, up_gradient.T
+    kept, leave = [], []
+    first_half = None
+    for slot in range(SLOTS):
+        recv = along_tensor(part, 1 << slot)
+        if slot == 2:
+            first_half = along_tensor(jnp.concatenate(leave, axis=1), 1)
+        if slot == 3:
+            first_half = jnp.concatenate(kept[:2], axis=1) + first_half.astype(F32)
+            travel = along_tensor(first_half[rows // 4 :].astype(BF16), 2)
+        keep, out = backward_products(dgt, dut, gate_weight, up_weight, slot * count, count)
+        kept.append(keep)
+        leave.append(out)
+        if slot == 2:
+            recv, part, dgt, dut, keep, first_half = in_order(recv, part, dgt, dut, keep, first_half)
+        elif slot == 3:
+            recv, part, travel = in_order(recv, part, travel)
+        else:
+            recv, part, dgt, dut = in_order(recv, part, dgt, dut)
+        part = summed(part, recv, slot)
+    first_half = first_half[: rows // 4] + travel.astype(F32)
+    g = part.astype(BF16)
+    gate_factor_gate = spread_rank(g[:, :R], onehot)
+    gate_factor_up = spread_rank(g[:, R:], onehot)
+    adapter_contribution = (
+        adapter_scale
+        * (
+            flipped_product(gate_factor_gate, agent_gate_down)
+            + flipped_product(gate_factor_up, agent_up_down)
+        )
+    ).astype(BF16)
+
+    width = 2 * count
+    sums = jnp.concatenate(kept[2:], axis=1)
+    q = rows // 2
+    recv = along_tensor(
+        jnp.concatenate([*leave[2:], adapter_contribution[q:]], axis=1), 1
+    )
+    z_parts = [along_tensor(first_half[2 * m : 2 * m + 2].astype(BF16), 4 * m) for m in (1, 2, 3)]
+    gate_lift_gradient = adapter_scale * rows_product(up_factor_gate, gate_gradient)
+    recv, gate_lift_gradient, *z_parts = in_order(recv, gate_lift_gradient, *z_parts)
+    first_half = first_half[:2] + sum(p.astype(F32) for p in z_parts)
+    sums = sums + recv[:, :width].astype(F32)
+    moved = jnp.concatenate([adapter_contribution[:q], recv[:, width:]], axis=1)
+
+    q = rows // 4
+    recv = along_tensor(jnp.concatenate([sums[q:].astype(BF16), moved[q:]], axis=1), 2)
+    up_lift_gradient = adapter_scale * rows_product(up_factor_up, up_gradient)
+    recv, up_lift_gradient = in_order(recv, up_lift_gradient)
+    sums = sums[:q] + recv[:, :width].astype(F32)
+    moved = jnp.concatenate([moved[:q], recv[:, width:]], axis=1)
+
+    last = jnp.concatenate([sums.astype(BF16), moved], axis=1)
+    z_parts = [along_tensor(last[2 * m : 2 * m + 2], 4 * m) for m in (1, 2, 3)]
+    gate_down_gradient = adapter_scale * rows_product(own_cols, gate_factor_gate)
+    up_down_gradient = adapter_scale * rows_product(own_cols, gate_factor_up)
+    gate_down_gradient, up_down_gradient, *z_parts = in_order(
+        gate_down_gradient, up_down_gradient, *z_parts
+    )
+    sums = sums[:2] + sum(p[:, :width].astype(F32) for p in z_parts)
+    moved = jnp.stack([moved[:2]] + [p[:, width:] for p in z_parts])
+    moved = moved.reshape(4, 2, 2, 2, feat_rows).transpose(0, 2, 3, 1, 4).reshape(N, 2 * feat_rows)
+    source = jnp.arange(N, dtype=jnp.int32)
+    sort = (source[:, None] == (t ^ source)[None, :]).astype(BF16)
+    sorted_rows = jnp.dot(sort, moved, preferred_element_type=F32).reshape(N, 2, feat_rows)
+    contribution = sorted_rows.transpose(1, 0, 2).reshape(2, d)
+    token_gradient = (jnp.concatenate([first_half, sums], axis=1) + contribution).astype(BF16)
+    return (
+        token_gradient,
+        gate_down_gradient,
+        up_down_gradient,
+        gate_lift_gradient,
+        up_lift_gradient,
+    )
+
+
 def solution(mesh):
+    sizes = dict(mesh.shape)
+
+    def per_device(*args):
+        tokens, b_gate = args[0], args[5]
+        fits = (
+            sizes["tensor"] == N
+            and tokens.shape[0] == 2
+            and b_gate.shape[1] % 128 == 0
+            and tokens.shape[1] % 2048 == 0
+        )
+        return (staged_device if fits else plain_device)(*args)
+
     in_specs = (
         P(("group", "tensor"), None),
         P(None, "tensor"),

time: 306 us -> 150 us (0.49)
  blocking collectives: 210 us -> 0 us
  Pallas kernels: 0 us -> 66.4 us
  matrix products: 88.2 us -> 31.6 us
  starting transfers between devices: 0 us -> 26.4 us
  waiting for transfers between devices: 0 us -> 14.9 us
  other arithmetic: 1.39 us -> 4.92 us
    psum x2 -> x0, blocking collectives: 116 us -> none  [the longest x1 57.9 us: per_device(): u_gate, u_up = lax.psum((part_gate, part_up), 'tensor')]
    unnamed x1 -> x0, blocking collectives: 69.9 us -> none
    pallas_call x0 -> x8, Pallas kernels: none -> 66.4 us  [the longest x4 38.7 us: backward_products(): pl.pallas_call(backward_kernel, grid=(count // depth,), in_specs=[right_b...]
    dot_general x6 -> x4, matrix products: 39 us -> 6.47 us  [flipped_product(): lax.dot_general(left, weight, (((1,), (1,)), ((), ())), preferred_element...]
    ppermute x0 -> x23, starting transfers between devices: none -> 26.4 us  [along_tensor(): return lax.ppermute(value, 'tensor', [(i, i ^ mask) for i in range(N)])]
    all_gather x1 -> x0, blocking collectives: 24.8 us -> none  [per_device(): complete_result = lax.all_gather(tokens, 'tensor', axis=0, tiled=True)]
    dot_general x10, matrix products: 49.2 us -> 25.1 us  [the longest x4 12 us: rows_product(): lax.dot_general(left, right, (((0,), (0,)), ((), ())), preferred_element_...]
    ppermute x0 -> x23, waiting for transfers between devices: none -> 14.9 us  [along_tensor(): return lax.ppermute(value, 'tensor', [(i, i ^ mask) for i in range(N)])]
  transfers between devices with their start and end apart: 0 -> 23, of which waited for: 0 -> 6; matrix products, arithmetic and copies ran while one was open for 0% -> 7% of each run, Pallas kernels for 0% -> 44%
where the time goes in v2:
time: 150 us; the launch traced here: 149 us
  Pallas kernels  66.4 us (44%)
  matrix products  31.6 us (21%)
  starting transfers between devices  26.4 us (18%)
  waiting for transfers between devices  14.9 us (10%)
  other arithmetic  4.92 us (3%)
  local copies, waits for them, and re-layouts  3.85 us (3%)
    pallas_call x4, Pallas kernels, backward_products(): pl.pallas_call(backward_kernel, grid=(count // depth,), in_specs=[right_b...  38.7 us
    pallas_call x4, Pallas kernels, forward_products(): pl.pallas_call(forward_kernel, grid=(count // depth,), in_specs=[pl.Block...  27.7 us
    ppermute x23, starting transfers between devices, along_tensor(): return lax.ppermute(value, 'tensor', [(i, i ^ mask) for i in range(N)])  26.4 us
    ppermute x23, waiting for transfers between devices, along_tensor(): return lax.ppermute(value, 'tensor', [(i, i ^ mask) for i in range(N)])  14.9 us
    dot_general x4, matrix products, rows_product(): lax.dot_general(left, right, (((0,), (0,)), ((), ())), preferred_element_...  12 us
    dot_general x4, matrix products, flipped_product(): lax.dot_general(left, weight, (((1,), (1,)), ((), ())), preferred_element...  6.47 us
    dot_general x1, matrix products, staged_device(): jnp.dot(up_factor_up, agent_up_lift, preferred_element_type=F32)  4.78 us
    dot_general x1, matrix products, staged_device(): jnp.dot(up_factor_gate, agent_gate_lift, preferred_element_type=F32)  4.78 us
  transfers between devices with their start and end apart: 23, of which 6 were waited for; matrix products, arithmetic and copies ran while one was open for 7% of the time, Pallas kernels for 44%

profile of v2, /device:TPU:0, one launch (start us, length us, event | category | flops | bytes accessed | tf_op | source)
XLA Modules:
  0.0 149.4 jit_solution(15037686031851165908)
XLA Ops:
  0.7 3.1 %collective-permute-start = (bf16[2,8192]{1,0:T(2,128)(2,1)}, bf16[2,8192]{1,0:T(2,128)(2,1)S(1)}, u32[]{:S(2)}, u32[]{:S(2)}) collective-permute-start(bf16[2,8192]{1,0:T(2,128)(2,1)} %param.9), channel_id=1, source_target_pairs={{0,4},{1,5},{2,6},{3,7},{4,0},{5,1},{6,2},{7,3},{8,12},{9,13},{10,... | collective-permute-start | bytes 98312 | tf_op jit(solution)/shard_map/ppermute | solution.py:178
  3.7 2.6 %collective-permute-start.1 = (bf16[2,8192]{1,0:T(2,128)(2,1)}, bf16[2,8192]{1,0:T(2,128)(2,1)S(1)}, u32[]{:S(2)}, u32[]{:S(2)}) collective-permute-start(bf16[2,8192]{1,0:T(2,128)(2,1)} %param.9), channel_id=1, source_target_pairs={{0,8},{1,9},{2,10},{3,11},{4,12},{5,13},{6,14},{7,15},{8,0},{9,1},... | collective-permute-start | bytes 98312 | tf_op jit(solution)/shard_map/ppermute | solution.py:178
  6.4 0.8 select_reduce_fusion
  7.2 2.2 %collective-permute-done.1 = bf16[2,8192]{1,0:T(2,128)(2,1)S(1)} collective-permute-done((bf16[2,8192]{1,0:T(2,128)(2,1)}, bf16[2,8192]{1,0:T(2,128)(2,1)S(1)}, u32[]{:S(2)}, u32[]{:S(2)}) %collective-permute-start.1) | collective-permute-done | bytes 32800 | tf_op jit(solution)/shard_map/ppermute | solution.py:178
  9.4 2.9 %collective-permute-done.2 = bf16[2,8192]{1,0:T(2,128)(2,1)S(1)} collective-permute-done((bf16[2,8192]{1,0:T(2,128)(2,1)}, bf16[2,8192]{1,0:T(2,128)(2,1)S(1)}, u32[]{:S(2)}, u32[]{:S(2)}) %collective-permute-start.2) | collective-permute-done | bytes 32800 | tf_op jit(solution)/shard_map/ppermute | solution.py:178
  12.3 0.9 pad_maximum_fusion.1
  13.2 1.6 %collective-permute-start.3 = (bf16[8,8192]{1,0:T(8,128)(2,1)S(1)}, bf16[8,8192]{1,0:T(8,128)(2,1)S(1)}, u32[]{:S(2)}, u32[]{:S(2)}) collective-permute-start(bf16[8,8192]{1,0:T(8,128)(2,1)S(1)} %pad_maximum_fusion.1), channel_id=1, source_target_pairs={{0,2},{1,3},{2,0},{3,1},{4,6},{5,7},{6,4},{7,5},{8,10},{9,11},{10,... | collective-permute-start | bytes 393224 | tf_op jit(solution)/shard_map/ppermute | solution.py:178
  14.8 3.4 %collective-permute-done.3 = bf16[8,8192]{1,0:T(8,128)(2,1)S(1)} collective-permute-done((bf16[8,8192]{1,0:T(8,128)(2,1)S(1)}, bf16[8,8192]{1,0:T(8,128)(2,1)S(1)}, u32[]{:S(2)}, u32[]{:S(2)}) %collective-permute-start.3) | collective-permute-done | bytes 131104 | tf_op jit(solution)/shard_map/ppermute | solution.py:178
  18.2 0.9 concatenate.47
  19.2 0.5 iota_xor_fusion
  19.8 1.3 fusion.23
  21.0 1.0 concatenate.48.x_ref
  22.5 1.9 %fusion.9 = f32[32,1024]{1,0:T(8,128)S(1)} fusion(f32[512,1024]{1,0:T(8,128)} %param.13, bf16[32,8192]{1,0:T(8,128)(2,1)S(1)} %concatenate.48.x_ref, s32[]{:T(128)S(6)} %select_n.7), kind=kOutput, calls=%fused_computation.20 | convolution fusion | flops 34078720 | bytes 2260996 | tf_op jit(solution)/shard_map/dot_general | solution.py:221
  24.7 0.5 collective-permute-start.5
  25.3 6.9 %forward_products.4 = (f32[32,1792]{1,0:T(8,128)S(1)}, f32[32,1792]{1,0:T(8,128)S(1)}) custom-call(bf16[32,8192]{1,0:T(8,128)(2,1)S(1)} %concatenate.48.x_ref, bf16[8192,1792]{1,0:T(8,128)(2,1)} %wg_ref.15, bf16[8192,1792]{1,0:T(8,128)(2,1)} %wu_ref.15, f32[32,1792]{1,0:T(8,128)S(1)} %broadcast_in_dim.16.g0_ref.u0_ref, ...), custom_call_target="tpu_custom_call" | custom-call | flops 469762048 | bytes 14680064 | tf_op jit(solution)/shard_map/forward_products/pallas_call | solution.py:122
  32.3 1.6 %collective-permute-start.6 = (f32[32,128]{1,0:T(8,128)S(1)}, f32[32,128]{1,0:T(8,128)S(1)}, u32[]{:S(2)}, u32[]{:S(2)}) collective-permute-start(f32[32,128]{1,0:T(8,128)S(1)} %bitcast.82), channel_id=1, source_target_pairs={{0,2},{1,3},{2,0},{3,1},{4,6},{5,7},{6,4},{7,5},{8,10},{9,11},{10,... | collective-permute-start | bytes 49160 | tf_op jit(solution)/shard_map/ppermute | solution.py:178
  33.8 6.9 %forward_products.5 = (f32[32,1792]{1,0:T(8,128)S(1)}, f32[32,1792]{1,0:T(8,128)S(1)}) custom-call(bf16[32,8192]{1,0:T(8,128)(2,1)S(1)} %concatenate.48.x_ref, bf16[8192,1792]{1,0:T(8,128)(2,1)} %wg_ref.15, bf16[8192,1792]{1,0:T(8,128)(2,1)} %wu_ref.15, f32[32,1792]{1,0:T(8,128)S(1)} %get-tuple-element.69.g0_ref, f32[32,1792]{1,0:T(8,128)S(1)} %get-tuple-element.70.u0_ref), custom_call_target="tpu_custom_call" | custom-call | flops 469762048 | bytes 14680064 | tf_op jit(solution)/shard_map/forward_products/pallas_call | solution.py:122
  40.9 6.9 %forward_products.6 = (f32[32,1792]{1,0:T(8,128)S(1)}, f32[32,1792]{1,0:T(8,128)S(1)}) custom-call(bf16[32,8192]{1,0:T(8,128)(2,1)S(1)} %concatenate.48.x_ref, bf16[8192,1792]{1,0:T(8,128)(2,1)} %wg_ref.15, bf16[8192,1792]{1,0:T(8,128)(2,1)} %wu_ref.15, f32[32,1792]{1,0:T(8,128)S(1)} %get-tuple-element.75.g0_ref, f32[32,1792]{1,0:T(8,128)S(1)} %get-tuple-element.76.u0_ref), custom_call_target="tpu_custom_call" | custom-call | flops 469762048 | bytes 14680064 | tf_op jit(solution)/shard_map/forward_products/pallas_call | solution.py:122
  47.8 0.9 collective-permute-start.8
  48.8 6.9 %forward_products.7 = (f32[32,1792]{1,0:T(8,128)S(1)}, f32[32,1792]{1,0:T(8,128)S(1)}) custom-call(bf16[32,8192]{1,0:T(8,128)(2,1)S(1)} %concatenate.48.x_ref, bf16[8192,1792]{1,0:T(8,128)(2,1)} %wg_ref.15, bf16[8192,1792]{1,0:T(8,128)(2,1)} %wu_ref.15, f32[32,1792]{1,0:T(8,128)S(1)} %get-tuple-element.81.g0_ref, f32[32,1792]{1,0:T(8,128)S(1)} %get-tuple-element.82.u0_ref), custom_call_target="tpu_custom_call" | custom-call | flops 469762048 | bytes 14680064 | tf_op jit(solution)/shard_map/forward_products/pallas_call | solution.py:122
  56.9 4.8 %convolution_multiply_fusion.2 = f32[32,1792]{0,1:T(8,128)S(1)} fusion(bf16[32,1024]{1,0:T(8,128)(2,1)S(1)} %convert_element_type.130, f32[1024,1792]{1,0:T(8,128)} %param.14), kind=kOutput, calls=%fused_computation.2 | convolution fusion | flops 119332864 | bytes 7634944 | tf_op jit(solution)/shard_map/dot_general | solution.py:234
  61.7 4.8 %convolution_multiply_fusion.3 = f32[32,1792]{0,1:T(8,128)S(1)} fusion(bf16[32,1024]{1,0:T(8,128)(2,1)S(1)} %convert_element_type.126, f32[1024,1792]{1,0:T(8,128)} %param.15), kind=kOutput, calls=%fused_computation.3 | convolution fusion | flops 119332864 | bytes 7634944 | tf_op jit(solution)/shard_map/dot_general | solution.py:237
  66.5 0.6 multiply_convert_fusion
  67.1 1.2 fusion
  68.4 4.2 %convolution_multiply_fusion.1 = f32[1024,1792]{1,0:T(8,128)} fusion(bf16[32,1024]{1,0:T(8,128)(2,1)S(1)} %copy-done.5, bf16[32,1792]{0,1:T(8,128)(2,1)S(1)} %get-tuple-element.134), kind=kOutput, calls=%fused_computation.1 | convolution fusion | flops 119275520 | bytes 7520256 | tf_op jit(solution)/shard_map/dot_general | solution.py:37
  72.6 1.2 fusion.3
  73.8 4.2 %convolution_multiply_fusion = f32[1024,1792]{1,0:T(8,128)} fusion(bf16[32,1024]{1,0:T(8,128)(2,1)S(1)} %convert_element_type.126, bf16[32,1792]{0,1:T(8,128)(2,1)S(1)} %get-tuple-element.133), kind=kOutput, calls=%fused_computation | convolution fusion | flops 119275520 | bytes 7520256 | tf_op jit(solution)/shard_map/dot_general | solution.py:37
  78.5 9.8 %backward_products.4 = (f32[16,2048]{1,0:T(8,128)S(1)}, bf16[16,2048]{1,0:T(8,128)(2,1)S(1)}) custom-call(bf16[1792,32]{1,0:T(8,128)(2,1)S(1)} %bitcast.67, bf16[1792,32]{1,0:T(8,128)(2,1)S(1)} %bitcast.63, bf16[8192,1792]{1,0:T(8,128)(2,1)} %wg_ref.15, bf16[8192,1792]{1,0:T(8,128)(2,1)} %wu_ref.15), custom_call_target="tpu_custom_call" | custom-call | flops 469762048 | bytes 14680064 | tf_op jit(solution)/shard_map/backward_products/pallas_call | solution.py:157
  88.4 0.6 collective-permute-start.10
  89.0 9.6 %backward_products.5 = (f32[16,2048]{1,0:T(8,128)S(1)}, bf16[16,2048]{1,0:T(8,128)(2,1)S(1)}) custom-call(bf16[1792,32]{1,0:T(8,128)(2,1)S(1)} %bitcast.68, bf16[1792,32]{1,0:T(8,128)(2,1)S(1)} %bitcast.64, bf16[8192,1792]{1,0:T(8,128)(2,1)} %wg_ref.15, bf16[8192,1792]{1,0:T(8,128)(2,1)} %wu_ref.15), custom_call_target="tpu_custom_call" | custom-call | flops 469762048 | bytes 14680064 | tf_op jit(solution)/shard_map/backward_products/pallas_call | solution.py:157
  98.7 1.2 collective-permute-start.11
  99.9 9.6 %backward_products.6 = (f32[16,2048]{1,0:T(8,128)S(1)}, bf16[16,2048]{1,0:T(8,128)(2,1)S(1)}) custom-call(bf16[1792,32]{1,0:T(8,128)(2,1)S(1)} %bitcast.69, bf16[1792,32]{1,0:T(8,128)(2,1)S(1)} %bitcast.65, bf16[8192,1792]{1,0:T(8,128)(2,1)} %wg_ref.15, bf16[8192,1792]{1,0:T(8,128)(2,1)} %wu_ref.15), custom_call_target="tpu_custom_call" | custom-call | flops 469762048 | bytes 14680064 | tf_op jit(solution)/shard_map/backward_products/pallas_call | solution.py:157
  109.6 1.6 %collective-permute-start.14 = (bf16[8,4096]{1,0:T(8,128)(2,1)S(1)}, bf16[8,4096]{1,0:T(8,128)(2,1)S(1)}, u32[]{:S(2)}, u32[]{:S(2)}) collective-permute-start(bf16[8,4096]{1,0:T(8,128)(2,1)S(1)} %slice.168), channel_id=1, source_target_pairs={{0,2},{1,3},{2,0},{3,1},{4,6},{5,7},{6,4},{7,5},{8,10},{9,11},{10,... | collective-permute-start | bytes 196616 | tf_op jit(solution)/shard_map/ppermute | solution.py:178
  111.2 3.0 %collective-permute-start.13 = (f32[32,128]{1,0:T(8,128)S(1)}, f32[32,128]{1,0:T(8,128)S(1)}, u32[]{:S(2)}, u32[]{:S(2)}) collective-permute-start(f32[32,128]{1,0:T(8,128)S(1)} %bitcast.85), channel_id=1, source_target_pairs={{0,8},{1,9},{2,10},{3,11},{4,12},{5,13},{6,14},{7,15},{8,0},{9,1},... | collective-permute-start | bytes 49160 | tf_op jit(solution)/shard_map/ppermute | solution.py:178
  114.2 9.6 %backward_products.7 = (f32[16,2048]{1,0:T(8,128)S(1)}, bf16[16,2048]{1,0:T(8,128)(2,1)S(1)}) custom-call(bf16[1792,32]{1,0:T(8,128)(2,1)S(1)} %bitcast.70, bf16[1792,32]{1,0:T(8,128)(2,1)S(1)} %bitcast.66, bf16[8192,1792]{1,0:T(8,128)(2,1)} %wg_ref.15, bf16[8192,1792]{1,0:T(8,128)(2,1)} %wu_ref.15), custom_call_target="tpu_custom_call" | custom-call | flops 469762048 | bytes 14680064 | tf_op jit(solution)/shard_map/backward_products/pallas_call | solution.py:157
  124.0 0.9 collective-permute-start.17
  124.9 3.5 %collective-permute-start.18 = (bf16[2,4096]{1,0:T(2,128)(2,1)S(1)}, bf16[2,4096]{1,0:T(2,128)(2,1)S(1)}, u32[]{:S(2)}, u32[]{:S(2)}) collective-permute-start(bf16[2,4096]{1,0:T(2,128)(2,1)S(1)} %get-tuple-element.138), channel_id=1, source_target_pairs={{0,12},{1,13},{2,14},{3,15},{4,8},{5,9},{6,10},{7,11},{8,4},{9,5},... | collective-permute-start | bytes 49160 | tf_op jit(solution)/shard_map/ppermute | solution.py:178
  128.7 2.0 %fusion.11 = f32[32,512]{1,0:T(8,128)S(1)} fusion(bf16[32,1024]{1,0:T(8,128)(2,1)S(1)} %convert_element_type.140, f32[512,1024]{1,0:T(8,128)} %param.12), kind=kOutput, calls=%fused_computation.22 | convolution fusion | flops 34078720 | bytes 2228224 | tf_op jit(solution)/shard_map/dot_general | solution.py:31
  130.9 1.8 %convolution_multiply_fusion.4 = f32[512,1024]{1,0:T(8,128)} fusion(bf16[32,1024]{1,0:T(8,128)(2,1)S(1)} %convert_element_type.143, bf16[32,8192]{1,0:T(8,128)(2,1)S(1)} %concatenate.48.x_ref, s32[]{:T(128)S(6)} %select_n.7), kind=kOutput, calls=%fused_computation.10 | convolution fusion | flops 34078720 | bytes 2195460 | tf_op jit(solution)/shard_map/dot_general | solution.py:37
  132.7 2.0 %fusion.7 = bf16[32,512]{1,0:T(8,128)(2,1)S(1)} fusion(f32[32,512]{1,0:T(8,128)S(1)} %fusion.11, bf16[32,1024]{1,0:T(8,128)(2,1)S(1)} %convert_element_type.143, f32[512,1024]{1,0:T(8,128)} %param.13), kind=kOutput, calls=%fused_computation.15 | convolution fusion | flops 34127872 | bytes 2260992 | tf_op jit(solution)/shard_map/dot_general | solution.py:31
  134.8 1.8 %convolution_multiply_fusion.5 = f32[512,1024]{1,0:T(8,128)} fusion(bf16[32,1024]{1,0:T(8,128)(2,1)S(1)} %convert_element_type.140, bf16[32,8192]{1,0:T(8,128)(2,1)S(1)} %concatenate.48.x_ref, s32[]{:T(128)S(6)} %select_n.7), kind=kOutput, calls=%fused_computation.11 | convolution fusion | flops 34078720 | bytes 2195460 | tf_op jit(solution)/shard_map/dot_general | solution.py:37
  136.7 0.6 collective-permute-start.19
  137.4 4.3 %collective-permute-done.19 = bf16[8,5120]{1,0:T(8,128)(2,1)S(1)} collective-permute-done((bf16[8,5120]{1,0:T(8,128)(2,1)S(1)}, bf16[8,5120]{1,0:T(8,128)(2,1)S(1)}, u32[]{:S(2)}, u32[]{:S(2)}) %collective-permute-start.19) | collective-permute-done | bytes 81952 | tf_op jit(solution)/shard_map/ppermute | solution.py:178
  141.8 0.9 collective-permute-start.21
  142.7 3.5 %collective-permute-start.22 = (bf16[2,6144]{1,0:T(2,128)(2,1)S(1)}, bf16[2,6144]{1,0:T(2,128)(2,1)S(1)}, u32[]{:S(2)}, u32[]{:S(2)}) collective-permute-start(bf16[2,6144]{1,0:T(2,128)(2,1)S(1)} %get-tuple-element.135), channel_id=1, source_target_pairs={{0,12},{1,13},{2,14},{3,15},{4,8},{5,9},{6,10},{7,11},{8,4},{9,5},... | collective-permute-start | bytes 73736 | tf_op jit(solution)/shard_map/ppermute | solution.py:178
  146.2 0.8 collective-permute-done.21
  147.0 1.4 collective-permute-done.22
  148.7 0.7 fusion.15
  (103 shorter events, 4.3 us)
Async XLA Ops:
  0.6 19.1 %copy-start = (bf16[32,1792]{1,0:T(8,128)(2,1)S(1)}, bf16[32,1792]{1,0:T(8,128)(2,1)}, u32[]{:S(2)}) copy-start(bf16[32,1792]{1,0:T(8,128)(2,1)} %param.17) | copy-start | bytes 344068
  0.6 21.4 %copy-start.2 = (f32[512,1024]{1,0:T(8,128)S(1)}, f32[512,1024]{1,0:T(8,128)}, u32[]{:S(2)}) copy-start(f32[512,1024]{1,0:T(8,128)} %param.12) | copy-start | bytes 6291460
  0.7 6.5 %collective-permute-start = (bf16[2,8192]{1,0:T(2,128)(2,1)}, bf16[2,8192]{1,0:T(2,128)(2,1)S(1)}, u32[]{:S(2)}, u32[]{:S(2)}) collective-permute-start(bf16[2,8192]{1,0:T(2,128)(2,1)} %param.9), channel_id=1, source_target_pairs={{0,4},{1,5},{2,6},{3,7},{4,0},{5,1},{6,2},{7,3},{8,12},{9,13},{10,... | collective-permute-start | bytes 98312 | tf_op jit(solution)/shard_map/ppermute | solution.py:178
  3.7 5.6 %collective-permute-start.1 = (bf16[2,8192]{1,0:T(2,128)(2,1)}, bf16[2,8192]{1,0:T(2,128)(2,1)S(1)}, u32[]{:S(2)}, u32[]{:S(2)}) collective-permute-start(bf16[2,8192]{1,0:T(2,128)(2,1)} %param.9), channel_id=1, source_target_pairs={{0,8},{1,9},{2,10},{3,11},{4,12},{5,13},{6,14},{7,15},{8,0},{9,1},... | collective-permute-start | bytes 98312 | tf_op jit(solution)/shard_map/ppermute | solution.py:178
  6.3 5.9 %collective-permute-start.2 = (bf16[2,8192]{1,0:T(2,128)(2,1)}, bf16[2,8192]{1,0:T(2,128)(2,1)S(1)}, u32[]{:S(2)}, u32[]{:S(2)}) collective-permute-start(bf16[2,8192]{1,0:T(2,128)(2,1)} %param.9), channel_id=1, source_target_pairs={{0,12},{1,13},{2,14},{3,15},{4,8},{5,9},{6,10},{7,11},{8,4},{9,5},... | collective-permute-start | bytes 98312 | tf_op jit(solution)/shard_map/ppermute | solution.py:178
  13.2 5.0 %collective-permute-start.3 = (bf16[8,8192]{1,0:T(8,128)(2,1)S(1)}, bf16[8,8192]{1,0:T(8,128)(2,1)S(1)}, u32[]{:S(2)}, u32[]{:S(2)}) collective-permute-start(bf16[8,8192]{1,0:T(8,128)(2,1)S(1)} %pad_maximum_fusion.1), channel_id=1, source_target_pairs={{0,2},{1,3},{2,0},{3,1},{4,6},{5,7},{6,4},{7,5},{8,10},{9,11},{10,... | collective-permute-start | bytes 393224 | tf_op jit(solution)/shard_map/ppermute | solution.py:178
  19.2 1.9 %collective-permute-start.4 = (bf16[16,8192]{1,0:T(8,128)(2,1)S(1)}, bf16[16,8192]{1,0:T(8,128)(2,1)S(1)}, u32[]{:S(2)}, u32[]{:S(2)}) collective-permute-start(bf16[16,8192]{1,0:T(8,128)(2,1)S(1)} %concatenate.47), channel_id=1, source_target_pairs={{0,1},{1,0},{2,3},{3,2},{4,5},{5,4},{6,7},{7,6},{8,9},{9,8},{10,11... | collective-permute-start | bytes 786440 | tf_op jit(solution)/shard_map/ppermute | solution.py:178
  24.7 7.5 %collective-permute-start.5 = (f32[32,128]{1,0:T(8,128)S(1)}, f32[32,128]{1,0:T(8,128)S(1)}, u32[]{:S(2)}, u32[]{:S(2)}) collective-permute-start(f32[32,128]{1,0:T(8,128)S(1)} %pad_maximum_fusion.10), channel_id=1, source_target_pairs={{0,1},{1,0},{2,3},{3,2},{4,5},{5,4},{6,7},{7,6},{8,9},{9,8},{10,11... | collective-permute-start | bytes 49160 | tf_op jit(solution)/shard_map/ppermute | solution.py:178
  32.3 8.5 %collective-permute-start.6 = (f32[32,128]{1,0:T(8,128)S(1)}, f32[32,128]{1,0:T(8,128)S(1)}, u32[]{:S(2)}, u32[]{:S(2)}) collective-permute-start(f32[32,128]{1,0:T(8,128)S(1)} %bitcast.82), channel_id=1, source_target_pairs={{0,2},{1,3},{2,0},{3,1},{4,6},{5,7},{6,4},{7,5},{8,10},{9,11},{10,... | collective-permute-start | bytes 49160 | tf_op jit(solution)/shard_map/ppermute | solution.py:178
  40.8 7.0 %collective-permute-start.7 = (f32[32,128]{1,0:T(8,128)S(1)}, f32[32,128]{1,0:T(8,128)S(1)}, u32[]{:S(2)}, u32[]{:S(2)}) collective-permute-start(f32[32,128]{1,0:T(8,128)S(1)} %bitcast.83), channel_id=1, source_target_pairs={{0,4},{1,5},{2,6},{3,7},{4,0},{5,1},{6,2},{7,3},{8,12},{9,13},{10,... | collective-permute-start | bytes 49160 | tf_op jit(solution)/shard_map/ppermute | solution.py:178
  47.8 7.9 %collective-permute-start.8 = (f32[32,128]{1,0:T(8,128)S(1)}, f32[32,128]{1,0:T(8,128)S(1)}, u32[]{:S(2)}, u32[]{:S(2)}) collective-permute-start(f32[32,128]{1,0:T(8,128)S(1)} %bitcast.86), channel_id=1, source_target_pairs={{0,8},{1,9},{2,10},{3,11},{4,12},{5,13},{6,14},{7,15},{8,0},{9,1},... | collective-permute-start | bytes 49160 | tf_op jit(solution)/shard_map/ppermute | solution.py:178
  56.1 5.6 %copy-start.4 = (bf16[32,1024]{1,0:T(8,128)(2,1)}, bf16[32,1024]{1,0:T(8,128)(2,1)S(1)}, u32[]{:S(2)}) copy-start(bf16[32,1024]{1,0:T(8,128)(2,1)S(1)} %convert_element_type.130) | copy-start | bytes 196612
  56.9 10.2 %slice-start = ((s8[7340032]{0:T(1024)(128)(4,1)}), s8[4194304]{0:T(1024)(128)(4,1)S(1)}, s32[]{:S(2)}) async-start(s8[7340032]{0:T(1024)(128)(4,1)} %bitcast.71), calls=%async_computation | async-start | bytes 8388608
  61.7 4.8 %copy-start.3 = (f32[32,1792]{0,1:T(8,128)S(1)}, f32[32,1792]{0,1:T(8,128)}, u32[]{:S(2)}) copy-start(f32[32,1792]{0,1:T(8,128)} %fusion.23) | copy-start | bytes 688132
  61.7 5.4 %slice-start.1 = ((s8[7340032]{0:T(1024)(128)(4,1)}), s8[3145728]{0:T(1024)(128)(4,1)S(1)}, s32[]{:S(2)}) async-start(s8[7340032]{0:T(1024)(128)(4,1)} %bitcast.71), calls=%async_computation.1 | async-start | bytes 6291456
  67.1 1.2 copy-start.5
  67.1 5.5 %slice-start.2 = ((s8[7340032]{0:T(1024)(128)(4,1)}), s8[3145728]{0:T(1024)(128)(4,1)S(1)}, s32[]{:S(2)}) async-start(s8[7340032]{0:T(1024)(128)(4,1)} %bitcast.73), calls=%async_computation.2 | async-start | bytes 6291456
  68.4 4.2 %slice-start.3 = ((s8[7340032]{0:T(1024)(128)(4,1)}), s8[4194304]{0:T(1024)(128)(4,1)S(1)}, s32[]{:S(2)}) async-start(s8[7340032]{0:T(1024)(128)(4,1)} %bitcast.73), calls=%async_computation.3 | async-start | bytes 8388608
  78.5 9.8 %collective-permute-start.9 = (f32[32,128]{1,0:T(8,128)S(1)}, f32[32,128]{1,0:T(8,128)S(1)}, u32[]{:S(2)}, u32[]{:S(2)}) collective-permute-start(f32[32,128]{1,0:T(8,128)S(1)} %pad_maximum_fusion.11), channel_id=1, source_target_pairs={{0,1},{1,0},{2,3},{3,2},{4,5},{5,4},{6,7},{7,6},{8,9},{9,8},{10,11... | collective-permute-start | bytes 49160 | tf_op jit(solution)/shard_map/ppermute | solution.py:178
  88.4 10.3 %collective-permute-start.10 = (f32[32,128]{1,0:T(8,128)S(1)}, f32[32,128]{1,0:T(8,128)S(1)}, u32[]{:S(2)}, u32[]{:S(2)}) collective-permute-start(f32[32,128]{1,0:T(8,128)S(1)} %bitcast.80), channel_id=1, source_target_pairs={{0,2},{1,3},{2,0},{3,1},{4,6},{5,7},{6,4},{7,5},{8,10},{9,11},{10,... | collective-permute-start | bytes 49160 | tf_op jit(solution)/shard_map/ppermute | solution.py:178
  98.6 10.9 %collective-permute-start.12 = (bf16[16,4096]{1,0:T(8,128)(2,1)S(1)}, bf16[16,4096]{1,0:T(8,128)(2,1)S(1)}, u32[]{:S(2)}, u32[]{:S(2)}) collective-permute-start(bf16[16,4096]{1,0:T(8,128)(2,1)S(1)} %pad_maximum_fusion.2), channel_id=1, source_target_pairs={{0,1},{1,0},{2,3},{3,2},{4,5},{5,4},{6,7},{7,6},{8,9},{9,8},{10,11... | collective-permute-start | bytes 393224 | tf_op jit(solution)/shard_map/ppermute | solution.py:178
  98.7 10.8 %collective-permute-start.11 = (f32[32,128]{1,0:T(8,128)S(1)}, f32[32,128]{1,0:T(8,128)S(1)}, u32[]{:S(2)}, u32[]{:S(2)}) collective-permute-start(f32[32,128]{1,0:T(8,128)S(1)} %bitcast.79), channel_id=1, source_target_pairs={{0,4},{1,5},{2,6},{3,7},{4,0},{5,1},{6,2},{7,3},{8,12},{9,13},{10,... | collective-permute-start | bytes 49160 | tf_op jit(solution)/shard_map/ppermute | solution.py:178
  109.6 14.2 %collective-permute-start.14 = (bf16[8,4096]{1,0:T(8,128)(2,1)S(1)}, bf16[8,4096]{1,0:T(8,128)(2,1)S(1)}, u32[]{:S(2)}, u32[]{:S(2)}) collective-permute-start(bf16[8,4096]{1,0:T(8,128)(2,1)S(1)} %slice.168), channel_id=1, source_target_pairs={{0,2},{1,3},{2,0},{3,1},{4,6},{5,7},{6,4},{7,5},{8,10},{9,11},{10,... | collective-permute-start | bytes 196616 | tf_op jit(solution)/shard_map/ppermute | solution.py:178
  111.2 12.6 %collective-permute-start.13 = (f32[32,128]{1,0:T(8,128)S(1)}, f32[32,128]{1,0:T(8,128)S(1)}, u32[]{:S(2)}, u32[]{:S(2)}) collective-permute-start(f32[32,128]{1,0:T(8,128)S(1)} %bitcast.85), channel_id=1, source_target_pairs={{0,8},{1,9},{2,10},{3,11},{4,12},{5,13},{6,14},{7,15},{8,0},{9,1},... | collective-permute-start | bytes 49160 | tf_op jit(solution)/shard_map/ppermute | solution.py:178
  123.9 12.7 %collective-permute-start.16 = (bf16[2,4096]{1,0:T(2,128)(2,1)S(1)}, bf16[2,4096]{1,0:T(2,128)(2,1)S(1)}, u32[]{:S(2)}, u32[]{:S(2)}) collective-permute-start(bf16[2,4096]{1,0:T(2,128)(2,1)S(1)} %get-tuple-element.140), channel_id=1, source_target_pairs={{0,4},{1,5},{2,6},{3,7},{4,0},{5,1},{6,2},{7,3},{8,12},{9,13},{10,... | collective-permute-start | bytes 49160 | tf_op jit(solution)/shard_map/ppermute | solution.py:178
  124.0 12.6 %collective-permute-start.17 = (bf16[2,4096]{1,0:T(2,128)(2,1)S(1)}, bf16[2,4096]{1,0:T(2,128)(2,1)S(1)}, u32[]{:S(2)}, u32[]{:S(2)}) collective-permute-start(bf16[2,4096]{1,0:T(2,128)(2,1)S(1)} %get-tuple-element.139), channel_id=1, source_target_pairs={{0,8},{1,9},{2,10},{3,11},{4,12},{5,13},{6,14},{7,15},{8,0},{9,1},... | collective-permute-start | bytes 49160 | tf_op jit(solution)/shard_map/ppermute | solution.py:178
  124.9 11.8 %collective-permute-start.18 = (bf16[2,4096]{1,0:T(2,128)(2,1)S(1)}, bf16[2,4096]{1,0:T(2,128)(2,1)S(1)}, u32[]{:S(2)}, u32[]{:S(2)}) collective-permute-start(bf16[2,4096]{1,0:T(2,128)(2,1)S(1)} %get-tuple-element.138), channel_id=1, source_target_pairs={{0,12},{1,13},{2,14},{3,15},{4,8},{5,9},{6,10},{7,11},{8,4},{9,5},... | collective-permute-start | bytes 49160 | tf_op jit(solution)/shard_map/ppermute | solution.py:178
  130.9 18.5 %copy-start.1 = (bf16[32,1792]{1,0:T(8,128)(2,1)S(1)}, bf16[32,1792]{1,0:T(8,128)(2,1)}, u32[]{:S(2)}) copy-start(bf16[32,1792]{1,0:T(8,128)(2,1)} %param.17) | copy-start | bytes 344068
  132.7 15.8 %copy-start.6 = (s32[16]{0:T(128)S(1)}, s32[16]{0:T(128)}, u32[]{:S(2)}) copy-start(s32[16]{0:T(128)} %iota_xor_fusion) | copy-start | bytes 196
  134.8 1.9 %collective-permute-start.15 = (bf16[16,4608]{1,0:T(8,128)(2,1)S(1)}, bf16[16,4608]{1,0:T(8,128)(2,1)S(1)}, u32[]{:S(2)}, u32[]{:S(2)}) collective-permute-start(bf16[16,4608]{1,0:T(8,128)(2,1)S(1)} %pad_maximum_fusion), channel_id=1, source_target_pairs={{0,1},{1,0},{2,3},{3,2},{4,5},{5,4},{6,7},{7,6},{8,9},{9,8},{10,11... | collective-permute-start | bytes 442376 | tf_op jit(solution)/shard_map/ppermute | solution.py:178
  136.7 4.9 %collective-permute-start.19 = (bf16[8,5120]{1,0:T(8,128)(2,1)S(1)}, bf16[8,5120]{1,0:T(8,128)(2,1)S(1)}, u32[]{:S(2)}, u32[]{:S(2)}) collective-permute-start(bf16[8,5120]{1,0:T(8,128)(2,1)S(1)} %pad_maximum_fusion.3), channel_id=1, source_target_pairs={{0,2},{1,3},{2,0},{3,1},{4,6},{5,7},{6,4},{7,5},{8,10},{9,11},{10,... | collective-permute-start | bytes 245768 | tf_op jit(solution)/shard_map/ppermute | solution.py:178
  141.7 4.5 %collective-permute-start.20 = (bf16[2,6144]{1,0:T(2,128)(2,1)S(1)}, bf16[2,6144]{1,0:T(2,128)(2,1)S(1)}, u32[]{:S(2)}, u32[]{:S(2)}) collective-permute-start(bf16[2,6144]{1,0:T(2,128)(2,1)S(1)} %get-tuple-element.137), channel_id=1, source_target_pairs={{0,4},{1,5},{2,6},{3,7},{4,0},{5,1},{6,2},{7,3},{8,12},{9,13},{10,... | collective-permute-start | bytes 73736 | tf_op jit(solution)/shard_map/ppermute | solution.py:178
  141.8 5.2 %collective-permute-start.21 = (bf16[2,6144]{1,0:T(2,128)(2,1)S(1)}, bf16[2,6144]{1,0:T(2,128)(2,1)S(1)}, u32[]{:S(2)}, u32[]{:S(2)}) collective-permute-start(bf16[2,6144]{1,0:T(2,128)(2,1)S(1)} %get-tuple-element.136), channel_id=1, source_target_pairs={{0,8},{1,9},{2,10},{3,11},{4,12},{5,13},{6,14},{7,15},{8,0},{9,1},... | collective-permute-start | bytes 73736 | tf_op jit(solution)/shard_map/ppermute | solution.py:178
  142.7 5.6 %collective-permute-start.22 = (bf16[2,6144]{1,0:T(2,128)(2,1)S(1)}, bf16[2,6144]{1,0:T(2,128)(2,1)S(1)}, u32[]{:S(2)}, u32[]{:S(2)}) collective-permute-start(bf16[2,6144]{1,0:T(2,128)(2,1)S(1)} %get-tuple-element.135), channel_id=1, source_target_pairs={{0,12},{1,13},{2,14},{3,15},{4,8},{5,9},{6,10},{7,11},{8,4},{9,5},... | collective-permute-start | bytes 73736 | tf_op jit(solution)/shard_map/ppermute | solution.py:178

commit v3 on v0

--- a/solution.py
+++ b/solution.py
@@ -1,13 +1,16 @@
 import jax
 import jax.numpy as jnp
 from jax import lax
+from jax.experimental import pallas as pl
+from jax.experimental.pallas import tpu as pltpu
 from jax.sharding import PartitionSpec as P
 
 R = 64
 AG = 16
 
-
 adapter_scale = 2.0
+BF16 = jnp.bfloat16
+F32 = jnp.float32
 
 
 def agent_mask(agent):
@@ -30,7 +33,13 @@
     )
 
 
-def per_device(tokens, gate_weight, up_weight, a_gate, a_up, b_gate, b_up, agent, d_hidden):
+def rows_product(left, right):
+    return lax.dot_general(
+        left, right, (((0,), (0,)), ((), ())), preferred_element_type=jnp.float32
+    )
+
+
+def plain_device(tokens, gate_weight, up_weight, a_gate, a_up, b_gate, b_up, agent, d_hidden):
     onehot = agent_mask(agent)
     feat_rows = a_gate.shape[0]
     feat_start = lax.axis_index("tensor") * feat_rows
@@ -80,18 +89,10 @@
         scatter_dimension=0,
         tiled=True,
     ).astype(jnp.bfloat16)
-    gate_down_gradient = adapter_scale * lax.dot_general(
-        own_cols, gate_factor_gate, (((0,), (0,)), ((), ())), preferred_element_type=jnp.float32
-    )
-    up_down_gradient = adapter_scale * lax.dot_general(
-        own_cols, gate_factor_up, (((0,), (0,)), ((), ())), preferred_element_type=jnp.float32
-    )
-    gate_lift_gradient = adapter_scale * lax.dot_general(
-        up_factor_gate, gate_gradient, (((0,), (0,)), ((), ())), preferred_element_type=jnp.float32
-    )
-    up_lift_gradient = adapter_scale * lax.dot_general(
-        up_factor_up, up_gradient, (((0,), (0,)), ((), ())), preferred_element_type=jnp.float32
-    )
+    gate_down_gradient = adapter_scale * rows_product(own_cols, gate_factor_gate)
+    up_down_gradient = adapter_scale * rows_product(own_cols, gate_factor_up)
+    gate_lift_gradient = adapter_scale * rows_product(up_factor_gate, gate_gradient)
+    up_lift_gradient = adapter_scale * rows_product(up_factor_up, up_gradient)
     return (
         token_gradient,
         gate_down_gradient,
@@ -101,7 +102,351 @@
     )
 
 
+def forward_kernel(side_ref, x_ref, w_ref, *refs):
+    before_ref, out_refs, total = refs[0], refs[-3:-1], refs[-1]
+    step = pl.program_id(0)
+
+    @pl.when(step == 0)
+    def _():
+        total[...] = before_ref[...] if len(refs) == 4 else jnp.zeros_like(total)
+
+    total[...] += jnp.dot(x_ref[...], w_ref[...], preferred_element_type=F32)
+
+    @pl.when(step == pl.num_programs(0) - 1)
+    def _():
+        half = out_refs[0].shape[0]
+        out_refs[0][...] = total[:half].astype(out_refs[0].dtype)
+        out_refs[1][...] = total[half:].astype(out_refs[1].dtype)
+
+
+def forward_products(side, x, weight, before, first, count, send, depth=512):
+    rows, features = x.shape
+    ff = weight.shape[1]
+    start = first // depth
+    per_side = features // depth
+    whole = pl.BlockSpec((rows, ff), lambda k, s: (0, 0))
+    half = pl.BlockSpec((rows // 2, ff), lambda k, s: (0, 0))
+    extra = () if before is None else (jnp.concatenate(before, axis=0),)
+    return pl.pallas_call(
+        forward_kernel,
+        grid_spec=pltpu.PrefetchScalarGridSpec(
+            num_scalar_prefetch=1,
+            grid=(count // depth,),
+            in_specs=[
+                pl.BlockSpec((rows, depth), lambda k, s: (0, k + start)),
+                pl.BlockSpec((depth, ff), lambda k, s: (s[0] * per_side + k + start, 0)),
+            ]
+            + [whole] * len(extra),
+            out_specs=[half, half],
+            scratch_shapes=[pltpu.VMEM((rows, ff), F32)],
+        ),
+        out_shape=[
+            jax.ShapeDtypeStruct((rows // 2, ff), F32),
+            jax.ShapeDtypeStruct((rows // 2, ff), send),
+        ],
+        compiler_params=pltpu.CompilerParams(vmem_limit_bytes=40 << 20),
+        cost_estimate=pl.CostEstimate(
+            flops=2 * rows * count * ff, bytes_accessed=2 * count * ff, transcendentals=0
+        ),
+        name="forward_products",
+    )(side, x, weight, *extra)
+
+
+def hidden_kernel(
+    eug_ref, euu_ref, bg_ref, bu_ref, g0_ref, g1_ref, u0_ref, u1_ref, dh_ref, dg_ref, du_ref, pg_ref, pu_ref
+):
+    @pl.when(pl.program_id(0) == 0)
+    def _():
+        pg_ref[...] = jnp.zeros_like(pg_ref)
+        pu_ref[...] = jnp.zeros_like(pu_ref)
+
+    bg = bg_ref[...].astype(BF16)
+    bu = bu_ref[...].astype(BF16)
+    gate = (
+        g0_ref[...]
+        + g1_ref[...].astype(F32)
+        + adapter_scale * jnp.dot(eug_ref[...], bg, preferred_element_type=F32)
+    )
+    up = (
+        u0_ref[...]
+        + u1_ref[...].astype(F32)
+        + adapter_scale * jnp.dot(euu_ref[...], bu, preferred_element_type=F32)
+    )
+    sig = jax.nn.sigmoid(gate)
+    hidden_grad = dh_ref[...]
+    dg = (hidden_grad * up * sig * (1.0 + gate * (1.0 - sig))).astype(BF16)
+    du = (hidden_grad * gate * sig).astype(BF16)
+    dg_ref[...] = dg
+    du_ref[...] = du
+    pg_ref[...] += flipped_product(dg, bg)
+    pu_ref[...] += flipped_product(du, bu)
+
+
+def hidden_gradients(eug, euu, b_gate, b_up, gate, up, hidden_grad, width=256):
+    rows, wide = eug.shape
+    ff = b_gate.shape[1]
+    fixed = pl.BlockSpec((rows, wide), lambda k: (0, 0))
+    b_block = pl.BlockSpec((wide, width), lambda k: (0, k))
+    block = pl.BlockSpec((rows, width), lambda k: (0, k))
+    return pl.pallas_call(
+        hidden_kernel,
+        grid=(ff // width,),
+        in_specs=[fixed, fixed, b_block, b_block, block, block, block, block, block],
+        out_specs=[block, block, fixed, fixed],
+        out_shape=[jax.ShapeDtypeStruct((rows, ff), BF16)] * 2
+        + [jax.ShapeDtypeStruct((rows, wide), F32)] * 2,
+        compiler_params=pltpu.CompilerParams(vmem_limit_bytes=40 << 20),
+        cost_estimate=pl.CostEstimate(
+            flops=8 * rows * wide * ff, bytes_accessed=8 * wide * ff, transcendentals=rows * ff
+        ),
+        name="hidden_gradients",
+    )(eug, euu, b_gate, b_up, *gate, *up, hidden_grad)
+
+
+def backward_kernel(side_ref, dg_ref, du_ref, wg_ref, wu_ref, keep_ref, send_ref):
+    total = flipped_product(dg_ref[...], wg_ref[...]) + flipped_product(du_ref[...], wu_ref[...])
+    q = total.shape[0] // 4
+    keep_ref[:q] = total[:q]
+    keep_ref[q:] = total[2 * q : 3 * q]
+    send_ref[:q] = total[q : 2 * q].astype(send_ref.dtype)
+    send_ref[q:] = total[3 * q :].astype(send_ref.dtype)
+
+
+def backward_products(side, dg, du, gate_weight, up_weight, first, count, depth=512):
+    rows, ff = dg.shape
+    start = first // depth
+    per_side = gate_weight.shape[0] // 2 // depth
+    weight_block = pl.BlockSpec((depth, ff), lambda k, s: (s[0] * per_side + k + start, 0))
+    left_block = pl.BlockSpec((rows, ff), lambda k, s: (0, 0))
+    out_block = pl.BlockSpec((rows // 2, depth), lambda k, s: (0, k))
+    return pl.pallas_call(
+        backward_kernel,
+        grid_spec=pltpu.PrefetchScalarGridSpec(
+            num_scalar_prefetch=1,
+            grid=(count // depth,),
+            in_specs=[left_block, left_block, weight_block, weight_block],
+            out_specs=[out_block, out_block],
+        ),
+        out_shape=[
+            jax.ShapeDtypeStruct((rows // 2, count), F32),
+            jax.ShapeDtypeStruct((rows // 2, count), BF16),
+        ],
+        compiler_params=pltpu.CompilerParams(vmem_limit_bytes=40 << 20),
+        cost_estimate=pl.CostEstimate(
+            flops=4 * rows * count * ff, bytes_accessed=4 * count * ff, transcendentals=0
+        ),
+        name="backward_products",
+    )(side, dg, du, gate_weight, up_weight)
+
+
+N = 16
+SLOTS = 4
+
+
+def along_tensor(value, mask):
+    return lax.ppermute(value, "tensor", [(i, i ^ mask) for i in range(N)])
+
+
+def across_groups(value):
+    return lax.ppermute(value, "group", [(0, 1), (1, 0)])
+
+
+def summed(value, recv, slot):
+    shape = value.shape
+    v, r = (w.reshape(2, 2, 2, 2, 2, shape[1]) for w in (value, recv))
+    r = (r[::-1], r[:, ::-1], r[:, :, :, ::-1], r[:, :, ::-1])[slot]
+    return (v + r).reshape(shape)
+
+
+def in_order(*values):
+    return lax.optimization_barrier(values)
+
+
+def from_far_z(value):
+    return [along_tensor(v, 4 * m) for m, v in zip((1, 2, 3), value)]
+
+
+def shared_device(tokens, gate_weight, up_weight, a_gate, a_up, b_gate, b_up, agent, d_hidden):
+    group = lax.axis_index("group")
+    t = lax.axis_index("tensor")
+    side = group.astype(jnp.int32).reshape(1)
+    d = tokens.shape[1]
+    half = d // 2
+    feat_rows = a_gate.shape[0]
+    per_half = half // feat_rows
+
+    x = jnp.stack(
+        [
+            lax.dynamic_slice_in_dim(tokens, group * half, half, 1),
+            across_groups(lax.dynamic_slice_in_dim(tokens, half - group * half, half, 1)),
+        ]
+    )
+    x = jnp.concatenate([x] + from_far_z([x] * 3), axis=1)
+    x = jnp.concatenate([x, along_tensor(x, 2)], axis=1)
+    x = jnp.concatenate([x, along_tensor(x, 1)], axis=1)
+    rows = x.shape[1]
+    x = x.reshape(2 * rows, half)
+
+    place = jnp.arange(rows, dtype=jnp.int32)
+    block = ((place >> 1) & 3) * 4 + ((place >> 3) & 1) * 2 + (place >> 4)
+    token_of = ((t ^ block) << 1) + (place & 1)
+    shuffle = token_of[:, None] == jnp.arange(rows, dtype=jnp.int32)[None, :]
+    agent_here = jnp.sum(jnp.where(shuffle, agent[None, :], 0), axis=1)
+    onehot = agent_mask(agent_here)
+    hidden_grad = jnp.dot(shuffle.astype(BF16), d_hidden, preferred_element_type=F32)
+
+    blocks = lax.dynamic_slice_in_dim(x, (t % per_half) * feat_rows, feat_rows, 1)
+    swapped = across_groups(blocks[rows:])
+    count = half // 2
+    gate = forward_products(side, x, gate_weight, None, 0, count, F32)
+    swapped, *gate = in_order(swapped, *gate)
+    own_cols = jnp.where(t // per_half == group, blocks[:rows], swapped)
+
+    part_gate = select_rank(
+        jnp.dot(own_cols, a_gate.astype(BF16), preferred_element_type=F32), onehot
+    )
+    part_up = select_rank(jnp.dot(own_cols, a_up.astype(BF16), preferred_element_type=F32), onehot)
+    part = jnp.concatenate([part_gate, part_up], axis=1)
+
+    part, *gate = in_order(part, *gate)
+    recv = along_tensor(part, 1)
+    gate = forward_products(side, x, gate_weight, gate, count, count, BF16)
+    recv, x, *gate = in_order(recv, x, *gate)
+    part = summed(part, recv, 0)
+
+    recv, far = along_tensor(part, 2), across_groups(gate[1])
+    up = forward_products(side, x, up_weight, None, 0, count, F32)
+    recv, far, x, *up = in_order(recv, far, x, *up)
+    gate = gate[0], far
+    part = summed(part, recv, 1)
+
+    recv = along_tensor(part, 4)
+    up = forward_products(side, x, up_weight, up, count, count, BF16)
+    recv, *up = in_order(recv, *up)
+    up = up[0], across_groups(up[1])
+    part = summed(part, recv, 2)
+    part = summed(part, along_tensor(part, 8), 3)
+    u = part.astype(BF16)
+    up_factor_gate = spread_rank(u[:, :R], onehot)
+    up_factor_up = spread_rank(u[:, R:], onehot)
+
+    gate_gradient, up_gradient, pg_gate, pg_up = hidden_gradients(
+        up_factor_gate, up_factor_up, b_gate, b_up, gate, up, hidden_grad
+    )
+
+    far = across_groups(jnp.stack([gate_gradient, up_gradient]))
+    part = jnp.concatenate([select_rank(pg_gate, onehot), select_rank(pg_up, onehot)], axis=1)
+    recv = along_tensor(part, 1)
+    gate_lift_gradient = adapter_scale * rows_product(up_factor_gate, gate_gradient)
+    far, recv, gate_lift_gradient = in_order(far, recv, gate_lift_gradient)
+    part = summed(part, recv, 0)
+    dg = jnp.concatenate([gate_gradient, far[0]], axis=0)
+    du = jnp.concatenate([up_gradient, far[1]], axis=0)
+
+    count = half // SLOTS
+
+    def backward(slot):
+        return backward_products(side, dg, du, gate_weight, up_weight, slot * count, count)
+
+    recv = along_tensor(part, 2)
+    keep_0, send_0 = backward(0)
+    recv, dg, du, keep_0, send_0 = in_order(recv, dg, du, keep_0, send_0)
+    part = summed(part, recv, 1)
+
+    recv = along_tensor(part, 4)
+    keep_1, send_1 = backward(1)
+    recv, dg, du, keep_1, send_1 = in_order(recv, dg, du, keep_1, send_1)
+    part = summed(part, recv, 2)
+
+    recv = along_tensor(part, 8)
+    far = along_tensor(jnp.concatenate([send_0, send_1], axis=1), 1)
+    keep_2, send_2 = backward(2)
+    recv, far, dg, du, keep_2, send_2 = in_order(recv, far, dg, du, keep_2, send_2)
+    part = summed(part, recv, 3)
+    g = part.astype(BF16)
+    gate_factor_gate = spread_rank(g[:, :R], onehot)
+    gate_factor_up = spread_rank(g[:, R:], onehot)
+
+    early = (jnp.concatenate([keep_0, keep_1], axis=1) + far.astype(F32)).reshape(2, 16, -1)
+    far = along_tensor(early[:, 8:].astype(BF16), 2)
+    keep_3, send_3 = backward(3)
+    far, keep_3, send_3 = in_order(far, keep_3, send_3)
+    early = early[:, :8] + far.astype(F32)
+    contribution = (
+        adapter_scale
+        * (
+            flipped_product(gate_factor_gate, a_gate.astype(BF16))
+            + flipped_product(gate_factor_up, a_up.astype(BF16))
+        )
+    ).astype(BF16)
+
+    def beside(sums, columns):
+        other = jnp.zeros_like(columns)
+        return jnp.concatenate([sums.astype(BF16), jnp.stack([columns, other])], axis=2)
+
+    width = 2 * count
+    sums = jnp.concatenate([keep_2, keep_3], axis=1).reshape(2, 16, -1)
+    send = jnp.concatenate([send_2, send_3], axis=1).reshape(2, 16, -1)
+    far = along_tensor(beside(send, contribution[16:]), 1)
+    parts = from_far_z([early[:, 2 * m : 2 * m + 2].astype(BF16) for m in (1, 2, 3)])
+    gate_down_gradient = adapter_scale * rows_product(own_cols, gate_factor_gate)
+    far, gate_down_gradient, *parts = in_order(far, gate_down_gradient, *parts)
+    early = early[:, :2] + sum(p.astype(F32) for p in parts)
+    sums = sums + far[:, :, :width].astype(F32)
+    moved = jnp.concatenate([contribution[:16], far[0, :, width:]], axis=1)
+
+    far = along_tensor(beside(sums[:, 8:], moved[8:]), 2)
+    up_down_gradient = adapter_scale * rows_product(own_cols, gate_factor_up)
+    far, up_down_gradient = in_order(far, up_down_gradient)
+    sums = sums[:, :8] + far[:, :, :width].astype(F32)
+    moved = jnp.concatenate([moved[:8], far[0, :, width:]], axis=1)
+
+    last = beside(sums, moved)
+    parts = from_far_z([last[:, 2 * m : 2 * m + 2] for m in (1, 2, 3)])
+    up_lift_gradient = adapter_scale * rows_product(up_factor_up, up_gradient)
+    up_lift_gradient, *parts = in_order(up_lift_gradient, *parts)
+    sums = sums[:, :2] + sum(p[:, :, :width].astype(F32) for p in parts)
+    sums = jnp.concatenate([early, sums], axis=2)
+    far = across_groups(sums[1].astype(BF16))
+
+    moved = jnp.stack([moved[:2]] + [p[0, :, width:] for p in parts])
+    moved = moved.reshape(4, 2, 2, 2, feat_rows).transpose(0, 2, 3, 1, 4).reshape(N, 2 * feat_rows)
+    source = jnp.arange(N, dtype=jnp.int32)
+    sort = (source[:, None] == (t ^ source)[None, :]).astype(BF16)
+    sorted_rows = jnp.dot(sort, moved, preferred_element_type=F32).reshape(N, 2, feat_rows)
+    contribution = sorted_rows.transpose(1, 0, 2).reshape(2, d)
+    far = far.astype(F32)
+    token_gradient = (
+        jnp.where(
+            group == 0,
+            jnp.concatenate([sums[0], far], axis=1),
+            jnp.concatenate([far, sums[0]], axis=1),
+        )
+        + contribution
+    ).astype(BF16)
+    return (
+        token_gradient,
+        gate_down_gradient,
+        up_down_gradient,
+        gate_lift_gradient,
+        up_lift_gradient,
+    )
+
+
 def solution(mesh):
+    sizes = dict(mesh.shape)
+
+    def per_device(*args):
+        tokens, b_gate = args[0], args[5]
+        fits = (
+            sizes["group"] == 2
+            and sizes["tensor"] == N
+            and tokens.shape[0] == 2
+            and b_gate.shape[1] % 256 == 0
+            and tokens.shape[1] % 4096 == 0
+        )
+        return (shared_device if fits else plain_device)(*args)
+
     in_specs = (
         P(("group", "tensor"), None),
         P(None, "tensor"),

time: 306 us -> 135 us (0.44)
  blocking collectives: 210 us -> 0 us
  matrix products: 88.2 us -> 16.5 us
  Pallas kernels: 0 us -> 44.9 us
  starting transfers between devices: 0 us -> 34.8 us
  waiting for transfers between devices: 0 us -> 21.8 us
  local copies, waits for them, and re-layouts: 4.06 us -> 9.23 us
  other arithmetic: 1.39 us -> 5.68 us
    psum x2 -> x0, blocking collectives: 116 us -> none  [the longest x1 57.9 us: per_device(): u_gate, u_up = lax.psum((part_gate, part_up), 'tensor')]
    unnamed x1 -> x0, blocking collectives: 69.9 us -> none
    pallas_call x0 -> x9, Pallas kernels: none -> 44.9 us  [the longest x4 18.8 us: forward_products(): pl.pallas_call(forward_kernel, grid_spec=pltpu.PrefetchScalarGridSpec(num...]
    dot_general x6 -> x2, matrix products: 39 us -> 2.32 us  [flipped_product(): lax.dot_general(left, weight, (((1,), (1,)), ((), ())), preferred_element...]
    dot_general x10 -> x8, matrix products: 49.2 us -> 14.2 us  [the longest x4 11.9 us: rows_product(): lax.dot_general(left, right, (((0,), (0,)), ((), ())), preferred_element_...]
    ppermute x0 -> x29, starting transfers between devices: none -> 34.8 us  [the longest x23 25 us: along_tensor(): return lax.ppermute(value, 'tensor', [(i, i ^ mask) for i in range(N)])]
    all_gather x1 -> x0, blocking collectives: 24.8 us -> none  [per_device(): complete_result = lax.all_gather(tokens, 'tensor', axis=0, tiled=True)]
    ppermute x0 -> x29, waiting for transfers between devices: none -> 21.8 us  [the longest x23 15.8 us: along_tensor(): return lax.ppermute(value, 'tensor', [(i, i ^ mask) for i in range(N)])]
  transfers between devices with their start and end apart: 0 -> 29, of which waited for: 0 -> 14; matrix products, arithmetic and copies ran while one was open for 0% -> 8% of each run, Pallas kernels for 0% -> 28%
where the time goes in v3:
time: 135 us; the launch traced here: 134 us
  Pallas kernels  44.9 us (33%)
  starting transfers between devices  34.8 us (26%)
  waiting for transfers between devices  21.8 us (16%)
  matrix products  16.5 us (12%)
  local copies, waits for them, and re-layouts  9.23 us (7%)
  other arithmetic  5.68 us (4%)
    ppermute x23, starting transfers between devices, along_tensor(): return lax.ppermute(value, 'tensor', [(i, i ^ mask) for i in range(N)])  25 us
    pallas_call x4, Pallas kernels, forward_products(): pl.pallas_call(forward_kernel, grid_spec=pltpu.PrefetchScalarGridSpec(num...  18.8 us
    pallas_call x4, Pallas kernels, backward_products(): pl.pallas_call(backward_kernel, grid_spec=pltpu.PrefetchScalarGridSpec(nu...  18.2 us
    ppermute x23, waiting for transfers between devices, along_tensor(): return lax.ppermute(value, 'tensor', [(i, i ^ mask) for i in range(N)])  15.8 us
    dot_general x4, matrix products, rows_product(): lax.dot_general(left, right, (((0,), (0,)), ((), ())), preferred_element_...  11.9 us
    ppermute x6, starting transfers between devices, across_groups(): return lax.ppermute(value, 'group', [(0, 1), (1, 0)])  9.77 us
    pallas_call x1, Pallas kernels, hidden_gradients(): pl.pallas_call(hidden_kernel, grid=(ff // width,), in_specs=[fixed, fixed...  7.82 us
    ppermute x6, waiting for transfers between devices, across_groups(): return lax.ppermute(value, 'group', [(0, 1), (1, 0)])  6.03 us
  transfers between devices with their start and end apart: 29, of which 14 were waited for; matrix products, arithmetic and copies ran while one was open for 8% of the time, Pallas kernels for 28%

profile of v3, /device:TPU:0, one launch (start us, length us, event | category | flops | bytes accessed | tf_op | source)
XLA Modules:
  0.0 134.2 jit_solution(5149038248467572729)
XLA Ops:
  1.5 3.0 %collective-permute-start = (bf16[2,4096]{1,0:T(2,128)(2,1)S(1)}, bf16[2,4096]{1,0:T(2,128)(2,1)S(1)}, u32[]{:S(2)}, u32[]{:S(2)}) collective-permute-start(bf16[2,4096]{1,0:T(2,128)(2,1)S(1)} %get-tuple-element.166), channel_id=1, source_target_pairs={{0,16},{16,0},{1,17},{17,1},{2,18},{18,2},{3,19},{19,3},{4,20},{20... | collective-permute-start | bytes 49160 | tf_op jit(solution)/shard_map/ppermute | solution.py:251
  4.5 1.7 %collective-permute-done = bf16[2,4096]{1,0:T(2,128)(2,1)S(1)} collective-permute-done((bf16[2,4096]{1,0:T(2,128)(2,1)S(1)}, bf16[2,4096]{1,0:T(2,128)(2,1)S(1)}, u32[]{:S(2)}, u32[]{:S(2)}) %collective-permute-start) | collective-permute-done | bytes 16416 | tf_op jit(solution)/shard_map/ppermute | solution.py:251
  6.3 4.2 %collective-permute-start.3 = (bf16[2,2,4096]{2,1,0:T(2,128)(2,1)S(1)}, bf16[2,2,4096]{2,1,0:T(2,128)(2,1)S(1)}, u32[]{:S(2)}, u32[]{:S(2)}) collective-permute-start(bf16[2,2,4096]{2,1,0:T(2,128)(2,1)S(1)} %pad_maximum_fusion.11), channel_id=1, source_target_pairs={{0,12},{1,13},{2,14},{3,15},{4,8},{5,9},{6,10},{7,11},{8,4},{9,5},... | collective-permute-start | bytes 98312 | tf_op jit(solution)/shard_map/ppermute | solution.py:247
  11.1 1.3 collective-permute-done.3
  12.4 2.9 %collective-permute-done.2 = bf16[2,2,4096]{2,1,0:T(2,128)(2,1)S(1)} collective-permute-done((bf16[2,2,4096]{2,1,0:T(2,128)(2,1)S(1)}, bf16[2,2,4096]{2,1,0:T(2,128)(2,1)S(1)}, u32[]{:S(2)}, u32[]{:S(2)}) %collective-permute-start.2) | collective-permute-done | bytes 32800 | tf_op jit(solution)/shard_map/ppermute | solution.py:247
  15.4 1.6 %collective-permute-start.4 = (bf16[2,8,4096]{2,1,0:T(8,128)(2,1)S(1)}, bf16[2,8,4096]{2,1,0:T(8,128)(2,1)S(1)}, u32[]{:S(2)}, u32[]{:S(2)}) collective-permute-start(bf16[2,8,4096]{2,1,0:T(8,128)(2,1)S(1)} %pad_maximum_fusion.6), channel_id=1, source_target_pairs={{0,2},{1,3},{2,0},{3,1},{4,6},{5,7},{6,4},{7,5},{8,10},{9,11},{10,... | collective-permute-start | bytes 393224 | tf_op jit(solution)/shard_map/ppermute | solution.py:247
  17.8 2.6 %collective-permute-done.4 = bf16[2,8,4096]{2,1,0:T(8,128)(2,1)S(1)} collective-permute-done((bf16[2,8,4096]{2,1,0:T(8,128)(2,1)S(1)}, bf16[2,8,4096]{2,1,0:T(8,128)(2,1)S(1)}, u32[]{:S(2)}, u32[]{:S(2)}) %collective-permute-start.4) | collective-permute-done | bytes 131104 | tf_op jit(solution)/shard_map/ppermute | solution.py:247
  21.0 1.2 collective-permute-done.5
  22.6 1.6 %collective-permute-start.6 = (bf16[32,512]{1,0:T(8,128)(2,1)S(1)}, bf16[32,512]{1,0:T(8,128)(2,1)S(1)}, u32[]{:S(2)}, u32[]{:S(2)}) collective-permute-start(bf16[32,512]{1,0:T(8,128)(2,1)S(1)} %dynamic-slice.1), channel_id=1, source_target_pairs={{0,16},{16,0},{1,17},{17,1},{2,18},{18,2},{3,19},{19,3},{4,20},{20... | collective-permute-start | bytes 98312 | tf_op jit(solution)/shard_map/ppermute | solution.py:251
  24.1 4.8 %forward_products.4 = (f32[32,1792]{1,0:T(8,128)S(1)}, f32[32,1792]{1,0:T(8,128)S(1)}) custom-call(s32[1]{0:T(128)} %bitcast.3.side_ref, bf16[64,4096]{1,0:T(8,128)(2,1)S(1)} %bitcast.83, bf16[8192,1792]{1,0:T(8,128)(2,1)} %wg_ref.7), custom_call_target="tpu_custom_call" | custom-call | flops 469762048 | bytes 7340032 | tf_op jit(solution)/shard_map/forward_products/pallas_call | solution.py:130
  29.0 0.9 fusion.3
  30.0 1.7 %reshape.177 = f32[32,16,64]{2,1,0:T(8,128)} reshape(f32[32,1024]{1,0:T(8,128)} %fusion.3) | data formatting | bytes 262144 | tf_op jit(solution)/shard_map/reshape | solution.py:21
  31.7 0.9 fusion.7
  32.6 1.0 reshape.176
  33.6 1.1 multiply_reduce_fusion.3
  34.9 4.7 %forward_products.5 = (f32[32,1792]{1,0:T(8,128)S(1)}, bf16[32,1792]{1,0:T(8,128)(2,1)S(1)}) custom-call(s32[1]{0:T(128)} %bitcast.3.side_ref, bf16[64,4096]{1,0:T(8,128)(2,1)S(1)} %bitcast.85, bf16[8192,1792]{1,0:T(8,128)(2,1)} %wg_ref.7, f32[64,1792]{1,0:T(8,128)S(1)} %pad_maximum_fusion.refs_0_), custom_call_target="tpu_custom_call" | custom-call | flops 469762048 | bytes 7340032 | tf_op jit(solution)/shard_map/forward_products/pallas_call | solution.py:130
  40.2 1.6 %collective-permute-start.8 = (f32[32,128]{1,0:T(8,128)S(1)}, f32[32,128]{1,0:T(8,128)S(1)}, u32[]{:S(2)}, u32[]{:S(2)}) collective-permute-start(f32[32,128]{1,0:T(8,128)S(1)} %bitcast.103), channel_id=1, source_target_pairs={{0,2},{1,3},{2,0},{3,1},{4,6},{5,7},{6,4},{7,5},{8,10},{9,11},{10,... | collective-permute-start | bytes 49160 | tf_op jit(solution)/shard_map/ppermute | solution.py:247
  41.7 4.7 %forward_products.6 = (f32[32,1792]{1,0:T(8,128)S(1)}, f32[32,1792]{1,0:T(8,128)S(1)}) custom-call(s32[1]{0:T(128)} %bitcast.3.side_ref, bf16[64,4096]{1,0:T(8,128)(2,1)S(1)} %bitcast.86, bf16[8192,1792]{1,0:T(8,128)(2,1)} %wu_ref.7), custom_call_target="tpu_custom_call" | custom-call | flops 469762048 | bytes 7340032 | tf_op jit(solution)/shard_map/forward_products/pallas_call | solution.py:130
  46.6 4.7 %forward_products.7 = (f32[32,1792]{1,0:T(8,128)S(1)}, bf16[32,1792]{1,0:T(8,128)(2,1)S(1)}) custom-call(s32[1]{0:T(128)} %bitcast.3.side_ref, bf16[64,4096]{1,0:T(8,128)(2,1)S(1)} %bitcast.87, bf16[8192,1792]{1,0:T(8,128)(2,1)} %wu_ref.7, f32[64,1792]{1,0:T(8,128)S(1)} %pad_maximum_fusion.1.refs_0_), custom_call_target="tpu_custom_call" | custom-call | flops 469762048 | bytes 7340032 | tf_op jit(solution)/shard_map/forward_products/pallas_call | solution.py:130
  51.3 2.1 %collective-permute-start.11 = (f32[32,128]{1,0:T(8,128)S(1)}, f32[32,128]{1,0:T(8,128)S(1)}, u32[]{:S(2)}, u32[]{:S(2)}) collective-permute-start(f32[32,128]{1,0:T(8,128)S(1)} %bitcast.105), channel_id=1, source_target_pairs={{0,8},{1,9},{2,10},{3,11},{4,12},{5,13},{6,14},{7,15},{8,0},{9,1},... | collective-permute-start | bytes 49160 | tf_op jit(solution)/shard_map/ppermute | solution.py:247
  54.0 1.5 %collective-permute-start.12 = (bf16[32,1792]{1,0:T(8,128)(2,1)S(1)}, bf16[32,1792]{1,0:T(8,128)(2,1)S(1)}, u32[]{:S(2)}, u32[]{:S(2)}) collective-permute-start(bf16[32,1792]{1,0:T(8,128)(2,1)S(1)} %get-tuple-element.101), channel_id=1, source_target_pairs={{0,16},{16,0},{1,17},{17,1},{2,18},{18,2},{3,19},{19,3},{4,20},{20... | collective-permute-start | bytes 344072 | tf_op jit(solution)/shard_map/ppermute | solution.py:251
  56.5 2.2 %collective-permute-done.12.u1_ref = bf16[32,1792]{1,0:T(8,128)(2,1)S(1)} collective-permute-done((bf16[32,1792]{1,0:T(8,128)(2,1)S(1)}, bf16[32,1792]{1,0:T(8,128)(2,1)S(1)}, u32[]{:S(2)}, u32[]{:S(2)}) %collective-permute-start.12) | collective-permute-done | bytes 114720 | tf_op jit(solution)/shard_map/ppermute | solution.py:251
  58.8 3.1 %copy-done.2 = f32[1024,1792]{1,0:T(8,128)S(1)} copy-done((f32[1024,1792]{1,0:T(8,128)S(1)}, f32[1024,1792]{1,0:T(8,128)}, u32[]{:S(2)}) %copy-start.2) | copy-done | bytes 7340056
  61.8 7.8 %hidden_gradients.1 = (bf16[32,1792]{1,0:T(8,128)(2,1)S(1)}, bf16[32,1792]{1,0:T(8,128)(2,1)S(1)}, f32[32,1024]{1,0:T(8,128)S(1)}, f32[32,1024]{1,0:T(8,128)S(1)}) custom-call(bf16[32,1024]{1,0:T(8,128)(2,1)S(1)} %convert_element_type.121.eug_ref, bf16[32,1024]{1,0:T(8,128)(2,1)S(1)} %convert_element_type.124.euu_ref, f32[1024,1792]{1,0:T(8,128)S(1)} %copy-done.2, ...), custom_call_target="tpu_custom_call" | custom-call | flops 469762048 | bytes 14680064 | tf_op jit(solution)/shard_map/hidden_gradients/pallas_call | solution.py:191
  69.8 4.2 %convolution_multiply_fusion.1 = f32[1024,1792]{1,0:T(8,128)} fusion(bf16[32,1024]{1,0:T(8,128)(2,1)S(1)} %convert_element_type.121.eug_ref, bf16[32,1792]{1,0:T(8,128)(2,1)S(1)} %get-tuple-element.104), kind=kOutput, calls=%fused_computation.1 | convolution fusion | flops 119275520 | bytes 7520256 | tf_op jit(solution)/shard_map/dot_general | solution.py:37
  74.0 1.6 %collective-permute-start.13 = (bf16[2,32,1792]{2,1,0:T(8,128)(2,1)S(1)}, bf16[2,32,1792]{2,1,0:T(8,128)(2,1)S(1)}, u32[]{:S(2)}, u32[]{:S(2)}) collective-permute-start(bf16[2,32,1792]{2,1,0:T(8,128)(2,1)S(1)} %pad_maximum_fusion.3), channel_id=1, source_target_pairs={{0,16},{16,0},{1,17},{17,1},{2,18},{18,2},{3,19},{19,3},{4,20},{20... | collective-permute-start | bytes 688136 | tf_op jit(solution)/shard_map/ppermute | solution.py:251
  76.0 4.2 %convolution_multiply_fusion = f32[1024,1792]{1,0:T(8,128)} fusion(bf16[32,1024]{1,0:T(8,128)(2,1)S(1)} %convert_element_type.124.euu_ref, bf16[32,1792]{1,0:T(8,128)(2,1)S(1)} %get-tuple-element.105), kind=kOutput, calls=%fused_computation | convolution fusion | flops 119275520 | bytes 7520256 | tf_op jit(solution)/shard_map/dot_general | solution.py:37
  80.9 4.6 %backward_products.4 = (f32[32,1024]{1,0:T(8,128)S(1)}, bf16[32,1024]{1,0:T(8,128)(2,1)S(1)}) custom-call(s32[1]{0:T(128)} %bitcast.3.side_ref, bf16[64,1792]{1,0:T(8,128)(2,1)S(1)} %get-tuple-element.125.dg_ref, bf16[64,1792]{1,0:T(8,128)(2,1)S(1)} %get-tuple-element.126.du_ref, bf16[8192,1792]{1,0:T(8,128)(2,1)} %wg_ref.7, bf16[8192,1792]{1,0:T(8,128)(2,1)} %wu_ref.7), custom_call_target="tpu_custom_call" | custom-call | flops 469762048 | bytes 7340032 | tf_op jit(solution)/shard_map/backward_products/pallas_call | solution.py:222
  85.5 2.1 %collective-permute-start.16 = (f32[32,128]{1,0:T(8,128)S(1)}, f32[32,128]{1,0:T(8,128)S(1)}, u32[]{:S(2)}, u32[]{:S(2)}) collective-permute-start(f32[32,128]{1,0:T(8,128)S(1)} %bitcast.101), channel_id=1, source_target_pairs={{0,4},{1,5},{2,6},{3,7},{4,0},{5,1},{6,2},{7,3},{8,12},{9,13},{10,... | collective-permute-start | bytes 49160 | tf_op jit(solution)/shard_map/ppermute | solution.py:247
  87.5 4.5 %backward_products.5 = (f32[32,1024]{1,0:T(8,128)S(1)}, bf16[32,1024]{1,0:T(8,128)(2,1)S(1)}) custom-call(s32[1]{0:T(128)} %bitcast.3.side_ref, bf16[64,1792]{1,0:T(8,128)(2,1)S(1)} %get-tuple-element.125.dg_ref, bf16[64,1792]{1,0:T(8,128)(2,1)S(1)} %get-tuple-element.126.du_ref, bf16[8192,1792]{1,0:T(8,128)(2,1)} %wg_ref.7, bf16[8192,1792]{1,0:T(8,128)(2,1)} %wu_ref.7), custom_call_target="tpu_custom_call" | custom-call | flops 469762048 | bytes 7340032 | tf_op jit(solution)/shard_map/backward_products/pallas_call | solution.py:222
  92.2 1.0 collective-permute-start.17
  93.2 4.5 %backward_products.6 = (f32[32,1024]{1,0:T(8,128)S(1)}, bf16[32,1024]{1,0:T(8,128)(2,1)S(1)}) custom-call(s32[1]{0:T(128)} %bitcast.3.side_ref, bf16[64,1792]{1,0:T(8,128)(2,1)S(1)} %get-tuple-element.125.dg_ref, bf16[64,1792]{1,0:T(8,128)(2,1)S(1)} %get-tuple-element.126.du_ref, bf16[8192,1792]{1,0:T(8,128)(2,1)} %wg_ref.7, bf16[8192,1792]{1,0:T(8,128)(2,1)} %wu_ref.7), custom_call_target="tpu_custom_call" | custom-call | flops 469762048 | bytes 7340032 | tf_op jit(solution)/shard_map/backward_products/pallas_call | solution.py:222
  98.6 1.1 fusion.5
  99.7 1.8 %convolution_multiply_fusion.3 = f32[512,1024]{1,0:T(8,128)} fusion(bf16[32,512]{1,0:T(8,128)(2,1)S(1)} %dynamic-slice_select_fusion, bf16[32,1024]{1,0:T(8,128)(2,1)S(1)} %convert_element_type.131), kind=kOutput, calls=%fused_computation.3 | convolution fusion | flops 34078720 | bytes 2195456 | tf_op jit(solution)/shard_map/dot_general | solution.py:37
  101.5 1.6 %collective-permute-start.19 = (bf16[2,8,2048]{2,1,0:T(8,128)(2,1)S(1)}, bf16[2,8,2048]{2,1,0:T(8,128)(2,1)S(1)}, u32[]{:S(2)}, u32[]{:S(2)}) collective-permute-start(bf16[2,8,2048]{2,1,0:T(8,128)(2,1)S(1)} %slice.215), channel_id=1, source_target_pairs={{0,2},{1,3},{2,0},{3,1},{4,6},{5,7},{6,4},{7,5},{8,10},{9,11},{10,... | collective-permute-start | bytes 196616 | tf_op jit(solution)/shard_map/ppermute | solution.py:247
  103.2 1.3 fusion.1
  104.5 4.6 %backward_products.7 = (f32[32,1024]{1,0:T(8,128)S(1)}, bf16[32,1024]{1,0:T(8,128)(2,1)S(1)}) custom-call(s32[1]{0:T(128)} %bitcast.3.side_ref, bf16[64,1792]{1,0:T(8,128)(2,1)S(1)} %get-tuple-element.125.dg_ref, bf16[64,1792]{1,0:T(8,128)(2,1)S(1)} %get-tuple-element.126.du_ref, bf16[8192,1792]{1,0:T(8,128)(2,1)} %wg_ref.7, bf16[8192,1792]{1,0:T(8,128)(2,1)} %wu_ref.7), custom_call_target="tpu_custom_call" | custom-call | flops 469762048 | bytes 7340032 | tf_op jit(solution)/shard_map/backward_products/pallas_call | solution.py:222
  110.6 1.8 %collective-permute-start.23 = (bf16[2,2,2048]{2,1,0:T(2,128)(2,1)S(1)}, bf16[2,2,2048]{2,1,0:T(2,128)(2,1)S(1)}, u32[]{:S(2)}, u32[]{:S(2)}) collective-permute-start(bf16[2,2,2048]{2,1,0:T(2,128)(2,1)S(1)} %get-tuple-element.160), channel_id=1, source_target_pairs={{0,12},{1,13},{2,14},{3,15},{4,8},{5,9},{6,10},{7,11},{8,4},{9,5},... | collective-permute-start | bytes 49160 | tf_op jit(solution)/shard_map/ppermute | solution.py:247
  112.8 2.3 %collective-permute-start.21 = (bf16[2,2,2048]{2,1,0:T(2,128)(2,1)S(1)}, bf16[2,2,2048]{2,1,0:T(2,128)(2,1)S(1)}, u32[]{:S(2)}, u32[]{:S(2)}) collective-permute-start(bf16[2,2,2048]{2,1,0:T(2,128)(2,1)S(1)} %get-tuple-element.162), channel_id=1, source_target_pairs={{0,4},{1,5},{2,6},{3,7},{4,0},{5,1},{6,2},{7,3},{8,12},{9,13},{10,... | collective-permute-start | bytes 49160 | tf_op jit(solution)/shard_map/ppermute | solution.py:247
  115.2 1.0 collective-permute-done.23
  117.7 1.8 %convolution_multiply_fusion.2 = f32[512,1024]{1,0:T(8,128)} fusion(bf16[32,512]{1,0:T(8,128)(2,1)S(1)} %dynamic-slice_select_fusion, bf16[32,1024]{1,0:T(8,128)(2,1)S(1)} %convert_element_type.134), kind=kOutput, calls=%fused_computation.2 | convolution fusion | flops 34078720 | bytes 2195456 | tf_op jit(solution)/shard_map/dot_general | solution.py:37
  119.5 2.3 %collective-permute-done.24 = bf16[2,8,3072]{2,1,0:T(8,128)(2,1)S(1)} collective-permute-done((bf16[2,8,3072]{2,1,0:T(8,128)(2,1)S(1)}, bf16[2,8,3072]{2,1,0:T(8,128)(2,1)S(1)}, u32[]{:S(2)}, u32[]{:S(2)}) %collective-permute-start.24) | collective-permute-done | bytes 98336 | tf_op jit(solution)/shard_map/ppermute | solution.py:247
  122.0 2.4 %collective-permute-start.27 = (bf16[2,2,4096]{2,1,0:T(2,128)(2,1)S(1)}, bf16[2,2,4096]{2,1,0:T(2,128)(2,1)S(1)}, u32[]{:S(2)}, u32[]{:S(2)}) collective-permute-start(bf16[2,2,4096]{2,1,0:T(2,128)(2,1)S(1)} %get-tuple-element.157), channel_id=1, source_target_pairs={{0,12},{1,13},{2,14},{3,15},{4,8},{5,9},{6,10},{7,11},{8,4},{9,5},... | collective-permute-start | bytes 98312 | tf_op jit(solution)/shard_map/ppermute | solution.py:247
  125.3 1.1 collective-permute-start.25
  126.5 1.3 collective-permute-done.27
  127.7 1.6 %collective-permute-done.26 = bf16[2,2,4096]{2,1,0:T(2,128)(2,1)S(1)} collective-permute-done((bf16[2,2,4096]{2,1,0:T(2,128)(2,1)S(1)}, bf16[2,2,4096]{2,1,0:T(2,128)(2,1)S(1)}, u32[]{:S(2)}, u32[]{:S(2)}) %collective-permute-start.26) | collective-permute-done | bytes 32800 | tf_op jit(solution)/shard_map/ppermute | solution.py:247
  129.7 1.5 %collective-permute-start.28 = (bf16[2,4096]{1,0:T(2,128)(2,1)S(1)}, bf16[2,4096]{1,0:T(2,128)(2,1)S(1)}, u32[]{:S(2)}, u32[]{:S(2)}) collective-permute-start(bf16[2,4096]{1,0:T(2,128)(2,1)S(1)} %fusion.26), channel_id=1, source_target_pairs={{0,16},{16,0},{1,17},{17,1},{2,18},{18,2},{3,19},{19,3},{4,20},{20... | collective-permute-start | bytes 49160 | tf_op jit(solution)/shard_map/ppermute | solution.py:251
  131.4 2.1 %collective-permute-done.28 = bf16[2,4096]{1,0:T(2,128)(2,1)S(1)} collective-permute-done((bf16[2,4096]{1,0:T(2,128)(2,1)S(1)}, bf16[2,4096]{1,0:T(2,128)(2,1)S(1)}, u32[]{:S(2)}, u32[]{:S(2)}) %collective-permute-start.28) | collective-permute-done | bytes 16416 | tf_op jit(solution)/shard_map/ppermute | solution.py:251
  (126 shorter events, 14.0 us)
Async XLA Ops:
  0.6 20.2 %copy-start = (bf16[32,1792]{1,0:T(8,128)(2,1)S(1)}, bf16[32,1792]{1,0:T(8,128)(2,1)}, u32[]{:S(2)}) copy-start(bf16[32,1792]{1,0:T(8,128)(2,1)} %param.17) | copy-start | bytes 344068
  1.5 4.8 %collective-permute-start = (bf16[2,4096]{1,0:T(2,128)(2,1)S(1)}, bf16[2,4096]{1,0:T(2,128)(2,1)S(1)}, u32[]{:S(2)}, u32[]{:S(2)}) collective-permute-start(bf16[2,4096]{1,0:T(2,128)(2,1)S(1)} %get-tuple-element.166), channel_id=1, source_target_pairs={{0,16},{16,0},{1,17},{17,1},{2,18},{18,2},{3,19},{19,3},{4,20},{20... | collective-permute-start | bytes 49160 | tf_op jit(solution)/shard_map/ppermute | solution.py:251
  6.3 6.1 %collective-permute-start.3 = (bf16[2,2,4096]{2,1,0:T(2,128)(2,1)S(1)}, bf16[2,2,4096]{2,1,0:T(2,128)(2,1)S(1)}, u32[]{:S(2)}, u32[]{:S(2)}) collective-permute-start(bf16[2,2,4096]{2,1,0:T(2,128)(2,1)S(1)} %pad_maximum_fusion.11), channel_id=1, source_target_pairs={{0,12},{1,13},{2,14},{3,15},{4,8},{5,9},{6,10},{7,11},{8,4},{9,5},... | collective-permute-start | bytes 98312 | tf_op jit(solution)/shard_map/ppermute | solution.py:247
  10.4 4.8 %collective-permute-start.2 = (bf16[2,2,4096]{2,1,0:T(2,128)(2,1)S(1)}, bf16[2,2,4096]{2,1,0:T(2,128)(2,1)S(1)}, u32[]{:S(2)}, u32[]{:S(2)}) collective-permute-start(bf16[2,2,4096]{2,1,0:T(2,128)(2,1)S(1)} %pad_maximum_fusion.11), channel_id=1, source_target_pairs={{0,8},{1,9},{2,10},{3,11},{4,12},{5,13},{6,14},{7,15},{8,0},{9,1},... | collective-permute-start | bytes 98312 | tf_op jit(solution)/shard_map/ppermute | solution.py:247
  10.4 4.8 %collective-permute-start.1 = (bf16[2,2,4096]{2,1,0:T(2,128)(2,1)S(1)}, bf16[2,2,4096]{2,1,0:T(2,128)(2,1)S(1)}, u32[]{:S(2)}, u32[]{:S(2)}) collective-permute-start(bf16[2,2,4096]{2,1,0:T(2,128)(2,1)S(1)} %pad_maximum_fusion.11), channel_id=1, source_target_pairs={{0,4},{1,5},{2,6},{3,7},{4,0},{5,1},{6,2},{7,3},{8,12},{9,13},{10,... | collective-permute-start | bytes 98312 | tf_op jit(solution)/shard_map/ppermute | solution.py:247
  15.4 5.0 %collective-permute-start.4 = (bf16[2,8,4096]{2,1,0:T(8,128)(2,1)S(1)}, bf16[2,8,4096]{2,1,0:T(8,128)(2,1)S(1)}, u32[]{:S(2)}, u32[]{:S(2)}) collective-permute-start(bf16[2,8,4096]{2,1,0:T(8,128)(2,1)S(1)} %pad_maximum_fusion.6), channel_id=1, source_target_pairs={{0,2},{1,3},{2,0},{3,1},{4,6},{5,7},{6,4},{7,5},{8,10},{9,11},{10,... | collective-permute-start | bytes 393224 | tf_op jit(solution)/shard_map/ppermute | solution.py:247
  20.6 1.6 %collective-permute-start.5 = (bf16[2,16,4096]{2,1,0:T(8,128)(2,1)S(1)}, bf16[2,16,4096]{2,1,0:T(8,128)(2,1)S(1)}, u32[]{:S(2)}, u32[]{:S(2)}) collective-permute-start(bf16[2,16,4096]{2,1,0:T(8,128)(2,1)S(1)} %concatenate.67), channel_id=1, source_target_pairs={{0,1},{1,0},{2,3},{3,2},{4,5},{5,4},{6,7},{7,6},{8,9},{9,8},{10,11... | collective-permute-start | bytes 786440 | tf_op jit(solution)/shard_map/ppermute | solution.py:247
  20.8 54.9 %copy-start.7 = (f32[32,16]{1,0:T(8,128)}, f32[32,16]{1,0:T(8,128)S(1)}, u32[]{:S(2)}) copy-start(f32[32,16]{1,0:T(8,128)S(1)} %fusion.27) | copy-start | bytes 6148
  22.6 6.4 %collective-permute-start.6 = (bf16[32,512]{1,0:T(8,128)(2,1)S(1)}, bf16[32,512]{1,0:T(8,128)(2,1)S(1)}, u32[]{:S(2)}, u32[]{:S(2)}) collective-permute-start(bf16[32,512]{1,0:T(8,128)(2,1)S(1)} %dynamic-slice.1), channel_id=1, source_target_pairs={{0,16},{16,0},{1,17},{17,1},{2,18},{18,2},{3,19},{19,3},{4,20},{20... | collective-permute-start | bytes 98312 | tf_op jit(solution)/shard_map/ppermute | solution.py:251
  24.1 4.9 %copy-start.5 = (f32[512,1024]{1,0:T(8,128)S(1)}, f32[512,1024]{1,0:T(8,128)}, u32[]{:S(2)}) copy-start(f32[512,1024]{1,0:T(8,128)} %param.13) | copy-start | bytes 6291460
  29.0 2.7 %copy-start.3 = (f32[512,1024]{1,0:T(8,128)S(1)}, f32[512,1024]{1,0:T(8,128)}, u32[]{:S(2)}) copy-start(f32[512,1024]{1,0:T(8,128)} %param.12) | copy-start | bytes 6291460
  34.8 4.8 %collective-permute-start.7 = (f32[32,128]{1,0:T(8,128)S(1)}, f32[32,128]{1,0:T(8,128)S(1)}, u32[]{:S(2)}, u32[]{:S(2)}) collective-permute-start(f32[32,128]{1,0:T(8,128)S(1)} %pad_maximum_fusion.13), channel_id=1, source_target_pairs={{0,1},{1,0},{2,3},{3,2},{4,5},{5,4},{6,7},{7,6},{8,9},{9,8},{10,11... | collective-permute-start | bytes 49160 | tf_op jit(solution)/shard_map/ppermute | solution.py:247
  39.6 6.8 %collective-permute-start.9 = (bf16[32,1792]{1,0:T(8,128)(2,1)S(1)}, bf16[32,1792]{1,0:T(8,128)(2,1)S(1)}, u32[]{:S(2)}, u32[]{:S(2)}) collective-permute-start(bf16[32,1792]{1,0:T(8,128)(2,1)S(1)} %get-tuple-element.87), channel_id=1, source_target_pairs={{0,16},{16,0},{1,17},{17,1},{2,18},{18,2},{3,19},{19,3},{4,20},{20... | collective-permute-start | bytes 344072 | tf_op jit(solution)/shard_map/ppermute | solution.py:251
  40.2 6.2 %collective-permute-start.8 = (f32[32,128]{1,0:T(8,128)S(1)}, f32[32,128]{1,0:T(8,128)S(1)}, u32[]{:S(2)}, u32[]{:S(2)}) collective-permute-start(f32[32,128]{1,0:T(8,128)S(1)} %bitcast.103), channel_id=1, source_target_pairs={{0,2},{1,3},{2,0},{3,1},{4,6},{5,7},{6,4},{7,5},{8,10},{9,11},{10,... | collective-permute-start | bytes 49160 | tf_op jit(solution)/shard_map/ppermute | solution.py:247
  46.5 4.8 %collective-permute-start.10 = (f32[32,128]{1,0:T(8,128)S(1)}, f32[32,128]{1,0:T(8,128)S(1)}, u32[]{:S(2)}, u32[]{:S(2)}) collective-permute-start(f32[32,128]{1,0:T(8,128)S(1)} %bitcast.102), channel_id=1, source_target_pairs={{0,4},{1,5},{2,6},{3,7},{4,0},{5,1},{6,2},{7,3},{8,12},{9,13},{10,... | collective-permute-start | bytes 49160 | tf_op jit(solution)/shard_map/ppermute | solution.py:247
  51.3 4.7 %collective-permute-start.11 = (f32[32,128]{1,0:T(8,128)S(1)}, f32[32,128]{1,0:T(8,128)S(1)}, u32[]{:S(2)}, u32[]{:S(2)}) collective-permute-start(f32[32,128]{1,0:T(8,128)S(1)} %bitcast.105), channel_id=1, source_target_pairs={{0,8},{1,9},{2,10},{3,11},{4,12},{5,13},{6,14},{7,15},{8,0},{9,1},... | collective-permute-start | bytes 49160 | tf_op jit(solution)/shard_map/ppermute | solution.py:247
  54.0 4.8 %collective-permute-start.12 = (bf16[32,1792]{1,0:T(8,128)(2,1)S(1)}, bf16[32,1792]{1,0:T(8,128)(2,1)S(1)}, u32[]{:S(2)}, u32[]{:S(2)}) collective-permute-start(bf16[32,1792]{1,0:T(8,128)(2,1)S(1)} %get-tuple-element.101), channel_id=1, source_target_pairs={{0,16},{16,0},{1,17},{17,1},{2,18},{18,2},{3,19},{19,3},{4,20},{20... | collective-permute-start | bytes 344072 | tf_op jit(solution)/shard_map/ppermute | solution.py:251
  58.8 3.1 %copy-start.2 = (f32[1024,1792]{1,0:T(8,128)S(1)}, f32[1024,1792]{1,0:T(8,128)}, u32[]{:S(2)}) copy-start(f32[1024,1792]{1,0:T(8,128)} %bg_ref.1) | copy-start | bytes 22020100
  74.0 6.2 %collective-permute-start.13 = (bf16[2,32,1792]{2,1,0:T(8,128)(2,1)S(1)}, bf16[2,32,1792]{2,1,0:T(8,128)(2,1)S(1)}, u32[]{:S(2)}, u32[]{:S(2)}) collective-permute-start(bf16[2,32,1792]{2,1,0:T(8,128)(2,1)S(1)} %pad_maximum_fusion.3), channel_id=1, source_target_pairs={{0,16},{16,0},{1,17},{17,1},{2,18},{18,2},{3,19},{19,3},{4,20},{20... | collective-permute-start | bytes 688136 | tf_op jit(solution)/shard_map/ppermute | solution.py:251
  76.0 4.2 %collective-permute-start.14 = (f32[32,128]{1,0:T(8,128)S(1)}, f32[32,128]{1,0:T(8,128)S(1)}, u32[]{:S(2)}, u32[]{:S(2)}) collective-permute-start(f32[32,128]{1,0:T(8,128)S(1)} %pad_maximum_fusion.14), channel_id=1, source_target_pairs={{0,1},{1,0},{2,3},{3,2},{4,5},{5,4},{6,7},{7,6},{8,9},{9,8},{10,11... | collective-permute-start | bytes 49160 | tf_op jit(solution)/shard_map/ppermute | solution.py:247
  80.2 5.2 %collective-permute-start.15 = (f32[32,128]{1,0:T(8,128)S(1)}, f32[32,128]{1,0:T(8,128)S(1)}, u32[]{:S(2)}, u32[]{:S(2)}) collective-permute-start(f32[32,128]{1,0:T(8,128)S(1)} %bitcast.99), channel_id=1, source_target_pairs={{0,2},{1,3},{2,0},{3,1},{4,6},{5,7},{6,4},{7,5},{8,10},{9,11},{10,... | collective-permute-start | bytes 49160 | tf_op jit(solution)/shard_map/ppermute | solution.py:247
  85.5 6.6 %collective-permute-start.16 = (f32[32,128]{1,0:T(8,128)S(1)}, f32[32,128]{1,0:T(8,128)S(1)}, u32[]{:S(2)}, u32[]{:S(2)}) collective-permute-start(f32[32,128]{1,0:T(8,128)S(1)} %bitcast.101), channel_id=1, source_target_pairs={{0,4},{1,5},{2,6},{3,7},{4,0},{5,1},{6,2},{7,3},{8,12},{9,13},{10,... | collective-permute-start | bytes 49160 | tf_op jit(solution)/shard_map/ppermute | solution.py:247
  92.1 5.7 %collective-permute-start.18 = (bf16[32,2048]{1,0:T(8,128)(2,1)S(1)}, bf16[32,2048]{1,0:T(8,128)(2,1)S(1)}, u32[]{:S(2)}, u32[]{:S(2)}) collective-permute-start(bf16[32,2048]{1,0:T(8,128)(2,1)S(1)} %pad_maximum_fusion.7), channel_id=1, source_target_pairs={{0,1},{1,0},{2,3},{3,2},{4,5},{5,4},{6,7},{7,6},{8,9},{9,8},{10,11... | collective-permute-start | bytes 393224 | tf_op jit(solution)/shard_map/ppermute | solution.py:247
  92.2 5.7 %copy-start.8 = (f32[32,16]{1,0:T(8,128)S(1)}, f32[32,16]{1,0:T(8,128)}, u32[]{:S(2)}) copy-start(f32[32,16]{1,0:T(8,128)} %copy-done.7) | copy-start | bytes 6148
  92.2 6.4 %copy-start.4 = (f32[512,1024]{1,0:T(8,128)S(1)}, f32[512,1024]{1,0:T(8,128)}, u32[]{:S(2)}) copy-start(f32[512,1024]{1,0:T(8,128)} %param.12) | copy-start | bytes 6291460
  92.2 5.5 %collective-permute-start.17 = (f32[32,128]{1,0:T(8,128)S(1)}, f32[32,128]{1,0:T(8,128)S(1)}, u32[]{:S(2)}, u32[]{:S(2)}) collective-permute-start(f32[32,128]{1,0:T(8,128)S(1)} %bitcast.106), channel_id=1, source_target_pairs={{0,8},{1,9},{2,10},{3,11},{4,12},{5,13},{6,14},{7,15},{8,0},{9,1},... | collective-permute-start | bytes 49160 | tf_op jit(solution)/shard_map/ppermute | solution.py:247
  97.8 0.7 copy-start.9
  98.6 2.8 %copy-start.10 = (bf16[32,2048]{1,0:T(8,128)(2,1)S(1)}, bf16[32,2048]{1,0:T(8,128)(2,1)}, u32[]{:S(2)}) copy-start(bf16[32,2048]{1,0:T(8,128)(2,1)} %copy-done.9) | copy-start | bytes 393220
  99.7 3.5 %copy-start.6 = (f32[512,1024]{1,0:T(8,128)S(1)}, f32[512,1024]{1,0:T(8,128)}, u32[]{:S(2)}) copy-start(f32[512,1024]{1,0:T(8,128)} %param.13) | copy-start | bytes 6291460
  101.5 7.6 %collective-permute-start.19 = (bf16[2,8,2048]{2,1,0:T(8,128)(2,1)S(1)}, bf16[2,8,2048]{2,1,0:T(8,128)(2,1)S(1)}, u32[]{:S(2)}, u32[]{:S(2)}) collective-permute-start(bf16[2,8,2048]{2,1,0:T(8,128)(2,1)S(1)} %slice.215), channel_id=1, source_target_pairs={{0,2},{1,3},{2,0},{3,1},{4,6},{5,7},{6,4},{7,5},{8,10},{9,11},{10,... | collective-permute-start | bytes 196616 | tf_op jit(solution)/shard_map/ppermute | solution.py:247
  109.1 0.6 copy-start.11
  110.6 5.6 %collective-permute-start.23 = (bf16[2,2,2048]{2,1,0:T(2,128)(2,1)S(1)}, bf16[2,2,2048]{2,1,0:T(2,128)(2,1)S(1)}, u32[]{:S(2)}, u32[]{:S(2)}) collective-permute-start(bf16[2,2,2048]{2,1,0:T(2,128)(2,1)S(1)} %get-tuple-element.160), channel_id=1, source_target_pairs={{0,12},{1,13},{2,14},{3,15},{4,8},{5,9},{6,10},{7,11},{8,4},{9,5},... | collective-permute-start | bytes 49160 | tf_op jit(solution)/shard_map/ppermute | solution.py:247
  112.4 4.6 %collective-permute-start.22 = (bf16[2,2,2048]{2,1,0:T(2,128)(2,1)S(1)}, bf16[2,2,2048]{2,1,0:T(2,128)(2,1)S(1)}, u32[]{:S(2)}, u32[]{:S(2)}) collective-permute-start(bf16[2,2,2048]{2,1,0:T(2,128)(2,1)S(1)} %get-tuple-element.161), channel_id=1, source_target_pairs={{0,8},{1,9},{2,10},{3,11},{4,12},{5,13},{6,14},{7,15},{8,0},{9,1},... | collective-permute-start | bytes 49160 | tf_op jit(solution)/shard_map/ppermute | solution.py:247
  112.8 4.2 %collective-permute-start.21 = (bf16[2,2,2048]{2,1,0:T(2,128)(2,1)S(1)}, bf16[2,2,2048]{2,1,0:T(2,128)(2,1)S(1)}, u32[]{:S(2)}, u32[]{:S(2)}) collective-permute-start(bf16[2,2,2048]{2,1,0:T(2,128)(2,1)S(1)} %get-tuple-element.162), channel_id=1, source_target_pairs={{0,4},{1,5},{2,6},{3,7},{4,0},{5,1},{6,2},{7,3},{8,12},{9,13},{10,... | collective-permute-start | bytes 49160 | tf_op jit(solution)/shard_map/ppermute | solution.py:247
  115.1 1.9 %collective-permute-start.20 = (bf16[2,16,2560]{2,1,0:T(8,128)(2,1)S(1)}, bf16[2,16,2560]{2,1,0:T(8,128)(2,1)S(1)}, u32[]{:S(2)}, u32[]{:S(2)}) collective-permute-start(bf16[2,16,2560]{2,1,0:T(8,128)(2,1)S(1)} %fusion.12), channel_id=1, source_target_pairs={{0,1},{1,0},{2,3},{3,2},{4,5},{5,4},{6,7},{7,6},{8,9},{9,8},{10,11... | collective-permute-start | bytes 491528 | tf_op jit(solution)/shard_map/ppermute | solution.py:247
  117.1 14.2 %copy-start.12 = (s32[16]{0:T(128)S(1)}, s32[16]{0:T(128)}, u32[]{:S(2)}) copy-start(s32[16]{0:T(128)} %iota_xor_fusion) | copy-start | bytes 196
  117.1 17.1 %copy-start.1 = (bf16[32,1792]{1,0:T(8,128)(2,1)S(1)}, bf16[32,1792]{1,0:T(8,128)(2,1)}, u32[]{:S(2)}) copy-start(bf16[32,1792]{1,0:T(8,128)(2,1)} %param.17) | copy-start | bytes 344068
  117.1 4.7 %collective-permute-start.24 = (bf16[2,8,3072]{2,1,0:T(8,128)(2,1)S(1)}, bf16[2,8,3072]{2,1,0:T(8,128)(2,1)S(1)}, u32[]{:S(2)}, u32[]{:S(2)}) collective-permute-start(bf16[2,8,3072]{2,1,0:T(8,128)(2,1)S(1)} %fusion.14), channel_id=1, source_target_pairs={{0,2},{1,3},{2,0},{3,1},{4,6},{5,7},{6,4},{7,5},{8,10},{9,11},{10,... | collective-permute-start | bytes 294920 | tf_op jit(solution)/shard_map/ppermute | solution.py:247
  122.0 5.8 %collective-permute-start.27 = (bf16[2,2,4096]{2,1,0:T(2,128)(2,1)S(1)}, bf16[2,2,4096]{2,1,0:T(2,128)(2,1)S(1)}, u32[]{:S(2)}, u32[]{:S(2)}) collective-permute-start(bf16[2,2,4096]{2,1,0:T(2,128)(2,1)S(1)} %get-tuple-element.157), channel_id=1, source_target_pairs={{0,12},{1,13},{2,14},{3,15},{4,8},{5,9},{6,10},{7,11},{8,4},{9,5},... | collective-permute-start | bytes 98312 | tf_op jit(solution)/shard_map/ppermute | solution.py:247
  124.4 4.9 %collective-permute-start.26 = (bf16[2,2,4096]{2,1,0:T(2,128)(2,1)S(1)}, bf16[2,2,4096]{2,1,0:T(2,128)(2,1)S(1)}, u32[]{:S(2)}, u32[]{:S(2)}) collective-permute-start(bf16[2,2,4096]{2,1,0:T(2,128)(2,1)S(1)} %get-tuple-element.158), channel_id=1, source_target_pairs={{0,8},{1,9},{2,10},{3,11},{4,12},{5,13},{6,14},{7,15},{8,0},{9,1},... | collective-permute-start | bytes 98312 | tf_op jit(solution)/shard_map/ppermute | solution.py:247
  125.3 4.3 %collective-permute-start.25 = (bf16[2,2,4096]{2,1,0:T(2,128)(2,1)S(1)}, bf16[2,2,4096]{2,1,0:T(2,128)(2,1)S(1)}, u32[]{:S(2)}, u32[]{:S(2)}) collective-permute-start(bf16[2,2,4096]{2,1,0:T(2,128)(2,1)S(1)} %get-tuple-element.159), channel_id=1, source_target_pairs={{0,4},{1,5},{2,6},{3,7},{4,0},{5,1},{6,2},{7,3},{8,12},{9,13},{10,... | collective-permute-start | bytes 98312 | tf_op jit(solution)/shard_map/ppermute | solution.py:247
  129.7 3.8 %collective-permute-start.28 = (bf16[2,4096]{1,0:T(2,128)(2,1)S(1)}, bf16[2,4096]{1,0:T(2,128)(2,1)S(1)}, u32[]{:S(2)}, u32[]{:S(2)}) collective-permute-start(bf16[2,4096]{1,0:T(2,128)(2,1)S(1)} %fusion.26), channel_id=1, source_target_pairs={{0,16},{16,0},{1,17},{17,1},{2,18},{18,2},{3,19},{19,3},{4,20},{20... | collective-permute-start | bytes 49160 | tf_op jit(solution)/shard_map/ppermute | solution.py:251

commit v4 on v0

--- a/solution.py
+++ b/solution.py
@@ -1,13 +1,18 @@
+import functools
+
 import jax
 import jax.numpy as jnp
 from jax import lax
+from jax.experimental import pallas as pl
+from jax.experimental.pallas import tpu as pltpu
 from jax.sharding import PartitionSpec as P
 
 R = 64
 AG = 16
 
-
 adapter_scale = 2.0
+BF16 = jnp.bfloat16
+F32 = jnp.float32
 
 
 def agent_mask(agent):
@@ -30,7 +35,13 @@
     )
 
 
-def per_device(tokens, gate_weight, up_weight, a_gate, a_up, b_gate, b_up, agent, d_hidden):
+def rows_product(left, right):
+    return lax.dot_general(
+        left, right, (((0,), (0,)), ((), ())), preferred_element_type=jnp.float32
+    )
+
+
+def plain_device(tokens, gate_weight, up_weight, a_gate, a_up, b_gate, b_up, agent, d_hidden):
     onehot = agent_mask(agent)
     feat_rows = a_gate.shape[0]
     feat_start = lax.axis_index("tensor") * feat_rows
@@ -80,18 +91,10 @@
         scatter_dimension=0,
         tiled=True,
     ).astype(jnp.bfloat16)
-    gate_down_gradient = adapter_scale * lax.dot_general(
-        own_cols, gate_factor_gate, (((0,), (0,)), ((), ())), preferred_element_type=jnp.float32
-    )
-    up_down_gradient = adapter_scale * lax.dot_general(
-        own_cols, gate_factor_up, (((0,), (0,)), ((), ())), preferred_element_type=jnp.float32
-    )
-    gate_lift_gradient = adapter_scale * lax.dot_general(
-        up_factor_gate, gate_gradient, (((0,), (0,)), ((), ())), preferred_element_type=jnp.float32
-    )
-    up_lift_gradient = adapter_scale * lax.dot_general(
-        up_factor_up, up_gradient, (((0,), (0,)), ((), ())), preferred_element_type=jnp.float32
-    )
+    gate_down_gradient = adapter_scale * rows_product(own_cols, gate_factor_gate)
+    up_down_gradient = adapter_scale * rows_product(own_cols, gate_factor_up)
+    gate_lift_gradient = adapter_scale * rows_product(up_factor_gate, gate_gradient)
+    up_lift_gradient = adapter_scale * rows_product(up_factor_up, up_gradient)
     return (
         token_gradient,
         gate_down_gradient,
@@ -101,7 +104,440 @@
     )
 
 
+def forward_kernel(first, side_ref, x_ref, wg_ref, wu_ref, keep_ref, send_ref, piece, sem):
+    pieces, depth, count = piece.shape[1:]
+    half = keep_ref.shape[1]
+    base = side_ref[0] * (pieces * depth)
+    copies = []
+    for i, w_ref in enumerate((wg_ref, wu_ref)):
+        for k in range(pieces):
+            source = pl.ds(pl.multiple_of(base + k * depth, depth), depth)
+            copy = pltpu.make_async_copy(
+                w_ref.at[source, pl.ds(first, count)], piece.at[i, k], sem.at[i, k]
+            )
+            copy.start()
+            copies.append(copy)
+    for i in range(2):
+        total = None
+        for k in range(pieces):
+            copies[i * pieces + k].wait()
+            term = jnp.dot(
+                x_ref[:, k * depth : (k + 1) * depth], piece[i, k], preferred_element_type=F32
+            )
+            total = term if total is None else total + term
+        keep_ref[i] = total[:half]
+        send_ref[i] = total[half:].astype(send_ref.dtype)
+
+
+def forward_products(side, x, gate_weight, up_weight, first, count, pieces=4):
+    rows, depth = x.shape
+    vmem = pl.BlockSpec(memory_space=pltpu.VMEM)
+    hbm = pl.BlockSpec(memory_space=pltpu.HBM)
+    return pl.pallas_call(
+        functools.partial(forward_kernel, first),
+        in_specs=[pl.BlockSpec(memory_space=pltpu.SMEM), vmem, hbm, hbm],
+        out_specs=[vmem] * 2,
+        out_shape=[
+            jax.ShapeDtypeStruct((2, rows // 2, count), F32),
+            jax.ShapeDtypeStruct((2, rows // 2, count), BF16),
+        ],
+        scratch_shapes=[
+            pltpu.VMEM((2, pieces, depth // pieces, count), BF16),
+            pltpu.SemaphoreType.DMA((2, pieces)),
+        ],
+        compiler_params=pltpu.CompilerParams(vmem_limit_bytes=20 << 20),
+        cost_estimate=pl.CostEstimate(
+            flops=4 * rows * count * depth, bytes_accessed=6 * count * depth, transcendentals=0
+        ),
+        name="forward_products",
+    )(
+        side,
+        x,
+        pltpu.with_memory_space_constraint(gate_weight, pltpu.HBM),
+        pltpu.with_memory_space_constraint(up_weight, pltpu.HBM),
+    )
+
+
+def hidden_kernel(
+    eug_ref, euu_ref, bg_ref, bu_ref, keep_ref, far_ref, dh_ref, d_ref, pg_ref, pu_ref
+):
+    @pl.when(pl.program_id(0) == 0)
+    def _():
+        pg_ref[...] = jnp.zeros_like(pg_ref)
+        pu_ref[...] = jnp.zeros_like(pu_ref)
+
+    bg = bg_ref[...].astype(BF16)
+    bu = bu_ref[...].astype(BF16)
+    gate = (
+        keep_ref[0]
+        + far_ref[0].astype(F32)
+        + adapter_scale * jnp.dot(eug_ref[...], bg, preferred_element_type=F32)
+    )
+    up = (
+        keep_ref[1]
+        + far_ref[1].astype(F32)
+        + adapter_scale * jnp.dot(euu_ref[...], bu, preferred_element_type=F32)
+    )
+    sig = jax.nn.sigmoid(gate)
+    hidden_grad = dh_ref[...]
+    dg = (hidden_grad * up * sig * (1.0 + gate * (1.0 - sig))).astype(BF16)
+    du = (hidden_grad * gate * sig).astype(BF16)
+    d_ref[0] = dg
+    d_ref[1] = du
+    pg_ref[...] += flipped_product(dg, bg)
+    pu_ref[...] += flipped_product(du, bu)
+
+
+def hidden_gradients(eug, euu, b_gate, b_up, keep, far, hidden_grad, first, width=256):
+    rows, wide = eug.shape
+    count = keep.shape[2]
+    start = first // width
+    fixed = pl.BlockSpec((rows, wide), lambda k: (0, 0))
+    b_block = pl.BlockSpec((wide, width), lambda k: (0, k + start))
+    block = pl.BlockSpec((2, rows, width), lambda k: (0, 0, k))
+    return pl.pallas_call(
+        hidden_kernel,
+        grid=(count // width,),
+        in_specs=[
+            fixed,
+            fixed,
+            b_block,
+            b_block,
+            block,
+            block,
+            pl.BlockSpec((rows, width), lambda k: (0, k + start)),
+        ],
+        out_specs=[block, fixed, fixed],
+        out_shape=[jax.ShapeDtypeStruct((2, rows, count), BF16)]
+        + [jax.ShapeDtypeStruct((rows, wide), F32)] * 2,
+        compiler_params=pltpu.CompilerParams(vmem_limit_bytes=20 << 20),
+        cost_estimate=pl.CostEstimate(
+            flops=8 * rows * wide * count, bytes_accessed=16 * wide * count, transcendentals=0
+        ),
+        name="hidden_gradients",
+    )(
+        eug,
+        euu,
+        pltpu.with_memory_space_constraint(b_gate, pltpu.HBM),
+        pltpu.with_memory_space_constraint(b_up, pltpu.HBM),
+        keep,
+        far,
+        hidden_grad,
+    )
+
+
+def backward_kernel(first, side_ref, dg_ref, du_ref, wg_ref, wu_ref, keep_ref, send_ref, piece, sem):
+    pieces, depth = piece.shape[1:3]
+    base = side_ref[0] * (wg_ref.shape[0] // 2) + first
+    copies = []
+    for k in range(pieces):
+        for i, w_ref in enumerate((wg_ref, wu_ref)):
+            source = pl.ds(pl.multiple_of(base + k * depth, depth), depth)
+            copy = pltpu.make_async_copy(w_ref.at[source], piece.at[i, k], sem.at[i, k])
+            copy.start()
+            copies.append(copy)
+    q = dg_ref.shape[0] // 4
+    for k in range(pieces):
+        copies[2 * k].wait()
+        total = flipped_product(dg_ref[...], piece[0, k])
+        copies[2 * k + 1].wait()
+        total += flipped_product(du_ref[...], piece[1, k])
+        out = pl.ds(k * depth, depth)
+        keep_ref[:q, out] = total[:q]
+        keep_ref[q:, out] = total[2 * q : 3 * q]
+        send_ref[:q, out] = total[q : 2 * q].astype(send_ref.dtype)
+        send_ref[q:, out] = total[3 * q :].astype(send_ref.dtype)
+
+
+def backward_products(side, dg, du, gate_weight, up_weight, first, count, pieces=4):
+    rows, ff = dg.shape
+    vmem = pl.BlockSpec(memory_space=pltpu.VMEM)
+    hbm = pl.BlockSpec(memory_space=pltpu.HBM)
+    return pl.pallas_call(
+        functools.partial(backward_kernel, first),
+        in_specs=[pl.BlockSpec(memory_space=pltpu.SMEM), vmem, vmem, hbm, hbm],
+        out_specs=[vmem] * 2,
+        out_shape=[
+            jax.ShapeDtypeStruct((rows // 2, count), F32),
+            jax.ShapeDtypeStruct((rows // 2, count), BF16),
+        ],
+        scratch_shapes=[
+            pltpu.VMEM((2, pieces, count // pieces, ff), BF16),
+            pltpu.SemaphoreType.DMA((2, pieces)),
+        ],
+        compiler_params=pltpu.CompilerParams(vmem_limit_bytes=20 << 20),
+        cost_estimate=pl.CostEstimate(
+            flops=4 * rows * count * ff, bytes_accessed=6 * count * ff, transcendentals=0
+        ),
+        name="backward_products",
+    )(
+        side,
+        dg,
+        du,
+        pltpu.with_memory_space_constraint(gate_weight, pltpu.HBM),
+        pltpu.with_memory_space_constraint(up_weight, pltpu.HBM),
+    )
+
+
+N = 16
+CORE, X = 1, 2
+
+
+def along_tensor(value, mask):
+    return lax.ppermute(value, "tensor", [(i, i ^ mask) for i in range(N)])
+
+
+def across_groups(value, mask=0):
+    both = ("group", "tensor")
+    return lax.ppermute(value, both, [(i, i ^ (N | mask)) for i in range(2 * N)])
+
+
+def from_far_z(values):
+    return [along_tensor(v, 4 * m) for m, v in zip((1, 2, 3), values)]
+
+
+def in_order(*values):
+    return lax.optimization_barrier(values)
+
+
+def add_core(value, recv):
+    half = value.shape[0] // 2
+    return value + jnp.concatenate([recv[half:], recv[:half]], axis=0)
+
+
+def add_x(value, recv):
+    q = value.shape[0] // 4
+    order = (1, 0, 3, 2)
+    return value + jnp.concatenate([recv[o * q : (o + 1) * q] for o in order], axis=0)
+
+
+def add_far_z(value, parts):
+    shape = value.shape
+    total = value.reshape(4, 4, 2, shape[1])
+    for m, part in zip((1, 2, 3), parts):
+        part = part.reshape(total.shape)
+        total = total + jnp.stack([part[:, q ^ m] for q in range(4)], axis=1)
+    return total.reshape(shape)
+
+
+def shared_device(tokens, gate_weight, up_weight, a_gate, a_up, b_gate, b_up, agent, d_hidden):
+    group = lax.axis_index("group")
+    t = lax.axis_index("tensor")
+    side = group.astype(jnp.int32).reshape(1)
+    d = tokens.shape[1]
+    half = d // 2
+    feat_rows = a_gate.shape[0]
+    per_half = half // feat_rows
+    rows = 2 * N
+    ff = b_gate.shape[1]
+
+    parts = from_far_z([tokens] * 3)
+    line = jnp.concatenate([tokens, *parts], axis=0)
+    mine = lax.dynamic_slice_in_dim(line, group * half, half, 1)
+    other = lax.dynamic_slice_in_dim(line, half - group * half, half, 1)
+    parts = [along_tensor(mine, X), across_groups(other), across_groups(other, X)]
+    x = jnp.stack(
+        [jnp.concatenate([mine, parts[0]], axis=0), jnp.concatenate([parts[1], parts[2]], axis=0)]
+    )
+    x = jnp.concatenate([x, along_tensor(x, CORE)], axis=1).reshape(2 * rows, half)
+
+    place = jnp.arange(rows, dtype=jnp.int32)
+    block = ((place >> 1) & 3) * 4 + ((place >> 3) & 1) * 2 + (place >> 4)
+    token_of = ((t ^ block) << 1) + (place & 1)
+    shuffle = token_of[:, None] == jnp.arange(rows, dtype=jnp.int32)[None, :]
+    agent_here = jnp.sum(jnp.where(shuffle, agent[None, :], 0), axis=1)
+    chosen = agent_here[:, None] == (jnp.arange(AG * R, dtype=jnp.int32) // R)[None, :]
+    hidden_grad = jnp.dot(shuffle.astype(BF16), d_hidden, preferred_element_type=F32)
+
+    def select(values):
+        kept = jnp.where(chosen, values, 0.0)
+        pair = sum(kept[:, c : c + 2 * R] for c in range(0, AG * R, 2 * R))
+        return pair[:, :R] + pair[:, R:]
+
+    def spread(small):
+        wide = jnp.concatenate([small] * AG, axis=1)
+        return jnp.where(chosen, wide, 0.0).astype(BF16)
+
+    blocks = lax.dynamic_slice_in_dim(x, (t % per_half) * feat_rows, feat_rows, 1)
+    swapped = across_groups(blocks[rows:])
+    cuts = [ff * c // 7 for c in (0, 2, 4, 5, 7)]
+
+    def forward(c):
+        return forward_products(
+            side, x, gate_weight, up_weight, cuts[c], cuts[c + 1] - cuts[c]
+        )
+
+    keep_0, send_0 = forward(0)
+    swapped, x, keep_0, send_0 = in_order(swapped, x, keep_0, send_0)
+    own_cols = jnp.where(t // per_half == group, blocks[:rows], swapped)
+    part = jnp.concatenate(
+        [
+            select(jnp.dot(own_cols, a_gate.astype(BF16), preferred_element_type=F32)),
+            select(jnp.dot(own_cols, a_up.astype(BF16), preferred_element_type=F32)),
+        ],
+        axis=1,
+    )
+
+    part, x = in_order(part, x)
+    recv = along_tensor(part, CORE)
+    keep_1, send_1 = forward(1)
+    recv, x, keep_1, send_1 = in_order(recv, x, keep_1, send_1)
+    part = add_core(part, recv)
+
+    recv = along_tensor(part, X)
+    far_a = across_groups(jnp.concatenate([send_0, send_1], axis=2))
+    keep_2, send_2 = forward(2)
+    recv, x, keep_2, send_2 = in_order(recv, x, keep_2, send_2)
+    part = add_x(part, recv)
+
+    parts = from_far_z([part] * 3)
+    keep_3, send_3 = forward(3)
+    far_a, keep_3, send_3, *parts = in_order(far_a, keep_3, send_3, *parts)
+    part = add_far_z(part, parts)
+    u = part.astype(BF16).astype(F32)
+    up_factor_gate = spread(u[:, :R])
+    up_factor_up = spread(u[:, R:])
+
+    far_b = across_groups(jnp.concatenate([send_2, send_3], axis=2))
+    d_a, pg_a, pu_a = hidden_gradients(
+        up_factor_gate,
+        up_factor_up,
+        b_gate,
+        b_up,
+        jnp.concatenate([keep_0, keep_1], axis=2),
+        far_a,
+        hidden_grad,
+        0,
+    )
+    far_b, d_a, pg_a, pu_a = in_order(far_b, d_a, pg_a, pu_a)
+    far_a = across_groups(d_a)
+    d_b, pg_b, pu_b = hidden_gradients(
+        up_factor_gate,
+        up_factor_up,
+        b_gate,
+        b_up,
+        jnp.concatenate([keep_2, keep_3], axis=2),
+        far_b,
+        hidden_grad,
+        cuts[2],
+    )
+    far_a, d_b, pg_b, pu_b = in_order(far_a, d_b, pg_b, pu_b)
+    far_b = across_groups(d_b)
+    part = jnp.concatenate([select(pg_a + pg_b), select(pu_a + pu_b)], axis=1)
+    recv = along_tensor(part, CORE)
+    own = jnp.concatenate([d_a, d_b], axis=2)
+    gate_lift_gradient = adapter_scale * rows_product(up_factor_gate, own[0])
+    far_b, recv, gate_lift_gradient = in_order(far_b, recv, gate_lift_gradient)
+    part = add_core(part, recv)
+    both = jnp.concatenate([own, jnp.concatenate([far_a, far_b], axis=2)], axis=1)
+    dg, du = both[0], both[1]
+
+    count = half // 4
+
+    def backward(c):
+        return backward_products(side, dg, du, gate_weight, up_weight, c * count, count)
+
+    recv = along_tensor(part, X)
+    keep_0, send_0 = backward(0)
+    recv, dg, du, keep_0, send_0 = in_order(recv, dg, du, keep_0, send_0)
+    part = add_x(part, recv)
+
+    parts = from_far_z([part] * 3)
+    keep_1, send_1 = backward(1)
+    dg, du, keep_1, send_1, *parts = in_order(dg, du, keep_1, send_1, *parts)
+    part = add_far_z(part, parts)
+    g = part.astype(BF16).astype(F32)
+    gate_factor_gate = spread(g[:, :R])
+    gate_factor_up = spread(g[:, R:])
+    moved = (
+        adapter_scale
+        * (
+            flipped_product(gate_factor_gate, a_gate.astype(BF16))
+            + flipped_product(gate_factor_up, a_up.astype(BF16))
+        )
+    ).astype(BF16)
+    moved, dg, du = in_order(moved, dg, du)
+
+    width = 2 * count
+    far = along_tensor(jnp.concatenate([send_0, send_1], axis=1), CORE)
+    far_moved = along_tensor(moved[16:], CORE)
+    keep_2, send_2 = backward(2)
+    far, far_moved, dg, du, keep_2, send_2 = in_order(far, far_moved, dg, du, keep_2, send_2)
+    early = jnp.concatenate([keep_0, keep_1], axis=1) + far.astype(F32)
+    moved = jnp.concatenate([moved[:16], far_moved], axis=1)
+
+    def out_of(sums, *extra):
+        low = sums.astype(BF16)
+        return [
+            along_tensor(jnp.concatenate([low[8:16], *extra], axis=1), X),
+            across_groups(low[16:24]),
+            across_groups(low[24:], X),
+        ]
+
+    def joined(sums, parts):
+        near = sums[:8] + parts[0][:, :width].astype(F32)
+        return jnp.concatenate([near, parts[1].astype(F32) + parts[2].astype(F32)], axis=1)
+
+    parts = out_of(early, moved[8:])
+    keep_3, send_3 = backward(3)
+    keep_3, send_3, *parts = in_order(keep_3, send_3, *parts)
+    early = joined(early, parts)
+    moved = jnp.concatenate([moved[:8], parts[0][:, width:]], axis=1)
+
+    far = along_tensor(jnp.concatenate([send_2, send_3], axis=1), CORE)
+    low = jnp.concatenate([early.astype(BF16), moved], axis=1)
+    parts = from_far_z([low[2 * m : 2 * m + 2] for m in (1, 2, 3)])
+    gate_down_gradient = adapter_scale * rows_product(own_cols, gate_factor_gate)
+    far, gate_down_gradient, *parts = in_order(far, gate_down_gradient, *parts)
+    early = early[:2] + sum(p[:, : 2 * width].astype(F32) for p in parts)
+    moved = jnp.stack([moved[:2]] + [p[:, 2 * width :] for p in parts])
+    late = jnp.concatenate([keep_2, keep_3], axis=1) + far.astype(F32)
+
+    parts = out_of(late)
+    own_cols, gate_factor_up, late = in_order(own_cols, gate_factor_up, late)
+    up_down_gradient = adapter_scale * rows_product(own_cols, gate_factor_up)
+    up_down_gradient, own, *parts = in_order(up_down_gradient, own, *parts)
+    late = joined(late, parts)
+
+    low = late.astype(BF16)
+    parts = from_far_z([low[2 * m : 2 * m + 2] for m in (1, 2, 3)])
+    up_lift_gradient = adapter_scale * rows_product(up_factor_up, own[1])
+    moved = moved.reshape(4, 2, 2, 2, feat_rows).transpose(0, 2, 3, 1, 4).reshape(N, 2 * feat_rows)
+    source = jnp.arange(N, dtype=jnp.int32)
+    sort = (source[:, None] == (t ^ source)[None, :]).astype(BF16)
+    sorted_rows = jnp.dot(sort, moved, preferred_element_type=F32).reshape(N, 2, feat_rows)
+    contribution = sorted_rows.transpose(1, 0, 2).reshape(2, d)
+    up_lift_gradient, contribution, *parts = in_order(up_lift_gradient, contribution, *parts)
+    late = late[:2] + sum(p.astype(F32) for p in parts)
+    near = jnp.concatenate([early[:, :width], late[:, :width]], axis=1)
+    far = jnp.concatenate([early[:, width:], late[:, width:]], axis=1)
+    sums = jnp.where(
+        group == 0, jnp.concatenate([near, far], axis=1), jnp.concatenate([far, near], axis=1)
+    )
+    token_gradient = (sums + contribution).astype(BF16)
+    return (
+        token_gradient,
+        gate_down_gradient,
+        up_down_gradient,
+        gate_lift_gradient,
+        up_lift_gradient,
+    )
+
+
 def solution(mesh):
+    sizes = dict(mesh.shape)
+
+    def per_device(*args):
+        tokens, b_gate = args[0], args[5]
+        fits = (
+            sizes["group"] == 2
+            and sizes["tensor"] == N
+            and tokens.shape[0] == 2
+            and b_gate.shape[1] % 1792 == 0
+            and tokens.shape[1] % 4096 == 0
+        )
+        return (shared_device if fits else plain_device)(*args)
+
     in_specs = (
         P(("group", "tensor"), None),
         P(None, "tensor"),

time: 306 us -> 127 us (0.42)
  blocking collectives: 210 us -> 0 us
  matrix products: 88.2 us -> 15.3 us
  Pallas kernels: 0 us -> 48.4 us
  starting transfers between devices: 0 us -> 42.3 us
  waiting for transfers between devices: 0 us -> 12.7 us
    psum x2 -> x0, blocking collectives: 116 us -> none  [the longest x1 57.9 us: per_device(): u_gate, u_up = lax.psum((part_gate, part_up), 'tensor')]
    unnamed x1 -> x0, blocking collectives: 69.9 us -> none
    pallas_call x0 -> x10, Pallas kernels: none -> 48.4 us  [the longest x4 24.2 us: backward_products(): pl.pallas_call(functools.partial(backward_kernel, first), in_specs=[pl.Bl...]
    ppermute x0 -> x37, starting transfers between devices: none -> 42.3 us  [the longest x26 29.7 us: along_tensor(): return lax.ppermute(value, 'tensor', [(i, i ^ mask) for i in range(N)])]
    dot_general x6 -> x2, matrix products: 39 us -> 2.43 us  [flipped_product(): lax.dot_general(left, weight, (((1,), (1,)), ((), ())), preferred_element...]
    dot_general x10 -> x8, matrix products: 49.2 us -> 12.9 us  [the longest x4 11.9 us: rows_product(): lax.dot_general(left, right, (((0,), (0,)), ((), ())), preferred_element_...]
    all_gather x1 -> x0, blocking collectives: 24.8 us -> none  [per_device(): complete_result = lax.all_gather(tokens, 'tensor', axis=0, tiled=True)]
    ppermute x0 -> x37, waiting for transfers between devices: none -> 12.7 us  [the longest x26 9.43 us: along_tensor(): return lax.ppermute(value, 'tensor', [(i, i ^ mask) for i in range(N)])]
  transfers between devices with their start and end apart: 0 -> 37, of which waited for: 0 -> 12; matrix products, arithmetic and copies ran while one was open for 0% -> 11% of each run, Pallas kernels for 0% -> 38%
where the time goes in v4:
time: 127 us
  Pallas kernels  48.4 us (38%)
  starting transfers between devices  42.3 us (33%)
  matrix products  15.3 us (12%)
  waiting for transfers between devices  12.7 us (10%)
  other arithmetic  4.35 us (3%)
  local copies, waits for them, and re-layouts  2.21 us (2%)
  between operations  1.5 us (1%)
    ppermute x26, starting transfers between devices, along_tensor(): return lax.ppermute(value, 'tensor', [(i, i ^ mask) for i in range(N)])  29.7 us
    pallas_call x4, Pallas kernels, backward_products(): pl.pallas_call(functools.partial(backward_kernel, first), in_specs=[pl.Bl...  24.2 us
    pallas_call x4, Pallas kernels, forward_products(): pl.pallas_call(functools.partial(forward_kernel, first), in_specs=[pl.Blo...  14.5 us
    ppermute x11, starting transfers between devices, across_groups(): lax.ppermute(value, both, [(i, i ^ (N | mask)) for i in range(2 * N)])  12.6 us
    dot_general x4, matrix products, rows_product(): lax.dot_general(left, right, (((0,), (0,)), ((), ())), preferred_element_...  11.9 us
    pallas_call x2, Pallas kernels, hidden_gradients(): pl.pallas_call(hidden_kernel, grid=(count // width,), in_specs=[fixed, fi...  9.81 us
    ppermute x26, waiting for transfers between devices, along_tensor(): return lax.ppermute(value, 'tensor', [(i, i ^ mask) for i in range(N)])  9.43 us
    ppermute x11, waiting for transfers between devices, across_groups(): lax.ppermute(value, both, [(i, i ^ (N | mask)) for i in range(2 * N)])  3.3 us
  transfers between devices with their start and end apart: 37, of which 12 were waited for; matrix products, arithmetic and copies ran while one was open for 11% of the time, Pallas kernels for 38%

profile of v4, /device:TPU:0, one launch (start us, length us, event | category | flops | bytes accessed | tf_op | source)
XLA Modules:
  0.0 126.8 jit_solution(2463613306745222340)
XLA Ops:
  0.6 4.1 %collective-permute-start.1 = (bf16[2,8192]{1,0:T(2,128)(2,1)}, bf16[2,8192]{1,0:T(2,128)(2,1)S(1)}, u32[]{:S(2)}, u32[]{:S(2)}) collective-permute-start(bf16[2,8192]{1,0:T(2,128)(2,1)} %param.9), channel_id=1, source_target_pairs={{0,8},{1,9},{2,10},{3,11},{4,12},{5,13},{6,14},{7,15},{8,0},{9,1},... | collective-permute-start | bytes 98312 | tf_op jit(solution)/shard_map/ppermute | solution.py:287
  4.7 1.6 %collective-permute-start = (bf16[2,8192]{1,0:T(2,128)(2,1)}, bf16[2,8192]{1,0:T(2,128)(2,1)S(1)}, u32[]{:S(2)}, u32[]{:S(2)}) collective-permute-start(bf16[2,8192]{1,0:T(2,128)(2,1)} %param.9), channel_id=1, source_target_pairs={{0,4},{1,5},{2,6},{3,7},{4,0},{5,1},{6,2},{7,3},{8,12},{9,13},{10,... | collective-permute-start | bytes 98312 | tf_op jit(solution)/shard_map/ppermute | solution.py:287
  6.3 0.8 select_reduce_fusion
  7.3 1.6 %collective-permute-done = bf16[2,8192]{1,0:T(2,128)(2,1)S(1)} collective-permute-done((bf16[2,8192]{1,0:T(2,128)(2,1)}, bf16[2,8192]{1,0:T(2,128)(2,1)S(1)}, u32[]{:S(2)}, u32[]{:S(2)}) %collective-permute-start) | collective-permute-done | bytes 32800 | tf_op jit(solution)/shard_map/ppermute | solution.py:287
  8.9 3.4 %collective-permute-done.2 = bf16[2,8192]{1,0:T(2,128)(2,1)S(1)} collective-permute-done((bf16[2,8192]{1,0:T(2,128)(2,1)}, bf16[2,8192]{1,0:T(2,128)(2,1)S(1)}, u32[]{:S(2)}, u32[]{:S(2)}) %collective-permute-start.2) | collective-permute-done | bytes 32800 | tf_op jit(solution)/shard_map/ppermute | solution.py:287
  12.2 0.9 pad_maximum_fusion.6
  13.2 1.6 %collective-permute-start.3 = (bf16[8,4096]{1,0:T(8,128)(2,1)S(1)}, bf16[8,4096]{1,0:T(8,128)(2,1)S(1)}, u32[]{:S(2)}, u32[]{:S(2)}) collective-permute-start(bf16[8,4096]{1,0:T(8,128)(2,1)S(1)} %get-tuple-element.211), channel_id=1, source_target_pairs={{0,2},{1,3},{2,0},{3,1},{4,6},{5,7},{6,4},{7,5},{8,10},{9,11},{10,... | collective-permute-start | bytes 196616 | tf_op jit(solution)/shard_map/ppermute | solution.py:287
  14.8 1.5 %collective-permute-start.5 = (bf16[8,4096]{1,0:T(8,128)(2,1)S(1)}, bf16[8,4096]{1,0:T(8,128)(2,1)S(1)}, u32[]{:S(2)}, u32[]{:S(2)}) collective-permute-start(bf16[8,4096]{1,0:T(8,128)(2,1)S(1)} %get-tuple-element.212), channel_id=1, source_target_pairs={{0,18},{1,19},{2,16},{3,17},{4,22},{5,23},{6,20},{7,21},{8,26},{9,... | collective-permute-start | bytes 196616 | tf_op jit(solution)/shard_map/ppermute | solution.py:292
  16.7 0.9 collective-permute-done.3
  17.7 2.3 %collective-permute-done.5 = bf16[8,4096]{1,0:T(8,128)(2,1)S(1)} collective-permute-done((bf16[8,4096]{1,0:T(8,128)(2,1)S(1)}, bf16[8,4096]{1,0:T(8,128)(2,1)S(1)}, u32[]{:S(2)}, u32[]{:S(2)}) %collective-permute-start.5) | collective-permute-done | bytes 65568 | tf_op jit(solution)/shard_map/ppermute | solution.py:292
  22.3 1.2 collective-permute-start.7
  23.5 4.0 %forward_products.4 = (f32[2,32,512]{2,1,0:T(8,128)S(1)}, bf16[2,32,512]{2,1,0:T(8,128)(2,1)S(1)}) custom-call(s32[1]{0:T(128)} %bitcast.3.side_ref, bf16[64,4096]{1,0:T(8,128)(2,1)S(1)} %bitcast.62, bf16[8192,1792]{1,0:T(8,128)(2,1)} %wg_ref.15, bf16[8192,1792]{1,0:T(8,128)(2,1)} %wu_ref.15), custom_call_target="tpu_custom_call" | custom-call | flops 536870912 | bytes 12582912 | tf_op jit(solution)/shard_map/forward_products/pallas_call | solution.py:136
  27.9 1.2 copy-done.2
  29.6 3.8 %forward_products.5 = (f32[2,32,512]{2,1,0:T(8,128)S(1)}, bf16[2,32,512]{2,1,0:T(8,128)(2,1)S(1)}) custom-call(s32[1]{0:T(128)} %bitcast.3.side_ref, bf16[64,4096]{1,0:T(8,128)(2,1)S(1)} %bitcast.64, bf16[8192,1792]{1,0:T(8,128)(2,1)} %wg_ref.15, bf16[8192,1792]{1,0:T(8,128)(2,1)} %wu_ref.15), custom_call_target="tpu_custom_call" | custom-call | flops 536870912 | bytes 12582912 | tf_op jit(solution)/shard_map/forward_products/pallas_call | solution.py:136
  33.5 1.0 collective-permute-start.9
  34.5 1.4 %collective-permute-start.10 = (bf16[2,32,1024]{2,1,0:T(8,128)(2,1)S(1)}, bf16[2,32,1024]{2,1,0:T(8,128)(2,1)S(1)}, u32[]{:S(2)}, u32[]{:S(2)}) collective-permute-start(bf16[2,32,1024]{2,1,0:T(8,128)(2,1)S(1)} %pad_maximum_fusion.7), channel_id=1, source_target_pairs={{0,16},{1,17},{2,18},{3,19},{4,20},{5,21},{6,22},{7,23},{8,24},{9,... | collective-permute-start | bytes 393224 | tf_op jit(solution)/shard_map/ppermute | solution.py:292
  36.0 2.8 %forward_products.6 = (f32[2,32,256]{2,1,0:T(8,128)S(1)}, bf16[2,32,256]{2,1,0:T(8,128)(2,1)S(1)}) custom-call(s32[1]{0:T(128)} %bitcast.3.side_ref, bf16[64,4096]{1,0:T(8,128)(2,1)S(1)} %bitcast.65, bf16[8192,1792]{1,0:T(8,128)(2,1)} %wg_ref.15, bf16[8192,1792]{1,0:T(8,128)(2,1)} %wu_ref.15), custom_call_target="tpu_custom_call" | custom-call | flops 268435456 | bytes 6291456 | tf_op jit(solution)/shard_map/forward_products/pallas_call | solution.py:136
  39.4 3.9 %collective-permute-start.11 = (f32[32,128]{1,0:T(8,128)S(1)}, f32[32,128]{1,0:T(8,128)S(1)}, u32[]{:S(2)}, u32[]{:S(2)}) collective-permute-start(f32[32,128]{1,0:T(8,128)S(1)} %maximum_add_fusion.3), channel_id=1, source_target_pairs={{0,4},{1,5},{2,6},{3,7},{4,0},{5,1},{6,2},{7,3},{8,12},{9,13},{10,... | collective-permute-start | bytes 49160 | tf_op jit(solution)/shard_map/ppermute | solution.py:287
  43.3 3.8 %forward_products.7 = (f32[2,32,512]{2,1,0:T(8,128)S(1)}, bf16[2,32,512]{2,1,0:T(8,128)(2,1)S(1)}) custom-call(s32[1]{0:T(128)} %bitcast.3.side_ref, bf16[64,4096]{1,0:T(8,128)(2,1)S(1)} %bitcast.66, bf16[8192,1792]{1,0:T(8,128)(2,1)} %wg_ref.15, bf16[8192,1792]{1,0:T(8,128)(2,1)} %wu_ref.15), custom_call_target="tpu_custom_call" | custom-call | flops 536870912 | bytes 12582912 | tf_op jit(solution)/shard_map/forward_products/pallas_call | solution.py:136
  47.6 0.8 collective-permute-start.14
  48.5 5.2 %hidden_gradients.2 = (bf16[2,32,1024]{2,1,0:T(8,128)(2,1)S(1)}, f32[32,1024]{1,0:T(8,128)S(1)}, f32[32,1024]{1,0:T(8,128)S(1)}) custom-call(bf16[32,1024]{1,0:T(8,128)(2,1)S(1)} %get-tuple-element.265.eug_ref, bf16[32,1024]{1,0:T(8,128)(2,1)S(1)} %get-tuple-element.266.euu_ref, f32[1024,1792]{1,0:T(8,128)} %bg_ref.3, f32[1024,1792]{1,0:T(8,128)} %bu_ref.3, ...), custom_call_target="tpu_custom_call" | custom-call | flops 268435456 | bytes 16777216 | tf_op jit(solution)/shard_map/hidden_gradients/pallas_call | solution.py:198
  53.7 1.4 %collective-permute-start.15 = (bf16[2,32,1024]{2,1,0:T(8,128)(2,1)S(1)}, bf16[2,32,1024]{2,1,0:T(8,128)(2,1)S(1)}, u32[]{:S(2)}, u32[]{:S(2)}) collective-permute-start(bf16[2,32,1024]{2,1,0:T(8,128)(2,1)S(1)} %get-tuple-element.132), channel_id=1, source_target_pairs={{0,16},{1,17},{2,18},{3,19},{4,20},{5,21},{6,22},{7,23},{8,24},{9,... | collective-permute-start | bytes 393224 | tf_op jit(solution)/shard_map/ppermute | solution.py:292
  55.1 4.6 %hidden_gradients.3 = (bf16[2,32,768]{2,1,0:T(8,128)(2,1)S(1)}, f32[32,1024]{1,0:T(8,128)S(1)}, f32[32,1024]{1,0:T(8,128)S(1)}) custom-call(bf16[32,1024]{1,0:T(8,128)(2,1)S(1)} %get-tuple-element.265.eug_ref, bf16[32,1024]{1,0:T(8,128)(2,1)S(1)} %get-tuple-element.266.euu_ref, f32[1024,1792]{1,0:T(8,128)} %bg_ref.3, f32[1024,1792]{1,0:T(8,128)} %bu_ref.3, ...), custom_call_target="tpu_custom_call" | custom-call | flops 201326592 | bytes 12582912 | tf_op jit(solution)/shard_map/hidden_gradients/pallas_call | solution.py:198
  60.9 4.2 %convolution_multiply_fusion.1 = f32[1024,1792]{1,0:T(8,128)} fusion(bf16[32,1024]{1,0:T(8,128)(2,1)S(1)} %get-tuple-element.265.eug_ref, bf16[2,32,1792]{2,1,0:T(8,128)(2,1)S(1)} %constant_dynamic-update-slice_fusion), kind=kOutput, calls=%fused_computation.1 | convolution fusion | flops 119275520 | bytes 7520256 | tf_op jit(solution)/shard_map/dot_general | solution.py:39
  65.4 0.8 collective-permute-start.18
  66.3 6.0 %backward_products.4 = (f32[32,1024]{1,0:T(8,128)S(1)}, bf16[32,1024]{1,0:T(8,128)(2,1)S(1)}) custom-call(s32[1]{0:T(128)} %bitcast.3.side_ref, bf16[64,1792]{1,0:T(8,128)(2,1)S(1)} %get-tuple-element.168.dg_ref, bf16[64,1792]{1,0:T(8,128)(2,1)S(1)} %get-tuple-element.169.du_ref, bf16[8192,1792]{1,0:T(8,128)(2,1)} %wg_ref.15, bf16[8192,1792]{1,0:T(8,128)(2,1)} %wu_ref.15), custom_call_target="tpu_custom_call" | custom-call | flops 469762048 | bytes 11010048 | tf_op jit(solution)/shard_map/backward_products/pallas_call | solution.py:256
  72.9 1.1 collective-permute-start.20
  74.0 2.9 %collective-permute-start.19 = (f32[32,128]{1,0:T(8,128)S(1)}, f32[32,128]{1,0:T(8,128)S(1)}, u32[]{:S(2)}, u32[]{:S(2)}) collective-permute-start(f32[32,128]{1,0:T(8,128)S(1)} %maximum_add_fusion.5), channel_id=1, source_target_pairs={{0,4},{1,5},{2,6},{3,7},{4,0},{5,1},{6,2},{7,3},{8,12},{9,13},{10,... | collective-permute-start | bytes 49160 | tf_op jit(solution)/shard_map/ppermute | solution.py:287
  76.9 6.0 %backward_products.5 = (f32[32,1024]{1,0:T(8,128)S(1)}, bf16[32,1024]{1,0:T(8,128)(2,1)S(1)}) custom-call(s32[1]{0:T(128)} %bitcast.3.side_ref, bf16[64,1792]{1,0:T(8,128)(2,1)S(1)} %get-tuple-element.168.dg_ref, bf16[64,1792]{1,0:T(8,128)(2,1)S(1)} %get-tuple-element.169.du_ref, bf16[8192,1792]{1,0:T(8,128)(2,1)} %wg_ref.15, bf16[8192,1792]{1,0:T(8,128)(2,1)} %wu_ref.15), custom_call_target="tpu_custom_call" | custom-call | flops 469762048 | bytes 11010048 | tf_op jit(solution)/shard_map/backward_products/pallas_call | solution.py:256
  83.9 2.0 %fusion.1 = bf16[32,512]{1,0:T(8,128)(2,1)S(1)} fusion(f32[32,512]{1,0:T(8,128)S(1)} %fusion.4, bf16[32,1024]{1,0:T(8,128)(2,1)S(1)} %fusion.12, f32[512,1024]{1,0:T(8,128)} %param.13), kind=kOutput, calls=%fused_computation.9 | convolution fusion | flops 34127872 | bytes 2260992 | tf_op jit(solution)/shard_map/dot_general | solution.py:33
  86.5 6.0 %backward_products.6 = (f32[32,1024]{1,0:T(8,128)S(1)}, bf16[32,1024]{1,0:T(8,128)(2,1)S(1)}) custom-call(s32[1]{0:T(128)} %bitcast.3.side_ref, bf16[64,1792]{1,0:T(8,128)(2,1)S(1)} %get-tuple-element.168.dg_ref, bf16[64,1792]{1,0:T(8,128)(2,1)S(1)} %get-tuple-element.169.du_ref, bf16[8192,1792]{1,0:T(8,128)(2,1)} %wg_ref.15, bf16[8192,1792]{1,0:T(8,128)(2,1)} %wu_ref.15), custom_call_target="tpu_custom_call" | custom-call | flops 469762048 | bytes 11010048 | tf_op jit(solution)/shard_map/backward_products/pallas_call | solution.py:256
  92.7 1.3 collective-permute-start.24
  93.9 1.8 %convolution_multiply_fusion.3 = f32[512,1024]{1,0:T(8,128)} fusion(bf16[32,512]{1,0:T(8,128)(2,1)S(1)} %dynamic-slice_select_fusion, bf16[32,1024]{1,0:T(8,128)(2,1)S(1)} %concatenate.128, s32[1024]{0:T(1024)S(1)} %add_select_fusion, s32[32]{0:T(128)S(1)} %select_reduce_fusion), kind=kOutput, calls=%fused_computation.3 | convolution fusion | flops 34144256 | bytes 2199680 | tf_op jit(solution)/shard_map/dot_general | solution.py:39
  95.7 1.2 collective-permute-start.26
  96.9 1.1 collective-permute-start.25
  98.0 6.0 %backward_products.7 = (f32[32,1024]{1,0:T(8,128)S(1)}, bf16[32,1024]{1,0:T(8,128)(2,1)S(1)}) custom-call(s32[1]{0:T(128)} %bitcast.3.side_ref, bf16[64,1792]{1,0:T(8,128)(2,1)S(1)} %get-tuple-element.168.dg_ref, bf16[64,1792]{1,0:T(8,128)(2,1)S(1)} %get-tuple-element.169.du_ref, bf16[8192,1792]{1,0:T(8,128)(2,1)} %wg_ref.15, bf16[8192,1792]{1,0:T(8,128)(2,1)} %wu_ref.15), custom_call_target="tpu_custom_call" | custom-call | flops 469762048 | bytes 11010048 | tf_op jit(solution)/shard_map/backward_products/pallas_call | solution.py:256
  104.7 1.1 collective-permute-start.29
  105.8 2.9 %collective-permute-start.28 = (bf16[2,6144]{1,0:T(2,128)(2,1)S(1)}, bf16[2,6144]{1,0:T(2,128)(2,1)S(1)}, u32[]{:S(2)}, u32[]{:S(2)}) collective-permute-start(bf16[2,6144]{1,0:T(2,128)(2,1)S(1)} %get-tuple-element.215), channel_id=1, source_target_pairs={{0,4},{1,5},{2,6},{3,7},{4,0},{5,1},{6,2},{7,3},{8,12},{9,13},{10,... | collective-permute-start | bytes 73736 | tf_op jit(solution)/shard_map/ppermute | solution.py:287
  108.8 1.1 collective-permute-done.30
  110.7 1.8 %collective-permute-start.33 = (bf16[8,2048]{1,0:T(8,128)(2,1)S(1)}, bf16[8,2048]{1,0:T(8,128)(2,1)S(1)}, u32[]{:S(2)}, u32[]{:S(2)}) collective-permute-start(bf16[8,2048]{1,0:T(8,128)(2,1)S(1)} %get-tuple-element.205), channel_id=1, source_target_pairs={{0,18},{1,19},{2,16},{3,17},{4,22},{5,23},{6,20},{7,21},{8,26},{9,... | collective-permute-start | bytes 98312 | tf_op jit(solution)/shard_map/ppermute | solution.py:292
  112.4 0.9 collective-permute-start.32
  113.4 0.8 collective-permute-start.31
  114.2 1.8 %convolution_multiply_fusion.2 = f32[512,1024]{1,0:T(8,128)} fusion(bf16[32,512]{1,0:T(8,128)(2,1)S(1)} %dynamic-slice_select_fusion, bf16[32,1024]{1,0:T(8,128)(2,1)S(1)} %fusion.12), kind=kOutput, calls=%fused_computation.2 | convolution fusion | flops 34078720 | bytes 2195456 | tf_op jit(solution)/shard_map/dot_general | solution.py:39
  116.4 0.9 collective-permute-done.31
  117.4 2.4 %collective-permute-start.36 = (bf16[2,4096]{1,0:T(2,128)(2,1)S(1)}, bf16[2,4096]{1,0:T(2,128)(2,1)S(1)}, u32[]{:S(2)}, u32[]{:S(2)}) collective-permute-start(bf16[2,4096]{1,0:T(2,128)(2,1)S(1)} %get-tuple-element.216), channel_id=1, source_target_pairs={{0,12},{1,13},{2,14},{3,15},{4,8},{5,9},{6,10},{7,11},{8,4},{9,5},... | collective-permute-start | bytes 49160 | tf_op jit(solution)/shard_map/ppermute | solution.py:287
  119.8 1.1 collective-permute-start.35
  121.0 0.9 collective-permute-start.34
  121.9 4.2 %convolution_multiply_fusion = f32[1024,1792]{1,0:T(8,128)} fusion(bf16[32,1024]{1,0:T(8,128)(2,1)S(1)} %get-tuple-element.266.euu_ref, bf16[2,32,1792]{2,1,0:T(8,128)(2,1)S(1)} %constant_dynamic-update-slice_fusion), kind=kOutput, calls=%fused_computation | convolution fusion | flops 119275520 | bytes 7520256 | tf_op jit(solution)/shard_map/dot_general | solution.py:39
  (145 shorter events, 10.9 us)
Async XLA Ops:
  0.6 20.6 %copy-start = (bf16[32,1792]{1,0:T(8,128)(2,1)S(1)}, bf16[32,1792]{1,0:T(8,128)(2,1)}, u32[]{:S(2)}) copy-start(bf16[32,1792]{1,0:T(8,128)(2,1)} %param.17) | copy-start | bytes 344068
  0.6 6.7 %collective-permute-start.1 = (bf16[2,8192]{1,0:T(2,128)(2,1)}, bf16[2,8192]{1,0:T(2,128)(2,1)S(1)}, u32[]{:S(2)}, u32[]{:S(2)}) collective-permute-start(bf16[2,8192]{1,0:T(2,128)(2,1)} %param.9), channel_id=1, source_target_pairs={{0,8},{1,9},{2,10},{3,11},{4,12},{5,13},{6,14},{7,15},{8,0},{9,1},... | collective-permute-start | bytes 98312 | tf_op jit(solution)/shard_map/ppermute | solution.py:287
  4.7 4.1 %collective-permute-start = (bf16[2,8192]{1,0:T(2,128)(2,1)}, bf16[2,8192]{1,0:T(2,128)(2,1)S(1)}, u32[]{:S(2)}, u32[]{:S(2)}) collective-permute-start(bf16[2,8192]{1,0:T(2,128)(2,1)} %param.9), channel_id=1, source_target_pairs={{0,4},{1,5},{2,6},{3,7},{4,0},{5,1},{6,2},{7,3},{8,12},{9,13},{10,... | collective-permute-start | bytes 98312 | tf_op jit(solution)/shard_map/ppermute | solution.py:287
  6.3 5.9 %collective-permute-start.2 = (bf16[2,8192]{1,0:T(2,128)(2,1)}, bf16[2,8192]{1,0:T(2,128)(2,1)S(1)}, u32[]{:S(2)}, u32[]{:S(2)}) collective-permute-start(bf16[2,8192]{1,0:T(2,128)(2,1)} %param.9), channel_id=1, source_target_pairs={{0,12},{1,13},{2,14},{3,15},{4,8},{5,9},{6,10},{7,11},{8,4},{9,5},... | collective-permute-start | bytes 98312 | tf_op jit(solution)/shard_map/ppermute | solution.py:287
  13.2 4.5 %collective-permute-start.3 = (bf16[8,4096]{1,0:T(8,128)(2,1)S(1)}, bf16[8,4096]{1,0:T(8,128)(2,1)S(1)}, u32[]{:S(2)}, u32[]{:S(2)}) collective-permute-start(bf16[8,4096]{1,0:T(8,128)(2,1)S(1)} %get-tuple-element.211), channel_id=1, source_target_pairs={{0,2},{1,3},{2,0},{3,1},{4,6},{5,7},{6,4},{7,5},{8,10},{9,11},{10,... | collective-permute-start | bytes 196616 | tf_op jit(solution)/shard_map/ppermute | solution.py:287
  14.8 5.2 %collective-permute-start.5 = (bf16[8,4096]{1,0:T(8,128)(2,1)S(1)}, bf16[8,4096]{1,0:T(8,128)(2,1)S(1)}, u32[]{:S(2)}, u32[]{:S(2)}) collective-permute-start(bf16[8,4096]{1,0:T(8,128)(2,1)S(1)} %get-tuple-element.212), channel_id=1, source_target_pairs={{0,18},{1,19},{2,16},{3,17},{4,22},{5,23},{6,20},{7,21},{8,26},{9,... | collective-permute-start | bytes 196616 | tf_op jit(solution)/shard_map/ppermute | solution.py:292
  16.2 4.4 %collective-permute-start.4 = (bf16[8,4096]{1,0:T(8,128)(2,1)S(1)}, bf16[8,4096]{1,0:T(8,128)(2,1)S(1)}, u32[]{:S(2)}, u32[]{:S(2)}) collective-permute-start(bf16[8,4096]{1,0:T(8,128)(2,1)S(1)} %get-tuple-element.212), channel_id=1, source_target_pairs={{0,16},{1,17},{2,18},{3,19},{4,20},{5,21},{6,22},{7,23},{8,24},{9,... | collective-permute-start | bytes 196616 | tf_op jit(solution)/shard_map/ppermute | solution.py:292
  20.7 1.6 %collective-permute-start.6 = (bf16[2,16,4096]{2,1,0:T(8,128)(2,1)S(1)}, bf16[2,16,4096]{2,1,0:T(8,128)(2,1)S(1)}, u32[]{:S(2)}, u32[]{:S(2)}) collective-permute-start(bf16[2,16,4096]{2,1,0:T(8,128)(2,1)S(1)} %pad_maximum_fusion.1), channel_id=1, source_target_pairs={{0,1},{1,0},{2,3},{3,2},{4,5},{5,4},{6,7},{7,6},{8,9},{9,8},{10,11... | collective-permute-start | bytes 786440 | tf_op jit(solution)/shard_map/ppermute | solution.py:287
  22.3 5.2 %collective-permute-start.7 = (bf16[32,512]{1,0:T(8,128)(2,1)S(1)}, bf16[32,512]{1,0:T(8,128)(2,1)S(1)}, u32[]{:S(2)}, u32[]{:S(2)}) collective-permute-start(bf16[32,512]{1,0:T(8,128)(2,1)S(1)} %dynamic-slice.1), channel_id=1, source_target_pairs={{0,16},{1,17},{2,18},{3,19},{4,20},{5,21},{6,22},{7,23},{8,24},{9,... | collective-permute-start | bytes 98312 | tf_op jit(solution)/shard_map/ppermute | solution.py:292
  23.5 4.1 %copy-start.3 = (f32[512,1024]{1,0:T(8,128)S(1)}, f32[512,1024]{1,0:T(8,128)}, u32[]{:S(2)}) copy-start(f32[512,1024]{1,0:T(8,128)} %param.13) | copy-start | bytes 6291460
  27.5 1.6 %copy-start.2 = (f32[512,1024]{1,0:T(8,128)S(1)}, f32[512,1024]{1,0:T(8,128)}, u32[]{:S(2)}) copy-start(f32[512,1024]{1,0:T(8,128)} %param.12) | copy-start | bytes 6291460
  29.6 3.9 %collective-permute-start.8 = (f32[32,128]{1,0:T(8,128)S(1)}, f32[32,128]{1,0:T(8,128)S(1)}, u32[]{:S(2)}, u32[]{:S(2)}) collective-permute-start(f32[32,128]{1,0:T(8,128)S(1)} %pad_maximum_fusion.18), channel_id=1, source_target_pairs={{0,1},{1,0},{2,3},{3,2},{4,5},{5,4},{6,7},{7,6},{8,9},{9,8},{10,11... | collective-permute-start | bytes 49160 | tf_op jit(solution)/shard_map/ppermute | solution.py:287
  33.5 5.3 %collective-permute-start.9 = (f32[32,128]{1,0:T(8,128)S(1)}, f32[32,128]{1,0:T(8,128)S(1)}, u32[]{:S(2)}, u32[]{:S(2)}) collective-permute-start(f32[32,128]{1,0:T(8,128)S(1)} %maximum_add_fusion.2), channel_id=1, source_target_pairs={{0,2},{1,3},{2,0},{3,1},{4,6},{5,7},{6,4},{7,5},{8,10},{9,11},{10,... | collective-permute-start | bytes 49160 | tf_op jit(solution)/shard_map/ppermute | solution.py:287
  34.5 12.7 %collective-permute-start.10 = (bf16[2,32,1024]{2,1,0:T(8,128)(2,1)S(1)}, bf16[2,32,1024]{2,1,0:T(8,128)(2,1)S(1)}, u32[]{:S(2)}, u32[]{:S(2)}) collective-permute-start(bf16[2,32,1024]{2,1,0:T(8,128)(2,1)S(1)} %pad_maximum_fusion.7), channel_id=1, source_target_pairs={{0,16},{1,17},{2,18},{3,19},{4,20},{5,21},{6,22},{7,23},{8,24},{9,... | collective-permute-start | bytes 393224 | tf_op jit(solution)/shard_map/ppermute | solution.py:292
  38.8 8.3 %collective-permute-start.13 = (f32[32,128]{1,0:T(8,128)S(1)}, f32[32,128]{1,0:T(8,128)S(1)}, u32[]{:S(2)}, u32[]{:S(2)}) collective-permute-start(f32[32,128]{1,0:T(8,128)S(1)} %maximum_add_fusion.3), channel_id=1, source_target_pairs={{0,12},{1,13},{2,14},{3,15},{4,8},{5,9},{6,10},{7,11},{8,4},{9,5},... | collective-permute-start | bytes 49160 | tf_op jit(solution)/shard_map/ppermute | solution.py:287
  39.2 7.9 %collective-permute-start.12 = (f32[32,128]{1,0:T(8,128)S(1)}, f32[32,128]{1,0:T(8,128)S(1)}, u32[]{:S(2)}, u32[]{:S(2)}) collective-permute-start(f32[32,128]{1,0:T(8,128)S(1)} %maximum_add_fusion.3), channel_id=1, source_target_pairs={{0,8},{1,9},{2,10},{3,11},{4,12},{5,13},{6,14},{7,15},{8,0},{9,1},... | collective-permute-start | bytes 49160 | tf_op jit(solution)/shard_map/ppermute | solution.py:287
  39.4 7.8 %collective-permute-start.11 = (f32[32,128]{1,0:T(8,128)S(1)}, f32[32,128]{1,0:T(8,128)S(1)}, u32[]{:S(2)}, u32[]{:S(2)}) collective-permute-start(f32[32,128]{1,0:T(8,128)S(1)} %maximum_add_fusion.3), channel_id=1, source_target_pairs={{0,4},{1,5},{2,6},{3,7},{4,0},{5,1},{6,2},{7,3},{8,12},{9,13},{10,... | collective-permute-start | bytes 49160 | tf_op jit(solution)/shard_map/ppermute | solution.py:287
  47.6 6.1 %collective-permute-start.14 = (bf16[2,32,768]{2,1,0:T(8,128)(2,1)S(1)}, bf16[2,32,768]{2,1,0:T(8,128)(2,1)S(1)}, u32[]{:S(2)}, u32[]{:S(2)}) collective-permute-start(bf16[2,32,768]{2,1,0:T(8,128)(2,1)S(1)} %pad_maximum_fusion.10), channel_id=1, source_target_pairs={{0,16},{1,17},{2,18},{3,19},{4,20},{5,21},{6,22},{7,23},{8,24},{9,... | collective-permute-start | bytes 294920 | tf_op jit(solution)/shard_map/ppermute | solution.py:292
  53.7 6.0 %collective-permute-start.15 = (bf16[2,32,1024]{2,1,0:T(8,128)(2,1)S(1)}, bf16[2,32,1024]{2,1,0:T(8,128)(2,1)S(1)}, u32[]{:S(2)}, u32[]{:S(2)}) collective-permute-start(bf16[2,32,1024]{2,1,0:T(8,128)(2,1)S(1)} %get-tuple-element.132), channel_id=1, source_target_pairs={{0,16},{1,17},{2,18},{3,19},{4,20},{5,21},{6,22},{7,23},{8,24},{9,... | collective-permute-start | bytes 393224 | tf_op jit(solution)/shard_map/ppermute | solution.py:292
  60.1 5.0 %collective-permute-start.17 = (f32[32,128]{1,0:T(8,128)S(1)}, f32[32,128]{1,0:T(8,128)S(1)}, u32[]{:S(2)}, u32[]{:S(2)}) collective-permute-start(f32[32,128]{1,0:T(8,128)S(1)} %pad_maximum_fusion.22), channel_id=1, source_target_pairs={{0,1},{1,0},{2,3},{3,2},{4,5},{5,4},{6,7},{7,6},{8,9},{9,8},{10,11... | collective-permute-start | bytes 49160 | tf_op jit(solution)/shard_map/ppermute | solution.py:287
  60.1 5.2 %collective-permute-start.16 = (bf16[2,32,768]{2,1,0:T(8,128)(2,1)S(1)}, bf16[2,32,768]{2,1,0:T(8,128)(2,1)S(1)}, u32[]{:S(2)}, u32[]{:S(2)}) collective-permute-start(bf16[2,32,768]{2,1,0:T(8,128)(2,1)S(1)} %get-tuple-element.142), channel_id=1, source_target_pairs={{0,16},{1,17},{2,18},{3,19},{4,20},{5,21},{6,22},{7,23},{8,24},{9,... | collective-permute-start | bytes 294920 | tf_op jit(solution)/shard_map/ppermute | solution.py:292
  65.4 7.0 %collective-permute-start.18 = (f32[32,128]{1,0:T(8,128)S(1)}, f32[32,128]{1,0:T(8,128)S(1)}, u32[]{:S(2)}, u32[]{:S(2)}) collective-permute-start(f32[32,128]{1,0:T(8,128)S(1)} %maximum_add_fusion.4), channel_id=1, source_target_pairs={{0,2},{1,3},{2,0},{3,1},{4,6},{5,7},{6,4},{7,5},{8,10},{9,11},{10,... | collective-permute-start | bytes 49160 | tf_op jit(solution)/shard_map/ppermute | solution.py:287
  72.4 10.5 %collective-permute-start.21 = (f32[32,128]{1,0:T(8,128)S(1)}, f32[32,128]{1,0:T(8,128)S(1)}, u32[]{:S(2)}, u32[]{:S(2)}) collective-permute-start(f32[32,128]{1,0:T(8,128)S(1)} %maximum_add_fusion.5), channel_id=1, source_target_pairs={{0,12},{1,13},{2,14},{3,15},{4,8},{5,9},{6,10},{7,11},{8,4},{9,5},... | collective-permute-start | bytes 49160 | tf_op jit(solution)/shard_map/ppermute | solution.py:287
  72.9 10.1 %collective-permute-start.20 = (f32[32,128]{1,0:T(8,128)S(1)}, f32[32,128]{1,0:T(8,128)S(1)}, u32[]{:S(2)}, u32[]{:S(2)}) collective-permute-start(f32[32,128]{1,0:T(8,128)S(1)} %maximum_add_fusion.5), channel_id=1, source_target_pairs={{0,8},{1,9},{2,10},{3,11},{4,12},{5,13},{6,14},{7,15},{8,0},{9,1},... | collective-permute-start | bytes 49160 | tf_op jit(solution)/shard_map/ppermute | solution.py:287
  74.0 9.0 %collective-permute-start.19 = (f32[32,128]{1,0:T(8,128)S(1)}, f32[32,128]{1,0:T(8,128)S(1)}, u32[]{:S(2)}, u32[]{:S(2)}) collective-permute-start(f32[32,128]{1,0:T(8,128)S(1)} %maximum_add_fusion.5), channel_id=1, source_target_pairs={{0,4},{1,5},{2,6},{3,7},{4,0},{5,1},{6,2},{7,3},{8,12},{9,13},{10,... | collective-permute-start | bytes 49160 | tf_op jit(solution)/shard_map/ppermute | solution.py:287
  85.9 6.6 %collective-permute-start.22 = (bf16[32,2048]{1,0:T(8,128)(2,1)S(1)}, bf16[32,2048]{1,0:T(8,128)(2,1)S(1)}, u32[]{:S(2)}, u32[]{:S(2)}) collective-permute-start(bf16[32,2048]{1,0:T(8,128)(2,1)S(1)} %pad_maximum_fusion.8), channel_id=1, source_target_pairs={{0,1},{1,0},{2,3},{3,2},{4,5},{5,4},{6,7},{7,6},{8,9},{9,8},{10,11... | collective-permute-start | bytes 393224 | tf_op jit(solution)/shard_map/ppermute | solution.py:287
  86.0 6.5 %collective-permute-start.23 = (bf16[16,512]{1,0:T(8,128)(2,1)S(1)}, bf16[16,512]{1,0:T(8,128)(2,1)S(1)}, u32[]{:S(2)}, u32[]{:S(2)}) collective-permute-start(bf16[16,512]{1,0:T(8,128)(2,1)S(1)} %get-tuple-element.226), channel_id=1, source_target_pairs={{0,1},{1,0},{2,3},{3,2},{4,5},{5,4},{6,7},{7,6},{8,9},{9,8},{10,11... | collective-permute-start | bytes 49160 | tf_op jit(solution)/shard_map/ppermute | solution.py:287
  92.7 11.4 %collective-permute-start.24 = (bf16[8,3072]{1,0:T(8,128)(2,1)S(1)}, bf16[8,3072]{1,0:T(8,128)(2,1)S(1)}, u32[]{:S(2)}, u32[]{:S(2)}) collective-permute-start(bf16[8,3072]{1,0:T(8,128)(2,1)S(1)} %pad_maximum_fusion.11), channel_id=1, source_target_pairs={{0,2},{1,3},{2,0},{3,1},{4,6},{5,7},{6,4},{7,5},{8,10},{9,11},{10,... | collective-permute-start | bytes 147464 | tf_op jit(solution)/shard_map/ppermute | solution.py:287
  95.7 8.4 %collective-permute-start.26 = (bf16[8,2048]{1,0:T(8,128)(2,1)S(1)}, bf16[8,2048]{1,0:T(8,128)(2,1)S(1)}, u32[]{:S(2)}, u32[]{:S(2)}) collective-permute-start(bf16[8,2048]{1,0:T(8,128)(2,1)S(1)} %get-tuple-element.208), channel_id=1, source_target_pairs={{0,18},{1,19},{2,16},{3,17},{4,22},{5,23},{6,20},{7,21},{8,26},{9,... | collective-permute-start | bytes 98312 | tf_op jit(solution)/shard_map/ppermute | solution.py:292
  96.9 7.1 %collective-permute-start.25 = (bf16[8,2048]{1,0:T(8,128)(2,1)S(1)}, bf16[8,2048]{1,0:T(8,128)(2,1)S(1)}, u32[]{:S(2)}, u32[]{:S(2)}) collective-permute-start(bf16[8,2048]{1,0:T(8,128)(2,1)S(1)} %get-tuple-element.209), channel_id=1, source_target_pairs={{0,16},{1,17},{2,18},{3,19},{4,20},{5,21},{6,22},{7,23},{8,24},{9,... | collective-permute-start | bytes 98312 | tf_op jit(solution)/shard_map/ppermute | solution.py:292
  104.1 11.9 %copy-start.4 = (s32[16]{0:T(128)S(1)}, s32[16]{0:T(128)}, u32[]{:S(2)}) copy-start(s32[16]{0:T(128)} %iota_xor_fusion) | copy-start | bytes 196
  104.3 5.7 %collective-permute-start.30 = (bf16[2,6144]{1,0:T(2,128)(2,1)S(1)}, bf16[2,6144]{1,0:T(2,128)(2,1)S(1)}, u32[]{:S(2)}, u32[]{:S(2)}) collective-permute-start(bf16[2,6144]{1,0:T(2,128)(2,1)S(1)} %get-tuple-element.213), channel_id=1, source_target_pairs={{0,12},{1,13},{2,14},{3,15},{4,8},{5,9},{6,10},{7,11},{8,4},{9,5},... | collective-permute-start | bytes 73736 | tf_op jit(solution)/shard_map/ppermute | solution.py:287
  104.7 5.3 %collective-permute-start.29 = (bf16[2,6144]{1,0:T(2,128)(2,1)S(1)}, bf16[2,6144]{1,0:T(2,128)(2,1)S(1)}, u32[]{:S(2)}, u32[]{:S(2)}) collective-permute-start(bf16[2,6144]{1,0:T(2,128)(2,1)S(1)} %get-tuple-element.214), channel_id=1, source_target_pairs={{0,8},{1,9},{2,10},{3,11},{4,12},{5,13},{6,14},{7,15},{8,0},{9,1},... | collective-permute-start | bytes 73736 | tf_op jit(solution)/shard_map/ppermute | solution.py:287
  105.8 4.7 %collective-permute-start.28 = (bf16[2,6144]{1,0:T(2,128)(2,1)S(1)}, bf16[2,6144]{1,0:T(2,128)(2,1)S(1)}, u32[]{:S(2)}, u32[]{:S(2)}) collective-permute-start(bf16[2,6144]{1,0:T(2,128)(2,1)S(1)} %get-tuple-element.215), channel_id=1, source_target_pairs={{0,4},{1,5},{2,6},{3,7},{4,0},{5,1},{6,2},{7,3},{8,12},{9,13},{10,... | collective-permute-start | bytes 73736 | tf_op jit(solution)/shard_map/ppermute | solution.py:287
  108.7 1.8 %collective-permute-start.27 = (bf16[32,2048]{1,0:T(8,128)(2,1)S(1)}, bf16[32,2048]{1,0:T(8,128)(2,1)S(1)}, u32[]{:S(2)}, u32[]{:S(2)}) collective-permute-start(bf16[32,2048]{1,0:T(8,128)(2,1)S(1)} %pad_maximum_fusion.9), channel_id=1, source_target_pairs={{0,1},{1,0},{2,3},{3,2},{4,5},{5,4},{6,7},{7,6},{8,9},{9,8},{10,11... | collective-permute-start | bytes 393224 | tf_op jit(solution)/shard_map/ppermute | solution.py:287
  110.7 5.6 %collective-permute-start.33 = (bf16[8,2048]{1,0:T(8,128)(2,1)S(1)}, bf16[8,2048]{1,0:T(8,128)(2,1)S(1)}, u32[]{:S(2)}, u32[]{:S(2)}) collective-permute-start(bf16[8,2048]{1,0:T(8,128)(2,1)S(1)} %get-tuple-element.205), channel_id=1, source_target_pairs={{0,18},{1,19},{2,16},{3,17},{4,22},{5,23},{6,20},{7,21},{8,26},{9,... | collective-permute-start | bytes 98312 | tf_op jit(solution)/shard_map/ppermute | solution.py:292
  112.4 3.9 %collective-permute-start.32 = (bf16[8,2048]{1,0:T(8,128)(2,1)S(1)}, bf16[8,2048]{1,0:T(8,128)(2,1)S(1)}, u32[]{:S(2)}, u32[]{:S(2)}) collective-permute-start(bf16[8,2048]{1,0:T(8,128)(2,1)S(1)} %get-tuple-element.206), channel_id=1, source_target_pairs={{0,16},{1,17},{2,18},{3,19},{4,20},{5,21},{6,22},{7,23},{8,24},{9,... | collective-permute-start | bytes 98312 | tf_op jit(solution)/shard_map/ppermute | solution.py:292
  113.4 3.9 %collective-permute-start.31 = (bf16[8,2048]{1,0:T(8,128)(2,1)S(1)}, bf16[8,2048]{1,0:T(8,128)(2,1)S(1)}, u32[]{:S(2)}, u32[]{:S(2)}) collective-permute-start(bf16[8,2048]{1,0:T(8,128)(2,1)S(1)} %get-tuple-element.207), channel_id=1, source_target_pairs={{0,2},{1,3},{2,0},{3,1},{4,6},{5,7},{6,4},{7,5},{8,10},{9,11},{10,... | collective-permute-start | bytes 98312 | tf_op jit(solution)/shard_map/ppermute | solution.py:287
  117.4 8.6 %collective-permute-start.36 = (bf16[2,4096]{1,0:T(2,128)(2,1)S(1)}, bf16[2,4096]{1,0:T(2,128)(2,1)S(1)}, u32[]{:S(2)}, u32[]{:S(2)}) collective-permute-start(bf16[2,4096]{1,0:T(2,128)(2,1)S(1)} %get-tuple-element.216), channel_id=1, source_target_pairs={{0,12},{1,13},{2,14},{3,15},{4,8},{5,9},{6,10},{7,11},{8,4},{9,5},... | collective-permute-start | bytes 49160 | tf_op jit(solution)/shard_map/ppermute | solution.py:287
  119.8 6.2 %collective-permute-start.35 = (bf16[2,4096]{1,0:T(2,128)(2,1)S(1)}, bf16[2,4096]{1,0:T(2,128)(2,1)S(1)}, u32[]{:S(2)}, u32[]{:S(2)}) collective-permute-start(bf16[2,4096]{1,0:T(2,128)(2,1)S(1)} %get-tuple-element.217), channel_id=1, source_target_pairs={{0,8},{1,9},{2,10},{3,11},{4,12},{5,13},{6,14},{7,15},{8,0},{9,1},... | collective-permute-start | bytes 49160 | tf_op jit(solution)/shard_map/ppermute | solution.py:287
  121.0 5.1 %collective-permute-start.34 = (bf16[2,4096]{1,0:T(2,128)(2,1)S(1)}, bf16[2,4096]{1,0:T(2,128)(2,1)S(1)}, u32[]{:S(2)}, u32[]{:S(2)}) collective-permute-start(bf16[2,4096]{1,0:T(2,128)(2,1)S(1)} %get-tuple-element.218), channel_id=1, source_target_pairs={{0,4},{1,5},{2,6},{3,7},{4,0},{5,1},{6,2},{7,3},{8,12},{9,13},{10,... | collective-permute-start | bytes 49160 | tf_op jit(solution)/shard_map/ppermute | solution.py:287
  121.9 4.9 %copy-start.1 = (bf16[32,1792]{1,0:T(8,128)(2,1)S(1)}, bf16[32,1792]{1,0:T(8,128)(2,1)}, u32[]{:S(2)}) copy-start(bf16[32,1792]{1,0:T(8,128)(2,1)} %param.17) | copy-start | bytes 344068

commit v5 on v4

--- a/solution.py
+++ b/solution.py
@@ -188,12 +188,11 @@
     pu_ref[...] += flipped_product(du, bu)
 
 
-def hidden_gradients(eug, euu, b_gate, b_up, keep, far, hidden_grad, first, width=256):
+def hidden_gradients(eug, euu, b_gate, b_up, keep, far, hidden_grad, width=256):
     rows, wide = eug.shape
     count = keep.shape[2]
-    start = first // width
     fixed = pl.BlockSpec((rows, wide), lambda k: (0, 0))
-    b_block = pl.BlockSpec((wide, width), lambda k: (0, k + start))
+    b_block = pl.BlockSpec((wide, width), lambda k: (0, k))
     block = pl.BlockSpec((2, rows, width), lambda k: (0, 0, k))
     return pl.pallas_call(
         hidden_kernel,
@@ -205,7 +204,7 @@
             b_block,
             block,
             block,
-            pl.BlockSpec((rows, width), lambda k: (0, k + start)),
+            pl.BlockSpec((rows, width), lambda k: (0, k)),
         ],
         out_specs=[block, fixed, fixed],
         out_shape=[jax.ShapeDtypeStruct((2, rows, count), BF16)]
@@ -226,30 +225,38 @@
     )
 
 
-def backward_kernel(first, side_ref, dg_ref, du_ref, wg_ref, wu_ref, keep_ref, send_ref, piece, sem):
-    pieces, depth = piece.shape[1:3]
+def backward_kernel(first, side_ref, dg_ref, du_ref, wg_ref, wu_ref, keep_ref, send_ref, rows_ref, sem):
+    pieces = sem.shape[1]
+    total_rows = rows_ref.shape[1]
+    depth = total_rows // pieces
     base = side_ref[0] * (wg_ref.shape[0] // 2) + first
     copies = []
     for k in range(pieces):
         for i, w_ref in enumerate((wg_ref, wu_ref)):
             source = pl.ds(pl.multiple_of(base + k * depth, depth), depth)
-            copy = pltpu.make_async_copy(w_ref.at[source], piece.at[i, k], sem.at[i, k])
+            copy = pltpu.make_async_copy(
+                w_ref.at[source], rows_ref.at[i, pl.ds(k * depth, depth)], sem.at[i, k]
+            )
             copy.start()
             copies.append(copy)
     q = dg_ref.shape[0] // 4
-    for k in range(pieces):
-        copies[2 * k].wait()
-        total = flipped_product(dg_ref[...], piece[0, k])
-        copies[2 * k + 1].wait()
-        total += flipped_product(du_ref[...], piece[1, k])
-        out = pl.ds(k * depth, depth)
+    step = 2 * depth
+    for k in range(0, total_rows, step):
+        at = 2 * (k // depth)
+        for copy in (copies[at], copies[at + 2]):
+            copy.wait()
+        total = flipped_product(dg_ref[...], rows_ref[0, k : k + step])
+        for copy in (copies[at + 1], copies[at + 3]):
+            copy.wait()
+        total += flipped_product(du_ref[...], rows_ref[1, k : k + step])
+        out = pl.ds(k, step)
         keep_ref[:q, out] = total[:q]
         keep_ref[q:, out] = total[2 * q : 3 * q]
         send_ref[:q, out] = total[q : 2 * q].astype(send_ref.dtype)
         send_ref[q:, out] = total[3 * q :].astype(send_ref.dtype)
 
 
-def backward_products(side, dg, du, gate_weight, up_weight, first, count, pieces=4):
+def backward_products(side, dg, du, gate_weight, up_weight, first, count, depth=256):
     rows, ff = dg.shape
     vmem = pl.BlockSpec(memory_space=pltpu.VMEM)
     hbm = pl.BlockSpec(memory_space=pltpu.HBM)
@@ -262,10 +269,10 @@
             jax.ShapeDtypeStruct((rows // 2, count), BF16),
         ],
         scratch_shapes=[
-            pltpu.VMEM((2, pieces, count // pieces, ff), BF16),
-            pltpu.SemaphoreType.DMA((2, pieces)),
+            pltpu.VMEM((2, count, ff), BF16),
+            pltpu.SemaphoreType.DMA((2, count // depth)),
         ],
-        compiler_params=pltpu.CompilerParams(vmem_limit_bytes=20 << 20),
+        compiler_params=pltpu.CompilerParams(vmem_limit_bytes=28 << 20),
         cost_estimate=pl.CostEstimate(
             flops=4 * rows * count * ff, bytes_accessed=6 * count * ff, transcendentals=0
         ),
@@ -311,13 +318,10 @@
     return value + jnp.concatenate([recv[o * q : (o + 1) * q] for o in order], axis=0)
 
 
-def add_far_z(value, parts):
+def add_z(value, recv, mask):
     shape = value.shape
-    total = value.reshape(4, 4, 2, shape[1])
-    for m, part in zip((1, 2, 3), parts):
-        part = part.reshape(total.shape)
-        total = total + jnp.stack([part[:, q ^ m] for q in range(4)], axis=1)
-    return total.reshape(shape)
+    v, r = (w.reshape(4, 4, 2, shape[1]) for w in (value, recv))
+    return (v + jnp.stack([r[:, q ^ mask] for q in range(4)], axis=1)).reshape(shape)
 
 
 def shared_device(tokens, gate_weight, up_weight, a_gate, a_up, b_gate, b_up, agent, d_hidden):
@@ -360,7 +364,7 @@
 
     blocks = lax.dynamic_slice_in_dim(x, (t % per_half) * feat_rows, feat_rows, 1)
     swapped = across_groups(blocks[rows:])
-    cuts = [ff * c // 7 for c in (0, 2, 4, 5, 7)]
+    cuts = [ff * c // 7 for c in (0, 1, 3, 5, 7)]
 
     def forward(c):
         return forward_products(
@@ -378,74 +382,66 @@
         axis=1,
     )
 
+    part = add_core(part, along_tensor(part, CORE))
     part, x = in_order(part, x)
-    recv = along_tensor(part, CORE)
+    recv = along_tensor(part, X)
     keep_1, send_1 = forward(1)
     recv, x, keep_1, send_1 = in_order(recv, x, keep_1, send_1)
-    part = add_core(part, recv)
-
-    recv = along_tensor(part, X)
-    far_a = across_groups(jnp.concatenate([send_0, send_1], axis=2))
+    part = add_x(part, recv)
+
+    recv = along_tensor(part, 4)
     keep_2, send_2 = forward(2)
     recv, x, keep_2, send_2 = in_order(recv, x, keep_2, send_2)
-    part = add_x(part, recv)
-
-    parts = from_far_z([part] * 3)
+    part = add_z(part, recv, 1)
+
+    recv = along_tensor(part, 8)
+    far_a = across_groups(jnp.concatenate([send_0, send_1, send_2], axis=2))
     keep_3, send_3 = forward(3)
-    far_a, keep_3, send_3, *parts = in_order(far_a, keep_3, send_3, *parts)
-    part = add_far_z(part, parts)
+    far_a, recv, keep_3, send_3 = in_order(far_a, recv, keep_3, send_3)
+    far_b = across_groups(send_3)
+    part = add_z(part, recv, 2)
     u = part.astype(BF16).astype(F32)
     up_factor_gate = spread(u[:, :R])
     up_factor_up = spread(u[:, R:])
 
-    far_b = across_groups(jnp.concatenate([send_2, send_3], axis=2))
-    d_a, pg_a, pu_a = hidden_gradients(
+    own, pg, pu = hidden_gradients(
         up_factor_gate,
         up_factor_up,
         b_gate,
         b_up,
-        jnp.concatenate([keep_0, keep_1], axis=2),
-        far_a,
+        jnp.concatenate([keep_0, keep_1, keep_2, keep_3], axis=2),
+        jnp.concatenate([far_a, far_b], axis=2),
         hidden_grad,
-        0,
-    )
-    far_b, d_a, pg_a, pu_a = in_order(far_b, d_a, pg_a, pu_a)
-    far_a = across_groups(d_a)
-    d_b, pg_b, pu_b = hidden_gradients(
-        up_factor_gate,
-        up_factor_up,
-        b_gate,
-        b_up,
-        jnp.concatenate([keep_2, keep_3], axis=2),
-        far_b,
-        hidden_grad,
-        cuts[2],
-    )
-    far_a, d_b, pg_b, pu_b = in_order(far_a, d_b, pg_b, pu_b)
-    far_b = across_groups(d_b)
-    part = jnp.concatenate([select(pg_a + pg_b), select(pu_a + pu_b)], axis=1)
+    )
+    far = across_groups(own)
+    part = jnp.concatenate([select(pg), select(pu)], axis=1)
     recv = along_tensor(part, CORE)
-    own = jnp.concatenate([d_a, d_b], axis=2)
     gate_lift_gradient = adapter_scale * rows_product(up_factor_gate, own[0])
-    far_b, recv, gate_lift_gradient = in_order(far_b, recv, gate_lift_gradient)
+    far, recv, gate_lift_gradient = in_order(far, recv, gate_lift_gradient)
     part = add_core(part, recv)
-    both = jnp.concatenate([own, jnp.concatenate([far_a, far_b], axis=2)], axis=1)
+    both = jnp.concatenate([own, far], axis=1)
     dg, du = both[0], both[1]
 
     count = half // 4
 
-    def backward(c):
-        return backward_products(side, dg, du, gate_weight, up_weight, c * count, count)
+    def backward(c, n):
+        return backward_products(side, dg, du, gate_weight, up_weight, c * count, n * count)
 
     recv = along_tensor(part, X)
-    keep_0, send_0 = backward(0)
+    keep_0, send_0 = backward(0, 1)
     recv, dg, du, keep_0, send_0 = in_order(recv, dg, du, keep_0, send_0)
     part = add_x(part, recv)
 
-    parts = from_far_z([part] * 3)
-    keep_1, send_1 = backward(1)
-    dg, du, keep_1, send_1, *parts = in_order(dg, du, keep_1, send_1, *parts)
-    part = add_far_z(part, parts)
+    recv = along_tensor(part, 4)
+    keep_1, send_1 = backward(1, 1)
+    recv, dg, du, keep_1, send_1 = in_order(recv, dg, du, keep_1, send_1)
+    part = add_z(part, recv, 1)
+
+    recv = along_tensor(part, 8)
+    keep_2, send_2 = backward(2, 2)
+    recv, keep_2, send_2, own, own_cols = in_order(recv, keep_2, send_2, own, own_cols)
+    part = add_z(part, recv, 2)
+    far = along_tensor(jnp.concatenate([send_0, send_1, send_2], axis=1), CORE)
     g = part.astype(BF16).astype(F32)
     gate_factor_gate = spread(g[:, :R])
     gate_factor_up = spread(g[:, R:])
@@ -456,61 +452,39 @@
             + flipped_product(gate_factor_up, a_up.astype(BF16))
         )
     ).astype(BF16)
-    moved, dg, du = in_order(moved, dg, du)
-
-    width = 2 * count
-    far = along_tensor(jnp.concatenate([send_0, send_1], axis=1), CORE)
+
     far_moved = along_tensor(moved[16:], CORE)
-    keep_2, send_2 = backward(2)
-    far, far_moved, dg, du, keep_2, send_2 = in_order(far, far_moved, dg, du, keep_2, send_2)
-    early = jnp.concatenate([keep_0, keep_1], axis=1) + far.astype(F32)
+    far, far_moved, own_cols = in_order(far, far_moved, own_cols)
+    sums = jnp.concatenate([keep_0, keep_1, keep_2], axis=1) + far.astype(F32)
     moved = jnp.concatenate([moved[:16], far_moved], axis=1)
 
-    def out_of(sums, *extra):
-        low = sums.astype(BF16)
-        return [
-            along_tensor(jnp.concatenate([low[8:16], *extra], axis=1), X),
-            across_groups(low[16:24]),
-            across_groups(low[24:], X),
-        ]
-
-    def joined(sums, parts):
-        near = sums[:8] + parts[0][:, :width].astype(F32)
-        return jnp.concatenate([near, parts[1].astype(F32) + parts[2].astype(F32)], axis=1)
-
-    parts = out_of(early, moved[8:])
-    keep_3, send_3 = backward(3)
-    keep_3, send_3, *parts = in_order(keep_3, send_3, *parts)
-    early = joined(early, parts)
-    moved = jnp.concatenate([moved[:8], parts[0][:, width:]], axis=1)
-
-    far = along_tensor(jnp.concatenate([send_2, send_3], axis=1), CORE)
-    low = jnp.concatenate([early.astype(BF16), moved], axis=1)
-    parts = from_far_z([low[2 * m : 2 * m + 2] for m in (1, 2, 3)])
+    low = sums.astype(BF16)
+    parts = [
+        along_tensor(jnp.concatenate([low[8:16], moved[8:]], axis=1), X),
+        across_groups(low[16:24]),
+        across_groups(low[24:], X),
+    ]
     gate_down_gradient = adapter_scale * rows_product(own_cols, gate_factor_gate)
-    far, gate_down_gradient, *parts = in_order(far, gate_down_gradient, *parts)
-    early = early[:2] + sum(p[:, : 2 * width].astype(F32) for p in parts)
-    moved = jnp.stack([moved[:2]] + [p[:, 2 * width :] for p in parts])
-    late = jnp.concatenate([keep_2, keep_3], axis=1) + far.astype(F32)
-
-    parts = out_of(late)
-    own_cols, gate_factor_up, late = in_order(own_cols, gate_factor_up, late)
     up_down_gradient = adapter_scale * rows_product(own_cols, gate_factor_up)
-    up_down_gradient, own, *parts = in_order(up_down_gradient, own, *parts)
-    late = joined(late, parts)
-
-    low = late.astype(BF16)
+    gate_down_gradient, up_down_gradient, own, *parts = in_order(
+        gate_down_gradient, up_down_gradient, own, *parts
+    )
+    near = sums[:8] + parts[0][:, :half].astype(F32)
+    sums = jnp.concatenate([near, parts[1].astype(F32) + parts[2].astype(F32)], axis=1)
+    moved = jnp.concatenate([moved[:8], parts[0][:, half:]], axis=1)
+
+    low = jnp.concatenate([sums.astype(BF16), moved], axis=1)
     parts = from_far_z([low[2 * m : 2 * m + 2] for m in (1, 2, 3)])
     up_lift_gradient = adapter_scale * rows_product(up_factor_up, own[1])
+    up_lift_gradient, *parts = in_order(up_lift_gradient, *parts)
+    sums = sums[:2] + sum(p[:, :d].astype(F32) for p in parts)
+    moved = jnp.stack([moved[:2]] + [p[:, d:] for p in parts])
     moved = moved.reshape(4, 2, 2, 2, feat_rows).transpose(0, 2, 3, 1, 4).reshape(N, 2 * feat_rows)
     source = jnp.arange(N, dtype=jnp.int32)
     sort = (source[:, None] == (t ^ source)[None, :]).astype(BF16)
     sorted_rows = jnp.dot(sort, moved, preferred_element_type=F32).reshape(N, 2, feat_rows)
     contribution = sorted_rows.transpose(1, 0, 2).reshape(2, d)
-    up_lift_gradient, contribution, *parts = in_order(up_lift_gradient, contribution, *parts)
-    late = late[:2] + sum(p.astype(F32) for p in parts)
-    near = jnp.concatenate([early[:, :width], late[:, :width]], axis=1)
-    far = jnp.concatenate([early[:, width:], late[:, width:]], axis=1)
+    near, far = sums[:, :half], sums[:, half:]
     sums = jnp.where(
         group == 0, jnp.concatenate([near, far], axis=1), jnp.concatenate([far, near], axis=1)
     )

time: 127 us -> 110 us (0.87)
  starting transfers between devices: 42.3 us -> 29.4 us
  Pallas kernels: 48.4 us -> 40.4 us
  waiting for transfers between devices: 12.7 us -> 16.7 us
  matrix products: 15.3 us -> 13.7 us
  local copies, waits for them, and re-layouts: 2.21 us -> 3.71 us
    ppermute x26 -> x19, starting transfers between devices: 29.7 us -> 19.9 us  [along_tensor(): return lax.ppermute(value, 'tensor', [(i, i ^ mask) for i in range(N)])]
    pallas_call x4 -> x3, Pallas kernels: 24.2 us -> 16.8 us  [backward_products(): pl.pallas_call(functools.partial(backward_kernel, first), in_specs=[pl.Bl...]
    ppermute x11 -> x8, starting transfers between devices: 12.6 us -> 9.47 us  [across_groups(): lax.ppermute(value, both, [(i, i ^ (N | mask)) for i in range(2 * N)])]
    ppermute x11 -> x8, waiting for transfers between devices: 3.3 us -> 5.95 us  [across_groups(): lax.ppermute(value, both, [(i, i ^ (N | mask)) for i in range(2 * N)])]
    dot_general x2, matrix products: 2.43 us -> 0.84 us  [flipped_product(): lax.dot_general(left, weight, (((1,), (1,)), ((), ())), preferred_element...]
    unnamed x12 -> x18, local copies, waits for them, and re-layouts: 1.36 us -> 2.93 us
    ppermute x26 -> x19, waiting for transfers between devices: 9.43 us -> 10.7 us  [along_tensor(): return lax.ppermute(value, 'tensor', [(i, i ^ mask) for i in range(N)])]
    pallas_call x2 -> x1, Pallas kernels: 9.81 us -> 9.09 us  [hidden_gradients(): pl.pallas_call(hidden_kernel, grid=(count // width,), in_specs=[fixed, fi...]
  transfers between devices with their start and end apart: 37 -> 27, of which waited for: 12 -> 11; matrix products, arithmetic and copies ran while one was open for 11% -> 13% of each run, Pallas kernels for 38% -> 28%
where the time goes in v5:
time: 110 us
  Pallas kernels  40.4 us (37%)
  starting transfers between devices  29.4 us (27%)
  waiting for transfers between devices  16.7 us (15%)
  matrix products  13.7 us (12%)
  other arithmetic  4.76 us (4%)
  local copies, waits for them, and re-layouts  3.71 us (3%)
  between operations  1.36 us (1%)
    ppermute x19, starting transfers between devices, along_tensor(): return lax.ppermute(value, 'tensor', [(i, i ^ mask) for i in range(N)])  19.9 us
    pallas_call x3, Pallas kernels, backward_products(): pl.pallas_call(functools.partial(backward_kernel, first), in_specs=[pl.Bl...  16.8 us
    pallas_call x4, Pallas kernels, forward_products(): pl.pallas_call(functools.partial(forward_kernel, first), in_specs=[pl.Blo...  14.6 us
    dot_general x4, matrix products, rows_product(): lax.dot_general(left, right, (((0,), (0,)), ((), ())), preferred_element_...  12 us
    ppermute x19, waiting for transfers between devices, along_tensor(): return lax.ppermute(value, 'tensor', [(i, i ^ mask) for i in range(N)])  10.7 us
    ppermute x8, starting transfers between devices, across_groups(): lax.ppermute(value, both, [(i, i ^ (N | mask)) for i in range(2 * N)])  9.47 us
    pallas_call x1, Pallas kernels, hidden_gradients(): pl.pallas_call(hidden_kernel, grid=(count // width,), in_specs=[fixed, fi...  9.09 us
    ppermute x8, waiting for transfers between devices, across_groups(): lax.ppermute(value, both, [(i, i ^ (N | mask)) for i in range(2 * N)])  5.95 us
  transfers between devices with their start and end apart: 27, of which 11 were waited for; matrix products, arithmetic and copies ran while one was open for 13% of the time, Pallas kernels for 28%

profile of v5, /device:TPU:0, one launch (start us, length us, event | category | flops | bytes accessed | tf_op | source)
XLA Modules:
  0.0 110.1 jit_solution(4328642173044577722)
XLA Ops:
  0.6 4.1 %collective-permute-start.1 = (bf16[2,8192]{1,0:T(2,128)(2,1)}, bf16[2,8192]{1,0:T(2,128)(2,1)S(1)}, u32[]{:S(2)}, u32[]{:S(2)}) collective-permute-start(bf16[2,8192]{1,0:T(2,128)(2,1)} %param.9), channel_id=1, source_target_pairs={{0,8},{1,9},{2,10},{3,11},{4,12},{5,13},{6,14},{7,15},{8,0},{9,1},... | collective-permute-start | bytes 98312 | tf_op jit(solution)/shard_map/ppermute | solution.py:294
  4.7 1.6 %collective-permute-start = (bf16[2,8192]{1,0:T(2,128)(2,1)}, bf16[2,8192]{1,0:T(2,128)(2,1)S(1)}, u32[]{:S(2)}, u32[]{:S(2)}) collective-permute-start(bf16[2,8192]{1,0:T(2,128)(2,1)} %param.9), channel_id=1, source_target_pairs={{0,4},{1,5},{2,6},{3,7},{4,0},{5,1},{6,2},{7,3},{8,12},{9,13},{10,... | collective-permute-start | bytes 98312 | tf_op jit(solution)/shard_map/ppermute | solution.py:294
  6.3 1.0 collective-permute-done.1
  7.3 1.6 %collective-permute-done = bf16[2,8192]{1,0:T(2,128)(2,1)S(1)} collective-permute-done((bf16[2,8192]{1,0:T(2,128)(2,1)}, bf16[2,8192]{1,0:T(2,128)(2,1)S(1)}, u32[]{:S(2)}, u32[]{:S(2)}) %collective-permute-start) | collective-permute-done | bytes 32800 | tf_op jit(solution)/shard_map/ppermute | solution.py:294
  8.9 3.4 %collective-permute-done.2 = bf16[2,8192]{1,0:T(2,128)(2,1)S(1)} collective-permute-done((bf16[2,8192]{1,0:T(2,128)(2,1)}, bf16[2,8192]{1,0:T(2,128)(2,1)S(1)}, u32[]{:S(2)}, u32[]{:S(2)}) %collective-permute-start.2) | collective-permute-done | bytes 32800 | tf_op jit(solution)/shard_map/ppermute | solution.py:294
  12.2 0.9 pad_maximum_fusion.7
  13.2 1.6 %collective-permute-start.3 = (bf16[8,4096]{1,0:T(8,128)(2,1)S(1)}, bf16[8,4096]{1,0:T(8,128)(2,1)S(1)}, u32[]{:S(2)}, u32[]{:S(2)}) collective-permute-start(bf16[8,4096]{1,0:T(8,128)(2,1)S(1)} %get-tuple-element.147), channel_id=1, source_target_pairs={{0,2},{1,3},{2,0},{3,1},{4,6},{5,7},{6,4},{7,5},{8,10},{9,11},{10,... | collective-permute-start | bytes 196616 | tf_op jit(solution)/shard_map/ppermute | solution.py:294
  14.8 1.5 %collective-permute-start.5 = (bf16[8,4096]{1,0:T(8,128)(2,1)S(1)}, bf16[8,4096]{1,0:T(8,128)(2,1)S(1)}, u32[]{:S(2)}, u32[]{:S(2)}) collective-permute-start(bf16[8,4096]{1,0:T(8,128)(2,1)S(1)} %get-tuple-element.148), channel_id=1, source_target_pairs={{0,18},{1,19},{2,16},{3,17},{4,22},{5,23},{6,20},{7,21},{8,26},{9,... | collective-permute-start | bytes 196616 | tf_op jit(solution)/shard_map/ppermute | solution.py:299
  16.8 0.9 collective-permute-done.3
  17.7 2.3 %collective-permute-done.5 = bf16[8,4096]{1,0:T(8,128)(2,1)S(1)} collective-permute-done((bf16[8,4096]{1,0:T(8,128)(2,1)S(1)}, bf16[8,4096]{1,0:T(8,128)(2,1)S(1)}, u32[]{:S(2)}, u32[]{:S(2)}) %collective-permute-start.5) | collective-permute-done | bytes 65568 | tf_op jit(solution)/shard_map/ppermute | solution.py:299
  19.9 0.7 collective-permute-done.4
  20.8 0.8 select_reduce_fusion
  21.6 0.7 collective-permute-done.6
  22.3 1.2 %collective-permute-start.7 = (bf16[32,512]{1,0:T(8,128)(2,1)S(1)}, bf16[32,512]{1,0:T(8,128)(2,1)S(1)}, u32[]{:S(2)}, u32[]{:S(2)}) collective-permute-start(bf16[32,512]{1,0:T(8,128)(2,1)S(1)} %dynamic-slice.1), channel_id=1, source_target_pairs={{0,16},{1,17},{2,18},{3,19},{4,20},{5,21},{6,22},{7,23},{8,24},{9,... | collective-permute-start | bytes 98312 | tf_op jit(solution)/shard_map/ppermute | solution.py:299
  23.5 3.0 %forward_products.4 = (f32[2,32,256]{2,1,0:T(8,128)S(1)}, bf16[2,32,256]{2,1,0:T(8,128)(2,1)S(1)}) custom-call(s32[1]{0:T(128)} %bitcast.3.side_ref, bf16[64,4096]{1,0:T(8,128)(2,1)S(1)} %bitcast.56, bf16[8192,1792]{1,0:T(8,128)(2,1)} %wg_ref.13, bf16[8192,1792]{1,0:T(8,128)(2,1)} %wu_ref.13), custom_call_target="tpu_custom_call" | custom-call | flops 268435456 | bytes 6291456 | tf_op jit(solution)/shard_map/forward_products/pallas_call | solution.py:136
  26.9 1.2 %copy-done.2 = f32[512,1024]{1,0:T(8,128)S(1)} copy-done((f32[512,1024]{1,0:T(8,128)S(1)}, f32[512,1024]{1,0:T(8,128)}, u32[]{:S(2)}) %copy-start.2) | copy-done | bytes 2097176
  28.8 0.9 collective-permute-done.8
  29.8 1.0 collective-permute-start.9
  30.8 3.8 %forward_products.5 = (f32[2,32,512]{2,1,0:T(8,128)S(1)}, bf16[2,32,512]{2,1,0:T(8,128)(2,1)S(1)}) custom-call(s32[1]{0:T(128)} %bitcast.3.side_ref, bf16[64,4096]{1,0:T(8,128)(2,1)S(1)} %bitcast.58, bf16[8192,1792]{1,0:T(8,128)(2,1)} %wg_ref.13, bf16[8192,1792]{1,0:T(8,128)(2,1)} %wu_ref.13), custom_call_target="tpu_custom_call" | custom-call | flops 536870912 | bytes 12582912 | tf_op jit(solution)/shard_map/forward_products/pallas_call | solution.py:136
  34.7 3.9 %forward_products.6 = (f32[2,32,512]{2,1,0:T(8,128)S(1)}, bf16[2,32,512]{2,1,0:T(8,128)(2,1)S(1)}) custom-call(s32[1]{0:T(128)} %bitcast.3.side_ref, bf16[64,4096]{1,0:T(8,128)(2,1)S(1)} %bitcast.59, bf16[8192,1792]{1,0:T(8,128)(2,1)} %wg_ref.13, bf16[8192,1792]{1,0:T(8,128)(2,1)} %wu_ref.13), custom_call_target="tpu_custom_call" | custom-call | flops 536870912 | bytes 12582912 | tf_op jit(solution)/shard_map/forward_products/pallas_call | solution.py:136
  38.7 1.4 %collective-permute-start.11 = (bf16[2,32,1280]{2,1,0:T(8,128)(2,1)S(1)}, bf16[2,32,1280]{2,1,0:T(8,128)(2,1)S(1)}, u32[]{:S(2)}, u32[]{:S(2)}) collective-permute-start(bf16[2,32,1280]{2,1,0:T(8,128)(2,1)S(1)} %pad_maximum_fusion.6), channel_id=1, source_target_pairs={{0,16},{1,17},{2,18},{3,19},{4,20},{5,21},{6,22},{7,23},{8,24},{9,... | collective-permute-start | bytes 491528 | tf_op jit(solution)/shard_map/ppermute | solution.py:299
  40.2 1.0 collective-permute-start.12
  41.1 3.8 %forward_products.7 = (f32[2,32,512]{2,1,0:T(8,128)S(1)}, bf16[2,32,512]{2,1,0:T(8,128)(2,1)S(1)}) custom-call(s32[1]{0:T(128)} %bitcast.3.side_ref, bf16[64,4096]{1,0:T(8,128)(2,1)S(1)} %bitcast.60, bf16[8192,1792]{1,0:T(8,128)(2,1)} %wg_ref.13, bf16[8192,1792]{1,0:T(8,128)(2,1)} %wu_ref.13), custom_call_target="tpu_custom_call" | custom-call | flops 536870912 | bytes 12582912 | tf_op jit(solution)/shard_map/forward_products/pallas_call | solution.py:136
  45.9 1.2 %collective-permute-start.13 = (bf16[2,32,512]{2,1,0:T(8,128)(2,1)S(1)}, bf16[2,32,512]{2,1,0:T(8,128)(2,1)S(1)}, u32[]{:S(2)}, u32[]{:S(2)}) collective-permute-start(bf16[2,32,512]{2,1,0:T(8,128)(2,1)S(1)} %get-tuple-element.96), channel_id=1, source_target_pairs={{0,16},{1,17},{2,18},{3,19},{4,20},{5,21},{6,22},{7,23},{8,24},{9,... | collective-permute-start | bytes 196616 | tf_op jit(solution)/shard_map/ppermute | solution.py:299
  47.2 3.0 %collective-permute-done.13 = bf16[2,32,512]{2,1,0:T(8,128)(2,1)S(1)} collective-permute-done((bf16[2,32,512]{2,1,0:T(8,128)(2,1)S(1)}, bf16[2,32,512]{2,1,0:T(8,128)(2,1)S(1)}, u32[]{:S(2)}, u32[]{:S(2)}) %collective-permute-start.13) | collective-permute-done | bytes 65568 | tf_op jit(solution)/shard_map/ppermute | solution.py:299
  50.2 0.9 pad_maximum_fusion.5.far_ref
  51.2 9.1 %hidden_gradients.1 = (bf16[2,32,1792]{2,1,0:T(8,128)(2,1)S(1)}, f32[32,1024]{1,0:T(8,128)S(1)}, f32[32,1024]{1,0:T(8,128)S(1)}) custom-call(bf16[32,1024]{1,0:T(8,128)(2,1)S(1)} %get-tuple-element.185.eug_ref, bf16[32,1024]{1,0:T(8,128)(2,1)S(1)} %get-tuple-element.186.euu_ref, f32[1024,1792]{1,0:T(8,128)} %bg_ref.1, f32[1024,1792]{1,0:T(8,128)} %bu_ref.1, ...), custom_call_target="tpu_custom_call" | custom-call | flops 469762048 | bytes 29360128 | tf_op jit(solution)/shard_map/hidden_gradients/pallas_call | solution.py:197
  60.3 1.2 %collective-permute-start.14 = (bf16[2,32,1792]{2,1,0:T(8,128)(2,1)S(1)}, bf16[2,32,1792]{2,1,0:T(8,128)(2,1)S(1)}, u32[]{:S(2)}, u32[]{:S(2)}) collective-permute-start(bf16[2,32,1792]{2,1,0:T(8,128)(2,1)S(1)} %get-tuple-element.129), channel_id=1, source_target_pairs={{0,16},{1,17},{2,18},{3,19},{4,20},{5,21},{6,22},{7,23},{8,24},{9,... | collective-permute-start | bytes 688136 | tf_op jit(solution)/shard_map/ppermute | solution.py:299
  61.5 4.2 %convolution_multiply_fusion.1 = f32[1024,1792]{1,0:T(8,128)} fusion(bf16[32,1024]{1,0:T(8,128)(2,1)S(1)} %get-tuple-element.185.eug_ref, bf16[2,32,1792]{2,1,0:T(8,128)(2,1)S(1)} %get-tuple-element.129), kind=kOutput, calls=%fused_computation.1 | convolution fusion | flops 119275520 | bytes 7520256 | tf_op jit(solution)/shard_map/dot_general | solution.py:39
  66.0 1.1 %collective-permute-done.15 = f32[32,128]{1,0:T(8,128)S(1)} collective-permute-done((f32[32,128]{1,0:T(8,128)S(1)}, f32[32,128]{1,0:T(8,128)S(1)}, u32[]{:S(2)}, u32[]{:S(2)}) %collective-permute-start.15) | collective-permute-done | bytes 16416 | tf_op jit(solution)/shard_map/ppermute | solution.py:294
  67.3 0.7 collective-permute-start.16
  68.0 4.7 %backward_products.3 = (f32[32,1024]{1,0:T(8,128)S(1)}, bf16[32,1024]{1,0:T(8,128)(2,1)S(1)}) custom-call(s32[1]{0:T(128)} %bitcast.3.side_ref, bf16[64,1792]{1,0:T(8,128)(2,1)S(1)} %get-tuple-element.112.dg_ref, bf16[64,1792]{1,0:T(8,128)(2,1)S(1)} %get-tuple-element.113.du_ref, bf16[8192,1792]{1,0:T(8,128)(2,1)} %wg_ref.13, bf16[8192,1792]{1,0:T(8,128)(2,1)} %wu_ref.13), custom_call_target="tpu_custom_call" | custom-call | flops 469762048 | bytes 11010048 | tf_op jit(solution)/shard_map/backward_products/pallas_call | solution.py:263
  72.7 1.9 %collective-permute-start.17 = (f32[32,128]{1,0:T(8,128)S(1)}, f32[32,128]{1,0:T(8,128)S(1)}, u32[]{:S(2)}, u32[]{:S(2)}) collective-permute-start(f32[32,128]{1,0:T(8,128)S(1)} %maximum_add_fusion.4), channel_id=1, source_target_pairs={{0,4},{1,5},{2,6},{3,7},{4,0},{5,1},{6,2},{7,3},{8,12},{9,13},{10,... | collective-permute-start | bytes 49160 | tf_op jit(solution)/shard_map/ppermute | solution.py:294
  74.6 4.7 %backward_products.4 = (f32[32,1024]{1,0:T(8,128)S(1)}, bf16[32,1024]{1,0:T(8,128)(2,1)S(1)}) custom-call(s32[1]{0:T(128)} %bitcast.3.side_ref, bf16[64,1792]{1,0:T(8,128)(2,1)S(1)} %get-tuple-element.112.dg_ref, bf16[64,1792]{1,0:T(8,128)(2,1)S(1)} %get-tuple-element.113.du_ref, bf16[8192,1792]{1,0:T(8,128)(2,1)} %wg_ref.13, bf16[8192,1792]{1,0:T(8,128)(2,1)} %wu_ref.13), custom_call_target="tpu_custom_call" | custom-call | flops 469762048 | bytes 11010048 | tf_op jit(solution)/shard_map/backward_products/pallas_call | solution.py:263
  79.3 2.3 %collective-permute-start.18 = (f32[32,128]{1,0:T(8,128)S(1)}, f32[32,128]{1,0:T(8,128)S(1)}, u32[]{:S(2)}, u32[]{:S(2)}) collective-permute-start(f32[32,128]{1,0:T(8,128)S(1)} %add.242), channel_id=1, source_target_pairs={{0,8},{1,9},{2,10},{3,11},{4,12},{5,13},{6,14},{7,15},{8,0},{9,1},... | collective-permute-start | bytes 49160 | tf_op jit(solution)/shard_map/ppermute | solution.py:294
  81.6 7.5 %backward_products.5 = (f32[32,2048]{1,0:T(8,128)S(1)}, bf16[32,2048]{1,0:T(8,128)(2,1)S(1)}) custom-call(s32[1]{0:T(128)} %bitcast.3.side_ref, bf16[64,1792]{1,0:T(8,128)(2,1)S(1)} %get-tuple-element.112.dg_ref, bf16[64,1792]{1,0:T(8,128)(2,1)S(1)} %get-tuple-element.113.du_ref, bf16[8192,1792]{1,0:T(8,128)(2,1)} %wg_ref.13, bf16[8192,1792]{1,0:T(8,128)(2,1)} %wu_ref.13), custom_call_target="tpu_custom_call" | custom-call | flops 939524096 | bytes 22020096 | tf_op jit(solution)/shard_map/backward_products/pallas_call | solution.py:263
  90.0 1.1 copy-done.4
  91.6 1.2 %collective-permute-done.20 = bf16[16,512]{1,0:T(8,128)(2,1)S(1)} collective-permute-done((bf16[16,512]{1,0:T(8,128)(2,1)S(1)}, bf16[16,512]{1,0:T(8,128)(2,1)S(1)}, u32[]{:S(2)}, u32[]{:S(2)}) %collective-permute-start.20) | collective-permute-done | bytes 16416 | tf_op jit(solution)/shard_map/ppermute | solution.py:294
  92.9 1.7 %collective-permute-start.23 = (bf16[8,4096]{1,0:T(8,128)(2,1)S(1)}, bf16[8,4096]{1,0:T(8,128)(2,1)S(1)}, u32[]{:S(2)}, u32[]{:S(2)}) collective-permute-start(bf16[8,4096]{1,0:T(8,128)(2,1)S(1)} %get-tuple-element.141), channel_id=1, source_target_pairs={{0,18},{1,19},{2,16},{3,17},{4,22},{5,23},{6,20},{7,21},{8,26},{9,... | collective-permute-start | bytes 196616 | tf_op jit(solution)/shard_map/ppermute | solution.py:299
  94.6 0.7 collective-permute-start.22
  95.4 1.1 %collective-permute-start.21 = (bf16[8,5120]{1,0:T(8,128)(2,1)S(1)}, bf16[8,5120]{1,0:T(8,128)(2,1)S(1)}, u32[]{:S(2)}, u32[]{:S(2)}) collective-permute-start(bf16[8,5120]{1,0:T(8,128)(2,1)S(1)} %pad_maximum_fusion.8), channel_id=1, source_target_pairs={{0,2},{1,3},{2,0},{3,1},{4,6},{5,7},{6,4},{7,5},{8,10},{9,11},{10,... | collective-permute-start | bytes 245768 | tf_op jit(solution)/shard_map/ppermute | solution.py:294
  96.5 1.8 %convolution_multiply_fusion.2 = f32[512,1024]{1,0:T(8,128)} fusion(bf16[32,512]{1,0:T(8,128)(2,1)S(1)} %dynamic-slice_select_fusion, bf16[32,1024]{1,0:T(8,128)(2,1)S(1)} %copy-done.6, s32[1024]{0:T(1024)S(1)} %add_select_fusion, s32[32]{0:T(128)S(1)} %select_reduce_fusion), kind=kOutput, calls=%fused_computation.2 | convolution fusion | flops 34144256 | bytes 2199680 | tf_op jit(solution)/shard_map/dot_general | solution.py:39
  98.3 1.8 %convolution_multiply_fusion.3 = f32[512,1024]{1,0:T(8,128)} fusion(bf16[32,512]{1,0:T(8,128)(2,1)S(1)} %dynamic-slice_select_fusion, bf16[32,1024]{1,0:T(8,128)(2,1)S(1)} %concatenate.102, s32[1024]{0:T(1024)S(1)} %add_select_fusion, s32[32]{0:T(128)S(1)} %select_reduce_fusion), kind=kOutput, calls=%fused_computation.3 | convolution fusion | flops 34144256 | bytes 2199680 | tf_op jit(solution)/shard_map/dot_general | solution.py:39
  100.3 0.6 collective-permute-start.26
  100.9 1.0 collective-permute-start.25
  101.9 2.9 %collective-permute-start.24 = (bf16[2,10240]{1,0:T(2,128)(2,1)S(1)}, bf16[2,10240]{1,0:T(2,128)(2,1)S(1)}, u32[]{:S(2)}, u32[]{:S(2)}) collective-permute-start(bf16[2,10240]{1,0:T(2,128)(2,1)S(1)} %get-tuple-element.146), channel_id=1, source_target_pairs={{0,4},{1,5},{2,6},{3,7},{4,0},{5,1},{6,2},{7,3},{8,12},{9,13},{10,... | collective-permute-start | bytes 122888 | tf_op jit(solution)/shard_map/ppermute | solution.py:294
  104.8 4.2 %convolution_multiply_fusion = f32[1024,1792]{1,0:T(8,128)} fusion(bf16[32,1024]{1,0:T(8,128)(2,1)S(1)} %get-tuple-element.186.euu_ref, bf16[2,32,1792]{2,1,0:T(8,128)(2,1)S(1)} %get-tuple-element.129), kind=kOutput, calls=%fused_computation | convolution fusion | flops 119275520 | bytes 7520256 | tf_op jit(solution)/shard_map/dot_general | solution.py:39
  109.4 0.7 fusion.19
  (115 shorter events, 5.4 us)
Async XLA Ops:
  0.6 27.9 %copy-start = (bf16[32,1792]{1,0:T(8,128)(2,1)S(1)}, bf16[32,1792]{1,0:T(8,128)(2,1)}, u32[]{:S(2)}) copy-start(bf16[32,1792]{1,0:T(8,128)(2,1)} %param.17) | copy-start | bytes 344068
  0.6 6.7 %collective-permute-start.1 = (bf16[2,8192]{1,0:T(2,128)(2,1)}, bf16[2,8192]{1,0:T(2,128)(2,1)S(1)}, u32[]{:S(2)}, u32[]{:S(2)}) collective-permute-start(bf16[2,8192]{1,0:T(2,128)(2,1)} %param.9), channel_id=1, source_target_pairs={{0,8},{1,9},{2,10},{3,11},{4,12},{5,13},{6,14},{7,15},{8,0},{9,1},... | collective-permute-start | bytes 98312 | tf_op jit(solution)/shard_map/ppermute | solution.py:294
  4.7 4.1 %collective-permute-start = (bf16[2,8192]{1,0:T(2,128)(2,1)}, bf16[2,8192]{1,0:T(2,128)(2,1)S(1)}, u32[]{:S(2)}, u32[]{:S(2)}) collective-permute-start(bf16[2,8192]{1,0:T(2,128)(2,1)} %param.9), channel_id=1, source_target_pairs={{0,4},{1,5},{2,6},{3,7},{4,0},{5,1},{6,2},{7,3},{8,12},{9,13},{10,... | collective-permute-start | bytes 98312 | tf_op jit(solution)/shard_map/ppermute | solution.py:294
  6.3 5.9 %collective-permute-start.2 = (bf16[2,8192]{1,0:T(2,128)(2,1)}, bf16[2,8192]{1,0:T(2,128)(2,1)S(1)}, u32[]{:S(2)}, u32[]{:S(2)}) collective-permute-start(bf16[2,8192]{1,0:T(2,128)(2,1)} %param.9), channel_id=1, source_target_pairs={{0,12},{1,13},{2,14},{3,15},{4,8},{5,9},{6,10},{7,11},{8,4},{9,5},... | collective-permute-start | bytes 98312 | tf_op jit(solution)/shard_map/ppermute | solution.py:294
  13.2 4.5 %collective-permute-start.3 = (bf16[8,4096]{1,0:T(8,128)(2,1)S(1)}, bf16[8,4096]{1,0:T(8,128)(2,1)S(1)}, u32[]{:S(2)}, u32[]{:S(2)}) collective-permute-start(bf16[8,4096]{1,0:T(8,128)(2,1)S(1)} %get-tuple-element.147), channel_id=1, source_target_pairs={{0,2},{1,3},{2,0},{3,1},{4,6},{5,7},{6,4},{7,5},{8,10},{9,11},{10,... | collective-permute-start | bytes 196616 | tf_op jit(solution)/shard_map/ppermute | solution.py:294
  14.8 5.2 %collective-permute-start.5 = (bf16[8,4096]{1,0:T(8,128)(2,1)S(1)}, bf16[8,4096]{1,0:T(8,128)(2,1)S(1)}, u32[]{:S(2)}, u32[]{:S(2)}) collective-permute-start(bf16[8,4096]{1,0:T(8,128)(2,1)S(1)} %get-tuple-element.148), channel_id=1, source_target_pairs={{0,18},{1,19},{2,16},{3,17},{4,22},{5,23},{6,20},{7,21},{8,26},{9,... | collective-permute-start | bytes 196616 | tf_op jit(solution)/shard_map/ppermute | solution.py:299
  16.3 4.4 %collective-permute-start.4 = (bf16[8,4096]{1,0:T(8,128)(2,1)S(1)}, bf16[8,4096]{1,0:T(8,128)(2,1)S(1)}, u32[]{:S(2)}, u32[]{:S(2)}) collective-permute-start(bf16[8,4096]{1,0:T(8,128)(2,1)S(1)} %get-tuple-element.148), channel_id=1, source_target_pairs={{0,16},{1,17},{2,18},{3,19},{4,20},{5,21},{6,22},{7,23},{8,24},{9,... | collective-permute-start | bytes 196616 | tf_op jit(solution)/shard_map/ppermute | solution.py:299
  20.7 1.6 %collective-permute-start.6 = (bf16[2,16,4096]{2,1,0:T(8,128)(2,1)S(1)}, bf16[2,16,4096]{2,1,0:T(8,128)(2,1)S(1)}, u32[]{:S(2)}, u32[]{:S(2)}) collective-permute-start(bf16[2,16,4096]{2,1,0:T(8,128)(2,1)S(1)} %pad_maximum_fusion.3), channel_id=1, source_target_pairs={{0,1},{1,0},{2,3},{3,2},{4,5},{5,4},{6,7},{7,6},{8,9},{9,8},{10,11... | collective-permute-start | bytes 786440 | tf_op jit(solution)/shard_map/ppermute | solution.py:294
  22.3 4.2 %collective-permute-start.7 = (bf16[32,512]{1,0:T(8,128)(2,1)S(1)}, bf16[32,512]{1,0:T(8,128)(2,1)S(1)}, u32[]{:S(2)}, u32[]{:S(2)}) collective-permute-start(bf16[32,512]{1,0:T(8,128)(2,1)S(1)} %dynamic-slice.1), channel_id=1, source_target_pairs={{0,16},{1,17},{2,18},{3,19},{4,20},{5,21},{6,22},{7,23},{8,24},{9,... | collective-permute-start | bytes 98312 | tf_op jit(solution)/shard_map/ppermute | solution.py:299
  23.5 3.0 %copy-start.3 = (f32[512,1024]{1,0:T(8,128)S(1)}, f32[512,1024]{1,0:T(8,128)}, u32[]{:S(2)}) copy-start(f32[512,1024]{1,0:T(8,128)} %param.13) | copy-start | bytes 6291460
  26.5 1.6 %copy-start.2 = (f32[512,1024]{1,0:T(8,128)S(1)}, f32[512,1024]{1,0:T(8,128)}, u32[]{:S(2)}) copy-start(f32[512,1024]{1,0:T(8,128)} %param.12) | copy-start | bytes 6291460
  28.6 1.2 %collective-permute-start.8 = (f32[32,128]{1,0:T(8,128)S(1)}, f32[32,128]{1,0:T(8,128)S(1)}, u32[]{:S(2)}, u32[]{:S(2)}) collective-permute-start(f32[32,128]{1,0:T(8,128)S(1)} %pad_maximum_fusion.15), channel_id=1, source_target_pairs={{0,1},{1,0},{2,3},{3,2},{4,5},{5,4},{6,7},{7,6},{8,9},{9,8},{10,11... | collective-permute-start | bytes 49160 | tf_op jit(solution)/shard_map/ppermute | solution.py:294
  29.8 4.8 %collective-permute-start.9 = (f32[32,128]{1,0:T(8,128)S(1)}, f32[32,128]{1,0:T(8,128)S(1)}, u32[]{:S(2)}, u32[]{:S(2)}) collective-permute-start(f32[32,128]{1,0:T(8,128)S(1)} %maximum_add_fusion.1), channel_id=1, source_target_pairs={{0,2},{1,3},{2,0},{3,1},{4,6},{5,7},{6,4},{7,5},{8,10},{9,11},{10,... | collective-permute-start | bytes 49160 | tf_op jit(solution)/shard_map/ppermute | solution.py:294
  34.7 4.0 %collective-permute-start.10 = (f32[32,128]{1,0:T(8,128)S(1)}, f32[32,128]{1,0:T(8,128)S(1)}, u32[]{:S(2)}, u32[]{:S(2)}) collective-permute-start(f32[32,128]{1,0:T(8,128)S(1)} %maximum_add_fusion.2), channel_id=1, source_target_pairs={{0,4},{1,5},{2,6},{3,7},{4,0},{5,1},{6,2},{7,3},{8,12},{9,13},{10,... | collective-permute-start | bytes 49160 | tf_op jit(solution)/shard_map/ppermute | solution.py:294
  38.7 6.3 %collective-permute-start.11 = (bf16[2,32,1280]{2,1,0:T(8,128)(2,1)S(1)}, bf16[2,32,1280]{2,1,0:T(8,128)(2,1)S(1)}, u32[]{:S(2)}, u32[]{:S(2)}) collective-permute-start(bf16[2,32,1280]{2,1,0:T(8,128)(2,1)S(1)} %pad_maximum_fusion.6), channel_id=1, source_target_pairs={{0,16},{1,17},{2,18},{3,19},{4,20},{5,21},{6,22},{7,23},{8,24},{9,... | collective-permute-start | bytes 491528 | tf_op jit(solution)/shard_map/ppermute | solution.py:299
  40.2 4.8 %collective-permute-start.12 = (f32[32,128]{1,0:T(8,128)S(1)}, f32[32,128]{1,0:T(8,128)S(1)}, u32[]{:S(2)}, u32[]{:S(2)}) collective-permute-start(f32[32,128]{1,0:T(8,128)S(1)} %add.222), channel_id=1, source_target_pairs={{0,8},{1,9},{2,10},{3,11},{4,12},{5,13},{6,14},{7,15},{8,0},{9,1},... | collective-permute-start | bytes 49160 | tf_op jit(solution)/shard_map/ppermute | solution.py:294
  45.0 0.7 copy-start.7
  45.9 4.3 %collective-permute-start.13 = (bf16[2,32,512]{2,1,0:T(8,128)(2,1)S(1)}, bf16[2,32,512]{2,1,0:T(8,128)(2,1)S(1)}, u32[]{:S(2)}, u32[]{:S(2)}) collective-permute-start(bf16[2,32,512]{2,1,0:T(8,128)(2,1)S(1)} %get-tuple-element.96), channel_id=1, source_target_pairs={{0,16},{1,17},{2,18},{3,19},{4,20},{5,21},{6,22},{7,23},{8,24},{9,... | collective-permute-start | bytes 196616 | tf_op jit(solution)/shard_map/ppermute | solution.py:299
  60.3 6.9 %collective-permute-start.14 = (bf16[2,32,1792]{2,1,0:T(8,128)(2,1)S(1)}, bf16[2,32,1792]{2,1,0:T(8,128)(2,1)S(1)}, u32[]{:S(2)}, u32[]{:S(2)}) collective-permute-start(bf16[2,32,1792]{2,1,0:T(8,128)(2,1)S(1)} %get-tuple-element.129), channel_id=1, source_target_pairs={{0,16},{1,17},{2,18},{3,19},{4,20},{5,21},{6,22},{7,23},{8,24},{9,... | collective-permute-start | bytes 688136 | tf_op jit(solution)/shard_map/ppermute | solution.py:299
  66.0 1.2 %collective-permute-start.15 = (f32[32,128]{1,0:T(8,128)S(1)}, f32[32,128]{1,0:T(8,128)S(1)}, u32[]{:S(2)}, u32[]{:S(2)}) collective-permute-start(f32[32,128]{1,0:T(8,128)S(1)} %pad_maximum_fusion.18), channel_id=1, source_target_pairs={{0,1},{1,0},{2,3},{3,2},{4,5},{5,4},{6,7},{7,6},{8,9},{9,8},{10,11... | collective-permute-start | bytes 49160 | tf_op jit(solution)/shard_map/ppermute | solution.py:294
  67.3 5.4 %collective-permute-start.16 = (f32[32,128]{1,0:T(8,128)S(1)}, f32[32,128]{1,0:T(8,128)S(1)}, u32[]{:S(2)}, u32[]{:S(2)}) collective-permute-start(f32[32,128]{1,0:T(8,128)S(1)} %maximum_add_fusion.3), channel_id=1, source_target_pairs={{0,2},{1,3},{2,0},{3,1},{4,6},{5,7},{6,4},{7,5},{8,10},{9,11},{10,... | collective-permute-start | bytes 49160 | tf_op jit(solution)/shard_map/ppermute | solution.py:294
  72.7 6.6 %collective-permute-start.17 = (f32[32,128]{1,0:T(8,128)S(1)}, f32[32,128]{1,0:T(8,128)S(1)}, u32[]{:S(2)}, u32[]{:S(2)}) collective-permute-start(f32[32,128]{1,0:T(8,128)S(1)} %maximum_add_fusion.4), channel_id=1, source_target_pairs={{0,4},{1,5},{2,6},{3,7},{4,0},{5,1},{6,2},{7,3},{8,12},{9,13},{10,... | collective-permute-start | bytes 49160 | tf_op jit(solution)/shard_map/ppermute | solution.py:294
  79.3 9.8 %collective-permute-start.18 = (f32[32,128]{1,0:T(8,128)S(1)}, f32[32,128]{1,0:T(8,128)S(1)}, u32[]{:S(2)}, u32[]{:S(2)}) collective-permute-start(f32[32,128]{1,0:T(8,128)S(1)} %add.242), channel_id=1, source_target_pairs={{0,8},{1,9},{2,10},{3,11},{4,12},{5,13},{6,14},{7,15},{8,0},{9,1},... | collective-permute-start | bytes 49160 | tf_op jit(solution)/shard_map/ppermute | solution.py:294
  89.3 2.2 %copy-start.5 = (bf16[32,1024]{1,0:T(8,128)(2,1)}, bf16[32,1024]{1,0:T(8,128)(2,1)S(1)}, u32[]{:S(2)}) copy-start(bf16[32,1024]{1,0:T(8,128)(2,1)S(1)} %concatenate.103) | copy-start | bytes 196612
  89.5 1.6 %copy-start.4 = (f32[512,1024]{1,0:T(8,128)S(1)}, f32[512,1024]{1,0:T(8,128)}, u32[]{:S(2)}) copy-start(f32[512,1024]{1,0:T(8,128)} %param.13) | copy-start | bytes 6291460
  89.9 2.9 %collective-permute-start.19 = (bf16[32,4096]{1,0:T(8,128)(2,1)S(1)}, bf16[32,4096]{1,0:T(8,128)(2,1)S(1)}, u32[]{:S(2)}, u32[]{:S(2)}) collective-permute-start(bf16[32,4096]{1,0:T(8,128)(2,1)S(1)} %pad_maximum_fusion.4), channel_id=1, source_target_pairs={{0,1},{1,0},{2,3},{3,2},{4,5},{5,4},{6,7},{7,6},{8,9},{9,8},{10,11... | collective-permute-start | bytes 786440 | tf_op jit(solution)/shard_map/ppermute | solution.py:294
  91.5 5.0 %copy-start.6 = (bf16[32,1024]{1,0:T(8,128)(2,1)S(1)}, bf16[32,1024]{1,0:T(8,128)(2,1)}, u32[]{:S(2)}) copy-start(bf16[32,1024]{1,0:T(8,128)(2,1)} %copy-done.5) | copy-start | bytes 196612
  91.5 1.2 %collective-permute-start.20 = (bf16[16,512]{1,0:T(8,128)(2,1)S(1)}, bf16[16,512]{1,0:T(8,128)(2,1)S(1)}, u32[]{:S(2)}, u32[]{:S(2)}) collective-permute-start(bf16[16,512]{1,0:T(8,128)(2,1)S(1)} %get-tuple-element.154), channel_id=1, source_target_pairs={{0,1},{1,0},{2,3},{3,2},{4,5},{5,4},{6,7},{7,6},{8,9},{9,8},{10,11... | collective-permute-start | bytes 49160 | tf_op jit(solution)/shard_map/ppermute | solution.py:294
  92.9 7.2 %collective-permute-start.23 = (bf16[8,4096]{1,0:T(8,128)(2,1)S(1)}, bf16[8,4096]{1,0:T(8,128)(2,1)S(1)}, u32[]{:S(2)}, u32[]{:S(2)}) collective-permute-start(bf16[8,4096]{1,0:T(8,128)(2,1)S(1)} %get-tuple-element.141), channel_id=1, source_target_pairs={{0,18},{1,19},{2,16},{3,17},{4,22},{5,23},{6,20},{7,21},{8,26},{9,... | collective-permute-start | bytes 196616 | tf_op jit(solution)/shard_map/ppermute | solution.py:299
  94.6 5.5 %collective-permute-start.22 = (bf16[8,4096]{1,0:T(8,128)(2,1)S(1)}, bf16[8,4096]{1,0:T(8,128)(2,1)S(1)}, u32[]{:S(2)}, u32[]{:S(2)}) collective-permute-start(bf16[8,4096]{1,0:T(8,128)(2,1)S(1)} %get-tuple-element.142), channel_id=1, source_target_pairs={{0,16},{1,17},{2,18},{3,19},{4,20},{5,21},{6,22},{7,23},{8,24},{9,... | collective-permute-start | bytes 196616 | tf_op jit(solution)/shard_map/ppermute | solution.py:299
  95.4 4.7 %collective-permute-start.21 = (bf16[8,5120]{1,0:T(8,128)(2,1)S(1)}, bf16[8,5120]{1,0:T(8,128)(2,1)S(1)}, u32[]{:S(2)}, u32[]{:S(2)}) collective-permute-start(bf16[8,5120]{1,0:T(8,128)(2,1)S(1)} %pad_maximum_fusion.8), channel_id=1, source_target_pairs={{0,2},{1,3},{2,0},{3,1},{4,6},{5,7},{6,4},{7,5},{8,10},{9,11},{10,... | collective-permute-start | bytes 245768 | tf_op jit(solution)/shard_map/ppermute | solution.py:294
  100.3 8.7 %collective-permute-start.26 = (bf16[2,10240]{1,0:T(2,128)(2,1)S(1)}, bf16[2,10240]{1,0:T(2,128)(2,1)S(1)}, u32[]{:S(2)}, u32[]{:S(2)}) collective-permute-start(bf16[2,10240]{1,0:T(2,128)(2,1)S(1)} %get-tuple-element.144), channel_id=1, source_target_pairs={{0,12},{1,13},{2,14},{3,15},{4,8},{5,9},{6,10},{7,11},{8,4},{9,5},... | collective-permute-start | bytes 122888 | tf_op jit(solution)/shard_map/ppermute | solution.py:294
  100.9 8.1 %collective-permute-start.25 = (bf16[2,10240]{1,0:T(2,128)(2,1)S(1)}, bf16[2,10240]{1,0:T(2,128)(2,1)S(1)}, u32[]{:S(2)}, u32[]{:S(2)}) collective-permute-start(bf16[2,10240]{1,0:T(2,128)(2,1)S(1)} %get-tuple-element.145), channel_id=1, source_target_pairs={{0,8},{1,9},{2,10},{3,11},{4,12},{5,13},{6,14},{7,15},{8,0},{9,1},... | collective-permute-start | bytes 122888 | tf_op jit(solution)/shard_map/ppermute | solution.py:294
  101.9 7.1 %collective-permute-start.24 = (bf16[2,10240]{1,0:T(2,128)(2,1)S(1)}, bf16[2,10240]{1,0:T(2,128)(2,1)S(1)}, u32[]{:S(2)}, u32[]{:S(2)}) collective-permute-start(bf16[2,10240]{1,0:T(2,128)(2,1)S(1)} %get-tuple-element.146), channel_id=1, source_target_pairs={{0,4},{1,5},{2,6},{3,7},{4,0},{5,1},{6,2},{7,3},{8,12},{9,13},{10,... | collective-permute-start | bytes 122888 | tf_op jit(solution)/shard_map/ppermute | solution.py:294
  104.8 5.3 %copy-start.1 = (bf16[32,1792]{1,0:T(8,128)(2,1)S(1)}, bf16[32,1792]{1,0:T(8,128)(2,1)}, u32[]{:S(2)}) copy-start(bf16[32,1792]{1,0:T(8,128)(2,1)} %param.17) | copy-start | bytes 344068

commit v6 on v5

--- a/solution.py
+++ b/solution.py
@@ -188,11 +188,12 @@
     pu_ref[...] += flipped_product(du, bu)
 
 
-def hidden_gradients(eug, euu, b_gate, b_up, keep, far, hidden_grad, width=256):
+def hidden_gradients(eug, euu, b_gate, b_up, keep, far, hidden_grad, first, width):
     rows, wide = eug.shape
     count = keep.shape[2]
+    start = first // width
     fixed = pl.BlockSpec((rows, wide), lambda k: (0, 0))
-    b_block = pl.BlockSpec((wide, width), lambda k: (0, k))
+    b_block = pl.BlockSpec((wide, width), lambda k: (0, k + start))
     block = pl.BlockSpec((2, rows, width), lambda k: (0, 0, k))
     return pl.pallas_call(
         hidden_kernel,
@@ -204,7 +205,7 @@
             b_block,
             block,
             block,
-            pl.BlockSpec((rows, width), lambda k: (0, k)),
+            pl.BlockSpec((rows, width), lambda k: (0, k + start)),
         ],
         out_specs=[block, fixed, fixed],
         out_shape=[jax.ShapeDtypeStruct((2, rows, count), BF16)]
@@ -230,24 +231,24 @@
     total_rows = rows_ref.shape[1]
     depth = total_rows // pieces
     base = side_ref[0] * (wg_ref.shape[0] // 2) + first
-    copies = []
-    for k in range(pieces):
+    copies = {}
+    for k in range(0, pieces, 2):
         for i, w_ref in enumerate((wg_ref, wu_ref)):
-            source = pl.ds(pl.multiple_of(base + k * depth, depth), depth)
-            copy = pltpu.make_async_copy(
-                w_ref.at[source], rows_ref.at[i, pl.ds(k * depth, depth)], sem.at[i, k]
-            )
-            copy.start()
-            copies.append(copy)
+            for j in (k, k + 1):
+                source = pl.ds(pl.multiple_of(base + j * depth, depth), depth)
+                copies[i, j] = pltpu.make_async_copy(
+                    w_ref.at[source], rows_ref.at[i, pl.ds(j * depth, depth)], sem.at[i, j]
+                )
+                copies[i, j].start()
     q = dg_ref.shape[0] // 4
     step = 2 * depth
     for k in range(0, total_rows, step):
-        at = 2 * (k // depth)
-        for copy in (copies[at], copies[at + 2]):
-            copy.wait()
+        j = k // depth
+        copies[0, j].wait()
+        copies[0, j + 1].wait()
         total = flipped_product(dg_ref[...], rows_ref[0, k : k + step])
-        for copy in (copies[at + 1], copies[at + 3]):
-            copy.wait()
+        copies[1, j].wait()
+        copies[1, j + 1].wait()
         total += flipped_product(du_ref[...], rows_ref[1, k : k + step])
         out = pl.ds(k, step)
         keep_ref[:q, out] = total[:q]
@@ -335,8 +336,8 @@
     rows = 2 * N
     ff = b_gate.shape[1]
 
-    parts = from_far_z([tokens] * 3)
-    line = jnp.concatenate([tokens, *parts], axis=0)
+    line = jnp.concatenate([tokens, along_tensor(tokens, 4)], axis=0)
+    line = jnp.concatenate([line, along_tensor(line, 8)], axis=0)
     mine = lax.dynamic_slice_in_dim(line, group * half, half, 1)
     other = lax.dynamic_slice_in_dim(line, half - group * half, half, 1)
     parts = [along_tensor(mine, X), across_groups(other), across_groups(other, X)]
@@ -364,7 +365,7 @@
 
     blocks = lax.dynamic_slice_in_dim(x, (t % per_half) * feat_rows, feat_rows, 1)
     swapped = across_groups(blocks[rows:])
-    cuts = [ff * c // 7 for c in (0, 1, 3, 5, 7)]
+    cuts = [ff * c // 7 for c in (0, 2, 4, 6, 7)]
 
     def forward(c):
         return forward_products(
@@ -404,17 +405,19 @@
     up_factor_gate = spread(u[:, :R])
     up_factor_up = spread(u[:, R:])
 
-    own, pg, pu = hidden_gradients(
-        up_factor_gate,
-        up_factor_up,
-        b_gate,
-        b_up,
-        jnp.concatenate([keep_0, keep_1, keep_2, keep_3], axis=2),
-        jnp.concatenate([far_a, far_b], axis=2),
-        hidden_grad,
-    )
+    def hidden(keep, far, first, width):
+        return hidden_gradients(
+            up_factor_gate, up_factor_up, b_gate, b_up, keep, far, hidden_grad, first, width
+        )
+
+    keep = jnp.concatenate([keep_0, keep_1, keep_2], axis=2)
+    own_a, pg_a, pu_a = hidden(keep, far_a, 0, 512)
+    far_b, own_a = in_order(far_b, own_a)
+    own_b, pg_b, pu_b = hidden(keep_3, far_b, cuts[3], 256)
+    own = jnp.concatenate([own_a, own_b], axis=2)
     far = across_groups(own)
-    part = jnp.concatenate([select(pg), select(pu)], axis=1)
+    part = jnp.concatenate([select(pg_a + pg_b), select(pu_a + pu_b)], axis=1)
+    part, own = in_order(part, own)
     recv = along_tensor(part, CORE)
     gate_lift_gradient = adapter_scale * rows_product(up_factor_gate, own[0])
     far, recv, gate_lift_gradient = in_order(far, recv, gate_lift_gradient)

time: 110 us -> 108 us (0.982)
  waiting for transfers between devices: 16.7 us -> 14.5 us
    ppermute x19 -> x18, waiting for transfers between devices: 10.7 us -> 8.1 us  [along_tensor(): return lax.ppermute(value, 'tensor', [(i, i ^ mask) for i in range(N)])]
    ppermute x19 -> x18, starting transfers between devices: 19.9 us -> 21.1 us  [along_tensor(): return lax.ppermute(value, 'tensor', [(i, i ^ mask) for i in range(N)])]
    unnamed x18 -> x13, local copies, waits for them, and re-layouts: 2.93 us -> 2.43 us
    pallas_call x1 -> x2, Pallas kernels: 9.09 us -> 9.2 us  [hidden_gradients(): pl.pallas_call(hidden_kernel, grid=(count // width,), in_specs=[fixed, fi...]
  transfers between devices with their start and end apart: 27 -> 26, of which waited for: 11 -> 11; matrix products, arithmetic and copies ran while one was open for 13% -> 13% of each run, Pallas kernels for 28% -> 35%
where the time goes in v6:
time: 108 us
  Pallas kernels  40.4 us (37%)
  starting transfers between devices  30.1 us (28%)
  waiting for transfers between devices  14.5 us (13%)
  matrix products  13.7 us (13%)
  other arithmetic  4.54 us (4%)
  local copies, waits for them, and re-layouts  3.21 us (3%)
  between operations  1.33 us (1%)
    ppermute x18, starting transfers between devices, along_tensor(): return lax.ppermute(value, 'tensor', [(i, i ^ mask) for i in range(N)])  21.1 us
    pallas_call x3, Pallas kernels, backward_products(): pl.pallas_call(functools.partial(backward_kernel, first), in_specs=[pl.Bl...  16.8 us
    pallas_call x4, Pallas kernels, forward_products(): pl.pallas_call(functools.partial(forward_kernel, first), in_specs=[pl.Blo...  14.5 us
    dot_general x4, matrix products, rows_product(): lax.dot_general(left, right, (((0,), (0,)), ((), ())), preferred_element_...  12 us
    pallas_call x2, Pallas kernels, hidden_gradients(): pl.pallas_call(hidden_kernel, grid=(count // width,), in_specs=[fixed, fi...  9.2 us
    ppermute x8, starting transfers between devices, across_groups(): lax.ppermute(value, both, [(i, i ^ (N | mask)) for i in range(2 * N)])  9 us
    ppermute x18, waiting for transfers between devices, along_tensor(): return lax.ppermute(value, 'tensor', [(i, i ^ mask) for i in range(N)])  8.1 us
    ppermute x8, waiting for transfers between devices, across_groups(): lax.ppermute(value, both, [(i, i ^ (N | mask)) for i in range(2 * N)])  6.35 us
  transfers between devices with their start and end apart: 26, of which 11 were waited for; matrix products, arithmetic and copies ran while one was open for 13% of the time, Pallas kernels for 35%

profile of v6, /device:TPU:0, one launch (start us, length us, event | category | flops | bytes accessed | tf_op | source)
XLA Modules:
  0.0 107.8 jit_solution(10443681800919064543)
XLA Ops:
  0.6 3.1 %collective-permute-start = (bf16[2,8192]{1,0:T(2,128)(2,1)}, bf16[2,8192]{1,0:T(2,128)(2,1)S(1)}, u32[]{:S(2)}, u32[]{:S(2)}) collective-permute-start(bf16[2,8192]{1,0:T(2,128)(2,1)} %param.9), channel_id=1, source_target_pairs={{0,4},{1,5},{2,6},{3,7},{4,0},{5,1},{6,2},{7,3},{8,12},{9,13},{10,... | collective-permute-start | bytes 98312 | tf_op jit(solution)/shard_map/ppermute | solution.py:295
  3.7 2.1 %collective-permute-done = bf16[2,8192]{1,0:T(2,128)(2,1)S(1)} collective-permute-done((bf16[2,8192]{1,0:T(2,128)(2,1)}, bf16[2,8192]{1,0:T(2,128)(2,1)S(1)}, u32[]{:S(2)}, u32[]{:S(2)}) %collective-permute-start) | collective-permute-done | bytes 32800 | tf_op jit(solution)/shard_map/ppermute | solution.py:295
  5.8 0.8 pad_maximum_fusion.8
  6.7 3.1 %collective-permute-start.1 = (bf16[4,8192]{1,0:T(4,128)(2,1)S(1)}, bf16[4,8192]{1,0:T(4,128)(2,1)S(1)}, u32[]{:S(2)}, u32[]{:S(2)}) collective-permute-start(bf16[4,8192]{1,0:T(4,128)(2,1)S(1)} %pad_maximum_fusion.8), channel_id=1, source_target_pairs={{0,8},{1,9},{2,10},{3,11},{4,12},{5,13},{6,14},{7,15},{8,0},{9,1},... | collective-permute-start | bytes 196616 | tf_op jit(solution)/shard_map/ppermute | solution.py:295
  9.8 2.2 %collective-permute-done.1 = bf16[4,8192]{1,0:T(4,128)(2,1)S(1)} collective-permute-done((bf16[4,8192]{1,0:T(4,128)(2,1)S(1)}, bf16[4,8192]{1,0:T(4,128)(2,1)S(1)}, u32[]{:S(2)}, u32[]{:S(2)}) %collective-permute-start.1) | collective-permute-done | bytes 65568 | tf_op jit(solution)/shard_map/ppermute | solution.py:295
  12.0 0.9 pad_maximum_fusion.6
  12.9 1.9 %collective-permute-start.2 = (bf16[8,4096]{1,0:T(8,128)(2,1)S(1)}, bf16[8,4096]{1,0:T(8,128)(2,1)S(1)}, u32[]{:S(2)}, u32[]{:S(2)}) collective-permute-start(bf16[8,4096]{1,0:T(8,128)(2,1)S(1)} %get-tuple-element.161), channel_id=1, source_target_pairs={{0,2},{1,3},{2,0},{3,1},{4,6},{5,7},{6,4},{7,5},{8,10},{9,11},{10,... | collective-permute-start | bytes 196616 | tf_op jit(solution)/shard_map/ppermute | solution.py:295
  14.8 1.5 %collective-permute-start.4 = (bf16[8,4096]{1,0:T(8,128)(2,1)S(1)}, bf16[8,4096]{1,0:T(8,128)(2,1)S(1)}, u32[]{:S(2)}, u32[]{:S(2)}) collective-permute-start(bf16[8,4096]{1,0:T(8,128)(2,1)S(1)} %get-tuple-element.162), channel_id=1, source_target_pairs={{0,18},{1,19},{2,16},{3,17},{4,22},{5,23},{6,20},{7,21},{8,26},{9,... | collective-permute-start | bytes 196616 | tf_op jit(solution)/shard_map/ppermute | solution.py:300
  16.5 0.8 collective-permute-done.2
  17.3 2.7 %collective-permute-done.4 = bf16[8,4096]{1,0:T(8,128)(2,1)S(1)} collective-permute-done((bf16[8,4096]{1,0:T(8,128)(2,1)S(1)}, bf16[8,4096]{1,0:T(8,128)(2,1)S(1)}, u32[]{:S(2)}, u32[]{:S(2)}) %collective-permute-start.4) | collective-permute-done | bytes 65568 | tf_op jit(solution)/shard_map/ppermute | solution.py:300
  20.0 0.7 collective-permute-done.3
  20.9 0.8 select_reduce_fusion
  21.7 0.6 collective-permute-done.5
  22.4 0.9 collective-permute-start.6
  23.3 4.0 %forward_products.4 = (f32[2,32,512]{2,1,0:T(8,128)S(1)}, bf16[2,32,512]{2,1,0:T(8,128)(2,1)S(1)}) custom-call(s32[1]{0:T(128)} %bitcast.3.side_ref, bf16[64,4096]{1,0:T(8,128)(2,1)S(1)} %bitcast.56, bf16[8192,1792]{1,0:T(8,128)(2,1)} %wg_ref.13, bf16[8192,1792]{1,0:T(8,128)(2,1)} %wu_ref.13), custom_call_target="tpu_custom_call" | custom-call | flops 536870912 | bytes 12582912 | tf_op jit(solution)/shard_map/forward_products/pallas_call | solution.py:136
  27.7 1.2 %copy-done.2 = f32[512,1024]{1,0:T(8,128)S(1)} copy-done((f32[512,1024]{1,0:T(8,128)S(1)}, f32[512,1024]{1,0:T(8,128)}, u32[]{:S(2)}) %copy-start.2) | copy-done | bytes 2097176
  29.6 0.9 collective-permute-done.7
  30.6 1.2 %collective-permute-start.8 = (f32[32,128]{1,0:T(8,128)S(1)}, f32[32,128]{1,0:T(8,128)S(1)}, u32[]{:S(2)}, u32[]{:S(2)}) collective-permute-start(f32[32,128]{1,0:T(8,128)S(1)} %maximum_add_fusion.1), channel_id=1, source_target_pairs={{0,2},{1,3},{2,0},{3,1},{4,6},{5,7},{6,4},{7,5},{8,10},{9,11},{10,... | collective-permute-start | bytes 49160 | tf_op jit(solution)/shard_map/ppermute | solution.py:295
  31.9 3.8 %forward_products.5 = (f32[2,32,512]{2,1,0:T(8,128)S(1)}, bf16[2,32,512]{2,1,0:T(8,128)(2,1)S(1)}) custom-call(s32[1]{0:T(128)} %bitcast.3.side_ref, bf16[64,4096]{1,0:T(8,128)(2,1)S(1)} %bitcast.58, bf16[8192,1792]{1,0:T(8,128)(2,1)} %wg_ref.13, bf16[8192,1792]{1,0:T(8,128)(2,1)} %wu_ref.13), custom_call_target="tpu_custom_call" | custom-call | flops 536870912 | bytes 12582912 | tf_op jit(solution)/shard_map/forward_products/pallas_call | solution.py:136
  35.7 1.6 %collective-permute-start.9 = (f32[32,128]{1,0:T(8,128)S(1)}, f32[32,128]{1,0:T(8,128)S(1)}, u32[]{:S(2)}, u32[]{:S(2)}) collective-permute-start(f32[32,128]{1,0:T(8,128)S(1)} %maximum_add_fusion.2), channel_id=1, source_target_pairs={{0,4},{1,5},{2,6},{3,7},{4,0},{5,1},{6,2},{7,3},{8,12},{9,13},{10,... | collective-permute-start | bytes 49160 | tf_op jit(solution)/shard_map/ppermute | solution.py:295
  37.4 3.8 %forward_products.6 = (f32[2,32,512]{2,1,0:T(8,128)S(1)}, bf16[2,32,512]{2,1,0:T(8,128)(2,1)S(1)}) custom-call(s32[1]{0:T(128)} %bitcast.3.side_ref, bf16[64,4096]{1,0:T(8,128)(2,1)S(1)} %bitcast.59, bf16[8192,1792]{1,0:T(8,128)(2,1)} %wg_ref.13, bf16[8192,1792]{1,0:T(8,128)(2,1)} %wu_ref.13), custom_call_target="tpu_custom_call" | custom-call | flops 536870912 | bytes 12582912 | tf_op jit(solution)/shard_map/forward_products/pallas_call | solution.py:136
  41.3 3.2 %collective-permute-start.11 = (f32[32,128]{1,0:T(8,128)S(1)}, f32[32,128]{1,0:T(8,128)S(1)}, u32[]{:S(2)}, u32[]{:S(2)}) collective-permute-start(f32[32,128]{1,0:T(8,128)S(1)} %add.222), channel_id=1, source_target_pairs={{0,8},{1,9},{2,10},{3,11},{4,12},{5,13},{6,14},{7,15},{8,0},{9,1},... | collective-permute-start | bytes 49160 | tf_op jit(solution)/shard_map/ppermute | solution.py:295
  44.5 1.4 %collective-permute-start.10 = (bf16[2,32,1536]{2,1,0:T(8,128)(2,1)S(1)}, bf16[2,32,1536]{2,1,0:T(8,128)(2,1)S(1)}, u32[]{:S(2)}, u32[]{:S(2)}) collective-permute-start(bf16[2,32,1536]{2,1,0:T(8,128)(2,1)S(1)} %pad_maximum_fusion.5), channel_id=1, source_target_pairs={{0,16},{1,17},{2,18},{3,19},{4,20},{5,21},{6,22},{7,23},{8,24},{9,... | collective-permute-start | bytes 589832 | tf_op jit(solution)/shard_map/ppermute | solution.py:300
  46.0 2.8 %forward_products.7 = (f32[2,32,256]{2,1,0:T(8,128)S(1)}, bf16[2,32,256]{2,1,0:T(8,128)(2,1)S(1)}) custom-call(s32[1]{0:T(128)} %bitcast.3.side_ref, bf16[64,4096]{1,0:T(8,128)(2,1)S(1)} %bitcast.60, bf16[8192,1792]{1,0:T(8,128)(2,1)} %wg_ref.13, bf16[8192,1792]{1,0:T(8,128)(2,1)} %wu_ref.13), custom_call_target="tpu_custom_call" | custom-call | flops 268435456 | bytes 6291456 | tf_op jit(solution)/shard_map/forward_products/pallas_call | solution.py:136
  48.9 1.9 %collective-permute-done.10.far_ref = bf16[2,32,1536]{2,1,0:T(8,128)(2,1)S(1)} collective-permute-done((bf16[2,32,1536]{2,1,0:T(8,128)(2,1)S(1)}, bf16[2,32,1536]{2,1,0:T(8,128)(2,1)S(1)}, u32[]{:S(2)}, u32[]{:S(2)}) %collective-permute-start.10) | collective-permute-done | bytes 196640 | tf_op jit(solution)/shard_map/ppermute | solution.py:300
  50.8 1.4 %collective-permute-start.12 = (bf16[2,32,256]{2,1,0:T(8,128)(2,1)S(1)}, bf16[2,32,256]{2,1,0:T(8,128)(2,1)S(1)}, u32[]{:S(2)}, u32[]{:S(2)}) collective-permute-start(bf16[2,32,256]{2,1,0:T(8,128)(2,1)S(1)} %get-tuple-element.104), channel_id=1, source_target_pairs={{0,16},{1,17},{2,18},{3,19},{4,20},{5,21},{6,22},{7,23},{8,24},{9,... | collective-permute-start | bytes 98312 | tf_op jit(solution)/shard_map/ppermute | solution.py:300
  52.5 7.0 %hidden_gradients.2 = (bf16[2,32,1536]{2,1,0:T(8,128)(2,1)S(1)}, f32[32,1024]{1,0:T(8,128)S(1)}, f32[32,1024]{1,0:T(8,128)S(1)}) custom-call(bf16[32,1024]{1,0:T(8,128)(2,1)S(1)} %get-tuple-element.199.eug_ref, bf16[32,1024]{1,0:T(8,128)(2,1)S(1)} %get-tuple-element.200.euu_ref, f32[1024,1792]{1,0:T(8,128)} %bg_ref.3, f32[1024,1792]{1,0:T(8,128)} %bu_ref.3, ...), custom_call_target="tpu_custom_call" | custom-call | flops 402653184 | bytes 25165824 | tf_op jit(solution)/shard_map/hidden_gradients/pallas_call | solution.py:198
  59.6 2.2 %hidden_gradients.3 = (bf16[2,32,256]{2,1,0:T(8,128)(2,1)S(1)}, f32[32,1024]{1,0:T(8,128)S(1)}, f32[32,1024]{1,0:T(8,128)S(1)}) custom-call(bf16[32,1024]{1,0:T(8,128)(2,1)S(1)} %get-tuple-element.199.eug_ref, bf16[32,1024]{1,0:T(8,128)(2,1)S(1)} %get-tuple-element.200.euu_ref, f32[1024,1792]{1,0:T(8,128)} %bg_ref.3, f32[1024,1792]{1,0:T(8,128)} %bu_ref.3, ...), custom_call_target="tpu_custom_call" | custom-call | flops 67108864 | bytes 4194304 | tf_op jit(solution)/shard_map/hidden_gradients/pallas_call | solution.py:198
  62.1 0.7 collective-permute-start.13
  62.9 4.2 %convolution_multiply_fusion.1 = f32[1024,1792]{1,0:T(8,128)} fusion(bf16[32,1024]{1,0:T(8,128)(2,1)S(1)} %get-tuple-element.199.eug_ref, bf16[2,32,1792]{2,1,0:T(8,128)(2,1)S(1)} %constant_dynamic-update-slice_fusion), kind=kOutput, calls=%fused_computation.1 | convolution fusion | flops 119275520 | bytes 7520256 | tf_op jit(solution)/shard_map/dot_general | solution.py:39
  67.1 1.1 collective-permute-done.13
  68.3 0.7 collective-permute-start.15
  69.0 4.7 %backward_products.3 = (f32[32,1024]{1,0:T(8,128)S(1)}, bf16[32,1024]{1,0:T(8,128)(2,1)S(1)}) custom-call(s32[1]{0:T(128)} %bitcast.3.side_ref, bf16[64,1792]{1,0:T(8,128)(2,1)S(1)} %get-tuple-element.126.dg_ref, bf16[64,1792]{1,0:T(8,128)(2,1)S(1)} %get-tuple-element.127.du_ref, bf16[8192,1792]{1,0:T(8,128)(2,1)} %wg_ref.13, bf16[8192,1792]{1,0:T(8,128)(2,1)} %wu_ref.13), custom_call_target="tpu_custom_call" | custom-call | flops 469762048 | bytes 11010048 | tf_op jit(solution)/shard_map/backward_products/pallas_call | solution.py:264
  74.1 4.7 %backward_products.4 = (f32[32,1024]{1,0:T(8,128)S(1)}, bf16[32,1024]{1,0:T(8,128)(2,1)S(1)}) custom-call(s32[1]{0:T(128)} %bitcast.3.side_ref, bf16[64,1792]{1,0:T(8,128)(2,1)S(1)} %get-tuple-element.126.dg_ref, bf16[64,1792]{1,0:T(8,128)(2,1)S(1)} %get-tuple-element.127.du_ref, bf16[8192,1792]{1,0:T(8,128)(2,1)} %wg_ref.13, bf16[8192,1792]{1,0:T(8,128)(2,1)} %wu_ref.13), custom_call_target="tpu_custom_call" | custom-call | flops 469762048 | bytes 11010048 | tf_op jit(solution)/shard_map/backward_products/pallas_call | solution.py:264
  78.8 0.4 collective-permute-start.17
  79.2 7.4 %backward_products.5 = (f32[32,2048]{1,0:T(8,128)S(1)}, bf16[32,2048]{1,0:T(8,128)(2,1)S(1)}) custom-call(s32[1]{0:T(128)} %bitcast.3.side_ref, bf16[64,1792]{1,0:T(8,128)(2,1)S(1)} %get-tuple-element.126.dg_ref, bf16[64,1792]{1,0:T(8,128)(2,1)S(1)} %get-tuple-element.127.du_ref, bf16[8192,1792]{1,0:T(8,128)(2,1)} %wg_ref.13, bf16[8192,1792]{1,0:T(8,128)(2,1)} %wu_ref.13), custom_call_target="tpu_custom_call" | custom-call | flops 939524096 | bytes 22020096 | tf_op jit(solution)/shard_map/backward_products/pallas_call | solution.py:264
  87.6 1.1 copy-done.4
  88.6 0.4 fusion.1
  89.2 1.2 %collective-permute-done.19 = bf16[16,512]{1,0:T(8,128)(2,1)S(1)} collective-permute-done((bf16[16,512]{1,0:T(8,128)(2,1)S(1)}, bf16[16,512]{1,0:T(8,128)(2,1)S(1)}, u32[]{:S(2)}, u32[]{:S(2)}) %collective-permute-start.19) | collective-permute-done | bytes 16416 | tf_op jit(solution)/shard_map/ppermute | solution.py:295
  90.4 1.5 %collective-permute-start.22 = (bf16[8,4096]{1,0:T(8,128)(2,1)S(1)}, bf16[8,4096]{1,0:T(8,128)(2,1)S(1)}, u32[]{:S(2)}, u32[]{:S(2)}) collective-permute-start(bf16[8,4096]{1,0:T(8,128)(2,1)S(1)} %get-tuple-element.155), channel_id=1, source_target_pairs={{0,18},{1,19},{2,16},{3,17},{4,22},{5,23},{6,20},{7,21},{8,26},{9,... | collective-permute-start | bytes 196616 | tf_op jit(solution)/shard_map/ppermute | solution.py:300
  91.9 1.4 %collective-permute-start.21 = (bf16[8,4096]{1,0:T(8,128)(2,1)S(1)}, bf16[8,4096]{1,0:T(8,128)(2,1)S(1)}, u32[]{:S(2)}, u32[]{:S(2)}) collective-permute-start(bf16[8,4096]{1,0:T(8,128)(2,1)S(1)} %get-tuple-element.156), channel_id=1, source_target_pairs={{0,16},{1,17},{2,18},{3,19},{4,20},{5,21},{6,22},{7,23},{8,24},{9,... | collective-permute-start | bytes 196616 | tf_op jit(solution)/shard_map/ppermute | solution.py:300
  93.3 0.7 collective-permute-start.20
  94.0 1.8 %convolution_multiply_fusion.2 = f32[512,1024]{1,0:T(8,128)} fusion(bf16[32,512]{1,0:T(8,128)(2,1)S(1)} %dynamic-slice_select_fusion, bf16[32,1024]{1,0:T(8,128)(2,1)S(1)} %concatenate.105, s32[1024]{0:T(1024)S(1)} %add_select_fusion, s32[32]{0:T(128)S(1)} %select_reduce_fusion), kind=kOutput, calls=%fused_computation.2 | convolution fusion | flops 34144256 | bytes 2199680 | tf_op jit(solution)/shard_map/dot_general | solution.py:39
  95.8 1.8 %convolution_multiply_fusion.3 = f32[512,1024]{1,0:T(8,128)} fusion(bf16[32,512]{1,0:T(8,128)(2,1)S(1)} %dynamic-slice_select_fusion, bf16[32,1024]{1,0:T(8,128)(2,1)S(1)} %concatenate.104, s32[1024]{0:T(1024)S(1)} %add_select_fusion, s32[32]{0:T(128)S(1)} %select_reduce_fusion), kind=kOutput, calls=%fused_computation.3 | convolution fusion | flops 34144256 | bytes 2199680 | tf_op jit(solution)/shard_map/dot_general | solution.py:39
  98.0 3.8 %collective-permute-start.25 = (bf16[2,10240]{1,0:T(2,128)(2,1)S(1)}, bf16[2,10240]{1,0:T(2,128)(2,1)S(1)}, u32[]{:S(2)}, u32[]{:S(2)}) collective-permute-start(bf16[2,10240]{1,0:T(2,128)(2,1)S(1)} %get-tuple-element.158), channel_id=1, source_target_pairs={{0,12},{1,13},{2,14},{3,15},{4,8},{5,9},{6,10},{7,11},{8,4},{9,5},... | collective-permute-start | bytes 122888 | tf_op jit(solution)/shard_map/ppermute | solution.py:295
  101.8 0.6 collective-permute-start.23
  102.5 4.2 %convolution_multiply_fusion = f32[1024,1792]{1,0:T(8,128)} fusion(bf16[32,1024]{1,0:T(8,128)(2,1)S(1)} %get-tuple-element.200.euu_ref, bf16[2,32,1792]{2,1,0:T(8,128)(2,1)S(1)} %constant_dynamic-update-slice_fusion), kind=kOutput, calls=%fused_computation | convolution fusion | flops 119275520 | bytes 7520256 | tf_op jit(solution)/shard_map/dot_general | solution.py:39
  107.1 0.7 fusion.19
  (110 shorter events, 4.7 us)
Async XLA Ops:
  0.6 28.7 %copy-start = (bf16[32,1792]{1,0:T(8,128)(2,1)S(1)}, bf16[32,1792]{1,0:T(8,128)(2,1)}, u32[]{:S(2)}) copy-start(bf16[32,1792]{1,0:T(8,128)(2,1)} %param.17) | copy-start | bytes 344068
  0.6 5.2 %collective-permute-start = (bf16[2,8192]{1,0:T(2,128)(2,1)}, bf16[2,8192]{1,0:T(2,128)(2,1)S(1)}, u32[]{:S(2)}, u32[]{:S(2)}) collective-permute-start(bf16[2,8192]{1,0:T(2,128)(2,1)} %param.9), channel_id=1, source_target_pairs={{0,4},{1,5},{2,6},{3,7},{4,0},{5,1},{6,2},{7,3},{8,12},{9,13},{10,... | collective-permute-start | bytes 98312 | tf_op jit(solution)/shard_map/ppermute | solution.py:295
  6.7 5.3 %collective-permute-start.1 = (bf16[4,8192]{1,0:T(4,128)(2,1)S(1)}, bf16[4,8192]{1,0:T(4,128)(2,1)S(1)}, u32[]{:S(2)}, u32[]{:S(2)}) collective-permute-start(bf16[4,8192]{1,0:T(4,128)(2,1)S(1)} %pad_maximum_fusion.8), channel_id=1, source_target_pairs={{0,8},{1,9},{2,10},{3,11},{4,12},{5,13},{6,14},{7,15},{8,0},{9,1},... | collective-permute-start | bytes 196616 | tf_op jit(solution)/shard_map/ppermute | solution.py:295
  12.9 4.3 %collective-permute-start.2 = (bf16[8,4096]{1,0:T(8,128)(2,1)S(1)}, bf16[8,4096]{1,0:T(8,128)(2,1)S(1)}, u32[]{:S(2)}, u32[]{:S(2)}) collective-permute-start(bf16[8,4096]{1,0:T(8,128)(2,1)S(1)} %get-tuple-element.161), channel_id=1, source_target_pairs={{0,2},{1,3},{2,0},{3,1},{4,6},{5,7},{6,4},{7,5},{8,10},{9,11},{10,... | collective-permute-start | bytes 196616 | tf_op jit(solution)/shard_map/ppermute | solution.py:295
  14.8 5.2 %collective-permute-start.4 = (bf16[8,4096]{1,0:T(8,128)(2,1)S(1)}, bf16[8,4096]{1,0:T(8,128)(2,1)S(1)}, u32[]{:S(2)}, u32[]{:S(2)}) collective-permute-start(bf16[8,4096]{1,0:T(8,128)(2,1)S(1)} %get-tuple-element.162), channel_id=1, source_target_pairs={{0,18},{1,19},{2,16},{3,17},{4,22},{5,23},{6,20},{7,21},{8,26},{9,... | collective-permute-start | bytes 196616 | tf_op jit(solution)/shard_map/ppermute | solution.py:300
  16.3 4.4 %collective-permute-start.3 = (bf16[8,4096]{1,0:T(8,128)(2,1)S(1)}, bf16[8,4096]{1,0:T(8,128)(2,1)S(1)}, u32[]{:S(2)}, u32[]{:S(2)}) collective-permute-start(bf16[8,4096]{1,0:T(8,128)(2,1)S(1)} %get-tuple-element.162), channel_id=1, source_target_pairs={{0,16},{1,17},{2,18},{3,19},{4,20},{5,21},{6,22},{7,23},{8,24},{9,... | collective-permute-start | bytes 196616 | tf_op jit(solution)/shard_map/ppermute | solution.py:300
  20.7 1.6 %collective-permute-start.5 = (bf16[2,16,4096]{2,1,0:T(8,128)(2,1)S(1)}, bf16[2,16,4096]{2,1,0:T(8,128)(2,1)S(1)}, u32[]{:S(2)}, u32[]{:S(2)}) collective-permute-start(bf16[2,16,4096]{2,1,0:T(8,128)(2,1)S(1)} %pad_maximum_fusion.3), channel_id=1, source_target_pairs={{0,1},{1,0},{2,3},{3,2},{4,5},{5,4},{6,7},{7,6},{8,9},{9,8},{10,11... | collective-permute-start | bytes 786440 | tf_op jit(solution)/shard_map/ppermute | solution.py:295
  22.4 4.9 %collective-permute-start.6 = (bf16[32,512]{1,0:T(8,128)(2,1)S(1)}, bf16[32,512]{1,0:T(8,128)(2,1)S(1)}, u32[]{:S(2)}, u32[]{:S(2)}) collective-permute-start(bf16[32,512]{1,0:T(8,128)(2,1)S(1)} %dynamic-slice.1), channel_id=1, source_target_pairs={{0,16},{1,17},{2,18},{3,19},{4,20},{5,21},{6,22},{7,23},{8,24},{9,... | collective-permute-start | bytes 98312 | tf_op jit(solution)/shard_map/ppermute | solution.py:300
  23.3 4.1 %copy-start.3 = (f32[512,1024]{1,0:T(8,128)S(1)}, f32[512,1024]{1,0:T(8,128)}, u32[]{:S(2)}) copy-start(f32[512,1024]{1,0:T(8,128)} %param.13) | copy-start | bytes 6291460
  27.3 1.6 %copy-start.2 = (f32[512,1024]{1,0:T(8,128)S(1)}, f32[512,1024]{1,0:T(8,128)}, u32[]{:S(2)}) copy-start(f32[512,1024]{1,0:T(8,128)} %param.12) | copy-start | bytes 6291460
  29.3 1.2 %collective-permute-start.7 = (f32[32,128]{1,0:T(8,128)S(1)}, f32[32,128]{1,0:T(8,128)S(1)}, u32[]{:S(2)}, u32[]{:S(2)}) collective-permute-start(f32[32,128]{1,0:T(8,128)S(1)} %pad_maximum_fusion.15), channel_id=1, source_target_pairs={{0,1},{1,0},{2,3},{3,2},{4,5},{5,4},{6,7},{7,6},{8,9},{9,8},{10,11... | collective-permute-start | bytes 49160 | tf_op jit(solution)/shard_map/ppermute | solution.py:295
  30.6 5.1 %collective-permute-start.8 = (f32[32,128]{1,0:T(8,128)S(1)}, f32[32,128]{1,0:T(8,128)S(1)}, u32[]{:S(2)}, u32[]{:S(2)}) collective-permute-start(f32[32,128]{1,0:T(8,128)S(1)} %maximum_add_fusion.1), channel_id=1, source_target_pairs={{0,2},{1,3},{2,0},{3,1},{4,6},{5,7},{6,4},{7,5},{8,10},{9,11},{10,... | collective-permute-start | bytes 49160 | tf_op jit(solution)/shard_map/ppermute | solution.py:295
  35.7 5.5 %collective-permute-start.9 = (f32[32,128]{1,0:T(8,128)S(1)}, f32[32,128]{1,0:T(8,128)S(1)}, u32[]{:S(2)}, u32[]{:S(2)}) collective-permute-start(f32[32,128]{1,0:T(8,128)S(1)} %maximum_add_fusion.2), channel_id=1, source_target_pairs={{0,4},{1,5},{2,6},{3,7},{4,0},{5,1},{6,2},{7,3},{8,12},{9,13},{10,... | collective-permute-start | bytes 49160 | tf_op jit(solution)/shard_map/ppermute | solution.py:295
  41.3 7.6 %collective-permute-start.11 = (f32[32,128]{1,0:T(8,128)S(1)}, f32[32,128]{1,0:T(8,128)S(1)}, u32[]{:S(2)}, u32[]{:S(2)}) collective-permute-start(f32[32,128]{1,0:T(8,128)S(1)} %add.222), channel_id=1, source_target_pairs={{0,8},{1,9},{2,10},{3,11},{4,12},{5,13},{6,14},{7,15},{8,0},{9,1},... | collective-permute-start | bytes 49160 | tf_op jit(solution)/shard_map/ppermute | solution.py:295
  44.5 6.2 %collective-permute-start.10 = (bf16[2,32,1536]{2,1,0:T(8,128)(2,1)S(1)}, bf16[2,32,1536]{2,1,0:T(8,128)(2,1)S(1)}, u32[]{:S(2)}, u32[]{:S(2)}) collective-permute-start(bf16[2,32,1536]{2,1,0:T(8,128)(2,1)S(1)} %pad_maximum_fusion.5), channel_id=1, source_target_pairs={{0,16},{1,17},{2,18},{3,19},{4,20},{5,21},{6,22},{7,23},{8,24},{9,... | collective-permute-start | bytes 589832 | tf_op jit(solution)/shard_map/ppermute | solution.py:300
  50.8 8.7 %collective-permute-start.12 = (bf16[2,32,256]{2,1,0:T(8,128)(2,1)S(1)}, bf16[2,32,256]{2,1,0:T(8,128)(2,1)S(1)}, u32[]{:S(2)}, u32[]{:S(2)}) collective-permute-start(bf16[2,32,256]{2,1,0:T(8,128)(2,1)S(1)} %get-tuple-element.104), channel_id=1, source_target_pairs={{0,16},{1,17},{2,18},{3,19},{4,20},{5,21},{6,22},{7,23},{8,24},{9,... | collective-permute-start | bytes 98312 | tf_op jit(solution)/shard_map/ppermute | solution.py:300
  62.1 6.1 %collective-permute-start.13 = (bf16[2,32,1792]{2,1,0:T(8,128)(2,1)S(1)}, bf16[2,32,1792]{2,1,0:T(8,128)(2,1)S(1)}, u32[]{:S(2)}, u32[]{:S(2)}) collective-permute-start(bf16[2,32,1792]{2,1,0:T(8,128)(2,1)S(1)} %constant_dynamic-update-slice_fusion), channel_id=1, source_target_pairs={{0,16},{1,17},{2,18},{3,19},{4,20},{5,21},{6,22},{7,23},{8,24},{9,... | collective-permute-start | bytes 688136 | tf_op jit(solution)/shard_map/ppermute | solution.py:300
  62.9 4.2 %collective-permute-start.14 = (f32[32,128]{1,0:T(8,128)S(1)}, f32[32,128]{1,0:T(8,128)S(1)}, u32[]{:S(2)}, u32[]{:S(2)}) collective-permute-start(f32[32,128]{1,0:T(8,128)S(1)} %pad_maximum_fusion.18), channel_id=1, source_target_pairs={{0,1},{1,0},{2,3},{3,2},{4,5},{5,4},{6,7},{7,6},{8,9},{9,8},{10,11... | collective-permute-start | bytes 49160 | tf_op jit(solution)/shard_map/ppermute | solution.py:295
  68.3 5.4 %collective-permute-start.15 = (f32[32,128]{1,0:T(8,128)S(1)}, f32[32,128]{1,0:T(8,128)S(1)}, u32[]{:S(2)}, u32[]{:S(2)}) collective-permute-start(f32[32,128]{1,0:T(8,128)S(1)} %maximum_add_fusion.3), channel_id=1, source_target_pairs={{0,2},{1,3},{2,0},{3,1},{4,6},{5,7},{6,4},{7,5},{8,10},{9,11},{10,... | collective-permute-start | bytes 49160 | tf_op jit(solution)/shard_map/ppermute | solution.py:295
  73.7 5.0 %collective-permute-start.16 = (f32[32,128]{1,0:T(8,128)S(1)}, f32[32,128]{1,0:T(8,128)S(1)}, u32[]{:S(2)}, u32[]{:S(2)}) collective-permute-start(f32[32,128]{1,0:T(8,128)S(1)} %maximum_add_fusion.4), channel_id=1, source_target_pairs={{0,4},{1,5},{2,6},{3,7},{4,0},{5,1},{6,2},{7,3},{8,12},{9,13},{10,... | collective-permute-start | bytes 49160 | tf_op jit(solution)/shard_map/ppermute | solution.py:295
  78.8 7.9 %collective-permute-start.17 = (f32[32,128]{1,0:T(8,128)S(1)}, f32[32,128]{1,0:T(8,128)S(1)}, u32[]{:S(2)}, u32[]{:S(2)}) collective-permute-start(f32[32,128]{1,0:T(8,128)S(1)} %add.244), channel_id=1, source_target_pairs={{0,8},{1,9},{2,10},{3,11},{4,12},{5,13},{6,14},{7,15},{8,0},{9,1},... | collective-permute-start | bytes 49160 | tf_op jit(solution)/shard_map/ppermute | solution.py:295
  87.0 1.6 %copy-start.4 = (f32[512,1024]{1,0:T(8,128)S(1)}, f32[512,1024]{1,0:T(8,128)}, u32[]{:S(2)}) copy-start(f32[512,1024]{1,0:T(8,128)} %param.13) | copy-start | bytes 6291460
  87.5 2.8 %collective-permute-start.18 = (bf16[32,4096]{1,0:T(8,128)(2,1)S(1)}, bf16[32,4096]{1,0:T(8,128)(2,1)S(1)}, u32[]{:S(2)}, u32[]{:S(2)}) collective-permute-start(bf16[32,4096]{1,0:T(8,128)(2,1)S(1)} %pad_maximum_fusion.4), channel_id=1, source_target_pairs={{0,1},{1,0},{2,3},{3,2},{4,5},{5,4},{6,7},{7,6},{8,9},{9,8},{10,11... | collective-permute-start | bytes 786440 | tf_op jit(solution)/shard_map/ppermute | solution.py:295
  89.1 1.2 %collective-permute-start.19 = (bf16[16,512]{1,0:T(8,128)(2,1)S(1)}, bf16[16,512]{1,0:T(8,128)(2,1)S(1)}, u32[]{:S(2)}, u32[]{:S(2)}) collective-permute-start(bf16[16,512]{1,0:T(8,128)(2,1)S(1)} %get-tuple-element.168), channel_id=1, source_target_pairs={{0,1},{1,0},{2,3},{3,2},{4,5},{5,4},{6,7},{7,6},{8,9},{9,8},{10,11... | collective-permute-start | bytes 49160 | tf_op jit(solution)/shard_map/ppermute | solution.py:295
  90.4 7.2 %collective-permute-start.22 = (bf16[8,4096]{1,0:T(8,128)(2,1)S(1)}, bf16[8,4096]{1,0:T(8,128)(2,1)S(1)}, u32[]{:S(2)}, u32[]{:S(2)}) collective-permute-start(bf16[8,4096]{1,0:T(8,128)(2,1)S(1)} %get-tuple-element.155), channel_id=1, source_target_pairs={{0,18},{1,19},{2,16},{3,17},{4,22},{5,23},{6,20},{7,21},{8,26},{9,... | collective-permute-start | bytes 196616 | tf_op jit(solution)/shard_map/ppermute | solution.py:300
  91.9 5.7 %collective-permute-start.21 = (bf16[8,4096]{1,0:T(8,128)(2,1)S(1)}, bf16[8,4096]{1,0:T(8,128)(2,1)S(1)}, u32[]{:S(2)}, u32[]{:S(2)}) collective-permute-start(bf16[8,4096]{1,0:T(8,128)(2,1)S(1)} %get-tuple-element.156), channel_id=1, source_target_pairs={{0,16},{1,17},{2,18},{3,19},{4,20},{5,21},{6,22},{7,23},{8,24},{9,... | collective-permute-start | bytes 196616 | tf_op jit(solution)/shard_map/ppermute | solution.py:300
  93.3 4.5 %collective-permute-start.20 = (bf16[8,5120]{1,0:T(8,128)(2,1)S(1)}, bf16[8,5120]{1,0:T(8,128)(2,1)S(1)}, u32[]{:S(2)}, u32[]{:S(2)}) collective-permute-start(bf16[8,5120]{1,0:T(8,128)(2,1)S(1)} %pad_maximum_fusion.7), channel_id=1, source_target_pairs={{0,2},{1,3},{2,0},{3,1},{4,6},{5,7},{6,4},{7,5},{8,10},{9,11},{10,... | collective-permute-start | bytes 245768 | tf_op jit(solution)/shard_map/ppermute | solution.py:295
  98.0 8.7 %collective-permute-start.25 = (bf16[2,10240]{1,0:T(2,128)(2,1)S(1)}, bf16[2,10240]{1,0:T(2,128)(2,1)S(1)}, u32[]{:S(2)}, u32[]{:S(2)}) collective-permute-start(bf16[2,10240]{1,0:T(2,128)(2,1)S(1)} %get-tuple-element.158), channel_id=1, source_target_pairs={{0,12},{1,13},{2,14},{3,15},{4,8},{5,9},{6,10},{7,11},{8,4},{9,5},... | collective-permute-start | bytes 122888 | tf_op jit(solution)/shard_map/ppermute | solution.py:295
  101.8 4.9 %collective-permute-start.24 = (bf16[2,10240]{1,0:T(2,128)(2,1)S(1)}, bf16[2,10240]{1,0:T(2,128)(2,1)S(1)}, u32[]{:S(2)}, u32[]{:S(2)}) collective-permute-start(bf16[2,10240]{1,0:T(2,128)(2,1)S(1)} %get-tuple-element.159), channel_id=1, source_target_pairs={{0,8},{1,9},{2,10},{3,11},{4,12},{5,13},{6,14},{7,15},{8,0},{9,1},... | collective-permute-start | bytes 122888 | tf_op jit(solution)/shard_map/ppermute | solution.py:295
  101.8 4.9 %collective-permute-start.23 = (bf16[2,10240]{1,0:T(2,128)(2,1)S(1)}, bf16[2,10240]{1,0:T(2,128)(2,1)S(1)}, u32[]{:S(2)}, u32[]{:S(2)}) collective-permute-start(bf16[2,10240]{1,0:T(2,128)(2,1)S(1)} %get-tuple-element.160), channel_id=1, source_target_pairs={{0,4},{1,5},{2,6},{3,7},{4,0},{5,1},{6,2},{7,3},{8,12},{9,13},{10,... | collective-permute-start | bytes 122888 | tf_op jit(solution)/shard_map/ppermute | solution.py:295
  102.5 5.3 %copy-start.1 = (bf16[32,1792]{1,0:T(8,128)(2,1)S(1)}, bf16[32,1792]{1,0:T(8,128)(2,1)}, u32[]{:S(2)}) copy-start(bf16[32,1792]{1,0:T(8,128)(2,1)} %param.17) | copy-start | bytes 344068

commit v7 on v6

--- a/solution.py
+++ b/solution.py
@@ -104,70 +104,138 @@
     )
 
 
-def forward_kernel(first, side_ref, x_ref, wg_ref, wu_ref, keep_ref, send_ref, piece, sem):
-    pieces, depth, count = piece.shape[1:]
+def columns_copies(side_ref, first, w_refs, out_ref, sem):
+    depth, count = out_ref.shape[1:]
+    source = pl.ds(pl.multiple_of(side_ref[0] * depth, depth), depth)
+    return [
+        pltpu.make_async_copy(w_ref.at[source, pl.ds(first, count)], out_ref.at[i], sem.at[i])
+        for i, w_ref in enumerate(w_refs)
+    ]
+
+
+def rows_copies(side_ref, first, w_refs, out_ref, sem):
+    count = out_ref.shape[1]
+    start = side_ref[0] * (w_refs[0].shape[0] // 2) + first
+    source = pl.ds(pl.multiple_of(start, 16), count)
+    return [
+        pltpu.make_async_copy(w_ref.at[source], out_ref.at[i], sem.at[i])
+        for i, w_ref in enumerate(w_refs)
+    ]
+
+
+VMEM = pl.BlockSpec(memory_space=pltpu.VMEM)
+HBM = pl.BlockSpec(memory_space=pltpu.HBM)
+SMEM = pl.BlockSpec(memory_space=pltpu.SMEM)
+ANYWHERE = pl.BlockSpec(memory_space=pl.ANY)
+PAIR = pltpu.SemaphoreType.DMA((2,))
+
+
+def weights_in_hbm(side, gate_weight, up_weight):
+    return (
+        side,
+        pltpu.with_memory_space_constraint(gate_weight, pltpu.HBM),
+        pltpu.with_memory_space_constraint(up_weight, pltpu.HBM),
+    )
+
+
+def cost(products, bytes_moved):
+    return pl.CostEstimate(flops=2 * products, bytes_accessed=bytes_moved, transcendentals=0)
+
+
+def first_kernel(side_ref, wg_ref, wu_ref, next_ref, sem):
+    copies = columns_copies(side_ref, 0, (wg_ref, wu_ref), next_ref, sem)
+    for copy in copies:
+        copy.start()
+    for copy in copies:
+        copy.wait()
+
+
+def first_columns(weights, count):
+    depth = weights[1].shape[0] // 2
+    return pl.pallas_call(
+        first_kernel,
+        in_specs=[SMEM, HBM, HBM],
+        out_specs=ANYWHERE,
+        out_shape=pltpu.VMEM((2, depth, count), BF16),
+        scratch_shapes=[PAIR],
+        compiler_params=pltpu.CompilerParams(vmem_limit_bytes=2 << 20),
+        cost_estimate=cost(0, 4 * depth * count),
+        name="first_columns",
+    )(*weights)
+
+
+def forward_kernel(after, side_ref, x_ref, w_ref, wg_ref, wu_ref, keep_ref, send_ref, *rest):
+    copies = columns_copies(side_ref, after, (wg_ref, wu_ref), *rest) if rest else []
+    for copy in copies:
+        copy.start()
     half = keep_ref.shape[1]
-    base = side_ref[0] * (pieces * depth)
-    copies = []
-    for i, w_ref in enumerate((wg_ref, wu_ref)):
-        for k in range(pieces):
-            source = pl.ds(pl.multiple_of(base + k * depth, depth), depth)
-            copy = pltpu.make_async_copy(
-                w_ref.at[source, pl.ds(first, count)], piece.at[i, k], sem.at[i, k]
-            )
-            copy.start()
-            copies.append(copy)
     for i in range(2):
-        total = None
-        for k in range(pieces):
-            copies[i * pieces + k].wait()
-            term = jnp.dot(
-                x_ref[:, k * depth : (k + 1) * depth], piece[i, k], preferred_element_type=F32
-            )
-            total = term if total is None else total + term
+        total = jnp.dot(x_ref[...], w_ref[i], preferred_element_type=F32)
         keep_ref[i] = total[:half]
         send_ref[i] = total[half:].astype(send_ref.dtype)
-
-
-def forward_products(side, x, gate_weight, up_weight, first, count, pieces=4):
+    for copy in copies:
+        copy.wait()
+
+
+def forward_products(weights, x, w, after, count_after):
     rows, depth = x.shape
-    vmem = pl.BlockSpec(memory_space=pltpu.VMEM)
-    hbm = pl.BlockSpec(memory_space=pltpu.HBM)
+    count = w.shape[2]
+    side, gate_weight, up_weight = weights
+    follow = count_after > 0
     return pl.pallas_call(
-        functools.partial(forward_kernel, first),
-        in_specs=[pl.BlockSpec(memory_space=pltpu.SMEM), vmem, hbm, hbm],
-        out_specs=[vmem] * 2,
+        functools.partial(forward_kernel, after),
+        in_specs=[SMEM, VMEM, VMEM, HBM, HBM],
+        out_specs=[VMEM] * 2 + [ANYWHERE] * follow,
         out_shape=[
             jax.ShapeDtypeStruct((2, rows // 2, count), F32),
             jax.ShapeDtypeStruct((2, rows // 2, count), BF16),
-        ],
-        scratch_shapes=[
-            pltpu.VMEM((2, pieces, depth // pieces, count), BF16),
-            pltpu.SemaphoreType.DMA((2, pieces)),
-        ],
-        compiler_params=pltpu.CompilerParams(vmem_limit_bytes=20 << 20),
-        cost_estimate=pl.CostEstimate(
-            flops=4 * rows * count * depth, bytes_accessed=6 * count * depth, transcendentals=0
-        ),
+        ]
+        + [pltpu.VMEM((2, depth, count_after), BF16)] * follow,
+        scratch_shapes=[PAIR] * follow,
+        compiler_params=pltpu.CompilerParams(vmem_limit_bytes=8 << 20),
+        cost_estimate=cost(2 * rows * count * depth, 6 * count * depth),
         name="forward_products",
+    )(side, x, w, gate_weight, up_weight)
+
+
+def narrow_kernel(g_ref, u_ref, g16_ref, u16_ref):
+    g16_ref[...] = g_ref[...].astype(BF16)
+    u16_ref[...] = u_ref[...].astype(BF16)
+
+
+def narrow(gate, up, depth):
+    rows, width = gate.shape
+    block = pl.BlockSpec((depth, width), lambda k: (k, 0))
+    return pl.pallas_call(
+        narrow_kernel,
+        grid=(rows // depth,),
+        in_specs=[block] * 2,
+        out_specs=[block] * 2,
+        out_shape=[jax.ShapeDtypeStruct(gate.shape, BF16)] * 2,
+        compiler_params=pltpu.CompilerParams(vmem_limit_bytes=16 << 20),
+        cost_estimate=cost(0, 12 * rows * width),
+        name="narrow",
     )(
-        side,
-        x,
-        pltpu.with_memory_space_constraint(gate_weight, pltpu.HBM),
-        pltpu.with_memory_space_constraint(up_weight, pltpu.HBM),
+        pltpu.with_memory_space_constraint(gate, pltpu.HBM),
+        pltpu.with_memory_space_constraint(up, pltpu.HBM),
     )
 
 
 def hidden_kernel(
-    eug_ref, euu_ref, bg_ref, bu_ref, keep_ref, far_ref, dh_ref, d_ref, pg_ref, pu_ref
+    side_ref, wg_ref, wu_ref, eug_ref, euu_ref, bg_ref, bu_ref, keep_ref, far_ref, dh_ref, d_ref,
+    pg_ref, pu_ref, *rest
 ):
+    def copies():
+        return rows_copies(side_ref, 0, (wg_ref, wu_ref), *rest) if rest else []
+
     @pl.when(pl.program_id(0) == 0)
     def _():
+        for copy in copies():
+            copy.start()
         pg_ref[...] = jnp.zeros_like(pg_ref)
         pu_ref[...] = jnp.zeros_like(pu_ref)
 
-    bg = bg_ref[...].astype(BF16)
-    bu = bu_ref[...].astype(BF16)
+    bg, bu = bg_ref[...], bu_ref[...]
     gate = (
         keep_ref[0]
         + far_ref[0].astype(F32)
@@ -187,11 +255,17 @@
     pg_ref[...] += flipped_product(dg, bg)
     pu_ref[...] += flipped_product(du, bu)
 
-
-def hidden_gradients(eug, euu, b_gate, b_up, keep, far, hidden_grad, first, width):
+    @pl.when(pl.program_id(0) == pl.num_programs(0) - 1)
+    def _():
+        for copy in copies():
+            copy.wait()
+
+
+def hidden_gradients(weights, eug, euu, b_gate, b_up, keep, far, hidden_grad, first, width, count_after):
     rows, wide = eug.shape
     count = keep.shape[2]
     start = first // width
+    follow = count_after > 0
     fixed = pl.BlockSpec((rows, wide), lambda k: (0, 0))
     b_block = pl.BlockSpec((wide, width), lambda k: (0, k + start))
     block = pl.BlockSpec((2, rows, width), lambda k: (0, 0, k))
@@ -199,6 +273,9 @@
         hidden_kernel,
         grid=(count // width,),
         in_specs=[
+            SMEM,
+            HBM,
+            HBM,
             fixed,
             fixed,
             b_block,
@@ -207,84 +284,56 @@
             block,
             pl.BlockSpec((rows, width), lambda k: (0, k + start)),
         ],
-        out_specs=[block, fixed, fixed],
+        out_specs=[block, fixed, fixed] + [ANYWHERE] * follow,
         out_shape=[jax.ShapeDtypeStruct((2, rows, count), BF16)]
-        + [jax.ShapeDtypeStruct((rows, wide), F32)] * 2,
-        compiler_params=pltpu.CompilerParams(vmem_limit_bytes=20 << 20),
-        cost_estimate=pl.CostEstimate(
-            flops=8 * rows * wide * count, bytes_accessed=16 * wide * count, transcendentals=0
-        ),
+        + [jax.ShapeDtypeStruct((rows, wide), F32)] * 2
+        + [pltpu.VMEM((2, count_after, weights[1].shape[1]), BF16)] * follow,
+        scratch_shapes=[PAIR] * follow,
+        compiler_params=pltpu.CompilerParams(vmem_limit_bytes=12 << 20),
+        cost_estimate=cost(4 * rows * wide * count, 12 * wide * count),
         name="hidden_gradients",
-    )(
-        eug,
-        euu,
-        pltpu.with_memory_space_constraint(b_gate, pltpu.HBM),
-        pltpu.with_memory_space_constraint(b_up, pltpu.HBM),
-        keep,
-        far,
-        hidden_grad,
-    )
-
-
-def backward_kernel(first, side_ref, dg_ref, du_ref, wg_ref, wu_ref, keep_ref, send_ref, rows_ref, sem):
-    pieces = sem.shape[1]
-    total_rows = rows_ref.shape[1]
-    depth = total_rows // pieces
-    base = side_ref[0] * (wg_ref.shape[0] // 2) + first
-    copies = {}
-    for k in range(0, pieces, 2):
-        for i, w_ref in enumerate((wg_ref, wu_ref)):
-            for j in (k, k + 1):
-                source = pl.ds(pl.multiple_of(base + j * depth, depth), depth)
-                copies[i, j] = pltpu.make_async_copy(
-                    w_ref.at[source], rows_ref.at[i, pl.ds(j * depth, depth)], sem.at[i, j]
-                )
-                copies[i, j].start()
+    )(*weights, eug, euu, b_gate, b_up, keep, far, hidden_grad)
+
+
+def backward_kernel(
+    after, side_ref, dg_ref, du_ref, w_ref, wg_ref, wu_ref, keep_ref, send_ref, *rest
+):
+    copies = rows_copies(side_ref, after, (wg_ref, wu_ref), *rest) if rest else []
+    for copy in copies:
+        copy.start()
     q = dg_ref.shape[0] // 4
-    step = 2 * depth
-    for k in range(0, total_rows, step):
-        j = k // depth
-        copies[0, j].wait()
-        copies[0, j + 1].wait()
-        total = flipped_product(dg_ref[...], rows_ref[0, k : k + step])
-        copies[1, j].wait()
-        copies[1, j + 1].wait()
-        total += flipped_product(du_ref[...], rows_ref[1, k : k + step])
+    step = 512
+    for k in range(0, w_ref.shape[1], step):
+        total = flipped_product(dg_ref[...], w_ref[0, k : k + step])
+        total += flipped_product(du_ref[...], w_ref[1, k : k + step])
         out = pl.ds(k, step)
         keep_ref[:q, out] = total[:q]
         keep_ref[q:, out] = total[2 * q : 3 * q]
         send_ref[:q, out] = total[q : 2 * q].astype(send_ref.dtype)
         send_ref[q:, out] = total[3 * q :].astype(send_ref.dtype)
-
-
-def backward_products(side, dg, du, gate_weight, up_weight, first, count, depth=256):
+    for copy in copies:
+        copy.wait()
+
+
+def backward_products(weights, dg, du, w, after, count_after):
     rows, ff = dg.shape
-    vmem = pl.BlockSpec(memory_space=pltpu.VMEM)
-    hbm = pl.BlockSpec(memory_space=pltpu.HBM)
+    count = w.shape[1]
+    side, gate_weight, up_weight = weights
+    follow = count_after > 0
     return pl.pallas_call(
-        functools.partial(backward_kernel, first),
-        in_specs=[pl.BlockSpec(memory_space=pltpu.SMEM), vmem, vmem, hbm, hbm],
-        out_specs=[vmem] * 2,
+        functools.partial(backward_kernel, after),
+        in_specs=[SMEM, VMEM, VMEM, VMEM, HBM, HBM],
+        out_specs=[VMEM] * 2 + [ANYWHERE] * follow,
         out_shape=[
             jax.ShapeDtypeStruct((rows // 2, count), F32),
             jax.ShapeDtypeStruct((rows // 2, count), BF16),
-        ],
-        scratch_shapes=[
-            pltpu.VMEM((2, count, ff), BF16),
-            pltpu.SemaphoreType.DMA((2, count // depth)),
-        ],
-        compiler_params=pltpu.CompilerParams(vmem_limit_bytes=28 << 20),
-        cost_estimate=pl.CostEstimate(
-            flops=4 * rows * count * ff, bytes_accessed=6 * count * ff, transcendentals=0
-        ),
+        ]
+        + [pltpu.VMEM((2, count_after, ff), BF16)] * follow,
+        scratch_shapes=[PAIR] * follow,
+        compiler_params=pltpu.CompilerParams(vmem_limit_bytes=8 << 20),
+        cost_estimate=cost(2 * rows * count * ff, 6 * count * ff),
         name="backward_products",
-    )(
-        side,
-        dg,
-        du,
-        pltpu.with_memory_space_constraint(gate_weight, pltpu.HBM),
-        pltpu.with_memory_space_constraint(up_weight, pltpu.HBM),
-    )
+    )(side, dg, du, w, gate_weight, up_weight)
 
 
 N = 16
@@ -336,11 +385,22 @@
     rows = 2 * N
     ff = b_gate.shape[1]
 
-    line = jnp.concatenate([tokens, along_tensor(tokens, 4)], axis=0)
-    line = jnp.concatenate([line, along_tensor(line, 8)], axis=0)
+    weights = weights_in_hbm(side, gate_weight, up_weight)
+    cuts = [ff * c // 7 for c in (0, 2, 4, 6, 7)]
+
+    recv = along_tensor(tokens, 4)
+    a_gate, a_up = narrow(a_gate, a_up, feat_rows // 2)
+    recv, a_gate, a_up = in_order(recv, a_gate, a_up)
+    line = jnp.concatenate([tokens, recv], axis=0)
+    recv = along_tensor(line, 8)
+    w = first_columns(weights, cuts[1])
+    recv, w = in_order(recv, w)
+    line = jnp.concatenate([line, recv], axis=0)
     mine = lax.dynamic_slice_in_dim(line, group * half, half, 1)
     other = lax.dynamic_slice_in_dim(line, half - group * half, half, 1)
     parts = [along_tensor(mine, X), across_groups(other), across_groups(other, X)]
+    b_gate, b_up = narrow(b_gate, b_up, b_gate.shape[0] // 8)
+    b_gate, b_up, *parts = in_order(b_gate, b_up, *parts)
     x = jnp.stack(
         [jnp.concatenate([mine, parts[0]], axis=0), jnp.concatenate([parts[1], parts[2]], axis=0)]
     )
@@ -365,20 +425,17 @@
 
     blocks = lax.dynamic_slice_in_dim(x, (t % per_half) * feat_rows, feat_rows, 1)
     swapped = across_groups(blocks[rows:])
-    cuts = [ff * c // 7 for c in (0, 2, 4, 6, 7)]
-
-    def forward(c):
-        return forward_products(
-            side, x, gate_weight, up_weight, cuts[c], cuts[c + 1] - cuts[c]
-        )
-
-    keep_0, send_0 = forward(0)
+    def forward(c, w):
+        after = cuts[c + 1]
+        return forward_products(weights, x, w, after, (cuts + cuts[-1:])[c + 2] - after)
+
+    keep_0, send_0, w = forward(0, w)
     swapped, x, keep_0, send_0 = in_order(swapped, x, keep_0, send_0)
     own_cols = jnp.where(t // per_half == group, blocks[:rows], swapped)
     part = jnp.concatenate(
         [
-            select(jnp.dot(own_cols, a_gate.astype(BF16), preferred_element_type=F32)),
-            select(jnp.dot(own_cols, a_up.astype(BF16), preferred_element_type=F32)),
+            select(jnp.dot(own_cols, a_gate, preferred_element_type=F32)),
+            select(jnp.dot(own_cols, a_up, preferred_element_type=F32)),
         ],
         axis=1,
     )
@@ -386,18 +443,18 @@
     part = add_core(part, along_tensor(part, CORE))
     part, x = in_order(part, x)
     recv = along_tensor(part, X)
-    keep_1, send_1 = forward(1)
+    keep_1, send_1, w = forward(1, w)
     recv, x, keep_1, send_1 = in_order(recv, x, keep_1, send_1)
     part = add_x(part, recv)
 
     recv = along_tensor(part, 4)
-    keep_2, send_2 = forward(2)
+    keep_2, send_2, w = forward(2, w)
     recv, x, keep_2, send_2 = in_order(recv, x, keep_2, send_2)
     part = add_z(part, recv, 1)
 
     recv = along_tensor(part, 8)
     far_a = across_groups(jnp.concatenate([send_0, send_1, send_2], axis=2))
-    keep_3, send_3 = forward(3)
+    keep_3, send_3 = forward(3, w)
     far_a, recv, keep_3, send_3 = in_order(far_a, recv, keep_3, send_3)
     far_b = across_groups(send_3)
     part = add_z(part, recv, 2)
@@ -405,15 +462,27 @@
     up_factor_gate = spread(u[:, :R])
     up_factor_up = spread(u[:, R:])
 
-    def hidden(keep, far, first, width):
+    steps = [half * c // 8 for c in (0, 2, 5, 8)]
+
+    def hidden(keep, far, first, width, count_after):
         return hidden_gradients(
-            up_factor_gate, up_factor_up, b_gate, b_up, keep, far, hidden_grad, first, width
+            weights,
+            up_factor_gate,
+            up_factor_up,
+            b_gate,
+            b_up,
+            keep,
+            far,
+            hidden_grad,
+            first,
+            width,
+            count_after,
         )
 
     keep = jnp.concatenate([keep_0, keep_1, keep_2], axis=2)
-    own_a, pg_a, pu_a = hidden(keep, far_a, 0, 512)
+    own_a, pg_a, pu_a = hidden(keep, far_a, 0, 512, 0)
     far_b, own_a = in_order(far_b, own_a)
-    own_b, pg_b, pu_b = hidden(keep_3, far_b, cuts[3], 256)
+    own_b, pg_b, pu_b, w = hidden(keep_3, far_b, cuts[3], 256, steps[1])
     own = jnp.concatenate([own_a, own_b], axis=2)
     far = across_groups(own)
     part = jnp.concatenate([select(pg_a + pg_b), select(pu_a + pu_b)], axis=1)
@@ -425,23 +494,22 @@
     both = jnp.concatenate([own, far], axis=1)
     dg, du = both[0], both[1]
 
-    count = half // 4
-
-    def backward(c, n):
-        return backward_products(side, dg, du, gate_weight, up_weight, c * count, n * count)
+    def backward(c, w):
+        after = steps[c + 1]
+        return backward_products(weights, dg, du, w, after, (steps + steps[-1:])[c + 2] - after)
 
     recv = along_tensor(part, X)
-    keep_0, send_0 = backward(0, 1)
+    keep_0, send_0, w = backward(0, w)
     recv, dg, du, keep_0, send_0 = in_order(recv, dg, du, keep_0, send_0)
     part = add_x(part, recv)
 
     recv = along_tensor(part, 4)
-    keep_1, send_1 = backward(1, 1)
+    keep_1, send_1, w = backward(1, w)
     recv, dg, du, keep_1, send_1 = in_order(recv, dg, du, keep_1, send_1)
     part = add_z(part, recv, 1)
 
     recv = along_tensor(part, 8)
-    keep_2, send_2 = backward(2, 2)
+    keep_2, send_2 = backward(2, w)
     recv, keep_2, send_2, own, own_cols = in_order(recv, keep_2, send_2, own, own_cols)
     part = add_z(part, recv, 2)
     far = along_tensor(jnp.concatenate([send_0, send_1, send_2], axis=1), CORE)
@@ -451,8 +519,8 @@
     moved = (
         adapter_scale
         * (
-            flipped_product(gate_factor_gate, a_gate.astype(BF16))
-            + flipped_product(gate_factor_up, a_up.astype(BF16))
+            flipped_product(gate_factor_gate, a_gate)
+            + flipped_product(gate_factor_up, a_up)
         )
     ).astype(BF16)
 

time: 108 us -> 124 us (1.15)
  local copies, waits for them, and re-layouts: 3.21 us -> 15.3 us
  Pallas kernels: 40.4 us -> 51.9 us
  waiting for transfers between devices: 14.5 us -> 10.3 us
  starting transfers between devices: 30.1 us -> 27.5 us
  other arithmetic: 4.54 us -> 3.21 us
    unnamed x13 -> x35, local copies, waits for them, and re-layouts: 2.43 us -> 14.6 us
    pallas_call x9 -> x12, Pallas kernels: 40.4 us -> 51.9 us  [the longest x3 17.1 us: backward_products(): pl.pallas_call(functools.partial(backward_kernel, after), in_specs=[SMEM,...]
    ppermute x8, waiting for transfers between devices: 6.35 us -> 1.16 us  [across_groups(): lax.ppermute(value, both, [(i, i ^ (N | mask)) for i in range(2 * N)])]
    ppermute x18, starting transfers between devices: 21.1 us -> 19.3 us  [along_tensor(): return lax.ppermute(value, 'tensor', [(i, i ^ mask) for i in range(N)])]
  transfers between devices with their start and end apart: 26 -> 26, of which waited for: 11 -> 9; matrix products, arithmetic and copies ran while one was open for 13% -> 11% of each run, Pallas kernels for 35% -> 39%
where the time goes in v7:
time: 124 us; the launch traced here: 123 us
  Pallas kernels  51.9 us (42%)
  starting transfers between devices  27.5 us (22%)
  local copies, waits for them, and re-layouts  15.3 us (12%)
  matrix products  13.7 us (11%)
  waiting for transfers between devices  10.3 us (8%)
  other arithmetic  3.21 us (3%)
  between operations  1.39 us (1%)
    ppermute x18, starting transfers between devices, along_tensor(): return lax.ppermute(value, 'tensor', [(i, i ^ mask) for i in range(N)])  19.3 us
    pallas_call x3, Pallas kernels, backward_products(): pl.pallas_call(functools.partial(backward_kernel, after), in_specs=[SMEM,...  17.1 us
    unnamed x35, local copies, waits for them, and re-layouts  14.6 us
    pallas_call x4, Pallas kernels, forward_products(): pl.pallas_call(functools.partial(forward_kernel, after), in_specs=[SMEM,...  14.2 us
    dot_general x4, matrix products, rows_product(): lax.dot_general(left, right, (((0,), (0,)), ((), ())), preferred_element_...  12 us
    pallas_call x2, Pallas kernels, narrow(): pl.pallas_call(narrow_kernel, grid=(rows // depth,), in_specs=[block] * 2...  9.41 us
    ppermute x18, waiting for transfers between devices, along_tensor(): return lax.ppermute(value, 'tensor', [(i, i ^ mask) for i in range(N)])  9.1 us
    ppermute x8, starting transfers between devices, across_groups(): lax.ppermute(value, both, [(i, i ^ (N | mask)) for i in range(2 * N)])  8.27 us
  transfers between devices with their start and end apart: 26, of which 9 were waited for; matrix products, arithmetic and copies ran while one was open for 11% of the time, Pallas kernels for 39%

profile of v7, /device:TPU:0, one launch (start us, length us, event | category | flops | bytes accessed | tf_op | source)
XLA Modules:
  0.0 123.4 jit_solution(5933106151635732960)
XLA Ops:
  0.6 3.1 %collective-permute-start = (bf16[2,8192]{1,0:T(2,128)(2,1)}, bf16[2,8192]{1,0:T(2,128)(2,1)S(1)}, u32[]{:S(2)}, u32[]{:S(2)}) collective-permute-start(bf16[2,8192]{1,0:T(2,128)(2,1)} %param.9), channel_id=1, source_target_pairs={{0,4},{1,5},{2,6},{3,7},{4,0},{5,1},{6,2},{7,3},{8,12},{9,13},{10,... | collective-permute-start | bytes 98312 | tf_op jit(solution)/shard_map/ppermute | solution.py:344
  3.7 2.3 %narrow.2 = (bf16[512,1024]{1,0:T(8,128)(2,1)S(1)}, bf16[512,1024]{1,0:T(8,128)(2,1)S(1)}) custom-call(f32[512,1024]{1,0:T(8,128)} %g_ref.2, f32[512,1024]{1,0:T(8,128)} %u_ref.2), custom_call_target="tpu_custom_call" | custom-call | bytes 6291456 | tf_op jit(solution)/shard_map/narrow/pallas_call | solution.py:209
  6.1 0.9 pad_maximum_fusion.8
  6.9 2.9 %collective-permute-start.1 = (bf16[4,8192]{1,0:T(4,128)(2,1)S(1)}, bf16[4,8192]{1,0:T(4,128)(2,1)S(1)}, u32[]{:S(2)}, u32[]{:S(2)}) collective-permute-start(bf16[4,8192]{1,0:T(4,128)(2,1)S(1)} %pad_maximum_fusion.8), channel_id=1, source_target_pairs={{0,8},{1,9},{2,10},{3,11},{4,12},{5,13},{6,14},{7,15},{8,0},{9,1},... | collective-permute-start | bytes 196616 | tf_op jit(solution)/shard_map/ppermute | solution.py:344
  9.8 3.6 %first_columns.1.w_ref = bf16[2,4096,512]{2,1,0:T(8,128)(2,1)S(1)} custom-call(s32[1]{0:T(128)} %bitcast.side_ref, bf16[8192,1792]{1,0:T(8,128)(2,1)} %wg_ref.19, bf16[8192,1792]{1,0:T(8,128)(2,1)} %wu_ref.19), custom_call_target="tpu_custom_call" | custom-call | bytes 8388608 | tf_op jit(solution)/shard_map/first_columns/pallas_call | solution.py:155
  13.4 3.3 %copy-done.2 = bf16[2,4096,512]{2,1,0:T(8,128)(2,1)} copy-done((bf16[2,4096,512]{2,1,0:T(8,128)(2,1)}, bf16[2,4096,512]{2,1,0:T(8,128)(2,1)S(1)}, u32[]{:S(2)}) %copy-start.2) | copy-done | bytes 8388632
  16.9 1.6 %collective-permute-start.2 = (bf16[8,4096]{1,0:T(8,128)(2,1)S(1)}, bf16[8,4096]{1,0:T(8,128)(2,1)S(1)}, u32[]{:S(2)}, u32[]{:S(2)}) collective-permute-start(bf16[8,4096]{1,0:T(8,128)(2,1)S(1)} %get-tuple-element.202), channel_id=1, source_target_pairs={{0,2},{1,3},{2,0},{3,1},{4,6},{5,7},{6,4},{7,5},{8,10},{9,11},{10,... | collective-permute-start | bytes 196616 | tf_op jit(solution)/shard_map/ppermute | solution.py:344
  18.4 1.4 %collective-permute-start.3 = (bf16[8,4096]{1,0:T(8,128)(2,1)S(1)}, bf16[8,4096]{1,0:T(8,128)(2,1)S(1)}, u32[]{:S(2)}, u32[]{:S(2)}) collective-permute-start(bf16[8,4096]{1,0:T(8,128)(2,1)S(1)} %get-tuple-element.201), channel_id=1, source_target_pairs={{0,16},{1,17},{2,18},{3,19},{4,20},{5,21},{6,22},{7,23},{8,24},{9,... | collective-permute-start | bytes 196616 | tf_op jit(solution)/shard_map/ppermute | solution.py:349
  20.4 7.1 %narrow.3 = (bf16[1024,1792]{1,0:T(8,128)(2,1)S(1)}, bf16[1024,1792]{1,0:T(8,128)(2,1)S(1)}) custom-call(f32[1024,1792]{1,0:T(8,128)} %g_ref.3, f32[1024,1792]{1,0:T(8,128)} %u_ref.3), custom_call_target="tpu_custom_call" | custom-call | bytes 22020096 | tf_op jit(solution)/shard_map/narrow/pallas_call | solution.py:209
  27.6 1.8 %copy-done.4 = bf16[1024,1792]{1,0:T(8,128)(2,1)} copy-done((bf16[1024,1792]{1,0:T(8,128)(2,1)}, bf16[1024,1792]{1,0:T(8,128)(2,1)S(1)}, u32[]{:S(2)}) %copy-start.4) | copy-done | bytes 3670040
  29.4 1.8 %copy-done.6 = bf16[1024,1792]{1,0:T(8,128)(2,1)} copy-done((bf16[1024,1792]{1,0:T(8,128)(2,1)}, bf16[1024,1792]{1,0:T(8,128)(2,1)S(1)}, u32[]{:S(2)}) %copy-start.6) | copy-done | bytes 3670040
  31.6 1.3 %collective-permute-done.5 = bf16[2,16,4096]{2,1,0:T(8,128)(2,1)S(1)} collective-permute-done((bf16[2,16,4096]{2,1,0:T(8,128)(2,1)S(1)}, bf16[2,16,4096]{2,1,0:T(8,128)(2,1)S(1)}, u32[]{:S(2)}, u32[]{:S(2)}) %collective-permute-start.5) | collective-permute-done | bytes 262176 | tf_op jit(solution)/shard_map/ppermute | solution.py:344
  33.0 1.5 %collective-permute-start.6 = (bf16[32,512]{1,0:T(8,128)(2,1)S(1)}, bf16[32,512]{1,0:T(8,128)(2,1)S(1)}, u32[]{:S(2)}, u32[]{:S(2)}) collective-permute-start(bf16[32,512]{1,0:T(8,128)(2,1)S(1)} %dynamic-slice.1), channel_id=1, source_target_pairs={{0,16},{1,17},{2,18},{3,19},{4,20},{5,21},{6,22},{7,23},{8,24},{9,... | collective-permute-start | bytes 98312 | tf_op jit(solution)/shard_map/ppermute | solution.py:349
  34.5 3.4 %copy-done.3 = bf16[2,4096,512]{2,1,0:T(8,128)(2,1)S(1)} copy-done((bf16[2,4096,512]{2,1,0:T(8,128)(2,1)S(1)}, bf16[2,4096,512]{2,1,0:T(8,128)(2,1)}, u32[]{:S(2)}) %copy-start.3) | copy-done | bytes 8388632
  37.8 4.9 %forward_products.4 = (f32[2,32,512]{2,1,0:T(8,128)S(1)}, bf16[2,32,512]{2,1,0:T(8,128)(2,1)S(1)}, bf16[2,4096,512]{2,1,0:T(8,128)(2,1)S(1)}) custom-call(s32[1]{0:T(128)} %bitcast.side_ref, bf16[64,4096]{1,0:T(8,128)(2,1)S(1)} %bitcast.60, bf16[2,4096,512]{2,1,0:T(8,128)(2,1)S(1)} %copy-done.3, bf16[8192,1792]{1,0:T(8,128)(2,1)} %wg_ref.19, ...), custom_call_target="tpu_custom_call" | custom-call | flops 536870912 | bytes 12582912 | tf_op jit(solution)/shard_map/forward_products/pallas_call | solution.py:185
  43.9 0.9 collective-permute-done.7
  44.9 1.5 %collective-permute-start.8 = (f32[32,128]{1,0:T(8,128)S(1)}, f32[32,128]{1,0:T(8,128)S(1)}, u32[]{:S(2)}, u32[]{:S(2)}) collective-permute-start(f32[32,128]{1,0:T(8,128)S(1)} %maximum_add_fusion.1), channel_id=1, source_target_pairs={{0,2},{1,3},{2,0},{3,1},{4,6},{5,7},{6,4},{7,5},{8,10},{9,11},{10,... | collective-permute-start | bytes 49160 | tf_op jit(solution)/shard_map/ppermute | solution.py:344
  46.4 4.9 %forward_products.5 = (f32[2,32,512]{2,1,0:T(8,128)S(1)}, bf16[2,32,512]{2,1,0:T(8,128)(2,1)S(1)}, bf16[2,4096,512]{2,1,0:T(8,128)(2,1)S(1)}) custom-call(s32[1]{0:T(128)} %bitcast.side_ref, bf16[64,4096]{1,0:T(8,128)(2,1)S(1)} %bitcast.62, bf16[2,4096,512]{2,1,0:T(8,128)(2,1)S(1)} %get-tuple-element.116.w_ref, bf16[8192,1792]{1,0:T(8,128)(2,1)} %wg_ref.19, ...), custom_call_target="tpu_custom_call" | custom-call | flops 536870912 | bytes 12582912 | tf_op jit(solution)/shard_map/forward_products/pallas_call | solution.py:185
  51.3 1.6 %collective-permute-start.9 = (f32[32,128]{1,0:T(8,128)S(1)}, f32[32,128]{1,0:T(8,128)S(1)}, u32[]{:S(2)}, u32[]{:S(2)}) collective-permute-start(f32[32,128]{1,0:T(8,128)S(1)} %maximum_add_fusion.2), channel_id=1, source_target_pairs={{0,4},{1,5},{2,6},{3,7},{4,0},{5,1},{6,2},{7,3},{8,12},{9,13},{10,... | collective-permute-start | bytes 49160 | tf_op jit(solution)/shard_map/ppermute | solution.py:344
  52.9 3.6 %forward_products.6 = (f32[2,32,512]{2,1,0:T(8,128)S(1)}, bf16[2,32,512]{2,1,0:T(8,128)(2,1)S(1)}, bf16[2,4096,256]{2,1,0:T(8,128)(2,1)S(1)}) custom-call(s32[1]{0:T(128)} %bitcast.side_ref, bf16[64,4096]{1,0:T(8,128)(2,1)S(1)} %bitcast.63, bf16[2,4096,512]{2,1,0:T(8,128)(2,1)S(1)} %get-tuple-element.121.w_ref, bf16[8192,1792]{1,0:T(8,128)(2,1)} %wg_ref.19, ...), custom_call_target="tpu_custom_call" | custom-call | flops 536870912 | bytes 12582912 | tf_op jit(solution)/shard_map/forward_products/pallas_call | solution.py:185
  56.6 0.7 collective-permute-start.10
  57.7 0.8 forward_products.7
  58.6 3.5 %collective-permute-done.11 = f32[32,128]{1,0:T(8,128)S(1)} collective-permute-done((f32[32,128]{1,0:T(8,128)S(1)}, f32[32,128]{1,0:T(8,128)S(1)}, u32[]{:S(2)}, u32[]{:S(2)}) %collective-permute-start.11) | collective-permute-done | bytes 16416 | tf_op jit(solution)/shard_map/ppermute | solution.py:344
  62.1 1.0 collective-permute-done.10.far_ref
  63.4 0.7 collective-permute-start.12
  64.2 2.0 %copy-done.5 = bf16[1024,1792]{1,0:T(8,128)(2,1)S(1)} copy-done((bf16[1024,1792]{1,0:T(8,128)(2,1)S(1)}, bf16[1024,1792]{1,0:T(8,128)(2,1)}, u32[]{:S(2)}) %copy-start.5) | copy-done | bytes 3670040
  66.2 2.0 %copy-done.7 = bf16[1024,1792]{1,0:T(8,128)(2,1)S(1)} copy-done((bf16[1024,1792]{1,0:T(8,128)(2,1)S(1)}, bf16[1024,1792]{1,0:T(8,128)(2,1)}, u32[]{:S(2)}) %copy-start.7) | copy-done | bytes 3670040
  68.3 4.3 %hidden_gradients.2 = (bf16[2,32,1536]{2,1,0:T(8,128)(2,1)S(1)}, f32[32,1024]{1,0:T(8,128)S(1)}, f32[32,1024]{1,0:T(8,128)S(1)}) custom-call(s32[1]{0:T(128)} %bitcast.side_ref, bf16[8192,1792]{1,0:T(8,128)(2,1)} %wg_ref.19, bf16[8192,1792]{1,0:T(8,128)(2,1)} %wu_ref.19, bf16[32,1024]{1,0:T(8,128)(2,1)S(1)} %get-tuple-element.239.eug_ref, ...), custom_call_target="tpu_custom_call" | custom-call | flops 402653184 | bytes 18874368 | tf_op jit(solution)/shard_map/hidden_gradients/pallas_call | solution.py:272
  72.6 3.3 %hidden_gradients.3 = (bf16[2,32,256]{2,1,0:T(8,128)(2,1)S(1)}, f32[32,1024]{1,0:T(8,128)S(1)}, f32[32,1024]{1,0:T(8,128)S(1)}, bf16[2,1024,1792]{2,1,0:T(8,128)(2,1)S(1)}) custom-call(s32[1]{0:T(128)} %bitcast.side_ref, bf16[8192,1792]{1,0:T(8,128)(2,1)} %wg_ref.19, bf16[8192,1792]{1,0:T(8,128)(2,1)} %wu_ref.19, ...), custom_call_target="tpu_custom_call" | custom-call | flops 67108864 | bytes 3145728 | tf_op jit(solution)/shard_map/hidden_gradients/pallas_call | solution.py:272
  76.2 1.4 %collective-permute-start.13 = (bf16[2,32,1792]{2,1,0:T(8,128)(2,1)S(1)}, bf16[2,32,1792]{2,1,0:T(8,128)(2,1)S(1)}, u32[]{:S(2)}, u32[]{:S(2)}) collective-permute-start(bf16[2,32,1792]{2,1,0:T(8,128)(2,1)S(1)} %constant_dynamic-update-slice_fusion), channel_id=1, source_target_pairs={{0,16},{1,17},{2,18},{3,19},{4,20},{5,21},{6,22},{7,23},{8,24},{9,... | collective-permute-start | bytes 688136 | tf_op jit(solution)/shard_map/ppermute | solution.py:349
  77.7 4.2 %convolution_multiply_fusion.1 = f32[1024,1792]{1,0:T(8,128)} fusion(bf16[32,1024]{1,0:T(8,128)(2,1)S(1)} %get-tuple-element.239.eug_ref, bf16[2,32,1792]{2,1,0:T(8,128)(2,1)S(1)} %constant_dynamic-update-slice_fusion), kind=kOutput, calls=%fused_computation.1 | convolution fusion | flops 119275520 | bytes 7520256 | tf_op jit(solution)/shard_map/dot_general | solution.py:39
  81.9 1.2 collective-permute-done.14
  83.2 0.6 collective-permute-start.15
  83.8 6.3 %backward_products.3 = (f32[32,1024]{1,0:T(8,128)S(1)}, bf16[32,1024]{1,0:T(8,128)(2,1)S(1)}, bf16[2,1536,1792]{2,1,0:T(8,128)(2,1)S(1)}) custom-call(s32[1]{0:T(128)} %bitcast.side_ref, bf16[64,1792]{1,0:T(8,128)(2,1)S(1)} %get-tuple-element.165.dg_ref, bf16[64,1792]{1,0:T(8,128)(2,1)S(1)} %get-tuple-element.166.du_ref, ...), custom_call_target="tpu_custom_call" | custom-call | flops 469762048 | bytes 11010048 | tf_op jit(solution)/shard_map/backward_products/pallas_call | solution.py:323
  90.7 7.4 %backward_products.4 = (f32[32,1536]{1,0:T(8,128)S(1)}, bf16[32,1536]{1,0:T(8,128)(2,1)S(1)}, bf16[2,1536,1792]{2,1,0:T(8,128)(2,1)S(1)}) custom-call(s32[1]{0:T(128)} %bitcast.side_ref, bf16[64,1792]{1,0:T(8,128)(2,1)S(1)} %get-tuple-element.165.dg_ref, bf16[64,1792]{1,0:T(8,128)(2,1)S(1)} %get-tuple-element.166.du_ref, ...), custom_call_target="tpu_custom_call" | custom-call | flops 704643072 | bytes 16515072 | tf_op jit(solution)/shard_map/backward_products/pallas_call | solution.py:323
  98.6 3.4 %backward_products.5 = (f32[32,1536]{1,0:T(8,128)S(1)}, bf16[32,1536]{1,0:T(8,128)(2,1)S(1)}) custom-call(s32[1]{0:T(128)} %bitcast.side_ref, bf16[64,1792]{1,0:T(8,128)(2,1)S(1)} %get-tuple-element.165.dg_ref, bf16[64,1792]{1,0:T(8,128)(2,1)S(1)} %get-tuple-element.166.du_ref, bf16[2,1536,1792]{2,1,0:T(8,128)(2,1)S(1)} %get-tuple-element.167.w_ref, ...), custom_call_target="tpu_custom_call" | custom-call | flops 704643072 | bytes 16515072 | tf_op jit(solution)/shard_map/backward_products/pallas_call | solution.py:323
  102.0 0.9 collective-permute-done.17
  104.8 0.8 collective-permute-done.19
  105.7 1.6 %collective-permute-start.20 = (bf16[8,5120]{1,0:T(8,128)(2,1)S(1)}, bf16[8,5120]{1,0:T(8,128)(2,1)S(1)}, u32[]{:S(2)}, u32[]{:S(2)}) collective-permute-start(bf16[8,5120]{1,0:T(8,128)(2,1)S(1)} %pad_maximum_fusion.7), channel_id=1, source_target_pairs={{0,2},{1,3},{2,0},{3,1},{4,6},{5,7},{6,4},{7,5},{8,10},{9,11},{10,... | collective-permute-start | bytes 245768 | tf_op jit(solution)/shard_map/ppermute | solution.py:344
  107.3 0.6 collective-permute-start.21
  107.9 1.4 %collective-permute-start.22 = (bf16[8,4096]{1,0:T(8,128)(2,1)S(1)}, bf16[8,4096]{1,0:T(8,128)(2,1)S(1)}, u32[]{:S(2)}, u32[]{:S(2)}) collective-permute-start(bf16[8,4096]{1,0:T(8,128)(2,1)S(1)} %get-tuple-element.195), channel_id=1, source_target_pairs={{0,18},{1,19},{2,16},{3,17},{4,22},{5,23},{6,20},{7,21},{8,26},{9,... | collective-permute-start | bytes 196616 | tf_op jit(solution)/shard_map/ppermute | solution.py:349
  109.3 1.8 %convolution_multiply_fusion.2 = f32[512,1024]{1,0:T(8,128)} fusion(bf16[32,512]{1,0:T(8,128)(2,1)S(1)} %copy-done.13, bf16[32,1024]{1,0:T(8,128)(2,1)S(1)} %concatenate.105, s32[1024]{0:T(1024)S(1)} %add_select_fusion, s32[32]{0:T(128)S(1)} %select_reduce_fusion), kind=kOutput, calls=%fused_computation.2 | convolution fusion | flops 34144256 | bytes 2199680 | tf_op jit(solution)/shard_map/dot_general | solution.py:39
  111.1 1.8 %convolution_multiply_fusion.3 = f32[512,1024]{1,0:T(8,128)} fusion(bf16[32,512]{1,0:T(8,128)(2,1)S(1)} %copy-done.13, bf16[32,1024]{1,0:T(8,128)(2,1)S(1)} %concatenate.104, s32[1024]{0:T(1024)S(1)} %add_select_fusion, s32[32]{0:T(128)S(1)} %select_reduce_fusion), kind=kOutput, calls=%fused_computation.3 | convolution fusion | flops 34144256 | bytes 2199680 | tf_op jit(solution)/shard_map/dot_general | solution.py:39
  113.2 1.6 %collective-permute-start.23 = (bf16[2,10240]{1,0:T(2,128)(2,1)S(1)}, bf16[2,10240]{1,0:T(2,128)(2,1)S(1)}, u32[]{:S(2)}, u32[]{:S(2)}) collective-permute-start(bf16[2,10240]{1,0:T(2,128)(2,1)S(1)} %get-tuple-element.200), channel_id=1, source_target_pairs={{0,4},{1,5},{2,6},{3,7},{4,0},{5,1},{6,2},{7,3},{8,12},{9,13},{10,... | collective-permute-start | bytes 122888 | tf_op jit(solution)/shard_map/ppermute | solution.py:344
  114.8 1.7 %collective-permute-start.24 = (bf16[2,10240]{1,0:T(2,128)(2,1)S(1)}, bf16[2,10240]{1,0:T(2,128)(2,1)S(1)}, u32[]{:S(2)}, u32[]{:S(2)}) collective-permute-start(bf16[2,10240]{1,0:T(2,128)(2,1)S(1)} %get-tuple-element.199), channel_id=1, source_target_pairs={{0,8},{1,9},{2,10},{3,11},{4,12},{5,13},{6,14},{7,15},{8,0},{9,1},... | collective-permute-start | bytes 122888 | tf_op jit(solution)/shard_map/ppermute | solution.py:344
  116.6 1.1 collective-permute-start.25
  117.7 4.2 %convolution_multiply_fusion = f32[1024,1792]{1,0:T(8,128)} fusion(bf16[32,1024]{1,0:T(8,128)(2,1)S(1)} %get-tuple-element.240.euu_ref, bf16[2,32,1792]{2,1,0:T(8,128)(2,1)S(1)} %constant_dynamic-update-slice_fusion), kind=kOutput, calls=%fused_computation | convolution fusion | flops 119275520 | bytes 7520256 | tf_op jit(solution)/shard_map/dot_general | solution.py:39
  122.7 0.7 fusion.14
  (135 shorter events, 7.6 us)
Async XLA Ops:
  0.6 43.0 %copy-start = (bf16[32,1792]{1,0:T(8,128)(2,1)S(1)}, bf16[32,1792]{1,0:T(8,128)(2,1)}, u32[]{:S(2)}) copy-start(bf16[32,1792]{1,0:T(8,128)(2,1)} %param.17) | copy-start | bytes 344068
  0.6 5.4 %collective-permute-start = (bf16[2,8192]{1,0:T(2,128)(2,1)}, bf16[2,8192]{1,0:T(2,128)(2,1)S(1)}, u32[]{:S(2)}, u32[]{:S(2)}) collective-permute-start(bf16[2,8192]{1,0:T(2,128)(2,1)} %param.9), channel_id=1, source_target_pairs={{0,4},{1,5},{2,6},{3,7},{4,0},{5,1},{6,2},{7,3},{8,12},{9,13},{10,... | collective-permute-start | bytes 98312 | tf_op jit(solution)/shard_map/ppermute | solution.py:344
  6.0 36.7 %copy-start.8 = (bf16[512,1024]{1,0:T(8,128)(2,1)}, bf16[512,1024]{1,0:T(8,128)(2,1)S(1)}, u32[]{:S(2)}) copy-start(bf16[512,1024]{1,0:T(8,128)(2,1)S(1)} %get-tuple-element.111) | copy-start | bytes 3145732
  6.1 37.1 %copy-start.10 = (bf16[512,1024]{1,0:T(8,128)(2,1)}, bf16[512,1024]{1,0:T(8,128)(2,1)S(1)}, u32[]{:S(2)}) copy-start(bf16[512,1024]{1,0:T(8,128)(2,1)S(1)} %get-tuple-element.112) | copy-start | bytes 3145732
  6.9 9.8 %collective-permute-start.1 = (bf16[4,8192]{1,0:T(4,128)(2,1)S(1)}, bf16[4,8192]{1,0:T(4,128)(2,1)S(1)}, u32[]{:S(2)}, u32[]{:S(2)}) collective-permute-start(bf16[4,8192]{1,0:T(4,128)(2,1)S(1)} %pad_maximum_fusion.8), channel_id=1, source_target_pairs={{0,8},{1,9},{2,10},{3,11},{4,12},{5,13},{6,14},{7,15},{8,0},{9,1},... | collective-permute-start | bytes 196616 | tf_op jit(solution)/shard_map/ppermute | solution.py:344
  9.8 6.9 %copy-start.14 = (bf16[2,8192]{1,0:T(2,128)(2,1)S(1)}, bf16[2,8192]{1,0:T(2,128)(2,1)}, u32[]{:S(2)}) copy-start(bf16[2,8192]{1,0:T(2,128)(2,1)} %param.9) | copy-start | bytes 98308
  13.4 3.3 %copy-start.2 = (bf16[2,4096,512]{2,1,0:T(8,128)(2,1)}, bf16[2,4096,512]{2,1,0:T(8,128)(2,1)S(1)}, u32[]{:S(2)}) copy-start(bf16[2,4096,512]{2,1,0:T(8,128)(2,1)S(1)} %first_columns.1.w_ref) | copy-start | bytes 25165828
  16.9 14.4 %collective-permute-start.2 = (bf16[8,4096]{1,0:T(8,128)(2,1)S(1)}, bf16[8,4096]{1,0:T(8,128)(2,1)S(1)}, u32[]{:S(2)}, u32[]{:S(2)}) collective-permute-start(bf16[8,4096]{1,0:T(8,128)(2,1)S(1)} %get-tuple-element.202), channel_id=1, source_target_pairs={{0,2},{1,3},{2,0},{3,1},{4,6},{5,7},{6,4},{7,5},{8,10},{9,11},{10,... | collective-permute-start | bytes 196616 | tf_op jit(solution)/shard_map/ppermute | solution.py:344
  18.4 12.8 %collective-permute-start.3 = (bf16[8,4096]{1,0:T(8,128)(2,1)S(1)}, bf16[8,4096]{1,0:T(8,128)(2,1)S(1)}, u32[]{:S(2)}, u32[]{:S(2)}) collective-permute-start(bf16[8,4096]{1,0:T(8,128)(2,1)S(1)} %get-tuple-element.201), channel_id=1, source_target_pairs={{0,16},{1,17},{2,18},{3,19},{4,20},{5,21},{6,22},{7,23},{8,24},{9,... | collective-permute-start | bytes 196616 | tf_op jit(solution)/shard_map/ppermute | solution.py:349
  19.9 11.4 %collective-permute-start.4 = (bf16[8,4096]{1,0:T(8,128)(2,1)S(1)}, bf16[8,4096]{1,0:T(8,128)(2,1)S(1)}, u32[]{:S(2)}, u32[]{:S(2)}) collective-permute-start(bf16[8,4096]{1,0:T(8,128)(2,1)S(1)} %get-tuple-element.201), channel_id=1, source_target_pairs={{0,18},{1,19},{2,16},{3,17},{4,22},{5,23},{6,20},{7,21},{8,26},{9,... | collective-permute-start | bytes 196616 | tf_op jit(solution)/shard_map/ppermute | solution.py:349
  20.4 11.0 %copy-start.15 = (s32[32]{0:T(128)S(1)}, s32[32]{0:T(128)}, u32[]{:S(2)}) copy-start(s32[32]{0:T(128)} %param.16) | copy-start | bytes 388
  27.5 1.8 %copy-start.4 = (bf16[1024,1792]{1,0:T(8,128)(2,1)}, bf16[1024,1792]{1,0:T(8,128)(2,1)S(1)}, u32[]{:S(2)}) copy-start(bf16[1024,1792]{1,0:T(8,128)(2,1)S(1)} %get-tuple-element.133.bg_ref) | copy-start | bytes 11010052
  29.4 1.8 %copy-start.6 = (bf16[1024,1792]{1,0:T(8,128)(2,1)}, bf16[1024,1792]{1,0:T(8,128)(2,1)S(1)}, u32[]{:S(2)}) copy-start(bf16[1024,1792]{1,0:T(8,128)(2,1)S(1)} %get-tuple-element.134.bu_ref) | copy-start | bytes 11010052
  31.3 1.6 %collective-permute-start.5 = (bf16[2,16,4096]{2,1,0:T(8,128)(2,1)S(1)}, bf16[2,16,4096]{2,1,0:T(8,128)(2,1)S(1)}, u32[]{:S(2)}, u32[]{:S(2)}) collective-permute-start(bf16[2,16,4096]{2,1,0:T(8,128)(2,1)S(1)} %pad_maximum_fusion.3), channel_id=1, source_target_pairs={{0,1},{1,0},{2,3},{3,2},{4,5},{5,4},{6,7},{7,6},{8,9},{9,8},{10,11... | collective-permute-start | bytes 786440 | tf_op jit(solution)/shard_map/ppermute | solution.py:344
  33.0 9.8 %collective-permute-start.6 = (bf16[32,512]{1,0:T(8,128)(2,1)S(1)}, bf16[32,512]{1,0:T(8,128)(2,1)S(1)}, u32[]{:S(2)}, u32[]{:S(2)}) collective-permute-start(bf16[32,512]{1,0:T(8,128)(2,1)S(1)} %dynamic-slice.1), channel_id=1, source_target_pairs={{0,16},{1,17},{2,18},{3,19},{4,20},{5,21},{6,22},{7,23},{8,24},{9,... | collective-permute-start | bytes 98312 | tf_op jit(solution)/shard_map/ppermute | solution.py:349
  34.5 3.4 %copy-start.3 = (bf16[2,4096,512]{2,1,0:T(8,128)(2,1)S(1)}, bf16[2,4096,512]{2,1,0:T(8,128)(2,1)}, u32[]{:S(2)}) copy-start(bf16[2,4096,512]{2,1,0:T(8,128)(2,1)} %copy-done.2) | copy-start | bytes 25165828
  42.8 3.6 %copy-start.12 = (bf16[32,512]{1,0:T(8,128)(2,1)}, bf16[32,512]{1,0:T(8,128)(2,1)S(1)}, u32[]{:S(2)}) copy-start(bf16[32,512]{1,0:T(8,128)(2,1)S(1)} %dynamic-slice_select_fusion) | copy-start | bytes 98308
  43.6 1.2 collective-permute-start.7
  44.9 6.4 %collective-permute-start.8 = (f32[32,128]{1,0:T(8,128)S(1)}, f32[32,128]{1,0:T(8,128)S(1)}, u32[]{:S(2)}, u32[]{:S(2)}) collective-permute-start(f32[32,128]{1,0:T(8,128)S(1)} %maximum_add_fusion.1), channel_id=1, source_target_pairs={{0,2},{1,3},{2,0},{3,1},{4,6},{5,7},{6,4},{7,5},{8,10},{9,11},{10,... | collective-permute-start | bytes 49160 | tf_op jit(solution)/shard_map/ppermute | solution.py:344
  51.3 5.3 %collective-permute-start.9 = (f32[32,128]{1,0:T(8,128)S(1)}, f32[32,128]{1,0:T(8,128)S(1)}, u32[]{:S(2)}, u32[]{:S(2)}) collective-permute-start(f32[32,128]{1,0:T(8,128)S(1)} %maximum_add_fusion.2), channel_id=1, source_target_pairs={{0,4},{1,5},{2,6},{3,7},{4,0},{5,1},{6,2},{7,3},{8,12},{9,13},{10,... | collective-permute-start | bytes 49160 | tf_op jit(solution)/shard_map/ppermute | solution.py:344
  56.6 6.5 %collective-permute-start.10 = (bf16[2,32,1536]{2,1,0:T(8,128)(2,1)S(1)}, bf16[2,32,1536]{2,1,0:T(8,128)(2,1)S(1)}, u32[]{:S(2)}, u32[]{:S(2)}) collective-permute-start(bf16[2,32,1536]{2,1,0:T(8,128)(2,1)S(1)} %pad_maximum_fusion.5), channel_id=1, source_target_pairs={{0,16},{1,17},{2,18},{3,19},{4,20},{5,21},{6,22},{7,23},{8,24},{9,... | collective-permute-start | bytes 589832 | tf_op jit(solution)/shard_map/ppermute | solution.py:349
  57.3 4.8 %collective-permute-start.11 = (f32[32,128]{1,0:T(8,128)S(1)}, f32[32,128]{1,0:T(8,128)S(1)}, u32[]{:S(2)}, u32[]{:S(2)}) collective-permute-start(f32[32,128]{1,0:T(8,128)S(1)} %add.222), channel_id=1, source_target_pairs={{0,8},{1,9},{2,10},{3,11},{4,12},{5,13},{6,14},{7,15},{8,0},{9,1},... | collective-permute-start | bytes 49160 | tf_op jit(solution)/shard_map/ppermute | solution.py:344
  63.4 9.2 %collective-permute-start.12 = (bf16[2,32,256]{2,1,0:T(8,128)(2,1)S(1)}, bf16[2,32,256]{2,1,0:T(8,128)(2,1)S(1)}, u32[]{:S(2)}, u32[]{:S(2)}) collective-permute-start(bf16[2,32,256]{2,1,0:T(8,128)(2,1)S(1)} %get-tuple-element.141), channel_id=1, source_target_pairs={{0,16},{1,17},{2,18},{3,19},{4,20},{5,21},{6,22},{7,23},{8,24},{9,... | collective-permute-start | bytes 98312 | tf_op jit(solution)/shard_map/ppermute | solution.py:349
  64.2 2.0 %copy-start.5 = (bf16[1024,1792]{1,0:T(8,128)(2,1)S(1)}, bf16[1024,1792]{1,0:T(8,128)(2,1)}, u32[]{:S(2)}) copy-start(bf16[1024,1792]{1,0:T(8,128)(2,1)} %copy-done.4) | copy-start | bytes 11010052
  66.2 2.0 %copy-start.7 = (bf16[1024,1792]{1,0:T(8,128)(2,1)S(1)}, bf16[1024,1792]{1,0:T(8,128)(2,1)}, u32[]{:S(2)}) copy-start(bf16[1024,1792]{1,0:T(8,128)(2,1)} %copy-done.6) | copy-start | bytes 11010052
  76.2 6.9 %collective-permute-start.13 = (bf16[2,32,1792]{2,1,0:T(8,128)(2,1)S(1)}, bf16[2,32,1792]{2,1,0:T(8,128)(2,1)S(1)}, u32[]{:S(2)}, u32[]{:S(2)}) collective-permute-start(bf16[2,32,1792]{2,1,0:T(8,128)(2,1)S(1)} %constant_dynamic-update-slice_fusion), channel_id=1, source_target_pairs={{0,16},{1,17},{2,18},{3,19},{4,20},{5,21},{6,22},{7,23},{8,24},{9,... | collective-permute-start | bytes 688136 | tf_op jit(solution)/shard_map/ppermute | solution.py:349
  81.9 1.2 collective-permute-start.14
  83.2 6.9 %collective-permute-start.15 = (f32[32,128]{1,0:T(8,128)S(1)}, f32[32,128]{1,0:T(8,128)S(1)}, u32[]{:S(2)}, u32[]{:S(2)}) collective-permute-start(f32[32,128]{1,0:T(8,128)S(1)} %maximum_add_fusion.3), channel_id=1, source_target_pairs={{0,2},{1,3},{2,0},{3,1},{4,6},{5,7},{6,4},{7,5},{8,10},{9,11},{10,... | collective-permute-start | bytes 49160 | tf_op jit(solution)/shard_map/ppermute | solution.py:344
  90.1 8.0 %collective-permute-start.16 = (f32[32,128]{1,0:T(8,128)S(1)}, f32[32,128]{1,0:T(8,128)S(1)}, u32[]{:S(2)}, u32[]{:S(2)}) collective-permute-start(f32[32,128]{1,0:T(8,128)S(1)} %maximum_add_fusion.4), channel_id=1, source_target_pairs={{0,4},{1,5},{2,6},{3,7},{4,0},{5,1},{6,2},{7,3},{8,12},{9,13},{10,... | collective-permute-start | bytes 49160 | tf_op jit(solution)/shard_map/ppermute | solution.py:344
  98.2 4.7 %collective-permute-start.17 = (f32[32,128]{1,0:T(8,128)S(1)}, f32[32,128]{1,0:T(8,128)S(1)}, u32[]{:S(2)}, u32[]{:S(2)}) collective-permute-start(f32[32,128]{1,0:T(8,128)S(1)} %add.244), channel_id=1, source_target_pairs={{0,8},{1,9},{2,10},{3,11},{4,12},{5,13},{6,14},{7,15},{8,0},{9,1},... | collective-permute-start | bytes 49160 | tf_op jit(solution)/shard_map/ppermute | solution.py:344
  98.6 4.5 %copy-start.11 = (bf16[512,1024]{1,0:T(8,128)(2,1)S(1)}, bf16[512,1024]{1,0:T(8,128)(2,1)}, u32[]{:S(2)}) copy-start(bf16[512,1024]{1,0:T(8,128)(2,1)} %copy-done.10) | copy-start | bytes 3145732
  98.6 5.2 %copy-start.9 = (bf16[512,1024]{1,0:T(8,128)(2,1)S(1)}, bf16[512,1024]{1,0:T(8,128)(2,1)}, u32[]{:S(2)}) copy-start(bf16[512,1024]{1,0:T(8,128)(2,1)} %copy-done.8) | copy-start | bytes 3145732
  98.6 10.7 %copy-start.13 = (bf16[32,512]{1,0:T(8,128)(2,1)S(1)}, bf16[32,512]{1,0:T(8,128)(2,1)}, u32[]{:S(2)}) copy-start(bf16[32,512]{1,0:T(8,128)(2,1)} %copy-done.12) | copy-start | bytes 98308
  103.7 1.9 %collective-permute-start.18 = (bf16[32,4096]{1,0:T(8,128)(2,1)S(1)}, bf16[32,4096]{1,0:T(8,128)(2,1)S(1)}, u32[]{:S(2)}, u32[]{:S(2)}) collective-permute-start(bf16[32,4096]{1,0:T(8,128)(2,1)S(1)} %pad_maximum_fusion.4), channel_id=1, source_target_pairs={{0,1},{1,0},{2,3},{3,2},{4,5},{5,4},{6,7},{7,6},{8,9},{9,8},{10,11... | collective-permute-start | bytes 786440 | tf_op jit(solution)/shard_map/ppermute | solution.py:344
  104.2 1.4 %collective-permute-start.19 = (bf16[16,512]{1,0:T(8,128)(2,1)S(1)}, bf16[16,512]{1,0:T(8,128)(2,1)S(1)}, u32[]{:S(2)}, u32[]{:S(2)}) collective-permute-start(bf16[16,512]{1,0:T(8,128)(2,1)S(1)} %get-tuple-element.208), channel_id=1, source_target_pairs={{0,1},{1,0},{2,3},{3,2},{4,5},{5,4},{6,7},{7,6},{8,9},{9,8},{10,11... | collective-permute-start | bytes 49160 | tf_op jit(solution)/shard_map/ppermute | solution.py:344
  105.7 7.3 %collective-permute-start.20 = (bf16[8,5120]{1,0:T(8,128)(2,1)S(1)}, bf16[8,5120]{1,0:T(8,128)(2,1)S(1)}, u32[]{:S(2)}, u32[]{:S(2)}) collective-permute-start(bf16[8,5120]{1,0:T(8,128)(2,1)S(1)} %pad_maximum_fusion.7), channel_id=1, source_target_pairs={{0,2},{1,3},{2,0},{3,1},{4,6},{5,7},{6,4},{7,5},{8,10},{9,11},{10,... | collective-permute-start | bytes 245768 | tf_op jit(solution)/shard_map/ppermute | solution.py:344
  107.3 5.6 %collective-permute-start.21 = (bf16[8,4096]{1,0:T(8,128)(2,1)S(1)}, bf16[8,4096]{1,0:T(8,128)(2,1)S(1)}, u32[]{:S(2)}, u32[]{:S(2)}) collective-permute-start(bf16[8,4096]{1,0:T(8,128)(2,1)S(1)} %get-tuple-element.196), channel_id=1, source_target_pairs={{0,16},{1,17},{2,18},{3,19},{4,20},{5,21},{6,22},{7,23},{8,24},{9,... | collective-permute-start | bytes 196616 | tf_op jit(solution)/shard_map/ppermute | solution.py:349
  107.9 5.2 %collective-permute-start.22 = (bf16[8,4096]{1,0:T(8,128)(2,1)S(1)}, bf16[8,4096]{1,0:T(8,128)(2,1)S(1)}, u32[]{:S(2)}, u32[]{:S(2)}) collective-permute-start(bf16[8,4096]{1,0:T(8,128)(2,1)S(1)} %get-tuple-element.195), channel_id=1, source_target_pairs={{0,18},{1,19},{2,16},{3,17},{4,22},{5,23},{6,20},{7,21},{8,26},{9,... | collective-permute-start | bytes 196616 | tf_op jit(solution)/shard_map/ppermute | solution.py:349
  113.1 10.3 %copy-start.1 = (bf16[32,1792]{1,0:T(8,128)(2,1)S(1)}, bf16[32,1792]{1,0:T(8,128)(2,1)}, u32[]{:S(2)}) copy-start(bf16[32,1792]{1,0:T(8,128)(2,1)} %param.17) | copy-start | bytes 344068
  113.2 8.7 %collective-permute-start.23 = (bf16[2,10240]{1,0:T(2,128)(2,1)S(1)}, bf16[2,10240]{1,0:T(2,128)(2,1)S(1)}, u32[]{:S(2)}, u32[]{:S(2)}) collective-permute-start(bf16[2,10240]{1,0:T(2,128)(2,1)S(1)} %get-tuple-element.200), channel_id=1, source_target_pairs={{0,4},{1,5},{2,6},{3,7},{4,0},{5,1},{6,2},{7,3},{8,12},{9,13},{10,... | collective-permute-start | bytes 122888 | tf_op jit(solution)/shard_map/ppermute | solution.py:344
  114.8 7.1 %collective-permute-start.24 = (bf16[2,10240]{1,0:T(2,128)(2,1)S(1)}, bf16[2,10240]{1,0:T(2,128)(2,1)S(1)}, u32[]{:S(2)}, u32[]{:S(2)}) collective-permute-start(bf16[2,10240]{1,0:T(2,128)(2,1)S(1)} %get-tuple-element.199), channel_id=1, source_target_pairs={{0,8},{1,9},{2,10},{3,11},{4,12},{5,13},{6,14},{7,15},{8,0},{9,1},... | collective-permute-start | bytes 122888 | tf_op jit(solution)/shard_map/ppermute | solution.py:344
  116.6 5.8 %collective-permute-start.25 = (bf16[2,10240]{1,0:T(2,128)(2,1)S(1)}, bf16[2,10240]{1,0:T(2,128)(2,1)S(1)}, u32[]{:S(2)}, u32[]{:S(2)}) collective-permute-start(bf16[2,10240]{1,0:T(2,128)(2,1)S(1)} %get-tuple-element.198), channel_id=1, source_target_pairs={{0,12},{1,13},{2,14},{3,15},{4,8},{5,9},{6,10},{7,11},{8,4},{9,5},... | collective-permute-start | bytes 122888 | tf_op jit(solution)/shard_map/ppermute | solution.py:344

commit v8 on v7

--- a/solution.py
+++ b/solution.py
@@ -104,98 +104,145 @@
     )
 
 
-def columns_copies(side_ref, first, w_refs, out_ref, sem):
-    depth, count = out_ref.shape[1:]
-    source = pl.ds(pl.multiple_of(side_ref[0] * depth, depth), depth)
-    return [
-        pltpu.make_async_copy(w_ref.at[source, pl.ds(first, count)], out_ref.at[i], sem.at[i])
-        for i, w_ref in enumerate(w_refs)
-    ]
-
-
-def rows_copies(side_ref, first, w_refs, out_ref, sem):
-    count = out_ref.shape[1]
-    start = side_ref[0] * (w_refs[0].shape[0] // 2) + first
-    source = pl.ds(pl.multiple_of(start, 16), count)
-    return [
-        pltpu.make_async_copy(w_ref.at[source], out_ref.at[i], sem.at[i])
-        for i, w_ref in enumerate(w_refs)
-    ]
-
-
 VMEM = pl.BlockSpec(memory_space=pltpu.VMEM)
 HBM = pl.BlockSpec(memory_space=pltpu.HBM)
 SMEM = pl.BlockSpec(memory_space=pltpu.SMEM)
 ANYWHERE = pl.BlockSpec(memory_space=pl.ANY)
-PAIR = pltpu.SemaphoreType.DMA((2,))
-
-
-def weights_in_hbm(side, gate_weight, up_weight):
-    return (
-        side,
-        pltpu.with_memory_space_constraint(gate_weight, pltpu.HBM),
-        pltpu.with_memory_space_constraint(up_weight, pltpu.HBM),
-    )
-
-
-def cost(products, bytes_moved):
-    return pl.CostEstimate(flops=2 * products, bytes_accessed=bytes_moved, transcendentals=0)
-
-
-def first_kernel(side_ref, wg_ref, wu_ref, next_ref, sem):
-    copies = columns_copies(side_ref, 0, (wg_ref, wu_ref), next_ref, sem)
-    for copy in copies:
-        copy.start()
-    for copy in copies:
-        copy.wait()
-
-
-def first_columns(weights, count):
-    depth = weights[1].shape[0] // 2
+PIECES = 16
+
+
+class Chunk:
+    def __init__(self, arrays, first_row, rows, first_column, columns, per_side=0):
+        self.arrays = [pltpu.with_memory_space_constraint(a, pltpu.HBM) for a in arrays]
+        self.first_row, self.rows, self.per_side = first_row, rows, per_side
+        self.first_column, self.columns = first_column, columns
+        self.out = pltpu.VMEM((2, rows, columns), arrays[0].dtype)
+
+    def copies(self, side_ref, refs, out_ref, sem):
+        depth = self.rows // PIECES
+        base = side_ref[0] * self.per_side + self.first_row
+        columns = pl.ds(self.first_column, self.columns)
+        return [
+            pltpu.make_async_copy(
+                ref.at[pl.ds(pl.multiple_of(base + k * depth, 16), depth), columns],
+                out_ref.at[i, pl.ds(k * depth, depth)],
+                sem.at[i, k],
+            )
+            for i, ref in enumerate(refs)
+            for k in range(PIECES)
+        ]
+
+
+def run(name, kernel, side, operands, out_shape, chunk, products=0):
+    n_in, n_out = len(operands), len(out_shape)
+    follow = chunk is not None
+
+    def body(side_ref, *refs):
+        values, rest = refs[:n_in], refs[n_in:]
+        if follow:
+            outs = rest[2 : 2 + n_out]
+            copies = chunk.copies(side_ref, rest[:2], *rest[2 + n_out :])
+        else:
+            outs, copies = rest, []
+        for copy in copies:
+            copy.start()
+        kernel(*values, *outs)
+        for copy in copies:
+            copy.wait()
+
+    moved = 4 * chunk.rows * chunk.columns if follow else 0
     return pl.pallas_call(
-        first_kernel,
-        in_specs=[SMEM, HBM, HBM],
-        out_specs=ANYWHERE,
-        out_shape=pltpu.VMEM((2, depth, count), BF16),
-        scratch_shapes=[PAIR],
-        compiler_params=pltpu.CompilerParams(vmem_limit_bytes=2 << 20),
-        cost_estimate=cost(0, 4 * depth * count),
-        name="first_columns",
-    )(*weights)
-
-
-def forward_kernel(after, side_ref, x_ref, w_ref, wg_ref, wu_ref, keep_ref, send_ref, *rest):
-    copies = columns_copies(side_ref, after, (wg_ref, wu_ref), *rest) if rest else []
-    for copy in copies:
-        copy.start()
+        body,
+        in_specs=[SMEM] + [VMEM] * n_in + [HBM] * (2 * follow),
+        out_specs=[VMEM] * n_out + [ANYWHERE] * follow,
+        out_shape=out_shape + ([chunk.out] if follow else []),
+        scratch_shapes=[pltpu.SemaphoreType.DMA((2, PIECES))] * follow,
+        compiler_params=pltpu.CompilerParams(vmem_limit_bytes=8 << 20),
+        cost_estimate=pl.CostEstimate(
+            flops=2 * products, bytes_accessed=max(moved, products // 20), transcendentals=0
+        ),
+        name=name,
+    )(side, *operands, *(chunk.arrays if follow else []))
+
+
+def first_kernel():
+    pass
+
+
+def forward_kernel(x_ref, w_ref, keep_ref, send_ref):
     half = keep_ref.shape[1]
     for i in range(2):
         total = jnp.dot(x_ref[...], w_ref[i], preferred_element_type=F32)
         keep_ref[i] = total[:half]
         send_ref[i] = total[half:].astype(send_ref.dtype)
-    for copy in copies:
-        copy.wait()
-
-
-def forward_products(weights, x, w, after, count_after):
+
+
+def forward_products(side, x, w, chunk):
     rows, depth = x.shape
     count = w.shape[2]
-    side, gate_weight, up_weight = weights
-    follow = count_after > 0
-    return pl.pallas_call(
-        functools.partial(forward_kernel, after),
-        in_specs=[SMEM, VMEM, VMEM, HBM, HBM],
-        out_specs=[VMEM] * 2 + [ANYWHERE] * follow,
-        out_shape=[
-            jax.ShapeDtypeStruct((2, rows // 2, count), F32),
-            jax.ShapeDtypeStruct((2, rows // 2, count), BF16),
-        ]
-        + [pltpu.VMEM((2, depth, count_after), BF16)] * follow,
-        scratch_shapes=[PAIR] * follow,
-        compiler_params=pltpu.CompilerParams(vmem_limit_bytes=8 << 20),
-        cost_estimate=cost(2 * rows * count * depth, 6 * count * depth),
-        name="forward_products",
-    )(side, x, w, gate_weight, up_weight)
+    out_shape = [jax.ShapeDtypeStruct((2, rows // 2, count), kind) for kind in (F32, BF16)]
+    products = 2 * rows * depth * count
+    return run("forward_products", forward_kernel, side, (x, w), out_shape, chunk, products)
+
+
+def hidden_kernel(eug_ref, euu_ref, b_ref, keep_ref, far_ref, dh_ref, d_ref, pg_ref, pu_ref):
+    count = keep_ref.shape[2]
+    step = 512 if count % 512 == 0 else 256
+    sums = None
+    for start in range(0, count, step):
+        at = pl.ds(start, step)
+        bg = b_ref[0, :, at].astype(BF16)
+        bu = b_ref[1, :, at].astype(BF16)
+        gate = (
+            keep_ref[0, :, at]
+            + far_ref[0, :, at].astype(F32)
+            + adapter_scale * jnp.dot(eug_ref[...], bg, preferred_element_type=F32)
+        )
+        up = (
+            keep_ref[1, :, at]
+            + far_ref[1, :, at].astype(F32)
+            + adapter_scale * jnp.dot(euu_ref[...], bu, preferred_element_type=F32)
+        )
+        sig = jax.nn.sigmoid(gate)
+        hidden_grad = dh_ref[:, at]
+        dg = (hidden_grad * up * sig * (1.0 + gate * (1.0 - sig))).astype(BF16)
+        du = (hidden_grad * gate * sig).astype(BF16)
+        d_ref[0, :, at] = dg
+        d_ref[1, :, at] = du
+        terms = flipped_product(dg, bg), flipped_product(du, bu)
+        sums = terms if sums is None else (sums[0] + terms[0], sums[1] + terms[1])
+    pg_ref[...], pu_ref[...] = sums
+
+
+def hidden_gradients(side, eug, euu, b, keep, far, hidden_grad, chunk):
+    rows, wide = eug.shape
+    count = keep.shape[2]
+    out_shape = [jax.ShapeDtypeStruct((2, rows, count), BF16)]
+    out_shape += [jax.ShapeDtypeStruct((rows, wide), F32)] * 2
+    operands = (eug, euu, b, keep, far, hidden_grad)
+    products = 4 * rows * wide * count
+    return run("hidden_gradients", hidden_kernel, side, operands, out_shape, chunk, products)
+
+
+def backward_kernel(dg_ref, du_ref, w_ref, keep_ref, send_ref):
+    q = dg_ref.shape[0] // 4
+    step = 512
+    for k in range(0, w_ref.shape[1], step):
+        total = flipped_product(dg_ref[...], w_ref[0, k : k + step])
+        total += flipped_product(du_ref[...], w_ref[1, k : k + step])
+        out = pl.ds(k, step)
+        keep_ref[:q, out] = total[:q]
+        keep_ref[q:, out] = total[2 * q : 3 * q]
+        send_ref[:q, out] = total[q : 2 * q].astype(send_ref.dtype)
+        send_ref[q:, out] = total[3 * q :].astype(send_ref.dtype)
+
+
+def backward_products(side, dg, du, w, chunk):
+    rows, ff = dg.shape
+    count = w.shape[1]
+    out_shape = [jax.ShapeDtypeStruct((rows // 2, count), kind) for kind in (F32, BF16)]
+    products = 2 * rows * ff * count
+    return run("backward_products", backward_kernel, side, (dg, du, w), out_shape, chunk, products)
 
 
 def narrow_kernel(g_ref, u_ref, g16_ref, u16_ref):
@@ -213,127 +260,12 @@
         out_specs=[block] * 2,
         out_shape=[jax.ShapeDtypeStruct(gate.shape, BF16)] * 2,
         compiler_params=pltpu.CompilerParams(vmem_limit_bytes=16 << 20),
-        cost_estimate=cost(0, 12 * rows * width),
+        cost_estimate=pl.CostEstimate(flops=0, bytes_accessed=12 * rows * width, transcendentals=0),
         name="narrow",
     )(
         pltpu.with_memory_space_constraint(gate, pltpu.HBM),
         pltpu.with_memory_space_constraint(up, pltpu.HBM),
     )
-
-
-def hidden_kernel(
-    side_ref, wg_ref, wu_ref, eug_ref, euu_ref, bg_ref, bu_ref, keep_ref, far_ref, dh_ref, d_ref,
-    pg_ref, pu_ref, *rest
-):
-    def copies():
-        return rows_copies(side_ref, 0, (wg_ref, wu_ref), *rest) if rest else []
-
-    @pl.when(pl.program_id(0) == 0)
-    def _():
-        for copy in copies():
-            copy.start()
-        pg_ref[...] = jnp.zeros_like(pg_ref)
-        pu_ref[...] = jnp.zeros_like(pu_ref)
-
-    bg, bu = bg_ref[...], bu_ref[...]
-    gate = (
-        keep_ref[0]
-        + far_ref[0].astype(F32)
-        + adapter_scale * jnp.dot(eug_ref[...], bg, preferred_element_type=F32)
-    )
-    up = (
-        keep_ref[1]
-        + far_ref[1].astype(F32)
-        + adapter_scale * jnp.dot(euu_ref[...], bu, preferred_element_type=F32)
-    )
-    sig = jax.nn.sigmoid(gate)
-    hidden_grad = dh_ref[...]
-    dg = (hidden_grad * up * sig * (1.0 + gate * (1.0 - sig))).astype(BF16)
-    du = (hidden_grad * gate * sig).astype(BF16)
-    d_ref[0] = dg
-    d_ref[1] = du
-    pg_ref[...] += flipped_product(dg, bg)
-    pu_ref[...] += flipped_product(du, bu)
-
-    @pl.when(pl.program_id(0) == pl.num_programs(0) - 1)
-    def _():
-        for copy in copies():
-            copy.wait()
-
-
-def hidden_gradients(weights, eug, euu, b_gate, b_up, keep, far, hidden_grad, first, width, count_after):
-    rows, wide = eug.shape
-    count = keep.shape[2]
-    start = first // width
-    follow = count_after > 0
-    fixed = pl.BlockSpec((rows, wide), lambda k: (0, 0))
-    b_block = pl.BlockSpec((wide, width), lambda k: (0, k + start))
-    block = pl.BlockSpec((2, rows, width), lambda k: (0, 0, k))
-    return pl.pallas_call(
-        hidden_kernel,
-        grid=(count // width,),
-        in_specs=[
-            SMEM,
-            HBM,
-            HBM,
-            fixed,
-            fixed,
-            b_block,
-            b_block,
-            block,
-            block,
-            pl.BlockSpec((rows, width), lambda k: (0, k + start)),
-        ],
-        out_specs=[block, fixed, fixed] + [ANYWHERE] * follow,
-        out_shape=[jax.ShapeDtypeStruct((2, rows, count), BF16)]
-        + [jax.ShapeDtypeStruct((rows, wide), F32)] * 2
-        + [pltpu.VMEM((2, count_after, weights[1].shape[1]), BF16)] * follow,
-        scratch_shapes=[PAIR] * follow,
-        compiler_params=pltpu.CompilerParams(vmem_limit_bytes=12 << 20),
-        cost_estimate=cost(4 * rows * wide * count, 12 * wide * count),
-        name="hidden_gradients",
-    )(*weights, eug, euu, b_gate, b_up, keep, far, hidden_grad)
-
-
-def backward_kernel(
-    after, side_ref, dg_ref, du_ref, w_ref, wg_ref, wu_ref, keep_ref, send_ref, *rest
-):
-    copies = rows_copies(side_ref, after, (wg_ref, wu_ref), *rest) if rest else []
-    for copy in copies:
-        copy.start()
-    q = dg_ref.shape[0] // 4
-    step = 512
-    for k in range(0, w_ref.shape[1], step):
-        total = flipped_product(dg_ref[...], w_ref[0, k : k + step])
-        total += flipped_product(du_ref[...], w_ref[1, k : k + step])
-        out = pl.ds(k, step)
-        keep_ref[:q, out] = total[:q]
-        keep_ref[q:, out] = total[2 * q : 3 * q]
-        send_ref[:q, out] = total[q : 2 * q].astype(send_ref.dtype)
-        send_ref[q:, out] = total[3 * q :].astype(send_ref.dtype)
-    for copy in copies:
-        copy.wait()
-
-
-def backward_products(weights, dg, du, w, after, count_after):
-    rows, ff = dg.shape
-    count = w.shape[1]
-    side, gate_weight, up_weight = weights
-    follow = count_after > 0
-    return pl.pallas_call(
-        functools.partial(backward_kernel, after),
-        in_specs=[SMEM, VMEM, VMEM, VMEM, HBM, HBM],
-        out_specs=[VMEM] * 2 + [ANYWHERE] * follow,
-        out_shape=[
-            jax.ShapeDtypeStruct((rows // 2, count), F32),
-            jax.ShapeDtypeStruct((rows // 2, count), BF16),
-        ]
-        + [pltpu.VMEM((2, count_after, ff), BF16)] * follow,
-        scratch_shapes=[PAIR] * follow,
-        compiler_params=pltpu.CompilerParams(vmem_limit_bytes=8 << 20),
-        cost_estimate=cost(2 * rows * count * ff, 6 * count * ff),
-        name="backward_products",
-    )(side, dg, du, w, gate_weight, up_weight)
 
 
 N = 16
@@ -385,26 +317,32 @@
     rows = 2 * N
     ff = b_gate.shape[1]
 
-    weights = weights_in_hbm(side, gate_weight, up_weight)
+    weights = gate_weight, up_weight
     cuts = [ff * c // 7 for c in (0, 2, 4, 6, 7)]
+    steps = [half * c // 8 for c in (0, 2, 5, 8)]
+    columns = [Chunk(weights, 0, half, c, n - c, half) for c, n in zip(cuts, cuts[1:])]
+    lifts = [
+        Chunk((b_gate, b_up), 0, b_gate.shape[0], c, n - c)
+        for c, n in ((0, cuts[3]), (cuts[3], ff))
+    ]
+    lines = [Chunk(weights, c, n - c, 0, ff, half) for c, n in zip(steps, steps[1:])]
 
     recv = along_tensor(tokens, 4)
     a_gate, a_up = narrow(a_gate, a_up, feat_rows // 2)
     recv, a_gate, a_up = in_order(recv, a_gate, a_up)
     line = jnp.concatenate([tokens, recv], axis=0)
     recv = along_tensor(line, 8)
-    w = first_columns(weights, cuts[1])
-    recv, w = in_order(recv, w)
     line = jnp.concatenate([line, recv], axis=0)
     mine = lax.dynamic_slice_in_dim(line, group * half, half, 1)
     other = lax.dynamic_slice_in_dim(line, half - group * half, half, 1)
     parts = [along_tensor(mine, X), across_groups(other), across_groups(other, X)]
-    b_gate, b_up = narrow(b_gate, b_up, b_gate.shape[0] // 8)
-    b_gate, b_up, *parts = in_order(b_gate, b_up, *parts)
     x = jnp.stack(
         [jnp.concatenate([mine, parts[0]], axis=0), jnp.concatenate([parts[1], parts[2]], axis=0)]
     )
-    x = jnp.concatenate([x, along_tensor(x, CORE)], axis=1).reshape(2 * rows, half)
+    recv = along_tensor(x, CORE)
+    side, x = in_order(side, x)
+    (w,) = run("first_columns", first_kernel, side, (), [], columns[0])
+    x = jnp.concatenate([x, recv], axis=1).reshape(2 * rows, half)
 
     place = jnp.arange(rows, dtype=jnp.int32)
     block = ((place >> 1) & 3) * 4 + ((place >> 3) & 1) * 2 + (place >> 4)
@@ -426,8 +364,7 @@
     blocks = lax.dynamic_slice_in_dim(x, (t % per_half) * feat_rows, feat_rows, 1)
     swapped = across_groups(blocks[rows:])
     def forward(c, w):
-        after = cuts[c + 1]
-        return forward_products(weights, x, w, after, (cuts + cuts[-1:])[c + 2] - after)
+        return forward_products(side, x, w, (columns + lifts)[c + 1])
 
     keep_0, send_0, w = forward(0, w)
     swapped, x, keep_0, send_0 = in_order(swapped, x, keep_0, send_0)
@@ -454,7 +391,7 @@
 
     recv = along_tensor(part, 8)
     far_a = across_groups(jnp.concatenate([send_0, send_1, send_2], axis=2))
-    keep_3, send_3 = forward(3, w)
+    keep_3, send_3, b = forward(3, w)
     far_a, recv, keep_3, send_3 = in_order(far_a, recv, keep_3, send_3)
     far_b = across_groups(send_3)
     part = add_z(part, recv, 2)
@@ -462,27 +399,13 @@
     up_factor_gate = spread(u[:, :R])
     up_factor_up = spread(u[:, R:])
 
-    steps = [half * c // 8 for c in (0, 2, 5, 8)]
-
-    def hidden(keep, far, first, width, count_after):
-        return hidden_gradients(
-            weights,
-            up_factor_gate,
-            up_factor_up,
-            b_gate,
-            b_up,
-            keep,
-            far,
-            hidden_grad,
-            first,
-            width,
-            count_after,
-        )
+    def hidden(b, keep, far, dh, chunk):
+        return hidden_gradients(side, up_factor_gate, up_factor_up, b, keep, far, dh, chunk)
 
     keep = jnp.concatenate([keep_0, keep_1, keep_2], axis=2)
-    own_a, pg_a, pu_a = hidden(keep, far_a, 0, 512, 0)
+    own_a, pg_a, pu_a, b = hidden(b, keep, far_a, hidden_grad[:, : cuts[3]], lifts[1])
     far_b, own_a = in_order(far_b, own_a)
-    own_b, pg_b, pu_b, w = hidden(keep_3, far_b, cuts[3], 256, steps[1])
+    own_b, pg_b, pu_b, w = hidden(b, keep_3, far_b, hidden_grad[:, cuts[3] :], lines[0])
     own = jnp.concatenate([own_a, own_b], axis=2)
     far = across_groups(own)
     part = jnp.concatenate([select(pg_a + pg_b), select(pu_a + pu_b)], axis=1)
@@ -495,8 +418,7 @@
     dg, du = both[0], both[1]
 
     def backward(c, w):
-        after = steps[c + 1]
-        return backward_products(weights, dg, du, w, after, (steps + steps[-1:])[c + 2] - after)
+        return backward_products(side, dg, du, w, (lines + [None])[c + 1])
 
     recv = along_tensor(part, X)
     keep_0, send_0, w = backward(0, w)

time: 124 us -> 123 us (level)
  local copies, waits for them, and re-layouts: 15.3 us -> 10 us
  starting transfers between devices: 27.5 us -> 30.1 us
  waiting for transfers between devices: 10.3 us -> 12 us
  other arithmetic: 3.21 us -> 4.52 us
    pallas_call x2 -> x1, Pallas kernels: 9.41 us -> 2.29 us  [narrow(): pl.pallas_call(narrow_kernel, grid=(rows // depth,), in_specs=[block] * 2...]
    pallas_call x10, Pallas kernels: 42.5 us -> 48.4 us  [run(): pl.pallas_call(body, in_specs=[SMEM] + [VMEM] * n_in + [HBM] * (2 * follo...]
    unnamed x35 -> x11, local copies, waits for them, and re-layouts: 14.6 us -> 9.23 us
    ppermute x8, waiting for transfers between devices: 1.16 us -> 3.91 us  [across_groups(): lax.ppermute(value, both, [(i, i ^ (N | mask)) for i in range(2 * N)])]
    ppermute x18, starting transfers between devices: 19.3 us -> 21.1 us  [along_tensor(): return lax.ppermute(value, 'tensor', [(i, i ^ mask) for i in range(N)])]
  transfers between devices with their start and end apart: 26 -> 26, of which waited for: 9 -> 9; matrix products, arithmetic and copies ran while one was open for 11% -> 11% of each run, Pallas kernels for 39% -> 38%
where the time goes in v8:
time: 123 us; the launch traced here: 122 us
  Pallas kernels  50.7 us (41%)
  starting transfers between devices  30.1 us (24%)
  matrix products  13.7 us (11%)
  waiting for transfers between devices  12 us (10%)
  local copies, waits for them, and re-layouts  10 us (8%)
  other arithmetic  4.52 us (4%)
  between operations  1.34 us (1%)
    pallas_call x10, Pallas kernels, run(): pl.pallas_call(body, in_specs=[SMEM] + [VMEM] * n_in + [HBM] * (2 * follo...  48.4 us
    ppermute x18, starting transfers between devices, along_tensor(): return lax.ppermute(value, 'tensor', [(i, i ^ mask) for i in range(N)])  21.1 us
    dot_general x4, matrix products, rows_product(): lax.dot_general(left, right, (((0,), (0,)), ((), ())), preferred_element_...  12 us
    unnamed x11, local copies, waits for them, and re-layouts  9.23 us
    ppermute x8, starting transfers between devices, across_groups(): lax.ppermute(value, both, [(i, i ^ (N | mask)) for i in range(2 * N)])  9.01 us
    ppermute x18, waiting for transfers between devices, along_tensor(): return lax.ppermute(value, 'tensor', [(i, i ^ mask) for i in range(N)])  8.05 us
    ppermute x8, waiting for transfers between devices, across_groups(): lax.ppermute(value, both, [(i, i ^ (N | mask)) for i in range(2 * N)])  3.91 us
  transfers between devices with their start and end apart: 26, of which 9 were waited for; matrix products, arithmetic and copies ran while one was open for 11% of the time, Pallas kernels for 38%

profile of v8, /device:TPU:0, one launch (start us, length us, event | category | flops | bytes accessed | tf_op | source)
XLA Modules:
  0.0 122.3 jit_solution(14645495587871342322)
XLA Ops:
  0.6 3.1 %collective-permute-start = (bf16[2,8192]{1,0:T(2,128)(2,1)}, bf16[2,8192]{1,0:T(2,128)(2,1)S(1)}, u32[]{:S(2)}, u32[]{:S(2)}) collective-permute-start(bf16[2,8192]{1,0:T(2,128)(2,1)} %param.9), channel_id=1, source_target_pairs={{0,4},{1,5},{2,6},{3,7},{4,0},{5,1},{6,2},{7,3},{8,12},{9,13},{10,... | collective-permute-start | bytes 98312 | tf_op jit(solution)/shard_map/ppermute | solution.py:276
  3.7 2.3 %narrow.1 = (bf16[512,1024]{1,0:T(8,128)(2,1)S(1)}, bf16[512,1024]{1,0:T(8,128)(2,1)S(1)}) custom-call(f32[512,1024]{1,0:T(8,128)} %g_ref.1, f32[512,1024]{1,0:T(8,128)} %u_ref.1), custom_call_target="tpu_custom_call" | custom-call | bytes 6291456 | tf_op jit(solution)/shard_map/narrow/pallas_call | solution.py:256
  6.0 0.8 pad_maximum_fusion.8
  6.9 2.9 %collective-permute-start.1 = (bf16[4,8192]{1,0:T(4,128)(2,1)S(1)}, bf16[4,8192]{1,0:T(4,128)(2,1)S(1)}, u32[]{:S(2)}, u32[]{:S(2)}) collective-permute-start(bf16[4,8192]{1,0:T(4,128)(2,1)S(1)} %pad_maximum_fusion.8), channel_id=1, source_target_pairs={{0,8},{1,9},{2,10},{3,11},{4,12},{5,13},{6,14},{7,15},{8,0},{9,1},... | collective-permute-start | bytes 196616 | tf_op jit(solution)/shard_map/ppermute | solution.py:276
  9.8 2.3 %collective-permute-done.1 = bf16[4,8192]{1,0:T(4,128)(2,1)S(1)} collective-permute-done((bf16[4,8192]{1,0:T(4,128)(2,1)S(1)}, bf16[4,8192]{1,0:T(4,128)(2,1)S(1)}, u32[]{:S(2)}, u32[]{:S(2)}) %collective-permute-start.1) | collective-permute-done | bytes 65568 | tf_op jit(solution)/shard_map/ppermute | solution.py:276
  12.1 0.9 pad_maximum_fusion.6
  13.0 1.8 %collective-permute-start.2 = (bf16[8,4096]{1,0:T(8,128)(2,1)S(1)}, bf16[8,4096]{1,0:T(8,128)(2,1)S(1)}, u32[]{:S(2)}, u32[]{:S(2)}) collective-permute-start(bf16[8,4096]{1,0:T(8,128)(2,1)S(1)} %get-tuple-element.191), channel_id=1, source_target_pairs={{0,2},{1,3},{2,0},{3,1},{4,6},{5,7},{6,4},{7,5},{8,10},{9,11},{10,... | collective-permute-start | bytes 196616 | tf_op jit(solution)/shard_map/ppermute | solution.py:276
  14.8 1.5 %collective-permute-start.3 = (bf16[8,4096]{1,0:T(8,128)(2,1)S(1)}, bf16[8,4096]{1,0:T(8,128)(2,1)S(1)}, u32[]{:S(2)}, u32[]{:S(2)}) collective-permute-start(bf16[8,4096]{1,0:T(8,128)(2,1)S(1)} %get-tuple-element.192), channel_id=1, source_target_pairs={{0,16},{1,17},{2,18},{3,19},{4,20},{5,21},{6,22},{7,23},{8,24},{9,... | collective-permute-start | bytes 196616 | tf_op jit(solution)/shard_map/ppermute | solution.py:281
  16.6 1.0 collective-permute-done.2
  17.6 2.1 %collective-permute-done.3 = bf16[8,4096]{1,0:T(8,128)(2,1)S(1)} collective-permute-done((bf16[8,4096]{1,0:T(8,128)(2,1)S(1)}, bf16[8,4096]{1,0:T(8,128)(2,1)S(1)}, u32[]{:S(2)}, u32[]{:S(2)}) %collective-permute-start.3) | collective-permute-done | bytes 65568 | tf_op jit(solution)/shard_map/ppermute | solution.py:281
  19.7 1.8 %collective-permute-done.4 = bf16[8,4096]{1,0:T(8,128)(2,1)S(1)} collective-permute-done((bf16[8,4096]{1,0:T(8,128)(2,1)S(1)}, bf16[8,4096]{1,0:T(8,128)(2,1)S(1)}, u32[]{:S(2)}, u32[]{:S(2)}) %collective-permute-start.4) | collective-permute-done | bytes 65568 | tf_op jit(solution)/shard_map/ppermute | solution.py:281
  21.7 0.8 select_reduce_fusion
  22.5 3.9 %first_columns.1.refs_1_ = bf16[2,4096,512]{2,1,0:T(8,128)(2,1)S(1)} custom-call(s32[1]{0:T(128)} %bitcast.side_ref, bf16[8192,1792]{1,0:T(8,128)(2,1)} %refs_3_.11, bf16[8192,1792]{1,0:T(8,128)(2,1)} %refs_4_.3), custom_call_target="tpu_custom_call" | custom-call | bytes 8388608 | tf_op jit(solution)/shard_map/first_columns/pallas_call | solution.py:154
  26.5 0.5 collective-permute-start.6
  26.9 4.9 %forward_products.4 = (f32[2,32,512]{2,1,0:T(8,128)S(1)}, bf16[2,32,512]{2,1,0:T(8,128)(2,1)S(1)}, bf16[2,4096,512]{2,1,0:T(8,128)(2,1)S(1)}) custom-call(s32[1]{0:T(128)} %bitcast.side_ref, bf16[64,4096]{1,0:T(8,128)(2,1)S(1)} %bitcast.60, bf16[2,4096,512]{2,1,0:T(8,128)(2,1)S(1)} %first_columns.1.refs_1_, bf16[8192,1792]{1,0:T(8,128)(2,1)} %refs_3_.11, ...), custom_call_target="tpu_custom_call" | custom-call | flops 536870912 | bytes 13421772 | tf_op jit(solution)/shard_map/forward_products/pallas_call | solution.py:154
  33.1 0.7 collective-permute-done.7
  34.3 4.9 %forward_products.5 = (f32[2,32,512]{2,1,0:T(8,128)S(1)}, bf16[2,32,512]{2,1,0:T(8,128)(2,1)S(1)}, bf16[2,4096,512]{2,1,0:T(8,128)(2,1)S(1)}) custom-call(s32[1]{0:T(128)} %bitcast.side_ref, bf16[64,4096]{1,0:T(8,128)(2,1)S(1)} %bitcast.62, bf16[2,4096,512]{2,1,0:T(8,128)(2,1)S(1)} %get-tuple-element.106.refs_1_, bf16[8192,1792]{1,0:T(8,128)(2,1)} %refs_3_.11, ...), custom_call_target="tpu_custom_call" | custom-call | flops 536870912 | bytes 13421772 | tf_op jit(solution)/shard_map/forward_products/pallas_call | solution.py:154
  39.2 1.9 %collective-permute-start.9 = (f32[32,128]{1,0:T(8,128)S(1)}, f32[32,128]{1,0:T(8,128)S(1)}, u32[]{:S(2)}, u32[]{:S(2)}) collective-permute-start(f32[32,128]{1,0:T(8,128)S(1)} %maximum_add_fusion.2), channel_id=1, source_target_pairs={{0,4},{1,5},{2,6},{3,7},{4,0},{5,1},{6,2},{7,3},{8,12},{9,13},{10,... | collective-permute-start | bytes 49160 | tf_op jit(solution)/shard_map/ppermute | solution.py:276
  41.1 3.9 %forward_products.6 = (f32[2,32,512]{2,1,0:T(8,128)S(1)}, bf16[2,32,512]{2,1,0:T(8,128)(2,1)S(1)}, bf16[2,4096,256]{2,1,0:T(8,128)(2,1)S(1)}) custom-call(s32[1]{0:T(128)} %bitcast.side_ref, bf16[64,4096]{1,0:T(8,128)(2,1)S(1)} %bitcast.63, bf16[2,4096,512]{2,1,0:T(8,128)(2,1)S(1)} %get-tuple-element.111.refs_1_, bf16[8192,1792]{1,0:T(8,128)(2,1)} %refs_3_.11, ...), custom_call_target="tpu_custom_call" | custom-call | flops 536870912 | bytes 13421772 | tf_op jit(solution)/shard_map/forward_products/pallas_call | solution.py:154
  45.0 1.7 %collective-permute-start.10 = (bf16[2,32,1536]{2,1,0:T(8,128)(2,1)S(1)}, bf16[2,32,1536]{2,1,0:T(8,128)(2,1)S(1)}, u32[]{:S(2)}, u32[]{:S(2)}) collective-permute-start(bf16[2,32,1536]{2,1,0:T(8,128)(2,1)S(1)} %pad_maximum_fusion.5), channel_id=1, source_target_pairs={{0,16},{1,17},{2,18},{3,19},{4,20},{5,21},{6,22},{7,23},{8,24},{9,... | collective-permute-start | bytes 589832 | tf_op jit(solution)/shard_map/ppermute | solution.py:281
  46.8 3.2 %collective-permute-start.11 = (f32[32,128]{1,0:T(8,128)S(1)}, f32[32,128]{1,0:T(8,128)S(1)}, u32[]{:S(2)}, u32[]{:S(2)}) collective-permute-start(f32[32,128]{1,0:T(8,128)S(1)} %add.222), channel_id=1, source_target_pairs={{0,8},{1,9},{2,10},{3,11},{4,12},{5,13},{6,14},{7,15},{8,0},{9,1},... | collective-permute-start | bytes 49160 | tf_op jit(solution)/shard_map/ppermute | solution.py:276
  50.1 5.0 %forward_products.7 = (f32[2,32,256]{2,1,0:T(8,128)S(1)}, bf16[2,32,256]{2,1,0:T(8,128)(2,1)S(1)}, f32[2,1024,1536]{2,1,0:T(8,128)S(1)}) custom-call(s32[1]{0:T(128)} %bitcast.side_ref, bf16[64,4096]{1,0:T(8,128)(2,1)S(1)} %bitcast.64, bf16[2,4096,256]{2,1,0:T(8,128)(2,1)S(1)} %get-tuple-element.119.refs_1_, f32[1024,1792]{1,0:T(8,128)} %refs_6_.2, ...), custom_call_target="tpu_custom_call" | custom-call | flops 268435456 | bytes 6710886 | tf_op jit(solution)/shard_map/forward_products/pallas_call | solution.py:154
  55.1 4.6 %copy-done.2 = f32[2,1024,1536]{2,1,0:T(8,128)} copy-done((f32[2,1024,1536]{2,1,0:T(8,128)}, f32[2,1024,1536]{2,1,0:T(8,128)S(1)}, u32[]{:S(2)}) %copy-start.2) | copy-done | bytes 12582936
  60.0 0.4 collective-permute-start.12
  60.6 4.6 %copy-done.3 = f32[2,1024,1536]{2,1,0:T(8,128)S(1)} copy-done((f32[2,1024,1536]{2,1,0:T(8,128)S(1)}, f32[2,1024,1536]{2,1,0:T(8,128)}, u32[]{:S(2)}) %copy-start.3) | copy-done | bytes 12582936
  65.1 4.4 %hidden_gradients.2 = (bf16[2,32,1536]{2,1,0:T(8,128)(2,1)S(1)}, f32[32,1024]{1,0:T(8,128)S(1)}, f32[32,1024]{1,0:T(8,128)S(1)}, f32[2,1024,256]{2,1,0:T(8,128)S(1)}) custom-call(s32[1]{0:T(128)} %bitcast.side_ref, bf16[32,1024]{1,0:T(8,128)(2,1)S(1)} %get-tuple-element.229.refs_0_, bf16[32,1024]{1,0:T(8,128)(2,1)S(1)} %get-tuple-element.230.refs_1_, ...), custom_call_target="tpu_custom_call" | custom-call | flops 402653184 | bytes 10066329 | tf_op jit(solution)/shard_map/hidden_gradients/pallas_call | solution.py:154
  69.6 3.9 %hidden_gradients.3 = (bf16[2,32,256]{2,1,0:T(8,128)(2,1)S(1)}, f32[32,1024]{1,0:T(8,128)S(1)}, f32[32,1024]{1,0:T(8,128)S(1)}, bf16[2,1024,1792]{2,1,0:T(8,128)(2,1)S(1)}) custom-call(s32[1]{0:T(128)} %bitcast.side_ref, bf16[32,1024]{1,0:T(8,128)(2,1)S(1)} %get-tuple-element.229.refs_0_, bf16[32,1024]{1,0:T(8,128)(2,1)S(1)} %get-tuple-element.230.refs_1_, ...), custom_call_target="tpu_custom_call" | custom-call | flops 67108864 | bytes 7340032 | tf_op jit(solution)/shard_map/hidden_gradients/pallas_call | solution.py:154
  73.8 1.7 %collective-permute-start.13 = (bf16[2,32,1792]{2,1,0:T(8,128)(2,1)S(1)}, bf16[2,32,1792]{2,1,0:T(8,128)(2,1)S(1)}, u32[]{:S(2)}, u32[]{:S(2)}) collective-permute-start(bf16[2,32,1792]{2,1,0:T(8,128)(2,1)S(1)} %constant_dynamic-update-slice_fusion), channel_id=1, source_target_pairs={{0,16},{1,17},{2,18},{3,19},{4,20},{5,21},{6,22},{7,23},{8,24},{9,... | collective-permute-start | bytes 688136 | tf_op jit(solution)/shard_map/ppermute | solution.py:281
  75.5 4.2 %convolution_multiply_fusion.1 = f32[1024,1792]{1,0:T(8,128)} fusion(bf16[32,1024]{1,0:T(8,128)(2,1)S(1)} %get-tuple-element.229.refs_0_, bf16[2,32,1792]{2,1,0:T(8,128)(2,1)S(1)} %constant_dynamic-update-slice_fusion), kind=kOutput, calls=%fused_computation.1 | convolution fusion | flops 119275520 | bytes 7520256 | tf_op jit(solution)/shard_map/dot_general | solution.py:39
  79.8 1.2 collective-permute-done.14
  81.0 1.6 %collective-permute-start.15 = (f32[32,128]{1,0:T(8,128)S(1)}, f32[32,128]{1,0:T(8,128)S(1)}, u32[]{:S(2)}, u32[]{:S(2)}) collective-permute-start(f32[32,128]{1,0:T(8,128)S(1)} %maximum_add_fusion.3), channel_id=1, source_target_pairs={{0,2},{1,3},{2,0},{3,1},{4,6},{5,7},{6,4},{7,5},{8,10},{9,11},{10,... | collective-permute-start | bytes 49160 | tf_op jit(solution)/shard_map/ppermute | solution.py:276
  82.6 6.4 %backward_products.3 = (f32[32,1024]{1,0:T(8,128)S(1)}, bf16[32,1024]{1,0:T(8,128)(2,1)S(1)}, bf16[2,1536,1792]{2,1,0:T(8,128)(2,1)S(1)}) custom-call(s32[1]{0:T(128)} %bitcast.side_ref, bf16[64,1792]{1,0:T(8,128)(2,1)S(1)} %get-tuple-element.155.refs_0_, bf16[64,1792]{1,0:T(8,128)(2,1)S(1)} %get-tuple-element.156.refs_1_, ...), custom_call_target="tpu_custom_call" | custom-call | flops 469762048 | bytes 11744051 | tf_op jit(solution)/shard_map/backward_products/pallas_call | solution.py:154
  89.1 7.6 %backward_products.4 = (f32[32,1536]{1,0:T(8,128)S(1)}, bf16[32,1536]{1,0:T(8,128)(2,1)S(1)}, bf16[2,1536,1792]{2,1,0:T(8,128)(2,1)S(1)}) custom-call(s32[1]{0:T(128)} %bitcast.side_ref, bf16[64,1792]{1,0:T(8,128)(2,1)S(1)} %get-tuple-element.155.refs_0_, bf16[64,1792]{1,0:T(8,128)(2,1)S(1)} %get-tuple-element.156.refs_1_, ...), custom_call_target="tpu_custom_call" | custom-call | flops 704643072 | bytes 17616076 | tf_op jit(solution)/shard_map/backward_products/pallas_call | solution.py:154
  97.0 3.4 %backward_products.5 = (f32[32,1536]{1,0:T(8,128)S(1)}, bf16[32,1536]{1,0:T(8,128)(2,1)S(1)}) custom-call(s32[1]{0:T(128)} %bitcast.side_ref, bf16[64,1792]{1,0:T(8,128)(2,1)S(1)} %get-tuple-element.155.refs_0_, bf16[64,1792]{1,0:T(8,128)(2,1)S(1)} %get-tuple-element.156.refs_1_, bf16[2,1536,1792]{2,1,0:T(8,128)(2,1)S(1)} %get-tuple-element.157.refs_2_), custom_call_target="tpu_custom_call" | custom-call | flops 704643072 | bytes 17616076 | tf_op jit(solution)/shard_map/backward_products/pallas_call | solution.py:154
  100.4 1.1 collective-permute-done.17
  102.8 0.6 collective-permute-start.19
  103.4 0.8 collective-permute-done.19
  104.3 0.6 collective-permute-start.20
  104.9 1.0 collective-permute-start.21
  105.9 1.9 %collective-permute-start.22 = (bf16[8,4096]{1,0:T(8,128)(2,1)S(1)}, bf16[8,4096]{1,0:T(8,128)(2,1)S(1)}, u32[]{:S(2)}, u32[]{:S(2)}) collective-permute-start(bf16[8,4096]{1,0:T(8,128)(2,1)S(1)} %get-tuple-element.185), channel_id=1, source_target_pairs={{0,18},{1,19},{2,16},{3,17},{4,22},{5,23},{6,20},{7,21},{8,26},{9,... | collective-permute-start | bytes 196616 | tf_op jit(solution)/shard_map/ppermute | solution.py:281
  107.9 1.8 %convolution_multiply_fusion.2 = f32[512,1024]{1,0:T(8,128)} fusion(bf16[32,512]{1,0:T(8,128)(2,1)S(1)} %dynamic-slice_select_fusion, bf16[32,1024]{1,0:T(8,128)(2,1)S(1)} %concatenate.105, s32[1024]{0:T(1024)S(1)} %add_select_fusion, s32[32]{0:T(128)S(1)} %select_reduce_fusion), kind=kOutput, calls=%fused_computation.2 | convolution fusion | flops 34144256 | bytes 2199680 | tf_op jit(solution)/shard_map/dot_general | solution.py:39
  109.7 1.8 %convolution_multiply_fusion.3 = f32[512,1024]{1,0:T(8,128)} fusion(bf16[32,512]{1,0:T(8,128)(2,1)S(1)} %dynamic-slice_select_fusion, bf16[32,1024]{1,0:T(8,128)(2,1)S(1)} %concatenate.104, s32[1024]{0:T(1024)S(1)} %add_select_fusion, s32[32]{0:T(128)S(1)} %select_reduce_fusion), kind=kOutput, calls=%fused_computation.3 | convolution fusion | flops 34144256 | bytes 2199680 | tf_op jit(solution)/shard_map/dot_general | solution.py:39
  111.7 2.1 %collective-permute-start.23 = (bf16[2,10240]{1,0:T(2,128)(2,1)S(1)}, bf16[2,10240]{1,0:T(2,128)(2,1)S(1)}, u32[]{:S(2)}, u32[]{:S(2)}) collective-permute-start(bf16[2,10240]{1,0:T(2,128)(2,1)S(1)} %get-tuple-element.190), channel_id=1, source_target_pairs={{0,4},{1,5},{2,6},{3,7},{4,0},{5,1},{6,2},{7,3},{8,12},{9,13},{10,... | collective-permute-start | bytes 122888 | tf_op jit(solution)/shard_map/ppermute | solution.py:276
  113.7 1.7 %collective-permute-start.24 = (bf16[2,10240]{1,0:T(2,128)(2,1)S(1)}, bf16[2,10240]{1,0:T(2,128)(2,1)S(1)}, u32[]{:S(2)}, u32[]{:S(2)}) collective-permute-start(bf16[2,10240]{1,0:T(2,128)(2,1)S(1)} %get-tuple-element.189), channel_id=1, source_target_pairs={{0,8},{1,9},{2,10},{3,11},{4,12},{5,13},{6,14},{7,15},{8,0},{9,1},... | collective-permute-start | bytes 122888 | tf_op jit(solution)/shard_map/ppermute | solution.py:276
  115.5 0.7 collective-permute-start.25
  116.2 4.2 %convolution_multiply_fusion = f32[1024,1792]{1,0:T(8,128)} fusion(bf16[32,1024]{1,0:T(8,128)(2,1)S(1)} %get-tuple-element.230.refs_1_, bf16[2,32,1792]{2,1,0:T(8,128)(2,1)S(1)} %constant_dynamic-update-slice_fusion), kind=kOutput, calls=%fused_computation | convolution fusion | flops 119275520 | bytes 7520256 | tf_op jit(solution)/shard_map/dot_general | solution.py:39
  120.4 0.9 collective-permute-done.25
  121.6 0.7 fusion.14
  (112 shorter events, 5.2 us)
Async XLA Ops:
  0.6 32.2 %copy-start = (bf16[32,1792]{1,0:T(8,128)(2,1)S(1)}, bf16[32,1792]{1,0:T(8,128)(2,1)}, u32[]{:S(2)}) copy-start(bf16[32,1792]{1,0:T(8,128)(2,1)} %param.17) | copy-start | bytes 344068
  0.6 5.4 %collective-permute-start = (bf16[2,8192]{1,0:T(2,128)(2,1)}, bf16[2,8192]{1,0:T(2,128)(2,1)S(1)}, u32[]{:S(2)}, u32[]{:S(2)}) collective-permute-start(bf16[2,8192]{1,0:T(2,128)(2,1)} %param.9), channel_id=1, source_target_pairs={{0,4},{1,5},{2,6},{3,7},{4,0},{5,1},{6,2},{7,3},{8,12},{9,13},{10,... | collective-permute-start | bytes 98312 | tf_op jit(solution)/shard_map/ppermute | solution.py:276
  6.9 5.2 %collective-permute-start.1 = (bf16[4,8192]{1,0:T(4,128)(2,1)S(1)}, bf16[4,8192]{1,0:T(4,128)(2,1)S(1)}, u32[]{:S(2)}, u32[]{:S(2)}) collective-permute-start(bf16[4,8192]{1,0:T(4,128)(2,1)S(1)} %pad_maximum_fusion.8), channel_id=1, source_target_pairs={{0,8},{1,9},{2,10},{3,11},{4,12},{5,13},{6,14},{7,15},{8,0},{9,1},... | collective-permute-start | bytes 196616 | tf_op jit(solution)/shard_map/ppermute | solution.py:276
  13.0 4.6 %collective-permute-start.2 = (bf16[8,4096]{1,0:T(8,128)(2,1)S(1)}, bf16[8,4096]{1,0:T(8,128)(2,1)S(1)}, u32[]{:S(2)}, u32[]{:S(2)}) collective-permute-start(bf16[8,4096]{1,0:T(8,128)(2,1)S(1)} %get-tuple-element.191), channel_id=1, source_target_pairs={{0,2},{1,3},{2,0},{3,1},{4,6},{5,7},{6,4},{7,5},{8,10},{9,11},{10,... | collective-permute-start | bytes 196616 | tf_op jit(solution)/shard_map/ppermute | solution.py:276
  14.8 4.8 %collective-permute-start.3 = (bf16[8,4096]{1,0:T(8,128)(2,1)S(1)}, bf16[8,4096]{1,0:T(8,128)(2,1)S(1)}, u32[]{:S(2)}, u32[]{:S(2)}) collective-permute-start(bf16[8,4096]{1,0:T(8,128)(2,1)S(1)} %get-tuple-element.192), channel_id=1, source_target_pairs={{0,16},{1,17},{2,18},{3,19},{4,20},{5,21},{6,22},{7,23},{8,24},{9,... | collective-permute-start | bytes 196616 | tf_op jit(solution)/shard_map/ppermute | solution.py:281
  16.3 5.2 %collective-permute-start.4 = (bf16[8,4096]{1,0:T(8,128)(2,1)S(1)}, bf16[8,4096]{1,0:T(8,128)(2,1)S(1)}, u32[]{:S(2)}, u32[]{:S(2)}) collective-permute-start(bf16[8,4096]{1,0:T(8,128)(2,1)S(1)} %get-tuple-element.192), channel_id=1, source_target_pairs={{0,18},{1,19},{2,16},{3,17},{4,22},{5,23},{6,20},{7,21},{8,26},{9,... | collective-permute-start | bytes 196616 | tf_op jit(solution)/shard_map/ppermute | solution.py:281
  21.5 4.8 %collective-permute-start.5 = (bf16[2,16,4096]{2,1,0:T(8,128)(2,1)S(1)}, bf16[2,16,4096]{2,1,0:T(8,128)(2,1)S(1)}, u32[]{:S(2)}, u32[]{:S(2)}) collective-permute-start(bf16[2,16,4096]{2,1,0:T(8,128)(2,1)S(1)} %pad_maximum_fusion.3), channel_id=1, source_target_pairs={{0,1},{1,0},{2,3},{3,2},{4,5},{5,4},{6,7},{7,6},{8,9},{9,8},{10,11... | collective-permute-start | bytes 786440 | tf_op jit(solution)/shard_map/ppermute | solution.py:276
  26.5 5.4 %collective-permute-start.6 = (bf16[32,512]{1,0:T(8,128)(2,1)S(1)}, bf16[32,512]{1,0:T(8,128)(2,1)S(1)}, u32[]{:S(2)}, u32[]{:S(2)}) collective-permute-start(bf16[32,512]{1,0:T(8,128)(2,1)S(1)} %dynamic-slice.1), channel_id=1, source_target_pairs={{0,16},{1,17},{2,18},{3,19},{4,20},{5,21},{6,22},{7,23},{8,24},{9,... | collective-permute-start | bytes 98312 | tf_op jit(solution)/shard_map/ppermute | solution.py:281
  32.7 1.2 collective-permute-start.7
  34.0 5.3 %collective-permute-start.8 = (f32[32,128]{1,0:T(8,128)S(1)}, f32[32,128]{1,0:T(8,128)S(1)}, u32[]{:S(2)}, u32[]{:S(2)}) collective-permute-start(f32[32,128]{1,0:T(8,128)S(1)} %maximum_add_fusion.1), channel_id=1, source_target_pairs={{0,2},{1,3},{2,0},{3,1},{4,6},{5,7},{6,4},{7,5},{8,10},{9,11},{10,... | collective-permute-start | bytes 49160 | tf_op jit(solution)/shard_map/ppermute | solution.py:276
  39.2 5.8 %collective-permute-start.9 = (f32[32,128]{1,0:T(8,128)S(1)}, f32[32,128]{1,0:T(8,128)S(1)}, u32[]{:S(2)}, u32[]{:S(2)}) collective-permute-start(f32[32,128]{1,0:T(8,128)S(1)} %maximum_add_fusion.2), channel_id=1, source_target_pairs={{0,4},{1,5},{2,6},{3,7},{4,0},{5,1},{6,2},{7,3},{8,12},{9,13},{10,... | collective-permute-start | bytes 49160 | tf_op jit(solution)/shard_map/ppermute | solution.py:276
  45.0 14.6 %collective-permute-start.10 = (bf16[2,32,1536]{2,1,0:T(8,128)(2,1)S(1)}, bf16[2,32,1536]{2,1,0:T(8,128)(2,1)S(1)}, u32[]{:S(2)}, u32[]{:S(2)}) collective-permute-start(bf16[2,32,1536]{2,1,0:T(8,128)(2,1)S(1)} %pad_maximum_fusion.5), channel_id=1, source_target_pairs={{0,16},{1,17},{2,18},{3,19},{4,20},{5,21},{6,22},{7,23},{8,24},{9,... | collective-permute-start | bytes 589832 | tf_op jit(solution)/shard_map/ppermute | solution.py:281
  46.8 12.9 %collective-permute-start.11 = (f32[32,128]{1,0:T(8,128)S(1)}, f32[32,128]{1,0:T(8,128)S(1)}, u32[]{:S(2)}, u32[]{:S(2)}) collective-permute-start(f32[32,128]{1,0:T(8,128)S(1)} %add.222), channel_id=1, source_target_pairs={{0,8},{1,9},{2,10},{3,11},{4,12},{5,13},{6,14},{7,15},{8,0},{9,1},... | collective-permute-start | bytes 49160 | tf_op jit(solution)/shard_map/ppermute | solution.py:276
  55.1 4.6 %copy-start.2 = (f32[2,1024,1536]{2,1,0:T(8,128)}, f32[2,1024,1536]{2,1,0:T(8,128)S(1)}, u32[]{:S(2)}) copy-start(f32[2,1024,1536]{2,1,0:T(8,128)S(1)} %get-tuple-element.123.refs_2_) | copy-start | bytes 37748740
  60.0 9.6 %collective-permute-start.12 = (bf16[2,32,256]{2,1,0:T(8,128)(2,1)S(1)}, bf16[2,32,256]{2,1,0:T(8,128)(2,1)S(1)}, u32[]{:S(2)}, u32[]{:S(2)}) collective-permute-start(bf16[2,32,256]{2,1,0:T(8,128)(2,1)S(1)} %get-tuple-element.131), channel_id=1, source_target_pairs={{0,16},{1,17},{2,18},{3,19},{4,20},{5,21},{6,22},{7,23},{8,24},{9,... | collective-permute-start | bytes 98312 | tf_op jit(solution)/shard_map/ppermute | solution.py:281
  60.6 4.6 %copy-start.3 = (f32[2,1024,1536]{2,1,0:T(8,128)S(1)}, f32[2,1024,1536]{2,1,0:T(8,128)}, u32[]{:S(2)}) copy-start(f32[2,1024,1536]{2,1,0:T(8,128)} %copy-done.2) | copy-start | bytes 37748740
  73.8 7.1 %collective-permute-start.13 = (bf16[2,32,1792]{2,1,0:T(8,128)(2,1)S(1)}, bf16[2,32,1792]{2,1,0:T(8,128)(2,1)S(1)}, u32[]{:S(2)}, u32[]{:S(2)}) collective-permute-start(bf16[2,32,1792]{2,1,0:T(8,128)(2,1)S(1)} %constant_dynamic-update-slice_fusion), channel_id=1, source_target_pairs={{0,16},{1,17},{2,18},{3,19},{4,20},{5,21},{6,22},{7,23},{8,24},{9,... | collective-permute-start | bytes 688136 | tf_op jit(solution)/shard_map/ppermute | solution.py:281
  79.7 1.2 collective-permute-start.14
  81.0 8.0 %collective-permute-start.15 = (f32[32,128]{1,0:T(8,128)S(1)}, f32[32,128]{1,0:T(8,128)S(1)}, u32[]{:S(2)}, u32[]{:S(2)}) collective-permute-start(f32[32,128]{1,0:T(8,128)S(1)} %maximum_add_fusion.3), channel_id=1, source_target_pairs={{0,2},{1,3},{2,0},{3,1},{4,6},{5,7},{6,4},{7,5},{8,10},{9,11},{10,... | collective-permute-start | bytes 49160 | tf_op jit(solution)/shard_map/ppermute | solution.py:276
  89.0 7.7 %collective-permute-start.16 = (f32[32,128]{1,0:T(8,128)S(1)}, f32[32,128]{1,0:T(8,128)S(1)}, u32[]{:S(2)}, u32[]{:S(2)}) collective-permute-start(f32[32,128]{1,0:T(8,128)S(1)} %maximum_add_fusion.4), channel_id=1, source_target_pairs={{0,4},{1,5},{2,6},{3,7},{4,0},{5,1},{6,2},{7,3},{8,12},{9,13},{10,... | collective-permute-start | bytes 49160 | tf_op jit(solution)/shard_map/ppermute | solution.py:276
  96.8 4.7 %collective-permute-start.17 = (f32[32,128]{1,0:T(8,128)S(1)}, f32[32,128]{1,0:T(8,128)S(1)}, u32[]{:S(2)}, u32[]{:S(2)}) collective-permute-start(f32[32,128]{1,0:T(8,128)S(1)} %add.244), channel_id=1, source_target_pairs={{0,8},{1,9},{2,10},{3,11},{4,12},{5,13},{6,14},{7,15},{8,0},{9,1},... | collective-permute-start | bytes 49160 | tf_op jit(solution)/shard_map/ppermute | solution.py:276
  102.3 1.9 %collective-permute-start.18 = (bf16[32,4096]{1,0:T(8,128)(2,1)S(1)}, bf16[32,4096]{1,0:T(8,128)(2,1)S(1)}, u32[]{:S(2)}, u32[]{:S(2)}) collective-permute-start(bf16[32,4096]{1,0:T(8,128)(2,1)S(1)} %pad_maximum_fusion.4), channel_id=1, source_target_pairs={{0,1},{1,0},{2,3},{3,2},{4,5},{5,4},{6,7},{7,6},{8,9},{9,8},{10,11... | collective-permute-start | bytes 786440 | tf_op jit(solution)/shard_map/ppermute | solution.py:276
  102.8 1.4 %collective-permute-start.19 = (bf16[16,512]{1,0:T(8,128)(2,1)S(1)}, bf16[16,512]{1,0:T(8,128)(2,1)S(1)}, u32[]{:S(2)}, u32[]{:S(2)}) collective-permute-start(bf16[16,512]{1,0:T(8,128)(2,1)S(1)} %get-tuple-element.198), channel_id=1, source_target_pairs={{0,1},{1,0},{2,3},{3,2},{4,5},{5,4},{6,7},{7,6},{8,9},{9,8},{10,11... | collective-permute-start | bytes 49160 | tf_op jit(solution)/shard_map/ppermute | solution.py:276
  104.3 7.2 %collective-permute-start.20 = (bf16[8,5120]{1,0:T(8,128)(2,1)S(1)}, bf16[8,5120]{1,0:T(8,128)(2,1)S(1)}, u32[]{:S(2)}, u32[]{:S(2)}) collective-permute-start(bf16[8,5120]{1,0:T(8,128)(2,1)S(1)} %pad_maximum_fusion.7), channel_id=1, source_target_pairs={{0,2},{1,3},{2,0},{3,1},{4,6},{5,7},{6,4},{7,5},{8,10},{9,11},{10,... | collective-permute-start | bytes 245768 | tf_op jit(solution)/shard_map/ppermute | solution.py:276
  104.9 6.5 %collective-permute-start.21 = (bf16[8,4096]{1,0:T(8,128)(2,1)S(1)}, bf16[8,4096]{1,0:T(8,128)(2,1)S(1)}, u32[]{:S(2)}, u32[]{:S(2)}) collective-permute-start(bf16[8,4096]{1,0:T(8,128)(2,1)S(1)} %get-tuple-element.186), channel_id=1, source_target_pairs={{0,16},{1,17},{2,18},{3,19},{4,20},{5,21},{6,22},{7,23},{8,24},{9,... | collective-permute-start | bytes 196616 | tf_op jit(solution)/shard_map/ppermute | solution.py:281
  105.9 5.5 %collective-permute-start.22 = (bf16[8,4096]{1,0:T(8,128)(2,1)S(1)}, bf16[8,4096]{1,0:T(8,128)(2,1)S(1)}, u32[]{:S(2)}, u32[]{:S(2)}) collective-permute-start(bf16[8,4096]{1,0:T(8,128)(2,1)S(1)} %get-tuple-element.185), channel_id=1, source_target_pairs={{0,18},{1,19},{2,16},{3,17},{4,22},{5,23},{6,20},{7,21},{8,26},{9,... | collective-permute-start | bytes 196616 | tf_op jit(solution)/shard_map/ppermute | solution.py:281
  111.5 10.8 %copy-start.1 = (bf16[32,1792]{1,0:T(8,128)(2,1)S(1)}, bf16[32,1792]{1,0:T(8,128)(2,1)}, u32[]{:S(2)}) copy-start(bf16[32,1792]{1,0:T(8,128)(2,1)} %param.17) | copy-start | bytes 344068
  111.7 8.7 %collective-permute-start.23 = (bf16[2,10240]{1,0:T(2,128)(2,1)S(1)}, bf16[2,10240]{1,0:T(2,128)(2,1)S(1)}, u32[]{:S(2)}, u32[]{:S(2)}) collective-permute-start(bf16[2,10240]{1,0:T(2,128)(2,1)S(1)} %get-tuple-element.190), channel_id=1, source_target_pairs={{0,4},{1,5},{2,6},{3,7},{4,0},{5,1},{6,2},{7,3},{8,12},{9,13},{10,... | collective-permute-start | bytes 122888 | tf_op jit(solution)/shard_map/ppermute | solution.py:276
  113.7 6.7 %collective-permute-start.24 = (bf16[2,10240]{1,0:T(2,128)(2,1)S(1)}, bf16[2,10240]{1,0:T(2,128)(2,1)S(1)}, u32[]{:S(2)}, u32[]{:S(2)}) collective-permute-start(bf16[2,10240]{1,0:T(2,128)(2,1)S(1)} %get-tuple-element.189), channel_id=1, source_target_pairs={{0,8},{1,9},{2,10},{3,11},{4,12},{5,13},{6,14},{7,15},{8,0},{9,1},... | collective-permute-start | bytes 122888 | tf_op jit(solution)/shard_map/ppermute | solution.py:276
  115.5 5.8 %collective-permute-start.25 = (bf16[2,10240]{1,0:T(2,128)(2,1)S(1)}, bf16[2,10240]{1,0:T(2,128)(2,1)S(1)}, u32[]{:S(2)}, u32[]{:S(2)}) collective-permute-start(bf16[2,10240]{1,0:T(2,128)(2,1)S(1)} %get-tuple-element.188), channel_id=1, source_target_pairs={{0,12},{1,13},{2,14},{3,15},{4,8},{5,9},{6,10},{7,11},{8,4},{9,5},... | collective-permute-start | bytes 122888 | tf_op jit(solution)/shard_map/ppermute | solution.py:276

commit v9 on v6

--- a/solution.py
+++ b/solution.py
@@ -158,71 +158,112 @@
     )
 
 
+def narrow_kernel(g_ref, u_ref, g16_ref, u16_ref):
+    g16_ref[...] = g_ref[...].astype(BF16)
+    u16_ref[...] = u_ref[...].astype(BF16)
+
+
+def narrow(gate, up, depth):
+    rows, width = gate.shape
+    block = pl.BlockSpec((depth, width), lambda k: (k, 0))
+    return pl.pallas_call(
+        narrow_kernel,
+        grid=(rows // depth,),
+        in_specs=[block] * 2,
+        out_specs=[block] * 2,
+        out_shape=[jax.ShapeDtypeStruct(gate.shape, BF16)] * 2,
+        compiler_params=pltpu.CompilerParams(vmem_limit_bytes=16 << 20),
+        cost_estimate=pl.CostEstimate(flops=0, bytes_accessed=12 * rows * width, transcendentals=0),
+        name="narrow",
+    )(
+        pltpu.with_memory_space_constraint(gate, pltpu.HBM),
+        pltpu.with_memory_space_constraint(up, pltpu.HBM),
+    )
+
+
 def hidden_kernel(
-    eug_ref, euu_ref, bg_ref, bu_ref, keep_ref, far_ref, dh_ref, d_ref, pg_ref, pu_ref
+    first, step, eug_ref, euu_ref, keep_ref, far_ref, dh_ref, bg_ref, bu_ref, d_ref, pg_ref, pu_ref,
+    b_ref, sem
 ):
-    @pl.when(pl.program_id(0) == 0)
-    def _():
-        pg_ref[...] = jnp.zeros_like(pg_ref)
-        pu_ref[...] = jnp.zeros_like(pu_ref)
-
-    bg = bg_ref[...].astype(BF16)
-    bu = bu_ref[...].astype(BF16)
-    gate = (
-        keep_ref[0]
-        + far_ref[0].astype(F32)
-        + adapter_scale * jnp.dot(eug_ref[...], bg, preferred_element_type=F32)
-    )
-    up = (
-        keep_ref[1]
-        + far_ref[1].astype(F32)
-        + adapter_scale * jnp.dot(euu_ref[...], bu, preferred_element_type=F32)
-    )
-    sig = jax.nn.sigmoid(gate)
-    hidden_grad = dh_ref[...]
-    dg = (hidden_grad * up * sig * (1.0 + gate * (1.0 - sig))).astype(BF16)
-    du = (hidden_grad * gate * sig).astype(BF16)
-    d_ref[0] = dg
-    d_ref[1] = du
-    pg_ref[...] += flipped_product(dg, bg)
-    pu_ref[...] += flipped_product(du, bu)
-
-
-def hidden_gradients(eug, euu, b_gate, b_up, keep, far, hidden_grad, first, width):
+    blocks, _, pieces = sem.shape
+    depth = b_ref.shape[2] // pieces
+
+    def copies(block):
+        return [
+            pltpu.make_async_copy(
+                ref.at[pl.ds(k * depth, depth), pl.ds(first + block * step, step)],
+                b_ref.at[block, i, pl.ds(k * depth, depth)],
+                sem.at[block, i, k],
+            )
+            for i, ref in enumerate((bg_ref, bu_ref))
+            for k in range(pieces)
+        ]
+
+    running = [copies(block) for block in range(blocks)]
+    for block in range(min(2, blocks)):
+        for copy in running[block]:
+            copy.start()
+    for block in range(blocks):
+        for copy in running[block]:
+            copy.wait()
+        if block + 2 < blocks:
+            for copy in running[block + 2]:
+                copy.start()
+        at = pl.ds(block * step, step)
+        bg = b_ref[block, 0].astype(BF16)
+        bu = b_ref[block, 1].astype(BF16)
+        gate = (
+            keep_ref[0, :, at]
+            + far_ref[0, :, at].astype(F32)
+            + adapter_scale * jnp.dot(eug_ref[...], bg, preferred_element_type=F32)
+        )
+        up = (
+            keep_ref[1, :, at]
+            + far_ref[1, :, at].astype(F32)
+            + adapter_scale * jnp.dot(euu_ref[...], bu, preferred_element_type=F32)
+        )
+        sig = jax.nn.sigmoid(gate)
+        hidden_grad = dh_ref[:, at]
+        dg = (hidden_grad * up * sig * (1.0 + gate * (1.0 - sig))).astype(BF16)
+        du = (hidden_grad * gate * sig).astype(BF16)
+        d_ref[0, :, at] = dg
+        d_ref[1, :, at] = du
+        if block == 0:
+            pg_ref[...] = flipped_product(dg, bg)
+            pu_ref[...] = flipped_product(du, bu)
+        else:
+            pg_ref[...] += flipped_product(dg, bg)
+            pu_ref[...] += flipped_product(du, bu)
+
+
+def hidden_gradients(eug, euu, b_gate, b_up, keep, far, hidden_grad, first, step, pieces=4):
     rows, wide = eug.shape
     count = keep.shape[2]
-    start = first // width
-    fixed = pl.BlockSpec((rows, wide), lambda k: (0, 0))
-    b_block = pl.BlockSpec((wide, width), lambda k: (0, k + start))
-    block = pl.BlockSpec((2, rows, width), lambda k: (0, 0, k))
+    vmem = pl.BlockSpec(memory_space=pltpu.VMEM)
+    hbm = pl.BlockSpec(memory_space=pltpu.HBM)
     return pl.pallas_call(
-        hidden_kernel,
-        grid=(count // width,),
-        in_specs=[
-            fixed,
-            fixed,
-            b_block,
-            b_block,
-            block,
-            block,
-            pl.BlockSpec((rows, width), lambda k: (0, k + start)),
-        ],
-        out_specs=[block, fixed, fixed],
+        functools.partial(hidden_kernel, first, step),
+        in_specs=[vmem] * 5 + [hbm] * 2,
+        out_specs=[vmem] * 3,
         out_shape=[jax.ShapeDtypeStruct((2, rows, count), BF16)]
         + [jax.ShapeDtypeStruct((rows, wide), F32)] * 2,
-        compiler_params=pltpu.CompilerParams(vmem_limit_bytes=20 << 20),
+        scratch_shapes=[
+            pltpu.VMEM((count // step, 2, wide, step), F32),
+            pltpu.SemaphoreType.DMA((count // step, 2, pieces)),
+        ],
+        compiler_params=pltpu.CompilerParams(vmem_limit_bytes=28 << 20),
         cost_estimate=pl.CostEstimate(
-            flops=8 * rows * wide * count, bytes_accessed=16 * wide * count, transcendentals=0
+            flops=8 * rows * wide * count, bytes_accessed=12 * wide * count, transcendentals=0
         ),
         name="hidden_gradients",
     )(
         eug,
         euu,
+        keep,
+        far,
+        hidden_grad[:, first : first + count],
         pltpu.with_memory_space_constraint(b_gate, pltpu.HBM),
         pltpu.with_memory_space_constraint(b_up, pltpu.HBM),
-        keep,
-        far,
-        hidden_grad,
     )
 
 
@@ -232,23 +273,30 @@
     depth = total_rows // pieces
     base = side_ref[0] * (wg_ref.shape[0] // 2) + first
     copies = {}
-    for k in range(0, pieces, 2):
+    for j in range(pieces):
         for i, w_ref in enumerate((wg_ref, wu_ref)):
-            for j in (k, k + 1):
-                source = pl.ds(pl.multiple_of(base + j * depth, depth), depth)
-                copies[i, j] = pltpu.make_async_copy(
-                    w_ref.at[source], rows_ref.at[i, pl.ds(j * depth, depth)], sem.at[i, j]
-                )
-                copies[i, j].start()
+            source = pl.ds(pl.multiple_of(base + j * depth, depth), depth)
+            copies[i, j] = pltpu.make_async_copy(
+                w_ref.at[source], rows_ref.at[i, pl.ds(j * depth, depth)], sem.at[i, j]
+            )
+
+    def start(j):
+        if j < pieces:
+            for at in ((0, j), (0, j + 1), (1, j), (1, j + 1)):
+                copies[at].start()
+
+    start(0)
+    start(2)
     q = dg_ref.shape[0] // 4
     step = 2 * depth
     for k in range(0, total_rows, step):
         j = k // depth
         copies[0, j].wait()
         copies[0, j + 1].wait()
-        total = flipped_product(dg_ref[...], rows_ref[0, k : k + step])
         copies[1, j].wait()
         copies[1, j + 1].wait()
+        start(j + 4)
+        total = flipped_product(dg_ref[...], rows_ref[0, k : k + step])
         total += flipped_product(du_ref[...], rows_ref[1, k : k + step])
         out = pl.ds(k, step)
         keep_ref[:q, out] = total[:q]
@@ -273,7 +321,7 @@
             pltpu.VMEM((2, count, ff), BF16),
             pltpu.SemaphoreType.DMA((2, count // depth)),
         ],
-        compiler_params=pltpu.CompilerParams(vmem_limit_bytes=28 << 20),
+        compiler_params=pltpu.CompilerParams(vmem_limit_bytes=36 << 20),
         cost_estimate=pl.CostEstimate(
             flops=4 * rows * count * ff, bytes_accessed=6 * count * ff, transcendentals=0
         ),
@@ -336,7 +384,10 @@
     rows = 2 * N
     ff = b_gate.shape[1]
 
-    line = jnp.concatenate([tokens, along_tensor(tokens, 4)], axis=0)
+    recv = along_tensor(tokens, 4)
+    a_gate, a_up = narrow(a_gate, a_up, feat_rows // 2)
+    recv, a_gate, a_up = in_order(recv, a_gate, a_up)
+    line = jnp.concatenate([tokens, recv], axis=0)
     line = jnp.concatenate([line, along_tensor(line, 8)], axis=0)
     mine = lax.dynamic_slice_in_dim(line, group * half, half, 1)
     other = lax.dynamic_slice_in_dim(line, half - group * half, half, 1)
@@ -377,8 +428,8 @@
     own_cols = jnp.where(t // per_half == group, blocks[:rows], swapped)
     part = jnp.concatenate(
         [
-            select(jnp.dot(own_cols, a_gate.astype(BF16), preferred_element_type=F32)),
-            select(jnp.dot(own_cols, a_up.astype(BF16), preferred_element_type=F32)),
+            select(jnp.dot(own_cols, a_gate, preferred_element_type=F32)),
+            select(jnp.dot(own_cols, a_up, preferred_element_type=F32)),
         ],
         axis=1,
     )
@@ -425,7 +476,7 @@
     both = jnp.concatenate([own, far], axis=1)
     dg, du = both[0], both[1]
 
-    count = half // 4
+    count = half // 8
 
     def backward(c, n):
         return backward_products(side, dg, du, gate_weight, up_weight, c * count, n * count)
@@ -441,7 +492,7 @@
     part = add_z(part, recv, 1)
 
     recv = along_tensor(part, 8)
-    keep_2, send_2 = backward(2, 2)
+    keep_2, send_2 = backward(2, 6)
     recv, keep_2, send_2, own, own_cols = in_order(recv, keep_2, send_2, own, own_cols)
     part = add_z(part, recv, 2)
     far = along_tensor(jnp.concatenate([send_0, send_1, send_2], axis=1), CORE)
@@ -451,8 +502,8 @@
     moved = (
         adapter_scale
         * (
-            flipped_product(gate_factor_gate, a_gate.astype(BF16))
-            + flipped_product(gate_factor_up, a_up.astype(BF16))
+            flipped_product(gate_factor_gate, a_gate)
+            + flipped_product(gate_factor_up, a_up)
         )
     ).astype(BF16)
 

time: 108 us -> 105 us (0.972)
  waiting for transfers between devices: 14.5 us -> 12.1 us
  local copies, waits for them, and re-layouts: 3.21 us -> 0.89 us
  Pallas kernels: 40.4 us -> 41.5 us
    unnamed x13 -> x7, local copies, waits for them, and re-layouts: 2.43 us -> 0.1 us
    ppermute x18, waiting for transfers between devices: 8.1 us -> 6.25 us  [along_tensor(): return lax.ppermute(value, 'tensor', [(i, i ^ mask) for i in range(N)])]
    pallas_call x2 -> x3, Pallas kernels: 9.2 us -> 10.8 us  [the longest x2 8.48 us: hidden_gradients(): pl.pallas_call(functools.partial(hidden_kernel, first, step), in_specs=[v...]
  transfers between devices with their start and end apart: 26 -> 26, of which waited for: 11 -> 11; matrix products, arithmetic and copies ran while one was open for 13% -> 13% of each run, Pallas kernels for 35% -> 38%
where the time goes in v9:
time: 105 us; the launch traced here: 104 us
  Pallas kernels  41.5 us (40%)
  starting transfers between devices  30.2 us (29%)
  matrix products  13.7 us (13%)
  waiting for transfers between devices  12.1 us (12%)
  other arithmetic  4.53 us (4%)
  between operations  1.33 us (1%)
    ppermute x18, starting transfers between devices, along_tensor(): return lax.ppermute(value, 'tensor', [(i, i ^ mask) for i in range(N)])  21.2 us
    pallas_call x3, Pallas kernels, backward_products(): pl.pallas_call(functools.partial(backward_kernel, first), in_specs=[pl.Bl...  16.3 us
    pallas_call x4, Pallas kernels, forward_products(): pl.pallas_call(functools.partial(forward_kernel, first), in_specs=[pl.Blo...  14.4 us
    dot_general x4, matrix products, rows_product(): lax.dot_general(left, right, (((0,), (0,)), ((), ())), preferred_element_...  12 us
    ppermute x8, starting transfers between devices, across_groups(): lax.ppermute(value, both, [(i, i ^ (N | mask)) for i in range(2 * N)])  9.05 us
    pallas_call x2, Pallas kernels, hidden_gradients(): pl.pallas_call(functools.partial(hidden_kernel, first, step), in_specs=[v...  8.48 us
    ppermute x18, waiting for transfers between devices, along_tensor(): return lax.ppermute(value, 'tensor', [(i, i ^ mask) for i in range(N)])  6.25 us
    ppermute x8, waiting for transfers between devices, across_groups(): lax.ppermute(value, both, [(i, i ^ (N | mask)) for i in range(2 * N)])  5.86 us
  transfers between devices with their start and end apart: 26, of which 11 were waited for; matrix products, arithmetic and copies ran while one was open for 13% of the time, Pallas kernels for 38%

profile of v9, /device:TPU:0, one launch (start us, length us, event | category | flops | bytes accessed | tf_op | source)
XLA Modules:
  0.0 104.3 jit_solution(13532852900769460175)
XLA Ops:
  0.6 3.1 %collective-permute-start = (bf16[2,8192]{1,0:T(2,128)(2,1)}, bf16[2,8192]{1,0:T(2,128)(2,1)S(1)}, u32[]{:S(2)}, u32[]{:S(2)}) collective-permute-start(bf16[2,8192]{1,0:T(2,128)(2,1)} %param.9), channel_id=1, source_target_pairs={{0,4},{1,5},{2,6},{3,7},{4,0},{5,1},{6,2},{7,3},{8,12},{9,13},{10,... | collective-permute-start | bytes 98312 | tf_op jit(solution)/shard_map/ppermute | solution.py:343
  3.7 2.3 %narrow.1 = (bf16[512,1024]{1,0:T(8,128)(2,1)S(1)}, bf16[512,1024]{1,0:T(8,128)(2,1)S(1)}) custom-call(f32[512,1024]{1,0:T(8,128)} %g_ref.1, f32[512,1024]{1,0:T(8,128)} %u_ref.1), custom_call_target="tpu_custom_call" | custom-call | bytes 6291456 | tf_op jit(solution)/shard_map/narrow/pallas_call | solution.py:169
  6.0 0.8 pad_maximum_fusion.8
  6.9 2.9 %collective-permute-start.1 = (bf16[4,8192]{1,0:T(4,128)(2,1)S(1)}, bf16[4,8192]{1,0:T(4,128)(2,1)S(1)}, u32[]{:S(2)}, u32[]{:S(2)}) collective-permute-start(bf16[4,8192]{1,0:T(4,128)(2,1)S(1)} %pad_maximum_fusion.8), channel_id=1, source_target_pairs={{0,8},{1,9},{2,10},{3,11},{4,12},{5,13},{6,14},{7,15},{8,0},{9,1},... | collective-permute-start | bytes 196616 | tf_op jit(solution)/shard_map/ppermute | solution.py:343
  9.8 2.3 %collective-permute-done.1 = bf16[4,8192]{1,0:T(4,128)(2,1)S(1)} collective-permute-done((bf16[4,8192]{1,0:T(4,128)(2,1)S(1)}, bf16[4,8192]{1,0:T(4,128)(2,1)S(1)}, u32[]{:S(2)}, u32[]{:S(2)}) %collective-permute-start.1) | collective-permute-done | bytes 65568 | tf_op jit(solution)/shard_map/ppermute | solution.py:343
  12.1 0.9 pad_maximum_fusion.6
  13.0 1.8 %collective-permute-start.2 = (bf16[8,4096]{1,0:T(8,128)(2,1)S(1)}, bf16[8,4096]{1,0:T(8,128)(2,1)S(1)}, u32[]{:S(2)}, u32[]{:S(2)}) collective-permute-start(bf16[8,4096]{1,0:T(8,128)(2,1)S(1)} %get-tuple-element.171), channel_id=1, source_target_pairs={{0,2},{1,3},{2,0},{3,1},{4,6},{5,7},{6,4},{7,5},{8,10},{9,11},{10,... | collective-permute-start | bytes 196616 | tf_op jit(solution)/shard_map/ppermute | solution.py:343
  14.8 1.5 %collective-permute-start.4 = (bf16[8,4096]{1,0:T(8,128)(2,1)S(1)}, bf16[8,4096]{1,0:T(8,128)(2,1)S(1)}, u32[]{:S(2)}, u32[]{:S(2)}) collective-permute-start(bf16[8,4096]{1,0:T(8,128)(2,1)S(1)} %get-tuple-element.172), channel_id=1, source_target_pairs={{0,18},{1,19},{2,16},{3,17},{4,22},{5,23},{6,20},{7,21},{8,26},{9,... | collective-permute-start | bytes 196616 | tf_op jit(solution)/shard_map/ppermute | solution.py:348
  16.6 1.2 %collective-permute-done.2 = bf16[8,4096]{1,0:T(8,128)(2,1)S(1)} collective-permute-done((bf16[8,4096]{1,0:T(8,128)(2,1)S(1)}, bf16[8,4096]{1,0:T(8,128)(2,1)S(1)}, u32[]{:S(2)}, u32[]{:S(2)}) %collective-permute-start.2) | collective-permute-done | bytes 65568 | tf_op jit(solution)/shard_map/ppermute | solution.py:343
  17.8 2.2 %collective-permute-done.4 = bf16[8,4096]{1,0:T(8,128)(2,1)S(1)} collective-permute-done((bf16[8,4096]{1,0:T(8,128)(2,1)S(1)}, bf16[8,4096]{1,0:T(8,128)(2,1)S(1)}, u32[]{:S(2)}, u32[]{:S(2)}) %collective-permute-start.4) | collective-permute-done | bytes 65568 | tf_op jit(solution)/shard_map/ppermute | solution.py:348
  20.0 0.7 collective-permute-done.3
  20.9 0.8 select_reduce_fusion
  21.7 0.6 collective-permute-done.5
  22.4 0.9 collective-permute-start.6
  23.3 3.9 %forward_products.4 = (f32[2,32,512]{2,1,0:T(8,128)S(1)}, bf16[2,32,512]{2,1,0:T(8,128)(2,1)S(1)}) custom-call(s32[1]{0:T(128)} %bitcast.3.side_ref, bf16[64,4096]{1,0:T(8,128)(2,1)S(1)} %bitcast.60, bf16[8192,1792]{1,0:T(8,128)(2,1)} %wg_ref.13, bf16[8192,1792]{1,0:T(8,128)(2,1)} %wu_ref.13), custom_call_target="tpu_custom_call" | custom-call | flops 536870912 | bytes 12582912 | tf_op jit(solution)/shard_map/forward_products/pallas_call | solution.py:136
  28.4 0.9 collective-permute-done.7
  29.3 1.2 %collective-permute-start.8 = (f32[32,128]{1,0:T(8,128)S(1)}, f32[32,128]{1,0:T(8,128)S(1)}, u32[]{:S(2)}, u32[]{:S(2)}) collective-permute-start(f32[32,128]{1,0:T(8,128)S(1)} %maximum_add_fusion.1), channel_id=1, source_target_pairs={{0,2},{1,3},{2,0},{3,1},{4,6},{5,7},{6,4},{7,5},{8,10},{9,11},{10,... | collective-permute-start | bytes 49160 | tf_op jit(solution)/shard_map/ppermute | solution.py:343
  30.5 3.8 %forward_products.5 = (f32[2,32,512]{2,1,0:T(8,128)S(1)}, bf16[2,32,512]{2,1,0:T(8,128)(2,1)S(1)}) custom-call(s32[1]{0:T(128)} %bitcast.3.side_ref, bf16[64,4096]{1,0:T(8,128)(2,1)S(1)} %bitcast.62, bf16[8192,1792]{1,0:T(8,128)(2,1)} %wg_ref.13, bf16[8192,1792]{1,0:T(8,128)(2,1)} %wu_ref.13), custom_call_target="tpu_custom_call" | custom-call | flops 536870912 | bytes 12582912 | tf_op jit(solution)/shard_map/forward_products/pallas_call | solution.py:136
  34.4 1.6 %collective-permute-start.9 = (f32[32,128]{1,0:T(8,128)S(1)}, f32[32,128]{1,0:T(8,128)S(1)}, u32[]{:S(2)}, u32[]{:S(2)}) collective-permute-start(f32[32,128]{1,0:T(8,128)S(1)} %maximum_add_fusion.2), channel_id=1, source_target_pairs={{0,4},{1,5},{2,6},{3,7},{4,0},{5,1},{6,2},{7,3},{8,12},{9,13},{10,... | collective-permute-start | bytes 49160 | tf_op jit(solution)/shard_map/ppermute | solution.py:343
  36.0 3.8 %forward_products.6 = (f32[2,32,512]{2,1,0:T(8,128)S(1)}, bf16[2,32,512]{2,1,0:T(8,128)(2,1)S(1)}) custom-call(s32[1]{0:T(128)} %bitcast.3.side_ref, bf16[64,4096]{1,0:T(8,128)(2,1)S(1)} %bitcast.63, bf16[8192,1792]{1,0:T(8,128)(2,1)} %wg_ref.13, bf16[8192,1792]{1,0:T(8,128)(2,1)} %wu_ref.13), custom_call_target="tpu_custom_call" | custom-call | flops 536870912 | bytes 12582912 | tf_op jit(solution)/shard_map/forward_products/pallas_call | solution.py:136
  39.9 3.2 %collective-permute-start.11 = (f32[32,128]{1,0:T(8,128)S(1)}, f32[32,128]{1,0:T(8,128)S(1)}, u32[]{:S(2)}, u32[]{:S(2)}) collective-permute-start(f32[32,128]{1,0:T(8,128)S(1)} %add.222), channel_id=1, source_target_pairs={{0,8},{1,9},{2,10},{3,11},{4,12},{5,13},{6,14},{7,15},{8,0},{9,1},... | collective-permute-start | bytes 49160 | tf_op jit(solution)/shard_map/ppermute | solution.py:343
  43.2 1.4 %collective-permute-start.10 = (bf16[2,32,1536]{2,1,0:T(8,128)(2,1)S(1)}, bf16[2,32,1536]{2,1,0:T(8,128)(2,1)S(1)}, u32[]{:S(2)}, u32[]{:S(2)}) collective-permute-start(bf16[2,32,1536]{2,1,0:T(8,128)(2,1)S(1)} %pad_maximum_fusion.5), channel_id=1, source_target_pairs={{0,16},{1,17},{2,18},{3,19},{4,20},{5,21},{6,22},{7,23},{8,24},{9,... | collective-permute-start | bytes 589832 | tf_op jit(solution)/shard_map/ppermute | solution.py:348
  44.6 2.8 %forward_products.7 = (f32[2,32,256]{2,1,0:T(8,128)S(1)}, bf16[2,32,256]{2,1,0:T(8,128)(2,1)S(1)}) custom-call(s32[1]{0:T(128)} %bitcast.3.side_ref, bf16[64,4096]{1,0:T(8,128)(2,1)S(1)} %bitcast.64, bf16[8192,1792]{1,0:T(8,128)(2,1)} %wg_ref.13, bf16[8192,1792]{1,0:T(8,128)(2,1)} %wu_ref.13), custom_call_target="tpu_custom_call" | custom-call | flops 268435456 | bytes 6291456 | tf_op jit(solution)/shard_map/forward_products/pallas_call | solution.py:136
  47.4 2.0 %collective-permute-done.10.far_ref = bf16[2,32,1536]{2,1,0:T(8,128)(2,1)S(1)} collective-permute-done((bf16[2,32,1536]{2,1,0:T(8,128)(2,1)S(1)}, bf16[2,32,1536]{2,1,0:T(8,128)(2,1)S(1)}, u32[]{:S(2)}, u32[]{:S(2)}) %collective-permute-start.10) | collective-permute-done | bytes 196640 | tf_op jit(solution)/shard_map/ppermute | solution.py:348
  49.5 1.3 %collective-permute-start.12 = (bf16[2,32,256]{2,1,0:T(8,128)(2,1)S(1)}, bf16[2,32,256]{2,1,0:T(8,128)(2,1)S(1)}, u32[]{:S(2)}, u32[]{:S(2)}) collective-permute-start(bf16[2,32,256]{2,1,0:T(8,128)(2,1)S(1)} %get-tuple-element.114), channel_id=1, source_target_pairs={{0,16},{1,17},{2,18},{3,19},{4,20},{5,21},{6,22},{7,23},{8,24},{9,... | collective-permute-start | bytes 98312 | tf_op jit(solution)/shard_map/ppermute | solution.py:348
  51.1 6.2 %hidden_gradients.2 = (bf16[2,32,1536]{2,1,0:T(8,128)(2,1)S(1)}, f32[32,1024]{1,0:T(8,128)S(1)}, f32[32,1024]{1,0:T(8,128)S(1)}) custom-call(bf16[32,1024]{1,0:T(8,128)(2,1)S(1)} %get-tuple-element.209.eug_ref, bf16[32,1024]{1,0:T(8,128)(2,1)S(1)} %get-tuple-element.210.euu_ref, f32[2,32,1536]{2,1,0:T(8,128)S(1)} %pad_maximum_fusion.1.keep_ref, ...), custom_call_target="tpu_custom_call" | custom-call | flops 402653184 | bytes 18874368 | tf_op jit(solution)/shard_map/hidden_gradients/pallas_call | solution.py:244
  57.3 2.3 %hidden_gradients.3 = (bf16[2,32,256]{2,1,0:T(8,128)(2,1)S(1)}, f32[32,1024]{1,0:T(8,128)S(1)}, f32[32,1024]{1,0:T(8,128)S(1)}) custom-call(bf16[32,1024]{1,0:T(8,128)(2,1)S(1)} %get-tuple-element.209.eug_ref, bf16[32,1024]{1,0:T(8,128)(2,1)S(1)} %get-tuple-element.210.euu_ref, f32[2,32,256]{2,1,0:T(8,128)S(1)} %get-tuple-element.113.keep_ref, ...), custom_call_target="tpu_custom_call" | custom-call | flops 67108864 | bytes 3145728 | tf_op jit(solution)/shard_map/hidden_gradients/pallas_call | solution.py:244
  59.9 0.8 collective-permute-start.13
  60.8 4.2 %convolution_multiply_fusion.1 = f32[1024,1792]{1,0:T(8,128)} fusion(bf16[32,1024]{1,0:T(8,128)(2,1)S(1)} %get-tuple-element.209.eug_ref, bf16[2,32,1792]{2,1,0:T(8,128)(2,1)S(1)} %constant_dynamic-update-slice_fusion), kind=kOutput, calls=%fused_computation.1 | convolution fusion | flops 119275520 | bytes 7520256 | tf_op jit(solution)/shard_map/dot_general | solution.py:39
  65.1 1.0 collective-permute-done.13
  66.1 0.7 collective-permute-start.15
  66.8 3.3 %backward_products.3 = (f32[32,512]{1,0:T(8,128)S(1)}, bf16[32,512]{1,0:T(8,128)(2,1)S(1)}) custom-call(s32[1]{0:T(128)} %bitcast.3.side_ref, bf16[64,1792]{1,0:T(8,128)(2,1)S(1)} %get-tuple-element.136.dg_ref, bf16[64,1792]{1,0:T(8,128)(2,1)S(1)} %get-tuple-element.137.du_ref, bf16[8192,1792]{1,0:T(8,128)(2,1)} %wg_ref.13, bf16[8192,1792]{1,0:T(8,128)(2,1)} %wu_ref.13), custom_call_target="tpu_custom_call" | custom-call | flops 234881024 | bytes 5505024 | tf_op jit(solution)/shard_map/backward_products/pallas_call | solution.py:312
  70.1 0.4 collective-permute-start.16
  70.5 3.3 %backward_products.4 = (f32[32,512]{1,0:T(8,128)S(1)}, bf16[32,512]{1,0:T(8,128)(2,1)S(1)}) custom-call(s32[1]{0:T(128)} %bitcast.3.side_ref, bf16[64,1792]{1,0:T(8,128)(2,1)S(1)} %get-tuple-element.136.dg_ref, bf16[64,1792]{1,0:T(8,128)(2,1)S(1)} %get-tuple-element.137.du_ref, bf16[8192,1792]{1,0:T(8,128)(2,1)} %wg_ref.13, bf16[8192,1792]{1,0:T(8,128)(2,1)} %wu_ref.13), custom_call_target="tpu_custom_call" | custom-call | flops 234881024 | bytes 5505024 | tf_op jit(solution)/shard_map/backward_products/pallas_call | solution.py:312
  74.3 9.8 %backward_products.5 = (f32[32,3072]{1,0:T(8,128)S(1)}, bf16[32,3072]{1,0:T(8,128)(2,1)S(1)}) custom-call(s32[1]{0:T(128)} %bitcast.3.side_ref, bf16[64,1792]{1,0:T(8,128)(2,1)S(1)} %get-tuple-element.136.dg_ref, bf16[64,1792]{1,0:T(8,128)(2,1)S(1)} %get-tuple-element.137.du_ref, bf16[8192,1792]{1,0:T(8,128)(2,1)} %wg_ref.13, bf16[8192,1792]{1,0:T(8,128)(2,1)} %wu_ref.13), custom_call_target="tpu_custom_call" | custom-call | flops 1409286144 | bytes 33030144 | tf_op jit(solution)/shard_map/backward_products/pallas_call | solution.py:312
  84.5 0.4 fusion.38
  85.0 0.4 fusion.1
  85.5 0.6 collective-permute-start.19
  86.0 0.8 collective-permute-done.19
  86.9 1.6 %collective-permute-start.22 = (bf16[8,4096]{1,0:T(8,128)(2,1)S(1)}, bf16[8,4096]{1,0:T(8,128)(2,1)S(1)}, u32[]{:S(2)}, u32[]{:S(2)}) collective-permute-start(bf16[8,4096]{1,0:T(8,128)(2,1)S(1)} %get-tuple-element.165), channel_id=1, source_target_pairs={{0,18},{1,19},{2,16},{3,17},{4,22},{5,23},{6,20},{7,21},{8,26},{9,... | collective-permute-start | bytes 196616 | tf_op jit(solution)/shard_map/ppermute | solution.py:348
  88.6 1.3 %collective-permute-start.21 = (bf16[8,4096]{1,0:T(8,128)(2,1)S(1)}, bf16[8,4096]{1,0:T(8,128)(2,1)S(1)}, u32[]{:S(2)}, u32[]{:S(2)}) collective-permute-start(bf16[8,4096]{1,0:T(8,128)(2,1)S(1)} %get-tuple-element.166), channel_id=1, source_target_pairs={{0,16},{1,17},{2,18},{3,19},{4,20},{5,21},{6,22},{7,23},{8,24},{9,... | collective-permute-start | bytes 196616 | tf_op jit(solution)/shard_map/ppermute | solution.py:348
  89.9 0.7 collective-permute-start.20
  90.6 1.8 %convolution_multiply_fusion.2 = f32[512,1024]{1,0:T(8,128)} fusion(bf16[32,512]{1,0:T(8,128)(2,1)S(1)} %dynamic-slice_select_fusion, bf16[32,1024]{1,0:T(8,128)(2,1)S(1)} %concatenate.105, s32[1024]{0:T(1024)S(1)} %add_select_fusion, s32[32]{0:T(128)S(1)} %select_reduce_fusion), kind=kOutput, calls=%fused_computation.2 | convolution fusion | flops 34144256 | bytes 2199680 | tf_op jit(solution)/shard_map/dot_general | solution.py:39
  92.4 1.8 %convolution_multiply_fusion.3 = f32[512,1024]{1,0:T(8,128)} fusion(bf16[32,512]{1,0:T(8,128)(2,1)S(1)} %dynamic-slice_select_fusion, bf16[32,1024]{1,0:T(8,128)(2,1)S(1)} %concatenate.104, s32[1024]{0:T(1024)S(1)} %add_select_fusion, s32[32]{0:T(128)S(1)} %select_reduce_fusion), kind=kOutput, calls=%fused_computation.3 | convolution fusion | flops 34144256 | bytes 2199680 | tf_op jit(solution)/shard_map/dot_general | solution.py:39
  94.6 3.7 %collective-permute-start.25 = (bf16[2,10240]{1,0:T(2,128)(2,1)S(1)}, bf16[2,10240]{1,0:T(2,128)(2,1)S(1)}, u32[]{:S(2)}, u32[]{:S(2)}) collective-permute-start(bf16[2,10240]{1,0:T(2,128)(2,1)S(1)} %get-tuple-element.168), channel_id=1, source_target_pairs={{0,12},{1,13},{2,14},{3,15},{4,8},{5,9},{6,10},{7,11},{8,4},{9,5},... | collective-permute-start | bytes 122888 | tf_op jit(solution)/shard_map/ppermute | solution.py:343
  98.3 0.7 collective-permute-start.23
  99.0 4.2 %convolution_multiply_fusion = f32[1024,1792]{1,0:T(8,128)} fusion(bf16[32,1024]{1,0:T(8,128)(2,1)S(1)} %get-tuple-element.210.euu_ref, bf16[2,32,1792]{2,1,0:T(8,128)(2,1)S(1)} %constant_dynamic-update-slice_fusion), kind=kOutput, calls=%fused_computation | convolution fusion | flops 119275520 | bytes 7520256 | tf_op jit(solution)/shard_map/dot_general | solution.py:39
  103.6 0.7 fusion.14
  (107 shorter events, 4.3 us)
Async XLA Ops:
  0.6 27.5 %copy-start = (bf16[32,1792]{1,0:T(8,128)(2,1)S(1)}, bf16[32,1792]{1,0:T(8,128)(2,1)}, u32[]{:S(2)}) copy-start(bf16[32,1792]{1,0:T(8,128)(2,1)} %param.17) | copy-start | bytes 344068
  0.6 5.4 %collective-permute-start = (bf16[2,8192]{1,0:T(2,128)(2,1)}, bf16[2,8192]{1,0:T(2,128)(2,1)S(1)}, u32[]{:S(2)}, u32[]{:S(2)}) collective-permute-start(bf16[2,8192]{1,0:T(2,128)(2,1)} %param.9), channel_id=1, source_target_pairs={{0,4},{1,5},{2,6},{3,7},{4,0},{5,1},{6,2},{7,3},{8,12},{9,13},{10,... | collective-permute-start | bytes 98312 | tf_op jit(solution)/shard_map/ppermute | solution.py:343
  6.9 5.2 %collective-permute-start.1 = (bf16[4,8192]{1,0:T(4,128)(2,1)S(1)}, bf16[4,8192]{1,0:T(4,128)(2,1)S(1)}, u32[]{:S(2)}, u32[]{:S(2)}) collective-permute-start(bf16[4,8192]{1,0:T(4,128)(2,1)S(1)} %pad_maximum_fusion.8), channel_id=1, source_target_pairs={{0,8},{1,9},{2,10},{3,11},{4,12},{5,13},{6,14},{7,15},{8,0},{9,1},... | collective-permute-start | bytes 196616 | tf_op jit(solution)/shard_map/ppermute | solution.py:343
  13.0 4.7 %collective-permute-start.2 = (bf16[8,4096]{1,0:T(8,128)(2,1)S(1)}, bf16[8,4096]{1,0:T(8,128)(2,1)S(1)}, u32[]{:S(2)}, u32[]{:S(2)}) collective-permute-start(bf16[8,4096]{1,0:T(8,128)(2,1)S(1)} %get-tuple-element.171), channel_id=1, source_target_pairs={{0,2},{1,3},{2,0},{3,1},{4,6},{5,7},{6,4},{7,5},{8,10},{9,11},{10,... | collective-permute-start | bytes 196616 | tf_op jit(solution)/shard_map/ppermute | solution.py:343
  14.8 5.2 %collective-permute-start.4 = (bf16[8,4096]{1,0:T(8,128)(2,1)S(1)}, bf16[8,4096]{1,0:T(8,128)(2,1)S(1)}, u32[]{:S(2)}, u32[]{:S(2)}) collective-permute-start(bf16[8,4096]{1,0:T(8,128)(2,1)S(1)} %get-tuple-element.172), channel_id=1, source_target_pairs={{0,18},{1,19},{2,16},{3,17},{4,22},{5,23},{6,20},{7,21},{8,26},{9,... | collective-permute-start | bytes 196616 | tf_op jit(solution)/shard_map/ppermute | solution.py:348
  16.3 4.4 %collective-permute-start.3 = (bf16[8,4096]{1,0:T(8,128)(2,1)S(1)}, bf16[8,4096]{1,0:T(8,128)(2,1)S(1)}, u32[]{:S(2)}, u32[]{:S(2)}) collective-permute-start(bf16[8,4096]{1,0:T(8,128)(2,1)S(1)} %get-tuple-element.172), channel_id=1, source_target_pairs={{0,16},{1,17},{2,18},{3,19},{4,20},{5,21},{6,22},{7,23},{8,24},{9,... | collective-permute-start | bytes 196616 | tf_op jit(solution)/shard_map/ppermute | solution.py:348
  20.7 1.6 %collective-permute-start.5 = (bf16[2,16,4096]{2,1,0:T(8,128)(2,1)S(1)}, bf16[2,16,4096]{2,1,0:T(8,128)(2,1)S(1)}, u32[]{:S(2)}, u32[]{:S(2)}) collective-permute-start(bf16[2,16,4096]{2,1,0:T(8,128)(2,1)S(1)} %pad_maximum_fusion.3), channel_id=1, source_target_pairs={{0,1},{1,0},{2,3},{3,2},{4,5},{5,4},{6,7},{7,6},{8,9},{9,8},{10,11... | collective-permute-start | bytes 786440 | tf_op jit(solution)/shard_map/ppermute | solution.py:343
  22.4 4.9 %collective-permute-start.6 = (bf16[32,512]{1,0:T(8,128)(2,1)S(1)}, bf16[32,512]{1,0:T(8,128)(2,1)S(1)}, u32[]{:S(2)}, u32[]{:S(2)}) collective-permute-start(bf16[32,512]{1,0:T(8,128)(2,1)S(1)} %dynamic-slice.1), channel_id=1, source_target_pairs={{0,16},{1,17},{2,18},{3,19},{4,20},{5,21},{6,22},{7,23},{8,24},{9,... | collective-permute-start | bytes 98312 | tf_op jit(solution)/shard_map/ppermute | solution.py:348
  28.1 1.2 %collective-permute-start.7 = (f32[32,128]{1,0:T(8,128)S(1)}, f32[32,128]{1,0:T(8,128)S(1)}, u32[]{:S(2)}, u32[]{:S(2)}) collective-permute-start(f32[32,128]{1,0:T(8,128)S(1)} %pad_maximum_fusion.15), channel_id=1, source_target_pairs={{0,1},{1,0},{2,3},{3,2},{4,5},{5,4},{6,7},{7,6},{8,9},{9,8},{10,11... | collective-permute-start | bytes 49160 | tf_op jit(solution)/shard_map/ppermute | solution.py:343
  29.3 5.0 %collective-permute-start.8 = (f32[32,128]{1,0:T(8,128)S(1)}, f32[32,128]{1,0:T(8,128)S(1)}, u32[]{:S(2)}, u32[]{:S(2)}) collective-permute-start(f32[32,128]{1,0:T(8,128)S(1)} %maximum_add_fusion.1), channel_id=1, source_target_pairs={{0,2},{1,3},{2,0},{3,1},{4,6},{5,7},{6,4},{7,5},{8,10},{9,11},{10,... | collective-permute-start | bytes 49160 | tf_op jit(solution)/shard_map/ppermute | solution.py:343
  34.4 5.5 %collective-permute-start.9 = (f32[32,128]{1,0:T(8,128)S(1)}, f32[32,128]{1,0:T(8,128)S(1)}, u32[]{:S(2)}, u32[]{:S(2)}) collective-permute-start(f32[32,128]{1,0:T(8,128)S(1)} %maximum_add_fusion.2), channel_id=1, source_target_pairs={{0,4},{1,5},{2,6},{3,7},{4,0},{5,1},{6,2},{7,3},{8,12},{9,13},{10,... | collective-permute-start | bytes 49160 | tf_op jit(solution)/shard_map/ppermute | solution.py:343
  39.9 7.5 %collective-permute-start.11 = (f32[32,128]{1,0:T(8,128)S(1)}, f32[32,128]{1,0:T(8,128)S(1)}, u32[]{:S(2)}, u32[]{:S(2)}) collective-permute-start(f32[32,128]{1,0:T(8,128)S(1)} %add.222), channel_id=1, source_target_pairs={{0,8},{1,9},{2,10},{3,11},{4,12},{5,13},{6,14},{7,15},{8,0},{9,1},... | collective-permute-start | bytes 49160 | tf_op jit(solution)/shard_map/ppermute | solution.py:343
  43.2 6.2 %collective-permute-start.10 = (bf16[2,32,1536]{2,1,0:T(8,128)(2,1)S(1)}, bf16[2,32,1536]{2,1,0:T(8,128)(2,1)S(1)}, u32[]{:S(2)}, u32[]{:S(2)}) collective-permute-start(bf16[2,32,1536]{2,1,0:T(8,128)(2,1)S(1)} %pad_maximum_fusion.5), channel_id=1, source_target_pairs={{0,16},{1,17},{2,18},{3,19},{4,20},{5,21},{6,22},{7,23},{8,24},{9,... | collective-permute-start | bytes 589832 | tf_op jit(solution)/shard_map/ppermute | solution.py:348
  49.5 7.8 %collective-permute-start.12 = (bf16[2,32,256]{2,1,0:T(8,128)(2,1)S(1)}, bf16[2,32,256]{2,1,0:T(8,128)(2,1)S(1)}, u32[]{:S(2)}, u32[]{:S(2)}) collective-permute-start(bf16[2,32,256]{2,1,0:T(8,128)(2,1)S(1)} %get-tuple-element.114), channel_id=1, source_target_pairs={{0,16},{1,17},{2,18},{3,19},{4,20},{5,21},{6,22},{7,23},{8,24},{9,... | collective-permute-start | bytes 98312 | tf_op jit(solution)/shard_map/ppermute | solution.py:348
  59.9 6.1 %collective-permute-start.13 = (bf16[2,32,1792]{2,1,0:T(8,128)(2,1)S(1)}, bf16[2,32,1792]{2,1,0:T(8,128)(2,1)S(1)}, u32[]{:S(2)}, u32[]{:S(2)}) collective-permute-start(bf16[2,32,1792]{2,1,0:T(8,128)(2,1)S(1)} %constant_dynamic-update-slice_fusion), channel_id=1, source_target_pairs={{0,16},{1,17},{2,18},{3,19},{4,20},{5,21},{6,22},{7,23},{8,24},{9,... | collective-permute-start | bytes 688136 | tf_op jit(solution)/shard_map/ppermute | solution.py:348
  60.8 4.2 %collective-permute-start.14 = (f32[32,128]{1,0:T(8,128)S(1)}, f32[32,128]{1,0:T(8,128)S(1)}, u32[]{:S(2)}, u32[]{:S(2)}) collective-permute-start(f32[32,128]{1,0:T(8,128)S(1)} %pad_maximum_fusion.18), channel_id=1, source_target_pairs={{0,1},{1,0},{2,3},{3,2},{4,5},{5,4},{6,7},{7,6},{8,9},{9,8},{10,11... | collective-permute-start | bytes 49160 | tf_op jit(solution)/shard_map/ppermute | solution.py:343
  66.1 4.0 %collective-permute-start.15 = (f32[32,128]{1,0:T(8,128)S(1)}, f32[32,128]{1,0:T(8,128)S(1)}, u32[]{:S(2)}, u32[]{:S(2)}) collective-permute-start(f32[32,128]{1,0:T(8,128)S(1)} %maximum_add_fusion.3), channel_id=1, source_target_pairs={{0,2},{1,3},{2,0},{3,1},{4,6},{5,7},{6,4},{7,5},{8,10},{9,11},{10,... | collective-permute-start | bytes 49160 | tf_op jit(solution)/shard_map/ppermute | solution.py:343
  70.1 3.8 %collective-permute-start.16 = (f32[32,128]{1,0:T(8,128)S(1)}, f32[32,128]{1,0:T(8,128)S(1)}, u32[]{:S(2)}, u32[]{:S(2)}) collective-permute-start(f32[32,128]{1,0:T(8,128)S(1)} %maximum_add_fusion.4), channel_id=1, source_target_pairs={{0,4},{1,5},{2,6},{3,7},{4,0},{5,1},{6,2},{7,3},{8,12},{9,13},{10,... | collective-permute-start | bytes 49160 | tf_op jit(solution)/shard_map/ppermute | solution.py:343
  74.0 10.1 %collective-permute-start.17 = (f32[32,128]{1,0:T(8,128)S(1)}, f32[32,128]{1,0:T(8,128)S(1)}, u32[]{:S(2)}, u32[]{:S(2)}) collective-permute-start(f32[32,128]{1,0:T(8,128)S(1)} %add.244), channel_id=1, source_target_pairs={{0,8},{1,9},{2,10},{3,11},{4,12},{5,13},{6,14},{7,15},{8,0},{9,1},... | collective-permute-start | bytes 49160 | tf_op jit(solution)/shard_map/ppermute | solution.py:343
  84.9 1.9 %collective-permute-start.18 = (bf16[32,4096]{1,0:T(8,128)(2,1)S(1)}, bf16[32,4096]{1,0:T(8,128)(2,1)S(1)}, u32[]{:S(2)}, u32[]{:S(2)}) collective-permute-start(bf16[32,4096]{1,0:T(8,128)(2,1)S(1)} %pad_maximum_fusion.4), channel_id=1, source_target_pairs={{0,1},{1,0},{2,3},{3,2},{4,5},{5,4},{6,7},{7,6},{8,9},{9,8},{10,11... | collective-permute-start | bytes 786440 | tf_op jit(solution)/shard_map/ppermute | solution.py:343
  85.5 1.4 %collective-permute-start.19 = (bf16[16,512]{1,0:T(8,128)(2,1)S(1)}, bf16[16,512]{1,0:T(8,128)(2,1)S(1)}, u32[]{:S(2)}, u32[]{:S(2)}) collective-permute-start(bf16[16,512]{1,0:T(8,128)(2,1)S(1)} %get-tuple-element.178), channel_id=1, source_target_pairs={{0,1},{1,0},{2,3},{3,2},{4,5},{5,4},{6,7},{7,6},{8,9},{9,8},{10,11... | collective-permute-start | bytes 49160 | tf_op jit(solution)/shard_map/ppermute | solution.py:343
  86.9 7.2 %collective-permute-start.22 = (bf16[8,4096]{1,0:T(8,128)(2,1)S(1)}, bf16[8,4096]{1,0:T(8,128)(2,1)S(1)}, u32[]{:S(2)}, u32[]{:S(2)}) collective-permute-start(bf16[8,4096]{1,0:T(8,128)(2,1)S(1)} %get-tuple-element.165), channel_id=1, source_target_pairs={{0,18},{1,19},{2,16},{3,17},{4,22},{5,23},{6,20},{7,21},{8,26},{9,... | collective-permute-start | bytes 196616 | tf_op jit(solution)/shard_map/ppermute | solution.py:348
  88.6 5.6 %collective-permute-start.21 = (bf16[8,4096]{1,0:T(8,128)(2,1)S(1)}, bf16[8,4096]{1,0:T(8,128)(2,1)S(1)}, u32[]{:S(2)}, u32[]{:S(2)}) collective-permute-start(bf16[8,4096]{1,0:T(8,128)(2,1)S(1)} %get-tuple-element.166), channel_id=1, source_target_pairs={{0,16},{1,17},{2,18},{3,19},{4,20},{5,21},{6,22},{7,23},{8,24},{9,... | collective-permute-start | bytes 196616 | tf_op jit(solution)/shard_map/ppermute | solution.py:348
  89.9 4.5 %collective-permute-start.20 = (bf16[8,5120]{1,0:T(8,128)(2,1)S(1)}, bf16[8,5120]{1,0:T(8,128)(2,1)S(1)}, u32[]{:S(2)}, u32[]{:S(2)}) collective-permute-start(bf16[8,5120]{1,0:T(8,128)(2,1)S(1)} %pad_maximum_fusion.7), channel_id=1, source_target_pairs={{0,2},{1,3},{2,0},{3,1},{4,6},{5,7},{6,4},{7,5},{8,10},{9,11},{10,... | collective-permute-start | bytes 245768 | tf_op jit(solution)/shard_map/ppermute | solution.py:343
  94.4 9.9 %copy-start.1 = (bf16[32,1792]{1,0:T(8,128)(2,1)S(1)}, bf16[32,1792]{1,0:T(8,128)(2,1)}, u32[]{:S(2)}) copy-start(bf16[32,1792]{1,0:T(8,128)(2,1)} %param.17) | copy-start | bytes 344068
  94.6 8.7 %collective-permute-start.25 = (bf16[2,10240]{1,0:T(2,128)(2,1)S(1)}, bf16[2,10240]{1,0:T(2,128)(2,1)S(1)}, u32[]{:S(2)}, u32[]{:S(2)}) collective-permute-start(bf16[2,10240]{1,0:T(2,128)(2,1)S(1)} %get-tuple-element.168), channel_id=1, source_target_pairs={{0,12},{1,13},{2,14},{3,15},{4,8},{5,9},{6,10},{7,11},{8,4},{9,5},... | collective-permute-start | bytes 122888 | tf_op jit(solution)/shard_map/ppermute | solution.py:343
  98.3 5.0 %collective-permute-start.24 = (bf16[2,10240]{1,0:T(2,128)(2,1)S(1)}, bf16[2,10240]{1,0:T(2,128)(2,1)S(1)}, u32[]{:S(2)}, u32[]{:S(2)}) collective-permute-start(bf16[2,10240]{1,0:T(2,128)(2,1)S(1)} %get-tuple-element.169), channel_id=1, source_target_pairs={{0,8},{1,9},{2,10},{3,11},{4,12},{5,13},{6,14},{7,15},{8,0},{9,1},... | collective-permute-start | bytes 122888 | tf_op jit(solution)/shard_map/ppermute | solution.py:343
  98.3 5.0 %collective-permute-start.23 = (bf16[2,10240]{1,0:T(2,128)(2,1)S(1)}, bf16[2,10240]{1,0:T(2,128)(2,1)S(1)}, u32[]{:S(2)}, u32[]{:S(2)}) collective-permute-start(bf16[2,10240]{1,0:T(2,128)(2,1)S(1)} %get-tuple-element.170), channel_id=1, source_target_pairs={{0,4},{1,5},{2,6},{3,7},{4,0},{5,1},{6,2},{7,3},{8,12},{9,13},{10,... | collective-permute-start | bytes 122888 | tf_op jit(solution)/shard_map/ppermute | solution.py:343

commit v10 on v9

--- a/solution.py
+++ b/solution.py
@@ -104,58 +104,53 @@
     )
 
 
-def forward_kernel(first, side_ref, x_ref, wg_ref, wu_ref, keep_ref, send_ref, piece, sem):
-    pieces, depth, count = piece.shape[1:]
-    half = keep_ref.shape[1]
+def forward_kernel(first, side_ref, x_ref, w_ref, keep_ref, send_ref, piece, sem):
+    pieces, depth, count = piece.shape
+    half = keep_ref.shape[0]
     base = side_ref[0] * (pieces * depth)
     copies = []
-    for i, w_ref in enumerate((wg_ref, wu_ref)):
-        for k in range(pieces):
-            source = pl.ds(pl.multiple_of(base + k * depth, depth), depth)
-            copy = pltpu.make_async_copy(
-                w_ref.at[source, pl.ds(first, count)], piece.at[i, k], sem.at[i, k]
-            )
-            copy.start()
-            copies.append(copy)
-    for i in range(2):
-        total = None
-        for k in range(pieces):
-            copies[i * pieces + k].wait()
-            term = jnp.dot(
-                x_ref[:, k * depth : (k + 1) * depth], piece[i, k], preferred_element_type=F32
-            )
-            total = term if total is None else total + term
-        keep_ref[i] = total[:half]
-        send_ref[i] = total[half:].astype(send_ref.dtype)
-
-
-def forward_products(side, x, gate_weight, up_weight, first, count, pieces=4):
+    for k in range(pieces):
+        source = pl.ds(pl.multiple_of(base + k * depth, depth), depth)
+        copy = pltpu.make_async_copy(w_ref.at[source, pl.ds(first, count)], piece.at[k], sem.at[k])
+        copy.start()
+        copies.append(copy)
+    total = None
+    step = 2
+    for k in range(0, pieces, step):
+        for copy in copies[k : k + step]:
+            copy.wait()
+        term = jnp.dot(
+            x_ref[:, k * depth : (k + step) * depth],
+            piece[k : k + step].reshape(step * depth, count),
+            preferred_element_type=F32,
+        )
+        total = term if total is None else total + term
+    keep_ref[...] = total[:half]
+    send_ref[...] = total[half:].astype(send_ref.dtype)
+
+
+def forward_products(side, x, weight, first, count, pieces=8):
     rows, depth = x.shape
     vmem = pl.BlockSpec(memory_space=pltpu.VMEM)
-    hbm = pl.BlockSpec(memory_space=pltpu.HBM)
     return pl.pallas_call(
         functools.partial(forward_kernel, first),
-        in_specs=[pl.BlockSpec(memory_space=pltpu.SMEM), vmem, hbm, hbm],
+        in_specs=[
+            pl.BlockSpec(memory_space=pltpu.SMEM),
+            vmem,
+            pl.BlockSpec(memory_space=pltpu.HBM),
+        ],
         out_specs=[vmem] * 2,
-        out_shape=[
-            jax.ShapeDtypeStruct((2, rows // 2, count), F32),
-            jax.ShapeDtypeStruct((2, rows // 2, count), BF16),
-        ],
+        out_shape=[jax.ShapeDtypeStruct((rows // 2, count), kind) for kind in (F32, BF16)],
         scratch_shapes=[
-            pltpu.VMEM((2, pieces, depth // pieces, count), BF16),
-            pltpu.SemaphoreType.DMA((2, pieces)),
+            pltpu.VMEM((pieces, depth // pieces, count), BF16),
+            pltpu.SemaphoreType.DMA((pieces,)),
         ],
         compiler_params=pltpu.CompilerParams(vmem_limit_bytes=20 << 20),
         cost_estimate=pl.CostEstimate(
-            flops=4 * rows * count * depth, bytes_accessed=6 * count * depth, transcendentals=0
+            flops=2 * rows * count * depth, bytes_accessed=3 * count * depth, transcendentals=0
         ),
         name="forward_products",
-    )(
-        side,
-        x,
-        pltpu.with_memory_space_constraint(gate_weight, pltpu.HBM),
-        pltpu.with_memory_space_constraint(up_weight, pltpu.HBM),
-    )
+    )(side, x, pltpu.with_memory_space_constraint(weight, pltpu.HBM))
 
 
 def narrow_kernel(g_ref, u_ref, g16_ref, u16_ref):
@@ -416,14 +411,13 @@
 
     blocks = lax.dynamic_slice_in_dim(x, (t % per_half) * feat_rows, feat_rows, 1)
     swapped = across_groups(blocks[rows:])
-    cuts = [ff * c // 7 for c in (0, 2, 4, 6, 7)]
-
-    def forward(c):
-        return forward_products(
-            side, x, gate_weight, up_weight, cuts[c], cuts[c + 1] - cuts[c]
-        )
-
-    keep_0, send_0 = forward(0)
+    cut = ff * 4 // 7
+
+    def forward(weight, late):
+        first, count = (cut, ff - cut) if late else (0, cut)
+        return forward_products(side, x, weight, first, count)
+
+    keep_0, send_0 = forward(gate_weight, False)
     swapped, x, keep_0, send_0 = in_order(swapped, x, keep_0, send_0)
     own_cols = jnp.where(t // per_half == group, blocks[:rows], swapped)
     part = jnp.concatenate(
@@ -437,20 +431,20 @@
     part = add_core(part, along_tensor(part, CORE))
     part, x = in_order(part, x)
     recv = along_tensor(part, X)
-    keep_1, send_1 = forward(1)
+    keep_1, send_1 = forward(up_weight, False)
     recv, x, keep_1, send_1 = in_order(recv, x, keep_1, send_1)
     part = add_x(part, recv)
 
     recv = along_tensor(part, 4)
-    keep_2, send_2 = forward(2)
-    recv, x, keep_2, send_2 = in_order(recv, x, keep_2, send_2)
+    far_a = across_groups(jnp.stack([send_0, send_1]))
+    keep_2, send_2 = forward(gate_weight, True)
+    recv, far_a, x, keep_2, send_2 = in_order(recv, far_a, x, keep_2, send_2)
     part = add_z(part, recv, 1)
 
     recv = along_tensor(part, 8)
-    far_a = across_groups(jnp.concatenate([send_0, send_1, send_2], axis=2))
-    keep_3, send_3 = forward(3)
-    far_a, recv, keep_3, send_3 = in_order(far_a, recv, keep_3, send_3)
-    far_b = across_groups(send_3)
+    keep_3, send_3 = forward(up_weight, True)
+    recv, keep_3, send_3 = in_order(recv, keep_3, send_3)
+    far_b = across_groups(jnp.stack([send_2, send_3]))
     part = add_z(part, recv, 2)
     u = part.astype(BF16).astype(F32)
     up_factor_gate = spread(u[:, :R])
@@ -461,10 +455,9 @@
             up_factor_gate, up_factor_up, b_gate, b_up, keep, far, hidden_grad, first, width
         )
 
-    keep = jnp.concatenate([keep_0, keep_1, keep_2], axis=2)
-    own_a, pg_a, pu_a = hidden(keep, far_a, 0, 512)
+    own_a, pg_a, pu_a = hidden(jnp.stack([keep_0, keep_1]), far_a, 0, 512)
     far_b, own_a = in_order(far_b, own_a)
-    own_b, pg_b, pu_b = hidden(keep_3, far_b, cuts[3], 256)
+    own_b, pg_b, pu_b = hidden(jnp.stack([keep_2, keep_3]), far_b, cut, 256)
     own = jnp.concatenate([own_a, own_b], axis=2)
     far = across_groups(own)
     part = jnp.concatenate([select(pg_a + pg_b), select(pu_a + pu_b)], axis=1)

time: 105 us -> 105 us (level)
  waiting for transfers between devices: 12.1 us -> 10.5 us
    ppermute x8, waiting for transfers between devices: 5.86 us -> 4.23 us  [across_groups(): lax.ppermute(value, both, [(i, i ^ (N | mask)) for i in range(2 * N)])]
  transfers between devices with their start and end apart: 26 -> 26, of which waited for: 11 -> 11; matrix products, arithmetic and copies ran while one was open for 13% -> 13% of each run, Pallas kernels for 38% -> 36%
where the time goes in v10:
time: 105 us; the launch traced here: 104 us
  Pallas kernels  42.1 us (40%)
  starting transfers between devices  31.1 us (30%)
  matrix products  13.7 us (13%)
  waiting for transfers between devices  10.5 us (10%)
  other arithmetic  4.54 us (4%)
  between operations  1.35 us (1%)
    ppermute x18, starting transfers between devices, along_tensor(): return lax.ppermute(value, 'tensor', [(i, i ^ mask) for i in range(N)])  22.1 us
    pallas_call x3, Pallas kernels, backward_products(): pl.pallas_call(functools.partial(backward_kernel, first), in_specs=[pl.Bl...  16.3 us
    pallas_call x4, Pallas kernels, forward_products(): pl.pallas_call(functools.partial(forward_kernel, first), in_specs=[pl.Blo...  14.8 us
    dot_general x4, matrix products, rows_product(): lax.dot_general(left, right, (((0,), (0,)), ((), ())), preferred_element_...  12 us
    ppermute x8, starting transfers between devices, across_groups(): lax.ppermute(value, both, [(i, i ^ (N | mask)) for i in range(2 * N)])  9 us
    pallas_call x2, Pallas kernels, hidden_gradients(): pl.pallas_call(functools.partial(hidden_kernel, first, step), in_specs=[v...  8.72 us
    ppermute x18, waiting for transfers between devices, along_tensor(): return lax.ppermute(value, 'tensor', [(i, i ^ mask) for i in range(N)])  6.25 us
    ppermute x8, waiting for transfers between devices, across_groups(): lax.ppermute(value, both, [(i, i ^ (N | mask)) for i in range(2 * N)])  4.23 us
  transfers between devices with their start and end apart: 26, of which 11 were waited for; matrix products, arithmetic and copies ran while one was open for 13% of the time, Pallas kernels for 36%

profile of v10, /device:TPU:0, one launch (start us, length us, event | category | flops | bytes accessed | tf_op | source)
XLA Modules:
  0.0 104.3 jit_solution(249216781611744704)
XLA Ops:
  0.6 3.1 %collective-permute-start = (bf16[2,8192]{1,0:T(2,128)(2,1)}, bf16[2,8192]{1,0:T(2,128)(2,1)S(1)}, u32[]{:S(2)}, u32[]{:S(2)}) collective-permute-start(bf16[2,8192]{1,0:T(2,128)(2,1)} %param.9), channel_id=1, source_target_pairs={{0,4},{1,5},{2,6},{3,7},{4,0},{5,1},{6,2},{7,3},{8,12},{9,13},{10,... | collective-permute-start | bytes 98312 | tf_op jit(solution)/shard_map/ppermute | solution.py:338
  3.7 2.3 %narrow.1 = (bf16[512,1024]{1,0:T(8,128)(2,1)S(1)}, bf16[512,1024]{1,0:T(8,128)(2,1)S(1)}) custom-call(f32[512,1024]{1,0:T(8,128)} %g_ref.1, f32[512,1024]{1,0:T(8,128)} %u_ref.1), custom_call_target="tpu_custom_call" | custom-call | bytes 6291456 | tf_op jit(solution)/shard_map/narrow/pallas_call | solution.py:164
  6.0 0.8 pad_maximum_fusion.10
  6.9 2.9 %collective-permute-start.1 = (bf16[4,8192]{1,0:T(4,128)(2,1)S(1)}, bf16[4,8192]{1,0:T(4,128)(2,1)S(1)}, u32[]{:S(2)}, u32[]{:S(2)}) collective-permute-start(bf16[4,8192]{1,0:T(4,128)(2,1)S(1)} %pad_maximum_fusion.10), channel_id=1, source_target_pairs={{0,8},{1,9},{2,10},{3,11},{4,12},{5,13},{6,14},{7,15},{8,0},{9,1},... | collective-permute-start | bytes 196616 | tf_op jit(solution)/shard_map/ppermute | solution.py:338
  9.8 2.3 %collective-permute-done.1 = bf16[4,8192]{1,0:T(4,128)(2,1)S(1)} collective-permute-done((bf16[4,8192]{1,0:T(4,128)(2,1)S(1)}, bf16[4,8192]{1,0:T(4,128)(2,1)S(1)}, u32[]{:S(2)}, u32[]{:S(2)}) %collective-permute-start.1) | collective-permute-done | bytes 65568 | tf_op jit(solution)/shard_map/ppermute | solution.py:338
  12.1 0.9 pad_maximum_fusion.6
  13.0 1.8 %collective-permute-start.2 = (bf16[8,4096]{1,0:T(8,128)(2,1)S(1)}, bf16[8,4096]{1,0:T(8,128)(2,1)S(1)}, u32[]{:S(2)}, u32[]{:S(2)}) collective-permute-start(bf16[8,4096]{1,0:T(8,128)(2,1)S(1)} %get-tuple-element.171), channel_id=1, source_target_pairs={{0,2},{1,3},{2,0},{3,1},{4,6},{5,7},{6,4},{7,5},{8,10},{9,11},{10,... | collective-permute-start | bytes 196616 | tf_op jit(solution)/shard_map/ppermute | solution.py:338
  14.8 1.5 %collective-permute-start.4 = (bf16[8,4096]{1,0:T(8,128)(2,1)S(1)}, bf16[8,4096]{1,0:T(8,128)(2,1)S(1)}, u32[]{:S(2)}, u32[]{:S(2)}) collective-permute-start(bf16[8,4096]{1,0:T(8,128)(2,1)S(1)} %get-tuple-element.172), channel_id=1, source_target_pairs={{0,18},{1,19},{2,16},{3,17},{4,22},{5,23},{6,20},{7,21},{8,26},{9,... | collective-permute-start | bytes 196616 | tf_op jit(solution)/shard_map/ppermute | solution.py:343
  16.6 1.2 %collective-permute-done.2 = bf16[8,4096]{1,0:T(8,128)(2,1)S(1)} collective-permute-done((bf16[8,4096]{1,0:T(8,128)(2,1)S(1)}, bf16[8,4096]{1,0:T(8,128)(2,1)S(1)}, u32[]{:S(2)}, u32[]{:S(2)}) %collective-permute-start.2) | collective-permute-done | bytes 65568 | tf_op jit(solution)/shard_map/ppermute | solution.py:338
  17.8 2.2 %collective-permute-done.4 = bf16[8,4096]{1,0:T(8,128)(2,1)S(1)} collective-permute-done((bf16[8,4096]{1,0:T(8,128)(2,1)S(1)}, bf16[8,4096]{1,0:T(8,128)(2,1)S(1)}, u32[]{:S(2)}, u32[]{:S(2)}) %collective-permute-start.4) | collective-permute-done | bytes 65568 | tf_op jit(solution)/shard_map/ppermute | solution.py:343
  20.0 0.7 collective-permute-done.3
  20.9 0.8 select_reduce_fusion
  21.7 0.6 collective-permute-done.5
  22.4 0.9 collective-permute-start.6
  23.3 4.1 %forward_products.4 = (f32[32,1024]{1,0:T(8,128)S(1)}, bf16[32,1024]{1,0:T(8,128)(2,1)S(1)}) custom-call(s32[1]{0:T(128)} %bitcast.3.side_ref, bf16[64,4096]{1,0:T(8,128)(2,1)S(1)} %bitcast.68, bf16[8192,1792]{1,0:T(8,128)(2,1)} %wg_ref.5), custom_call_target="tpu_custom_call" | custom-call | flops 536870912 | bytes 12582912 | tf_op jit(solution)/shard_map/forward_products/pallas_call | solution.py:135
  28.5 0.9 collective-permute-done.7
  29.5 1.2 %collective-permute-start.8 = (f32[32,128]{1,0:T(8,128)S(1)}, f32[32,128]{1,0:T(8,128)S(1)}, u32[]{:S(2)}, u32[]{:S(2)}) collective-permute-start(f32[32,128]{1,0:T(8,128)S(1)} %maximum_add_fusion.1), channel_id=1, source_target_pairs={{0,2},{1,3},{2,0},{3,1},{4,6},{5,7},{6,4},{7,5},{8,10},{9,11},{10,... | collective-permute-start | bytes 49160 | tf_op jit(solution)/shard_map/ppermute | solution.py:338
  30.7 4.0 %forward_products.5 = (f32[32,1024]{1,0:T(8,128)S(1)}, bf16[32,1024]{1,0:T(8,128)(2,1)S(1)}) custom-call(s32[1]{0:T(128)} %bitcast.3.side_ref, bf16[64,4096]{1,0:T(8,128)(2,1)S(1)} %bitcast.70, bf16[8192,1792]{1,0:T(8,128)(2,1)} %wu_ref.5), custom_call_target="tpu_custom_call" | custom-call | flops 536870912 | bytes 12582912 | tf_op jit(solution)/shard_map/forward_products/pallas_call | solution.py:135
  34.8 1.6 %collective-permute-start.9 = (f32[32,128]{1,0:T(8,128)S(1)}, f32[32,128]{1,0:T(8,128)S(1)}, u32[]{:S(2)}, u32[]{:S(2)}) collective-permute-start(f32[32,128]{1,0:T(8,128)S(1)} %maximum_add_fusion.2), channel_id=1, source_target_pairs={{0,4},{1,5},{2,6},{3,7},{4,0},{5,1},{6,2},{7,3},{8,12},{9,13},{10,... | collective-permute-start | bytes 49160 | tf_op jit(solution)/shard_map/ppermute | solution.py:338
  36.4 1.2 %collective-permute-start.10 = (bf16[2,32,1024]{2,1,0:T(8,128)(2,1)S(1)}, bf16[2,32,1024]{2,1,0:T(8,128)(2,1)S(1)}, u32[]{:S(2)}, u32[]{:S(2)}) collective-permute-start(bf16[2,32,1024]{2,1,0:T(8,128)(2,1)S(1)} %pad_maximum_fusion.7), channel_id=1, source_target_pairs={{0,16},{1,17},{2,18},{3,19},{4,20},{5,21},{6,22},{7,23},{8,24},{9,... | collective-permute-start | bytes 393224 | tf_op jit(solution)/shard_map/ppermute | solution.py:343
  37.7 3.3 %forward_products.6 = (f32[32,768]{1,0:T(8,128)S(1)}, bf16[32,768]{1,0:T(8,128)(2,1)S(1)}) custom-call(s32[1]{0:T(128)} %bitcast.3.side_ref, bf16[64,4096]{1,0:T(8,128)(2,1)S(1)} %bitcast.71, bf16[8192,1792]{1,0:T(8,128)(2,1)} %wg_ref.5), custom_call_target="tpu_custom_call" | custom-call | flops 402653184 | bytes 9437184 | tf_op jit(solution)/shard_map/forward_products/pallas_call | solution.py:135
  41.0 0.4 collective-permute-done.10.far_ref
  41.5 3.2 %collective-permute-start.11 = (f32[32,128]{1,0:T(8,128)S(1)}, f32[32,128]{1,0:T(8,128)S(1)}, u32[]{:S(2)}, u32[]{:S(2)}) collective-permute-start(f32[32,128]{1,0:T(8,128)S(1)} %add.222), channel_id=1, source_target_pairs={{0,8},{1,9},{2,10},{3,11},{4,12},{5,13},{6,14},{7,15},{8,0},{9,1},... | collective-permute-start | bytes 49160 | tf_op jit(solution)/shard_map/ppermute | solution.py:338
  44.8 3.3 %forward_products.7 = (f32[32,768]{1,0:T(8,128)S(1)}, bf16[32,768]{1,0:T(8,128)(2,1)S(1)}) custom-call(s32[1]{0:T(128)} %bitcast.3.side_ref, bf16[64,4096]{1,0:T(8,128)(2,1)S(1)} %bitcast.72, bf16[8192,1792]{1,0:T(8,128)(2,1)} %wu_ref.5), custom_call_target="tpu_custom_call" | custom-call | flops 402653184 | bytes 9437184 | tf_op jit(solution)/shard_map/forward_products/pallas_call | solution.py:135
  48.5 1.2 %collective-permute-start.12 = (bf16[2,32,768]{2,1,0:T(8,128)(2,1)S(1)}, bf16[2,32,768]{2,1,0:T(8,128)(2,1)S(1)}, u32[]{:S(2)}, u32[]{:S(2)}) collective-permute-start(bf16[2,32,768]{2,1,0:T(8,128)(2,1)S(1)} %pad_maximum_fusion.8), channel_id=1, source_target_pairs={{0,16},{1,17},{2,18},{3,19},{4,20},{5,21},{6,22},{7,23},{8,24},{9,... | collective-permute-start | bytes 294920 | tf_op jit(solution)/shard_map/ppermute | solution.py:343
  49.8 4.7 %hidden_gradients.2 = (bf16[2,32,1024]{2,1,0:T(8,128)(2,1)S(1)}, f32[32,1024]{1,0:T(8,128)S(1)}, f32[32,1024]{1,0:T(8,128)S(1)}) custom-call(bf16[32,1024]{1,0:T(8,128)(2,1)S(1)} %get-tuple-element.209.eug_ref, bf16[32,1024]{1,0:T(8,128)(2,1)S(1)} %get-tuple-element.210.euu_ref, f32[2,32,1024]{2,1,0:T(8,128)S(1)} %pad_maximum_fusion.3.keep_ref, ...), custom_call_target="tpu_custom_call" | custom-call | flops 268435456 | bytes 12582912 | tf_op jit(solution)/shard_map/hidden_gradients/pallas_call | solution.py:239
  54.6 4.0 %hidden_gradients.3 = (bf16[2,32,768]{2,1,0:T(8,128)(2,1)S(1)}, f32[32,1024]{1,0:T(8,128)S(1)}, f32[32,1024]{1,0:T(8,128)S(1)}) custom-call(bf16[32,1024]{1,0:T(8,128)(2,1)S(1)} %get-tuple-element.209.eug_ref, bf16[32,1024]{1,0:T(8,128)(2,1)S(1)} %get-tuple-element.210.euu_ref, f32[2,32,768]{2,1,0:T(8,128)S(1)} %pad_maximum_fusion.5.keep_ref, ...), custom_call_target="tpu_custom_call" | custom-call | flops 201326592 | bytes 9437184 | tf_op jit(solution)/shard_map/hidden_gradients/pallas_call | solution.py:239
  58.9 0.9 collective-permute-start.13
  59.9 4.2 %convolution_multiply_fusion.1 = f32[1024,1792]{1,0:T(8,128)} fusion(bf16[32,1024]{1,0:T(8,128)(2,1)S(1)} %get-tuple-element.209.eug_ref, bf16[2,32,1792]{2,1,0:T(8,128)(2,1)S(1)} %constant_dynamic-update-slice_fusion), kind=kOutput, calls=%fused_computation.1 | convolution fusion | flops 119275520 | bytes 7520256 | tf_op jit(solution)/shard_map/dot_general | solution.py:39
  64.1 0.9 collective-permute-done.13
  65.1 0.7 collective-permute-start.15
  65.8 3.3 %backward_products.3 = (f32[32,512]{1,0:T(8,128)S(1)}, bf16[32,512]{1,0:T(8,128)(2,1)S(1)}) custom-call(s32[1]{0:T(128)} %bitcast.3.side_ref, bf16[64,1792]{1,0:T(8,128)(2,1)S(1)} %get-tuple-element.136.dg_ref, bf16[64,1792]{1,0:T(8,128)(2,1)S(1)} %get-tuple-element.137.du_ref, bf16[8192,1792]{1,0:T(8,128)(2,1)} %wg_ref.5, bf16[8192,1792]{1,0:T(8,128)(2,1)} %wu_ref.5), custom_call_target="tpu_custom_call" | custom-call | flops 234881024 | bytes 5505024 | tf_op jit(solution)/shard_map/backward_products/pallas_call | solution.py:307
  69.5 3.3 %backward_products.4 = (f32[32,512]{1,0:T(8,128)S(1)}, bf16[32,512]{1,0:T(8,128)(2,1)S(1)}) custom-call(s32[1]{0:T(128)} %bitcast.3.side_ref, bf16[64,1792]{1,0:T(8,128)(2,1)S(1)} %get-tuple-element.136.dg_ref, bf16[64,1792]{1,0:T(8,128)(2,1)S(1)} %get-tuple-element.137.du_ref, bf16[8192,1792]{1,0:T(8,128)(2,1)} %wg_ref.5, bf16[8192,1792]{1,0:T(8,128)(2,1)} %wu_ref.5), custom_call_target="tpu_custom_call" | custom-call | flops 234881024 | bytes 5505024 | tf_op jit(solution)/shard_map/backward_products/pallas_call | solution.py:307
  72.9 1.3 %collective-permute-start.17 = (f32[32,128]{1,0:T(8,128)S(1)}, f32[32,128]{1,0:T(8,128)S(1)}, u32[]{:S(2)}, u32[]{:S(2)}) collective-permute-start(f32[32,128]{1,0:T(8,128)S(1)} %add.244), channel_id=1, source_target_pairs={{0,8},{1,9},{2,10},{3,11},{4,12},{5,13},{6,14},{7,15},{8,0},{9,1},... | collective-permute-start | bytes 49160 | tf_op jit(solution)/shard_map/ppermute | solution.py:338
  74.3 9.8 %backward_products.5 = (f32[32,3072]{1,0:T(8,128)S(1)}, bf16[32,3072]{1,0:T(8,128)(2,1)S(1)}) custom-call(s32[1]{0:T(128)} %bitcast.3.side_ref, bf16[64,1792]{1,0:T(8,128)(2,1)S(1)} %get-tuple-element.136.dg_ref, bf16[64,1792]{1,0:T(8,128)(2,1)S(1)} %get-tuple-element.137.du_ref, bf16[8192,1792]{1,0:T(8,128)(2,1)} %wg_ref.5, bf16[8192,1792]{1,0:T(8,128)(2,1)} %wu_ref.5), custom_call_target="tpu_custom_call" | custom-call | flops 1409286144 | bytes 33030144 | tf_op jit(solution)/shard_map/backward_products/pallas_call | solution.py:307
  84.4 0.4 fusion.38
  84.9 0.4 fusion.1
  85.4 0.6 collective-permute-start.19
  86.0 0.8 collective-permute-done.19
  86.9 1.7 %collective-permute-start.22 = (bf16[8,4096]{1,0:T(8,128)(2,1)S(1)}, bf16[8,4096]{1,0:T(8,128)(2,1)S(1)}, u32[]{:S(2)}, u32[]{:S(2)}) collective-permute-start(bf16[8,4096]{1,0:T(8,128)(2,1)S(1)} %get-tuple-element.165), channel_id=1, source_target_pairs={{0,18},{1,19},{2,16},{3,17},{4,22},{5,23},{6,20},{7,21},{8,26},{9,... | collective-permute-start | bytes 196616 | tf_op jit(solution)/shard_map/ppermute | solution.py:343
  88.6 1.2 %collective-permute-start.21 = (bf16[8,4096]{1,0:T(8,128)(2,1)S(1)}, bf16[8,4096]{1,0:T(8,128)(2,1)S(1)}, u32[]{:S(2)}, u32[]{:S(2)}) collective-permute-start(bf16[8,4096]{1,0:T(8,128)(2,1)S(1)} %get-tuple-element.166), channel_id=1, source_target_pairs={{0,16},{1,17},{2,18},{3,19},{4,20},{5,21},{6,22},{7,23},{8,24},{9,... | collective-permute-start | bytes 196616 | tf_op jit(solution)/shard_map/ppermute | solution.py:343
  89.8 0.7 collective-permute-start.20
  90.5 1.8 %convolution_multiply_fusion.2 = f32[512,1024]{1,0:T(8,128)} fusion(bf16[32,512]{1,0:T(8,128)(2,1)S(1)} %dynamic-slice_select_fusion, bf16[32,1024]{1,0:T(8,128)(2,1)S(1)} %concatenate.97, s32[1024]{0:T(1024)S(1)} %add_select_fusion, s32[32]{0:T(128)S(1)} %select_reduce_fusion), kind=kOutput, calls=%fused_computation.2 | convolution fusion | flops 34144256 | bytes 2199680 | tf_op jit(solution)/shard_map/dot_general | solution.py:39
  92.3 1.8 %convolution_multiply_fusion.3 = f32[512,1024]{1,0:T(8,128)} fusion(bf16[32,512]{1,0:T(8,128)(2,1)S(1)} %dynamic-slice_select_fusion, bf16[32,1024]{1,0:T(8,128)(2,1)S(1)} %concatenate.96, s32[1024]{0:T(1024)S(1)} %add_select_fusion, s32[32]{0:T(128)S(1)} %select_reduce_fusion), kind=kOutput, calls=%fused_computation.3 | convolution fusion | flops 34144256 | bytes 2199680 | tf_op jit(solution)/shard_map/dot_general | solution.py:39
  94.5 2.7 %collective-permute-start.25 = (bf16[2,10240]{1,0:T(2,128)(2,1)S(1)}, bf16[2,10240]{1,0:T(2,128)(2,1)S(1)}, u32[]{:S(2)}, u32[]{:S(2)}) collective-permute-start(bf16[2,10240]{1,0:T(2,128)(2,1)S(1)} %get-tuple-element.168), channel_id=1, source_target_pairs={{0,12},{1,13},{2,14},{3,15},{4,8},{5,9},{6,10},{7,11},{8,4},{9,5},... | collective-permute-start | bytes 122888 | tf_op jit(solution)/shard_map/ppermute | solution.py:338
  97.6 1.3 %collective-permute-start.23 = (bf16[2,10240]{1,0:T(2,128)(2,1)S(1)}, bf16[2,10240]{1,0:T(2,128)(2,1)S(1)}, u32[]{:S(2)}, u32[]{:S(2)}) collective-permute-start(bf16[2,10240]{1,0:T(2,128)(2,1)S(1)} %get-tuple-element.170), channel_id=1, source_target_pairs={{0,4},{1,5},{2,6},{3,7},{4,0},{5,1},{6,2},{7,3},{8,12},{9,13},{10,... | collective-permute-start | bytes 122888 | tf_op jit(solution)/shard_map/ppermute | solution.py:338
  99.0 4.2 %convolution_multiply_fusion = f32[1024,1792]{1,0:T(8,128)} fusion(bf16[32,1024]{1,0:T(8,128)(2,1)S(1)} %get-tuple-element.210.euu_ref, bf16[2,32,1792]{2,1,0:T(8,128)(2,1)S(1)} %constant_dynamic-update-slice_fusion), kind=kOutput, calls=%fused_computation | convolution fusion | flops 119275520 | bytes 7520256 | tf_op jit(solution)/shard_map/dot_general | solution.py:39
  103.6 0.7 fusion.14
  (109 shorter events, 4.7 us)
Async XLA Ops:
  0.6 27.6 %copy-start = (bf16[32,1792]{1,0:T(8,128)(2,1)S(1)}, bf16[32,1792]{1,0:T(8,128)(2,1)}, u32[]{:S(2)}) copy-start(bf16[32,1792]{1,0:T(8,128)(2,1)} %param.17) | copy-start | bytes 344068
  0.6 5.4 %collective-permute-start = (bf16[2,8192]{1,0:T(2,128)(2,1)}, bf16[2,8192]{1,0:T(2,128)(2,1)S(1)}, u32[]{:S(2)}, u32[]{:S(2)}) collective-permute-start(bf16[2,8192]{1,0:T(2,128)(2,1)} %param.9), channel_id=1, source_target_pairs={{0,4},{1,5},{2,6},{3,7},{4,0},{5,1},{6,2},{7,3},{8,12},{9,13},{10,... | collective-permute-start | bytes 98312 | tf_op jit(solution)/shard_map/ppermute | solution.py:338
  6.9 5.2 %collective-permute-start.1 = (bf16[4,8192]{1,0:T(4,128)(2,1)S(1)}, bf16[4,8192]{1,0:T(4,128)(2,1)S(1)}, u32[]{:S(2)}, u32[]{:S(2)}) collective-permute-start(bf16[4,8192]{1,0:T(4,128)(2,1)S(1)} %pad_maximum_fusion.10), channel_id=1, source_target_pairs={{0,8},{1,9},{2,10},{3,11},{4,12},{5,13},{6,14},{7,15},{8,0},{9,1},... | collective-permute-start | bytes 196616 | tf_op jit(solution)/shard_map/ppermute | solution.py:338
  13.0 4.7 %collective-permute-start.2 = (bf16[8,4096]{1,0:T(8,128)(2,1)S(1)}, bf16[8,4096]{1,0:T(8,128)(2,1)S(1)}, u32[]{:S(2)}, u32[]{:S(2)}) collective-permute-start(bf16[8,4096]{1,0:T(8,128)(2,1)S(1)} %get-tuple-element.171), channel_id=1, source_target_pairs={{0,2},{1,3},{2,0},{3,1},{4,6},{5,7},{6,4},{7,5},{8,10},{9,11},{10,... | collective-permute-start | bytes 196616 | tf_op jit(solution)/shard_map/ppermute | solution.py:338
  14.8 5.2 %collective-permute-start.4 = (bf16[8,4096]{1,0:T(8,128)(2,1)S(1)}, bf16[8,4096]{1,0:T(8,128)(2,1)S(1)}, u32[]{:S(2)}, u32[]{:S(2)}) collective-permute-start(bf16[8,4096]{1,0:T(8,128)(2,1)S(1)} %get-tuple-element.172), channel_id=1, source_target_pairs={{0,18},{1,19},{2,16},{3,17},{4,22},{5,23},{6,20},{7,21},{8,26},{9,... | collective-permute-start | bytes 196616 | tf_op jit(solution)/shard_map/ppermute | solution.py:343
  16.3 4.4 %collective-permute-start.3 = (bf16[8,4096]{1,0:T(8,128)(2,1)S(1)}, bf16[8,4096]{1,0:T(8,128)(2,1)S(1)}, u32[]{:S(2)}, u32[]{:S(2)}) collective-permute-start(bf16[8,4096]{1,0:T(8,128)(2,1)S(1)} %get-tuple-element.172), channel_id=1, source_target_pairs={{0,16},{1,17},{2,18},{3,19},{4,20},{5,21},{6,22},{7,23},{8,24},{9,... | collective-permute-start | bytes 196616 | tf_op jit(solution)/shard_map/ppermute | solution.py:343
  20.7 1.6 %collective-permute-start.5 = (bf16[2,16,4096]{2,1,0:T(8,128)(2,1)S(1)}, bf16[2,16,4096]{2,1,0:T(8,128)(2,1)S(1)}, u32[]{:S(2)}, u32[]{:S(2)}) collective-permute-start(bf16[2,16,4096]{2,1,0:T(8,128)(2,1)S(1)} %pad_maximum_fusion.2), channel_id=1, source_target_pairs={{0,1},{1,0},{2,3},{3,2},{4,5},{5,4},{6,7},{7,6},{8,9},{9,8},{10,11... | collective-permute-start | bytes 786440 | tf_op jit(solution)/shard_map/ppermute | solution.py:338
  22.4 5.1 %collective-permute-start.6 = (bf16[32,512]{1,0:T(8,128)(2,1)S(1)}, bf16[32,512]{1,0:T(8,128)(2,1)S(1)}, u32[]{:S(2)}, u32[]{:S(2)}) collective-permute-start(bf16[32,512]{1,0:T(8,128)(2,1)S(1)} %dynamic-slice.1), channel_id=1, source_target_pairs={{0,16},{1,17},{2,18},{3,19},{4,20},{5,21},{6,22},{7,23},{8,24},{9,... | collective-permute-start | bytes 98312 | tf_op jit(solution)/shard_map/ppermute | solution.py:343
  28.2 1.2 %collective-permute-start.7 = (f32[32,128]{1,0:T(8,128)S(1)}, f32[32,128]{1,0:T(8,128)S(1)}, u32[]{:S(2)}, u32[]{:S(2)}) collective-permute-start(f32[32,128]{1,0:T(8,128)S(1)} %pad_maximum_fusion.17), channel_id=1, source_target_pairs={{0,1},{1,0},{2,3},{3,2},{4,5},{5,4},{6,7},{7,6},{8,9},{9,8},{10,11... | collective-permute-start | bytes 49160 | tf_op jit(solution)/shard_map/ppermute | solution.py:338
  29.5 5.2 %collective-permute-start.8 = (f32[32,128]{1,0:T(8,128)S(1)}, f32[32,128]{1,0:T(8,128)S(1)}, u32[]{:S(2)}, u32[]{:S(2)}) collective-permute-start(f32[32,128]{1,0:T(8,128)S(1)} %maximum_add_fusion.1), channel_id=1, source_target_pairs={{0,2},{1,3},{2,0},{3,1},{4,6},{5,7},{6,4},{7,5},{8,10},{9,11},{10,... | collective-permute-start | bytes 49160 | tf_op jit(solution)/shard_map/ppermute | solution.py:338
  34.8 6.3 %collective-permute-start.9 = (f32[32,128]{1,0:T(8,128)S(1)}, f32[32,128]{1,0:T(8,128)S(1)}, u32[]{:S(2)}, u32[]{:S(2)}) collective-permute-start(f32[32,128]{1,0:T(8,128)S(1)} %maximum_add_fusion.2), channel_id=1, source_target_pairs={{0,4},{1,5},{2,6},{3,7},{4,0},{5,1},{6,2},{7,3},{8,12},{9,13},{10,... | collective-permute-start | bytes 49160 | tf_op jit(solution)/shard_map/ppermute | solution.py:338
  36.4 5.1 %collective-permute-start.10 = (bf16[2,32,1024]{2,1,0:T(8,128)(2,1)S(1)}, bf16[2,32,1024]{2,1,0:T(8,128)(2,1)S(1)}, u32[]{:S(2)}, u32[]{:S(2)}) collective-permute-start(bf16[2,32,1024]{2,1,0:T(8,128)(2,1)S(1)} %pad_maximum_fusion.7), channel_id=1, source_target_pairs={{0,16},{1,17},{2,18},{3,19},{4,20},{5,21},{6,22},{7,23},{8,24},{9,... | collective-permute-start | bytes 393224 | tf_op jit(solution)/shard_map/ppermute | solution.py:343
  41.5 6.6 %collective-permute-start.11 = (f32[32,128]{1,0:T(8,128)S(1)}, f32[32,128]{1,0:T(8,128)S(1)}, u32[]{:S(2)}, u32[]{:S(2)}) collective-permute-start(f32[32,128]{1,0:T(8,128)S(1)} %add.222), channel_id=1, source_target_pairs={{0,8},{1,9},{2,10},{3,11},{4,12},{5,13},{6,14},{7,15},{8,0},{9,1},... | collective-permute-start | bytes 49160 | tf_op jit(solution)/shard_map/ppermute | solution.py:338
  48.5 6.0 %collective-permute-start.12 = (bf16[2,32,768]{2,1,0:T(8,128)(2,1)S(1)}, bf16[2,32,768]{2,1,0:T(8,128)(2,1)S(1)}, u32[]{:S(2)}, u32[]{:S(2)}) collective-permute-start(bf16[2,32,768]{2,1,0:T(8,128)(2,1)S(1)} %pad_maximum_fusion.8), channel_id=1, source_target_pairs={{0,16},{1,17},{2,18},{3,19},{4,20},{5,21},{6,22},{7,23},{8,24},{9,... | collective-permute-start | bytes 294920 | tf_op jit(solution)/shard_map/ppermute | solution.py:343
  58.9 6.1 %collective-permute-start.13 = (bf16[2,32,1792]{2,1,0:T(8,128)(2,1)S(1)}, bf16[2,32,1792]{2,1,0:T(8,128)(2,1)S(1)}, u32[]{:S(2)}, u32[]{:S(2)}) collective-permute-start(bf16[2,32,1792]{2,1,0:T(8,128)(2,1)S(1)} %constant_dynamic-update-slice_fusion), channel_id=1, source_target_pairs={{0,16},{1,17},{2,18},{3,19},{4,20},{5,21},{6,22},{7,23},{8,24},{9,... | collective-permute-start | bytes 688136 | tf_op jit(solution)/shard_map/ppermute | solution.py:343
  59.9 4.2 %collective-permute-start.14 = (f32[32,128]{1,0:T(8,128)S(1)}, f32[32,128]{1,0:T(8,128)S(1)}, u32[]{:S(2)}, u32[]{:S(2)}) collective-permute-start(f32[32,128]{1,0:T(8,128)S(1)} %pad_maximum_fusion.20), channel_id=1, source_target_pairs={{0,1},{1,0},{2,3},{3,2},{4,5},{5,4},{6,7},{7,6},{8,9},{9,8},{10,11... | collective-permute-start | bytes 49160 | tf_op jit(solution)/shard_map/ppermute | solution.py:338
  65.1 4.0 %collective-permute-start.15 = (f32[32,128]{1,0:T(8,128)S(1)}, f32[32,128]{1,0:T(8,128)S(1)}, u32[]{:S(2)}, u32[]{:S(2)}) collective-permute-start(f32[32,128]{1,0:T(8,128)S(1)} %maximum_add_fusion.3), channel_id=1, source_target_pairs={{0,2},{1,3},{2,0},{3,1},{4,6},{5,7},{6,4},{7,5},{8,10},{9,11},{10,... | collective-permute-start | bytes 49160 | tf_op jit(solution)/shard_map/ppermute | solution.py:338
  69.1 3.8 %collective-permute-start.16 = (f32[32,128]{1,0:T(8,128)S(1)}, f32[32,128]{1,0:T(8,128)S(1)}, u32[]{:S(2)}, u32[]{:S(2)}) collective-permute-start(f32[32,128]{1,0:T(8,128)S(1)} %maximum_add_fusion.4), channel_id=1, source_target_pairs={{0,4},{1,5},{2,6},{3,7},{4,0},{5,1},{6,2},{7,3},{8,12},{9,13},{10,... | collective-permute-start | bytes 49160 | tf_op jit(solution)/shard_map/ppermute | solution.py:338
  72.9 11.1 %collective-permute-start.17 = (f32[32,128]{1,0:T(8,128)S(1)}, f32[32,128]{1,0:T(8,128)S(1)}, u32[]{:S(2)}, u32[]{:S(2)}) collective-permute-start(f32[32,128]{1,0:T(8,128)S(1)} %add.244), channel_id=1, source_target_pairs={{0,8},{1,9},{2,10},{3,11},{4,12},{5,13},{6,14},{7,15},{8,0},{9,1},... | collective-permute-start | bytes 49160 | tf_op jit(solution)/shard_map/ppermute | solution.py:338
  84.9 1.9 %collective-permute-start.18 = (bf16[32,4096]{1,0:T(8,128)(2,1)S(1)}, bf16[32,4096]{1,0:T(8,128)(2,1)S(1)}, u32[]{:S(2)}, u32[]{:S(2)}) collective-permute-start(bf16[32,4096]{1,0:T(8,128)(2,1)S(1)} %pad_maximum_fusion.4), channel_id=1, source_target_pairs={{0,1},{1,0},{2,3},{3,2},{4,5},{5,4},{6,7},{7,6},{8,9},{9,8},{10,11... | collective-permute-start | bytes 786440 | tf_op jit(solution)/shard_map/ppermute | solution.py:338
  85.4 1.4 %collective-permute-start.19 = (bf16[16,512]{1,0:T(8,128)(2,1)S(1)}, bf16[16,512]{1,0:T(8,128)(2,1)S(1)}, u32[]{:S(2)}, u32[]{:S(2)}) collective-permute-start(bf16[16,512]{1,0:T(8,128)(2,1)S(1)} %get-tuple-element.178), channel_id=1, source_target_pairs={{0,1},{1,0},{2,3},{3,2},{4,5},{5,4},{6,7},{7,6},{8,9},{9,8},{10,11... | collective-permute-start | bytes 49160 | tf_op jit(solution)/shard_map/ppermute | solution.py:338
  86.9 7.2 %collective-permute-start.22 = (bf16[8,4096]{1,0:T(8,128)(2,1)S(1)}, bf16[8,4096]{1,0:T(8,128)(2,1)S(1)}, u32[]{:S(2)}, u32[]{:S(2)}) collective-permute-start(bf16[8,4096]{1,0:T(8,128)(2,1)S(1)} %get-tuple-element.165), channel_id=1, source_target_pairs={{0,18},{1,19},{2,16},{3,17},{4,22},{5,23},{6,20},{7,21},{8,26},{9,... | collective-permute-start | bytes 196616 | tf_op jit(solution)/shard_map/ppermute | solution.py:343
  88.6 5.5 %collective-permute-start.21 = (bf16[8,4096]{1,0:T(8,128)(2,1)S(1)}, bf16[8,4096]{1,0:T(8,128)(2,1)S(1)}, u32[]{:S(2)}, u32[]{:S(2)}) collective-permute-start(bf16[8,4096]{1,0:T(8,128)(2,1)S(1)} %get-tuple-element.166), channel_id=1, source_target_pairs={{0,16},{1,17},{2,18},{3,19},{4,20},{5,21},{6,22},{7,23},{8,24},{9,... | collective-permute-start | bytes 196616 | tf_op jit(solution)/shard_map/ppermute | solution.py:343
  89.8 4.5 %collective-permute-start.20 = (bf16[8,5120]{1,0:T(8,128)(2,1)S(1)}, bf16[8,5120]{1,0:T(8,128)(2,1)S(1)}, u32[]{:S(2)}, u32[]{:S(2)}) collective-permute-start(bf16[8,5120]{1,0:T(8,128)(2,1)S(1)} %pad_maximum_fusion.9), channel_id=1, source_target_pairs={{0,2},{1,3},{2,0},{3,1},{4,6},{5,7},{6,4},{7,5},{8,10},{9,11},{10,... | collective-permute-start | bytes 245768 | tf_op jit(solution)/shard_map/ppermute | solution.py:338
  94.4 9.9 %copy-start.1 = (bf16[32,1792]{1,0:T(8,128)(2,1)S(1)}, bf16[32,1792]{1,0:T(8,128)(2,1)}, u32[]{:S(2)}) copy-start(bf16[32,1792]{1,0:T(8,128)(2,1)} %param.17) | copy-start | bytes 344068
  94.5 8.7 %collective-permute-start.25 = (bf16[2,10240]{1,0:T(2,128)(2,1)S(1)}, bf16[2,10240]{1,0:T(2,128)(2,1)S(1)}, u32[]{:S(2)}, u32[]{:S(2)}) collective-permute-start(bf16[2,10240]{1,0:T(2,128)(2,1)S(1)} %get-tuple-element.168), channel_id=1, source_target_pairs={{0,12},{1,13},{2,14},{3,15},{4,8},{5,9},{6,10},{7,11},{8,4},{9,5},... | collective-permute-start | bytes 122888 | tf_op jit(solution)/shard_map/ppermute | solution.py:338
  97.3 5.9 %collective-permute-start.24 = (bf16[2,10240]{1,0:T(2,128)(2,1)S(1)}, bf16[2,10240]{1,0:T(2,128)(2,1)S(1)}, u32[]{:S(2)}, u32[]{:S(2)}) collective-permute-start(bf16[2,10240]{1,0:T(2,128)(2,1)S(1)} %get-tuple-element.169), channel_id=1, source_target_pairs={{0,8},{1,9},{2,10},{3,11},{4,12},{5,13},{6,14},{7,15},{8,0},{9,1},... | collective-permute-start | bytes 122888 | tf_op jit(solution)/shard_map/ppermute | solution.py:338
  97.6 5.6 %collective-permute-start.23 = (bf16[2,10240]{1,0:T(2,128)(2,1)S(1)}, bf16[2,10240]{1,0:T(2,128)(2,1)S(1)}, u32[]{:S(2)}, u32[]{:S(2)}) collective-permute-start(bf16[2,10240]{1,0:T(2,128)(2,1)S(1)} %get-tuple-element.170), channel_id=1, source_target_pairs={{0,4},{1,5},{2,6},{3,7},{4,0},{5,1},{6,2},{7,3},{8,12},{9,13},{10,... | collective-permute-start | bytes 122888 | tf_op jit(solution)/shard_map/ppermute | solution.py:338

commit v11 on v10

--- a/solution.py
+++ b/solution.py
@@ -330,6 +330,46 @@
     )
 
 
+def outer_kernel(pairs, *refs):
+    ins, outs, parts, sem = refs[: 2 * pairs], refs[2 * pairs : 3 * pairs], refs[-2], refs[-1]
+    depth = parts.shape[1]
+    copies = []
+    for i in range(pairs):
+        left_ref, right_ref, out_ref = ins[2 * i], ins[2 * i + 1], outs[i]
+        for k in range(0, out_ref.shape[0], depth):
+            at = len(copies)
+            parts[at] = adapter_scale * rows_product(left_ref[:, k : k + depth], right_ref[...])
+            copy = pltpu.make_async_copy(parts.at[at], out_ref.at[pl.ds(k, depth)], sem.at[at])
+            copy.start()
+            copies.append(copy)
+    for copy in copies:
+        copy.wait()
+
+
+def outer_products(*pairs, depth=128):
+    shapes = [(left.shape[1], right.shape[1]) for left, right in pairs]
+    count = sum(rows // depth for rows, _ in shapes)
+    width = shapes[0][1]
+    rows = pairs[0][0].shape[0]
+    return pl.pallas_call(
+        functools.partial(outer_kernel, len(pairs)),
+        in_specs=[pl.BlockSpec(memory_space=pltpu.VMEM)] * (2 * len(pairs)),
+        out_specs=[pl.BlockSpec(memory_space=pltpu.HBM)] * len(pairs),
+        out_shape=[jax.ShapeDtypeStruct(shape, F32) for shape in shapes],
+        scratch_shapes=[
+            pltpu.VMEM((count, depth, width), F32),
+            pltpu.SemaphoreType.DMA((count,)),
+        ],
+        compiler_params=pltpu.CompilerParams(vmem_limit_bytes=16 << 20),
+        cost_estimate=pl.CostEstimate(
+            flops=2 * count * depth * width * rows,
+            bytes_accessed=4 * count * depth * width,
+            transcendentals=0,
+        ),
+        name="outer_products",
+    )(*[operand for pair in pairs for operand in pair])
+
+
 N = 16
 CORE, X = 1, 2
 
@@ -463,7 +503,7 @@
     part = jnp.concatenate([select(pg_a + pg_b), select(pu_a + pu_b)], axis=1)
     part, own = in_order(part, own)
     recv = along_tensor(part, CORE)
-    gate_lift_gradient = adapter_scale * rows_product(up_factor_gate, own[0])
+    (gate_lift_gradient,) = outer_products((up_factor_gate, own[0]))
     far, recv, gate_lift_gradient = in_order(far, recv, gate_lift_gradient)
     part = add_core(part, recv)
     both = jnp.concatenate([own, far], axis=1)
@@ -501,7 +541,7 @@
     ).astype(BF16)
 
     far_moved = along_tensor(moved[16:], CORE)
-    far, far_moved, own_cols = in_order(far, far_moved, own_cols)
+    far, far_moved, own = in_order(far, far_moved, own)
     sums = jnp.concatenate([keep_0, keep_1, keep_2], axis=1) + far.astype(F32)
     moved = jnp.concatenate([moved[:16], far_moved], axis=1)
 
@@ -511,19 +551,20 @@
         across_groups(low[16:24]),
         across_groups(low[24:], X),
     ]
-    gate_down_gradient = adapter_scale * rows_product(own_cols, gate_factor_gate)
-    up_down_gradient = adapter_scale * rows_product(own_cols, gate_factor_up)
-    gate_down_gradient, up_down_gradient, own, *parts = in_order(
-        gate_down_gradient, up_down_gradient, own, *parts
-    )
+    (up_lift_gradient,) = outer_products((up_factor_up, own[1]))
+    up_lift_gradient, own_cols, *parts = in_order(up_lift_gradient, own_cols, *parts)
     near = sums[:8] + parts[0][:, :half].astype(F32)
     sums = jnp.concatenate([near, parts[1].astype(F32) + parts[2].astype(F32)], axis=1)
     moved = jnp.concatenate([moved[:8], parts[0][:, half:]], axis=1)
 
     low = jnp.concatenate([sums.astype(BF16), moved], axis=1)
     parts = from_far_z([low[2 * m : 2 * m + 2] for m in (1, 2, 3)])
-    up_lift_gradient = adapter_scale * rows_product(up_factor_up, own[1])
-    up_lift_gradient, *parts = in_order(up_lift_gradient, *parts)
+    gate_down_gradient, up_down_gradient = outer_products(
+        (own_cols, gate_factor_gate), (own_cols, gate_factor_up)
+    )
+    gate_down_gradient, up_down_gradient, *parts = in_order(
+        gate_down_gradient, up_down_gradient, *parts
+    )
     sums = sums[:2] + sum(p[:, :d].astype(F32) for p in parts)
     moved = jnp.stack([moved[:2]] + [p[:, d:] for p in parts])
     moved = moved.reshape(4, 2, 2, 2, feat_rows).transpose(0, 2, 3, 1, 4).reshape(N, 2 * feat_rows)

time: 105 us -> 104 us (level)
  matrix products: 13.7 us -> 1.76 us
  Pallas kernels: 42.1 us -> 51.2 us
  waiting for transfers between devices: 10.5 us -> 12.3 us
    dot_general x4 -> x0, matrix products: 12 us -> none  [rows_product(): lax.dot_general(left, right, (((0,), (0,)), ((), ())), preferred_element_...]
    pallas_call x0 -> x3, Pallas kernels: none -> 9.08 us  [outer_products(): pl.pallas_call(functools.partial(outer_kernel, len(pairs)), in_specs=[pl....]
  transfers between devices with their start and end apart: 26 -> 26, of which waited for: 11 -> 12; matrix products, arithmetic and copies ran while one was open for 13% -> 2% of each run, Pallas kernels for 36% -> 46%
where the time goes in v11:
time: 104 us; the launch traced here: 103 us
  Pallas kernels  51.2 us (49%)
  starting transfers between devices  31.1 us (30%)
  waiting for transfers between devices  12.3 us (12%)
  other arithmetic  4.63 us (4%)
  matrix products  1.76 us (2%)
  between operations  1.39 us (1%)
    ppermute x18, starting transfers between devices, along_tensor(): return lax.ppermute(value, 'tensor', [(i, i ^ mask) for i in range(N)])  22.1 us
    pallas_call x3, Pallas kernels, backward_products(): pl.pallas_call(functools.partial(backward_kernel, first), in_specs=[pl.Bl...  16.3 us
    pallas_call x4, Pallas kernels, forward_products(): pl.pallas_call(functools.partial(forward_kernel, first), in_specs=[pl.Blo...  14.8 us
    pallas_call x3, Pallas kernels, outer_products(): pl.pallas_call(functools.partial(outer_kernel, len(pairs)), in_specs=[pl....  9.08 us
    ppermute x8, starting transfers between devices, across_groups(): lax.ppermute(value, both, [(i, i ^ (N | mask)) for i in range(2 * N)])  9 us
    pallas_call x2, Pallas kernels, hidden_gradients(): pl.pallas_call(functools.partial(hidden_kernel, first, step), in_specs=[v...  8.72 us
    ppermute x18, waiting for transfers between devices, along_tensor(): return lax.ppermute(value, 'tensor', [(i, i ^ mask) for i in range(N)])  7.28 us
    ppermute x8, waiting for transfers between devices, across_groups(): lax.ppermute(value, both, [(i, i ^ (N | mask)) for i in range(2 * N)])  5.01 us
  transfers between devices with their start and end apart: 26, of which 12 were waited for; matrix products, arithmetic and copies ran while one was open for 2% of the time, Pallas kernels for 46%

profile of v11, /device:TPU:0, one launch (start us, length us, event | category | flops | bytes accessed | tf_op | source)
XLA Modules:
  0.0 103.3 jit_solution(16915134202586925265)
XLA Ops:
  0.6 3.1 %collective-permute-start = (bf16[2,8192]{1,0:T(2,128)(2,1)}, bf16[2,8192]{1,0:T(2,128)(2,1)S(1)}, u32[]{:S(2)}, u32[]{:S(2)}) collective-permute-start(bf16[2,8192]{1,0:T(2,128)(2,1)} %param.9), channel_id=1, source_target_pairs={{0,4},{1,5},{2,6},{3,7},{4,0},{5,1},{6,2},{7,3},{8,12},{9,13},{10,... | collective-permute-start | bytes 98312 | tf_op jit(solution)/shard_map/ppermute | solution.py:378
  3.7 2.3 %narrow.1 = (bf16[512,1024]{1,0:T(8,128)(2,1)S(1)}, bf16[512,1024]{1,0:T(8,128)(2,1)S(1)}) custom-call(f32[512,1024]{1,0:T(8,128)} %g_ref.1, f32[512,1024]{1,0:T(8,128)} %u_ref.1), custom_call_target="tpu_custom_call" | custom-call | bytes 6291456 | tf_op jit(solution)/shard_map/narrow/pallas_call | solution.py:164
  6.0 0.8 pad_maximum_fusion.10
  6.9 2.9 %collective-permute-start.1 = (bf16[4,8192]{1,0:T(4,128)(2,1)S(1)}, bf16[4,8192]{1,0:T(4,128)(2,1)S(1)}, u32[]{:S(2)}, u32[]{:S(2)}) collective-permute-start(bf16[4,8192]{1,0:T(4,128)(2,1)S(1)} %pad_maximum_fusion.10), channel_id=1, source_target_pairs={{0,8},{1,9},{2,10},{3,11},{4,12},{5,13},{6,14},{7,15},{8,0},{9,1},... | collective-permute-start | bytes 196616 | tf_op jit(solution)/shard_map/ppermute | solution.py:378
  9.8 2.3 %collective-permute-done.1 = bf16[4,8192]{1,0:T(4,128)(2,1)S(1)} collective-permute-done((bf16[4,8192]{1,0:T(4,128)(2,1)S(1)}, bf16[4,8192]{1,0:T(4,128)(2,1)S(1)}, u32[]{:S(2)}, u32[]{:S(2)}) %collective-permute-start.1) | collective-permute-done | bytes 65568 | tf_op jit(solution)/shard_map/ppermute | solution.py:378
  12.1 0.9 pad_maximum_fusion.6
  13.0 1.8 %collective-permute-start.2 = (bf16[8,4096]{1,0:T(8,128)(2,1)S(1)}, bf16[8,4096]{1,0:T(8,128)(2,1)S(1)}, u32[]{:S(2)}, u32[]{:S(2)}) collective-permute-start(bf16[8,4096]{1,0:T(8,128)(2,1)S(1)} %get-tuple-element.175), channel_id=1, source_target_pairs={{0,2},{1,3},{2,0},{3,1},{4,6},{5,7},{6,4},{7,5},{8,10},{9,11},{10,... | collective-permute-start | bytes 196616 | tf_op jit(solution)/shard_map/ppermute | solution.py:378
  14.8 1.5 %collective-permute-start.4 = (bf16[8,4096]{1,0:T(8,128)(2,1)S(1)}, bf16[8,4096]{1,0:T(8,128)(2,1)S(1)}, u32[]{:S(2)}, u32[]{:S(2)}) collective-permute-start(bf16[8,4096]{1,0:T(8,128)(2,1)S(1)} %get-tuple-element.176), channel_id=1, source_target_pairs={{0,18},{1,19},{2,16},{3,17},{4,22},{5,23},{6,20},{7,21},{8,26},{9,... | collective-permute-start | bytes 196616 | tf_op jit(solution)/shard_map/ppermute | solution.py:383
  16.6 1.2 %collective-permute-done.2 = bf16[8,4096]{1,0:T(8,128)(2,1)S(1)} collective-permute-done((bf16[8,4096]{1,0:T(8,128)(2,1)S(1)}, bf16[8,4096]{1,0:T(8,128)(2,1)S(1)}, u32[]{:S(2)}, u32[]{:S(2)}) %collective-permute-start.2) | collective-permute-done | bytes 65568 | tf_op jit(solution)/shard_map/ppermute | solution.py:378
  17.8 2.2 %collective-permute-done.4 = bf16[8,4096]{1,0:T(8,128)(2,1)S(1)} collective-permute-done((bf16[8,4096]{1,0:T(8,128)(2,1)S(1)}, bf16[8,4096]{1,0:T(8,128)(2,1)S(1)}, u32[]{:S(2)}, u32[]{:S(2)}) %collective-permute-start.4) | collective-permute-done | bytes 65568 | tf_op jit(solution)/shard_map/ppermute | solution.py:383
  20.0 0.7 collective-permute-done.3
  20.9 0.8 select_reduce_fusion
  21.7 0.6 collective-permute-done.5
  22.4 0.9 collective-permute-start.6
  23.3 4.1 %forward_products.4 = (f32[32,1024]{1,0:T(8,128)S(1)}, bf16[32,1024]{1,0:T(8,128)(2,1)S(1)}) custom-call(s32[1]{0:T(128)} %bitcast.3.side_ref, bf16[64,4096]{1,0:T(8,128)(2,1)S(1)} %bitcast.64, bf16[8192,1792]{1,0:T(8,128)(2,1)} %wg_ref.5), custom_call_target="tpu_custom_call" | custom-call | flops 536870912 | bytes 12582912 | tf_op jit(solution)/shard_map/forward_products/pallas_call | solution.py:135
  28.5 0.9 collective-permute-done.7
  29.5 1.2 %collective-permute-start.8 = (f32[32,128]{1,0:T(8,128)S(1)}, f32[32,128]{1,0:T(8,128)S(1)}, u32[]{:S(2)}, u32[]{:S(2)}) collective-permute-start(f32[32,128]{1,0:T(8,128)S(1)} %maximum_add_fusion.1), channel_id=1, source_target_pairs={{0,2},{1,3},{2,0},{3,1},{4,6},{5,7},{6,4},{7,5},{8,10},{9,11},{10,... | collective-permute-start | bytes 49160 | tf_op jit(solution)/shard_map/ppermute | solution.py:378
  30.7 4.0 %forward_products.5 = (f32[32,1024]{1,0:T(8,128)S(1)}, bf16[32,1024]{1,0:T(8,128)(2,1)S(1)}) custom-call(s32[1]{0:T(128)} %bitcast.3.side_ref, bf16[64,4096]{1,0:T(8,128)(2,1)S(1)} %bitcast.66, bf16[8192,1792]{1,0:T(8,128)(2,1)} %wu_ref.5), custom_call_target="tpu_custom_call" | custom-call | flops 536870912 | bytes 12582912 | tf_op jit(solution)/shard_map/forward_products/pallas_call | solution.py:135
  34.8 1.6 %collective-permute-start.9 = (f32[32,128]{1,0:T(8,128)S(1)}, f32[32,128]{1,0:T(8,128)S(1)}, u32[]{:S(2)}, u32[]{:S(2)}) collective-permute-start(f32[32,128]{1,0:T(8,128)S(1)} %maximum_add_fusion.2), channel_id=1, source_target_pairs={{0,4},{1,5},{2,6},{3,7},{4,0},{5,1},{6,2},{7,3},{8,12},{9,13},{10,... | collective-permute-start | bytes 49160 | tf_op jit(solution)/shard_map/ppermute | solution.py:378
  36.4 1.2 %collective-permute-start.10 = (bf16[2,32,1024]{2,1,0:T(8,128)(2,1)S(1)}, bf16[2,32,1024]{2,1,0:T(8,128)(2,1)S(1)}, u32[]{:S(2)}, u32[]{:S(2)}) collective-permute-start(bf16[2,32,1024]{2,1,0:T(8,128)(2,1)S(1)} %pad_maximum_fusion.7), channel_id=1, source_target_pairs={{0,16},{1,17},{2,18},{3,19},{4,20},{5,21},{6,22},{7,23},{8,24},{9,... | collective-permute-start | bytes 393224 | tf_op jit(solution)/shard_map/ppermute | solution.py:383
  37.7 3.3 %forward_products.6 = (f32[32,768]{1,0:T(8,128)S(1)}, bf16[32,768]{1,0:T(8,128)(2,1)S(1)}) custom-call(s32[1]{0:T(128)} %bitcast.3.side_ref, bf16[64,4096]{1,0:T(8,128)(2,1)S(1)} %bitcast.67, bf16[8192,1792]{1,0:T(8,128)(2,1)} %wg_ref.5), custom_call_target="tpu_custom_call" | custom-call | flops 402653184 | bytes 9437184 | tf_op jit(solution)/shard_map/forward_products/pallas_call | solution.py:135
  41.0 0.4 collective-permute-done.10.far_ref
  41.5 3.2 %collective-permute-start.11 = (f32[32,128]{1,0:T(8,128)S(1)}, f32[32,128]{1,0:T(8,128)S(1)}, u32[]{:S(2)}, u32[]{:S(2)}) collective-permute-start(f32[32,128]{1,0:T(8,128)S(1)} %add.222), channel_id=1, source_target_pairs={{0,8},{1,9},{2,10},{3,11},{4,12},{5,13},{6,14},{7,15},{8,0},{9,1},... | collective-permute-start | bytes 49160 | tf_op jit(solution)/shard_map/ppermute | solution.py:378
  44.8 3.3 %forward_products.7 = (f32[32,768]{1,0:T(8,128)S(1)}, bf16[32,768]{1,0:T(8,128)(2,1)S(1)}) custom-call(s32[1]{0:T(128)} %bitcast.3.side_ref, bf16[64,4096]{1,0:T(8,128)(2,1)S(1)} %bitcast.68, bf16[8192,1792]{1,0:T(8,128)(2,1)} %wu_ref.5), custom_call_target="tpu_custom_call" | custom-call | flops 402653184 | bytes 9437184 | tf_op jit(solution)/shard_map/forward_products/pallas_call | solution.py:135
  48.5 1.2 %collective-permute-start.12 = (bf16[2,32,768]{2,1,0:T(8,128)(2,1)S(1)}, bf16[2,32,768]{2,1,0:T(8,128)(2,1)S(1)}, u32[]{:S(2)}, u32[]{:S(2)}) collective-permute-start(bf16[2,32,768]{2,1,0:T(8,128)(2,1)S(1)} %pad_maximum_fusion.8), channel_id=1, source_target_pairs={{0,16},{1,17},{2,18},{3,19},{4,20},{5,21},{6,22},{7,23},{8,24},{9,... | collective-permute-start | bytes 294920 | tf_op jit(solution)/shard_map/ppermute | solution.py:383
  49.8 4.7 %hidden_gradients.2 = (bf16[2,32,1024]{2,1,0:T(8,128)(2,1)S(1)}, f32[32,1024]{1,0:T(8,128)S(1)}, f32[32,1024]{1,0:T(8,128)S(1)}) custom-call(bf16[32,1024]{1,0:T(8,128)(2,1)S(1)} %get-tuple-element.215.eug_ref.refs_0_, bf16[32,1024]{1,0:T(8,128)(2,1)S(1)} %get-tuple-element.216.euu_ref.refs_0_, f32[2,32,1024]{2,1,0:T(8,128)S(1)} %pad_maximum_fusion.3.keep_ref, ...), custom_call_target="tpu_custom_call" | custom-call | flops 268435456 | bytes 12582912 | tf_op jit(solution)/shard_map/hidden_gradients/pallas_call | solution.py:239
  54.6 4.0 %hidden_gradients.3 = (bf16[2,32,768]{2,1,0:T(8,128)(2,1)S(1)}, f32[32,1024]{1,0:T(8,128)S(1)}, f32[32,1024]{1,0:T(8,128)S(1)}) custom-call(bf16[32,1024]{1,0:T(8,128)(2,1)S(1)} %get-tuple-element.215.eug_ref.refs_0_, bf16[32,1024]{1,0:T(8,128)(2,1)S(1)} %get-tuple-element.216.euu_ref.refs_0_, f32[2,32,768]{2,1,0:T(8,128)S(1)} %pad_maximum_fusion.5.keep_ref, ...), custom_call_target="tpu_custom_call" | custom-call | flops 201326592 | bytes 9437184 | tf_op jit(solution)/shard_map/hidden_gradients/pallas_call | solution.py:239
  58.9 0.9 collective-permute-start.13
  60.0 3.4 %outer_products.3 = f32[1024,1792]{1,0:T(8,128)} custom-call(bf16[32,1024]{1,0:T(8,128)(2,1)S(1)} %get-tuple-element.215.eug_ref.refs_0_, bf16[32,1792]{1,0:T(8,128)(2,1)S(1)} %slice_bitcast_fusion.3.refs_1_), custom_call_target="tpu_custom_call" | custom-call | flops 117440512 | bytes 7340032 | tf_op jit(solution)/shard_map/outer_products/pallas_call | solution.py:354
  63.4 1.6 %collective-permute-done.13 = bf16[2,32,1792]{2,1,0:T(8,128)(2,1)S(1)} collective-permute-done((bf16[2,32,1792]{2,1,0:T(8,128)(2,1)S(1)}, bf16[2,32,1792]{2,1,0:T(8,128)(2,1)S(1)}, u32[]{:S(2)}, u32[]{:S(2)}) %collective-permute-start.13) | collective-permute-done | bytes 229408 | tf_op jit(solution)/shard_map/ppermute | solution.py:383
  65.1 0.7 collective-permute-start.15
  65.8 3.3 %backward_products.3 = (f32[32,512]{1,0:T(8,128)S(1)}, bf16[32,512]{1,0:T(8,128)(2,1)S(1)}) custom-call(s32[1]{0:T(128)} %bitcast.3.side_ref, bf16[64,1792]{1,0:T(8,128)(2,1)S(1)} %get-tuple-element.138.dg_ref, bf16[64,1792]{1,0:T(8,128)(2,1)S(1)} %get-tuple-element.139.du_ref, bf16[8192,1792]{1,0:T(8,128)(2,1)} %wg_ref.5, bf16[8192,1792]{1,0:T(8,128)(2,1)} %wu_ref.5), custom_call_target="tpu_custom_call" | custom-call | flops 234881024 | bytes 5505024 | tf_op jit(solution)/shard_map/backward_products/pallas_call | solution.py:307
  69.5 3.3 %backward_products.4 = (f32[32,512]{1,0:T(8,128)S(1)}, bf16[32,512]{1,0:T(8,128)(2,1)S(1)}) custom-call(s32[1]{0:T(128)} %bitcast.3.side_ref, bf16[64,1792]{1,0:T(8,128)(2,1)S(1)} %get-tuple-element.138.dg_ref, bf16[64,1792]{1,0:T(8,128)(2,1)S(1)} %get-tuple-element.139.du_ref, bf16[8192,1792]{1,0:T(8,128)(2,1)} %wg_ref.5, bf16[8192,1792]{1,0:T(8,128)(2,1)} %wu_ref.5), custom_call_target="tpu_custom_call" | custom-call | flops 234881024 | bytes 5505024 | tf_op jit(solution)/shard_map/backward_products/pallas_call | solution.py:307
  72.9 1.3 %collective-permute-start.17 = (f32[32,128]{1,0:T(8,128)S(1)}, f32[32,128]{1,0:T(8,128)S(1)}, u32[]{:S(2)}, u32[]{:S(2)}) collective-permute-start(f32[32,128]{1,0:T(8,128)S(1)} %add.244), channel_id=1, source_target_pairs={{0,8},{1,9},{2,10},{3,11},{4,12},{5,13},{6,14},{7,15},{8,0},{9,1},... | collective-permute-start | bytes 49160 | tf_op jit(solution)/shard_map/ppermute | solution.py:378
  74.3 9.8 %backward_products.5 = (f32[32,3072]{1,0:T(8,128)S(1)}, bf16[32,3072]{1,0:T(8,128)(2,1)S(1)}) custom-call(s32[1]{0:T(128)} %bitcast.3.side_ref, bf16[64,1792]{1,0:T(8,128)(2,1)S(1)} %get-tuple-element.138.dg_ref, bf16[64,1792]{1,0:T(8,128)(2,1)S(1)} %get-tuple-element.139.du_ref, bf16[8192,1792]{1,0:T(8,128)(2,1)} %wg_ref.5, bf16[8192,1792]{1,0:T(8,128)(2,1)} %wu_ref.5), custom_call_target="tpu_custom_call" | custom-call | flops 1409286144 | bytes 33030144 | tf_op jit(solution)/shard_map/backward_products/pallas_call | solution.py:307
  84.5 0.4 fusion.47
  85.1 0.4 fusion.1
  85.5 0.6 collective-permute-start.19
  86.1 0.8 collective-permute-done.19
  87.0 1.7 %collective-permute-start.22 = (bf16[8,4096]{1,0:T(8,128)(2,1)S(1)}, bf16[8,4096]{1,0:T(8,128)(2,1)S(1)}, u32[]{:S(2)}, u32[]{:S(2)}) collective-permute-start(bf16[8,4096]{1,0:T(8,128)(2,1)S(1)} %get-tuple-element.169), channel_id=1, source_target_pairs={{0,18},{1,19},{2,16},{3,17},{4,22},{5,23},{6,20},{7,21},{8,26},{9,... | collective-permute-start | bytes 196616 | tf_op jit(solution)/shard_map/ppermute | solution.py:383
  88.7 1.2 %collective-permute-start.21 = (bf16[8,4096]{1,0:T(8,128)(2,1)S(1)}, bf16[8,4096]{1,0:T(8,128)(2,1)S(1)}, u32[]{:S(2)}, u32[]{:S(2)}) collective-permute-start(bf16[8,4096]{1,0:T(8,128)(2,1)S(1)} %get-tuple-element.170), channel_id=1, source_target_pairs={{0,16},{1,17},{2,18},{3,19},{4,20},{5,21},{6,22},{7,23},{8,24},{9,... | collective-permute-start | bytes 196616 | tf_op jit(solution)/shard_map/ppermute | solution.py:383
  89.9 0.7 collective-permute-start.20
  90.6 3.4 %outer_products.4 = f32[1024,1792]{1,0:T(8,128)} custom-call(bf16[32,1024]{1,0:T(8,128)(2,1)S(1)} %get-tuple-element.216.euu_ref.refs_0_, bf16[32,1792]{1,0:T(8,128)(2,1)S(1)} %slice_bitcast_fusion.2.refs_1_), custom_call_target="tpu_custom_call" | custom-call | flops 117440512 | bytes 7340032 | tf_op jit(solution)/shard_map/outer_products/pallas_call | solution.py:354
  94.6 2.7 %collective-permute-start.25 = (bf16[2,10240]{1,0:T(2,128)(2,1)S(1)}, bf16[2,10240]{1,0:T(2,128)(2,1)S(1)}, u32[]{:S(2)}, u32[]{:S(2)}) collective-permute-start(bf16[2,10240]{1,0:T(2,128)(2,1)S(1)} %get-tuple-element.172), channel_id=1, source_target_pairs={{0,12},{1,13},{2,14},{3,15},{4,8},{5,9},{6,10},{7,11},{8,4},{9,5},... | collective-permute-start | bytes 122888 | tf_op jit(solution)/shard_map/ppermute | solution.py:378
  97.7 1.3 %collective-permute-start.23 = (bf16[2,10240]{1,0:T(2,128)(2,1)S(1)}, bf16[2,10240]{1,0:T(2,128)(2,1)S(1)}, u32[]{:S(2)}, u32[]{:S(2)}) collective-permute-start(bf16[2,10240]{1,0:T(2,128)(2,1)S(1)} %get-tuple-element.174), channel_id=1, source_target_pairs={{0,4},{1,5},{2,6},{3,7},{4,0},{5,1},{6,2},{7,3},{8,12},{9,13},{10,... | collective-permute-start | bytes 122888 | tf_op jit(solution)/shard_map/ppermute | solution.py:378
  99.1 2.3 %outer_products.5 = (f32[512,1024]{1,0:T(8,128)}, f32[512,1024]{1,0:T(8,128)}) custom-call(bf16[32,512]{1,0:T(8,128)(2,1)S(1)} %dynamic-slice_select_fusion.refs_0_.refs_2_, bf16[32,1024]{1,0:T(8,128)(2,1)S(1)} %get-tuple-element.211.refs_1_, bf16[32,512]{1,0:T(8,128)(2,1)S(1)} %dynamic-slice_select_fusion.refs_0_.refs_2_, ...), custom_call_target="tpu_custom_call" | custom-call | flops 67108864 | bytes 4194304 | tf_op jit(solution)/shard_map/outer_products/pallas_call | solution.py:354
  101.4 0.8 collective-permute-done.24
  102.6 0.7 fusion.10
  (111 shorter events, 5.0 us)
Async XLA Ops:
  0.6 27.6 %copy-start = (bf16[32,1792]{1,0:T(8,128)(2,1)S(1)}, bf16[32,1792]{1,0:T(8,128)(2,1)}, u32[]{:S(2)}) copy-start(bf16[32,1792]{1,0:T(8,128)(2,1)} %param.17) | copy-start | bytes 344068
  0.6 5.4 %collective-permute-start = (bf16[2,8192]{1,0:T(2,128)(2,1)}, bf16[2,8192]{1,0:T(2,128)(2,1)S(1)}, u32[]{:S(2)}, u32[]{:S(2)}) collective-permute-start(bf16[2,8192]{1,0:T(2,128)(2,1)} %param.9), channel_id=1, source_target_pairs={{0,4},{1,5},{2,6},{3,7},{4,0},{5,1},{6,2},{7,3},{8,12},{9,13},{10,... | collective-permute-start | bytes 98312 | tf_op jit(solution)/shard_map/ppermute | solution.py:378
  6.9 5.2 %collective-permute-start.1 = (bf16[4,8192]{1,0:T(4,128)(2,1)S(1)}, bf16[4,8192]{1,0:T(4,128)(2,1)S(1)}, u32[]{:S(2)}, u32[]{:S(2)}) collective-permute-start(bf16[4,8192]{1,0:T(4,128)(2,1)S(1)} %pad_maximum_fusion.10), channel_id=1, source_target_pairs={{0,8},{1,9},{2,10},{3,11},{4,12},{5,13},{6,14},{7,15},{8,0},{9,1},... | collective-permute-start | bytes 196616 | tf_op jit(solution)/shard_map/ppermute | solution.py:378
  13.0 4.7 %collective-permute-start.2 = (bf16[8,4096]{1,0:T(8,128)(2,1)S(1)}, bf16[8,4096]{1,0:T(8,128)(2,1)S(1)}, u32[]{:S(2)}, u32[]{:S(2)}) collective-permute-start(bf16[8,4096]{1,0:T(8,128)(2,1)S(1)} %get-tuple-element.175), channel_id=1, source_target_pairs={{0,2},{1,3},{2,0},{3,1},{4,6},{5,7},{6,4},{7,5},{8,10},{9,11},{10,... | collective-permute-start | bytes 196616 | tf_op jit(solution)/shard_map/ppermute | solution.py:378
  14.8 5.2 %collective-permute-start.4 = (bf16[8,4096]{1,0:T(8,128)(2,1)S(1)}, bf16[8,4096]{1,0:T(8,128)(2,1)S(1)}, u32[]{:S(2)}, u32[]{:S(2)}) collective-permute-start(bf16[8,4096]{1,0:T(8,128)(2,1)S(1)} %get-tuple-element.176), channel_id=1, source_target_pairs={{0,18},{1,19},{2,16},{3,17},{4,22},{5,23},{6,20},{7,21},{8,26},{9,... | collective-permute-start | bytes 196616 | tf_op jit(solution)/shard_map/ppermute | solution.py:383
  16.3 4.4 %collective-permute-start.3 = (bf16[8,4096]{1,0:T(8,128)(2,1)S(1)}, bf16[8,4096]{1,0:T(8,128)(2,1)S(1)}, u32[]{:S(2)}, u32[]{:S(2)}) collective-permute-start(bf16[8,4096]{1,0:T(8,128)(2,1)S(1)} %get-tuple-element.176), channel_id=1, source_target_pairs={{0,16},{1,17},{2,18},{3,19},{4,20},{5,21},{6,22},{7,23},{8,24},{9,... | collective-permute-start | bytes 196616 | tf_op jit(solution)/shard_map/ppermute | solution.py:383
  20.7 1.6 %collective-permute-start.5 = (bf16[2,16,4096]{2,1,0:T(8,128)(2,1)S(1)}, bf16[2,16,4096]{2,1,0:T(8,128)(2,1)S(1)}, u32[]{:S(2)}, u32[]{:S(2)}) collective-permute-start(bf16[2,16,4096]{2,1,0:T(8,128)(2,1)S(1)} %pad_maximum_fusion.2), channel_id=1, source_target_pairs={{0,1},{1,0},{2,3},{3,2},{4,5},{5,4},{6,7},{7,6},{8,9},{9,8},{10,11... | collective-permute-start | bytes 786440 | tf_op jit(solution)/shard_map/ppermute | solution.py:378
  22.4 5.1 %collective-permute-start.6 = (bf16[32,512]{1,0:T(8,128)(2,1)S(1)}, bf16[32,512]{1,0:T(8,128)(2,1)S(1)}, u32[]{:S(2)}, u32[]{:S(2)}) collective-permute-start(bf16[32,512]{1,0:T(8,128)(2,1)S(1)} %dynamic-slice.1), channel_id=1, source_target_pairs={{0,16},{1,17},{2,18},{3,19},{4,20},{5,21},{6,22},{7,23},{8,24},{9,... | collective-permute-start | bytes 98312 | tf_op jit(solution)/shard_map/ppermute | solution.py:383
  28.2 1.2 %collective-permute-start.7 = (f32[32,128]{1,0:T(8,128)S(1)}, f32[32,128]{1,0:T(8,128)S(1)}, u32[]{:S(2)}, u32[]{:S(2)}) collective-permute-start(f32[32,128]{1,0:T(8,128)S(1)} %pad_maximum_fusion.17), channel_id=1, source_target_pairs={{0,1},{1,0},{2,3},{3,2},{4,5},{5,4},{6,7},{7,6},{8,9},{9,8},{10,11... | collective-permute-start | bytes 49160 | tf_op jit(solution)/shard_map/ppermute | solution.py:378
  29.5 5.2 %collective-permute-start.8 = (f32[32,128]{1,0:T(8,128)S(1)}, f32[32,128]{1,0:T(8,128)S(1)}, u32[]{:S(2)}, u32[]{:S(2)}) collective-permute-start(f32[32,128]{1,0:T(8,128)S(1)} %maximum_add_fusion.1), channel_id=1, source_target_pairs={{0,2},{1,3},{2,0},{3,1},{4,6},{5,7},{6,4},{7,5},{8,10},{9,11},{10,... | collective-permute-start | bytes 49160 | tf_op jit(solution)/shard_map/ppermute | solution.py:378
  34.8 6.3 %collective-permute-start.9 = (f32[32,128]{1,0:T(8,128)S(1)}, f32[32,128]{1,0:T(8,128)S(1)}, u32[]{:S(2)}, u32[]{:S(2)}) collective-permute-start(f32[32,128]{1,0:T(8,128)S(1)} %maximum_add_fusion.2), channel_id=1, source_target_pairs={{0,4},{1,5},{2,6},{3,7},{4,0},{5,1},{6,2},{7,3},{8,12},{9,13},{10,... | collective-permute-start | bytes 49160 | tf_op jit(solution)/shard_map/ppermute | solution.py:378
  36.4 5.1 %collective-permute-start.10 = (bf16[2,32,1024]{2,1,0:T(8,128)(2,1)S(1)}, bf16[2,32,1024]{2,1,0:T(8,128)(2,1)S(1)}, u32[]{:S(2)}, u32[]{:S(2)}) collective-permute-start(bf16[2,32,1024]{2,1,0:T(8,128)(2,1)S(1)} %pad_maximum_fusion.7), channel_id=1, source_target_pairs={{0,16},{1,17},{2,18},{3,19},{4,20},{5,21},{6,22},{7,23},{8,24},{9,... | collective-permute-start | bytes 393224 | tf_op jit(solution)/shard_map/ppermute | solution.py:383
  41.5 6.6 %collective-permute-start.11 = (f32[32,128]{1,0:T(8,128)S(1)}, f32[32,128]{1,0:T(8,128)S(1)}, u32[]{:S(2)}, u32[]{:S(2)}) collective-permute-start(f32[32,128]{1,0:T(8,128)S(1)} %add.222), channel_id=1, source_target_pairs={{0,8},{1,9},{2,10},{3,11},{4,12},{5,13},{6,14},{7,15},{8,0},{9,1},... | collective-permute-start | bytes 49160 | tf_op jit(solution)/shard_map/ppermute | solution.py:378
  48.5 6.0 %collective-permute-start.12 = (bf16[2,32,768]{2,1,0:T(8,128)(2,1)S(1)}, bf16[2,32,768]{2,1,0:T(8,128)(2,1)S(1)}, u32[]{:S(2)}, u32[]{:S(2)}) collective-permute-start(bf16[2,32,768]{2,1,0:T(8,128)(2,1)S(1)} %pad_maximum_fusion.8), channel_id=1, source_target_pairs={{0,16},{1,17},{2,18},{3,19},{4,20},{5,21},{6,22},{7,23},{8,24},{9,... | collective-permute-start | bytes 294920 | tf_op jit(solution)/shard_map/ppermute | solution.py:383
  58.9 6.1 %collective-permute-start.13 = (bf16[2,32,1792]{2,1,0:T(8,128)(2,1)S(1)}, bf16[2,32,1792]{2,1,0:T(8,128)(2,1)S(1)}, u32[]{:S(2)}, u32[]{:S(2)}) collective-permute-start(bf16[2,32,1792]{2,1,0:T(8,128)(2,1)S(1)} %constant_dynamic-update-slice_fusion), channel_id=1, source_target_pairs={{0,16},{1,17},{2,18},{3,19},{4,20},{5,21},{6,22},{7,23},{8,24},{9,... | collective-permute-start | bytes 688136 | tf_op jit(solution)/shard_map/ppermute | solution.py:383
  59.9 3.4 %collective-permute-start.14 = (f32[32,128]{1,0:T(8,128)S(1)}, f32[32,128]{1,0:T(8,128)S(1)}, u32[]{:S(2)}, u32[]{:S(2)}) collective-permute-start(f32[32,128]{1,0:T(8,128)S(1)} %pad_maximum_fusion.20), channel_id=1, source_target_pairs={{0,1},{1,0},{2,3},{3,2},{4,5},{5,4},{6,7},{7,6},{8,9},{9,8},{10,11... | collective-permute-start | bytes 49160 | tf_op jit(solution)/shard_map/ppermute | solution.py:378
  65.1 4.0 %collective-permute-start.15 = (f32[32,128]{1,0:T(8,128)S(1)}, f32[32,128]{1,0:T(8,128)S(1)}, u32[]{:S(2)}, u32[]{:S(2)}) collective-permute-start(f32[32,128]{1,0:T(8,128)S(1)} %maximum_add_fusion.3), channel_id=1, source_target_pairs={{0,2},{1,3},{2,0},{3,1},{4,6},{5,7},{6,4},{7,5},{8,10},{9,11},{10,... | collective-permute-start | bytes 49160 | tf_op jit(solution)/shard_map/ppermute | solution.py:378
  69.1 3.8 %collective-permute-start.16 = (f32[32,128]{1,0:T(8,128)S(1)}, f32[32,128]{1,0:T(8,128)S(1)}, u32[]{:S(2)}, u32[]{:S(2)}) collective-permute-start(f32[32,128]{1,0:T(8,128)S(1)} %maximum_add_fusion.4), channel_id=1, source_target_pairs={{0,4},{1,5},{2,6},{3,7},{4,0},{5,1},{6,2},{7,3},{8,12},{9,13},{10,... | collective-permute-start | bytes 49160 | tf_op jit(solution)/shard_map/ppermute | solution.py:378
  72.9 11.1 %collective-permute-start.17 = (f32[32,128]{1,0:T(8,128)S(1)}, f32[32,128]{1,0:T(8,128)S(1)}, u32[]{:S(2)}, u32[]{:S(2)}) collective-permute-start(f32[32,128]{1,0:T(8,128)S(1)} %add.244), channel_id=1, source_target_pairs={{0,8},{1,9},{2,10},{3,11},{4,12},{5,13},{6,14},{7,15},{8,0},{9,1},... | collective-permute-start | bytes 49160 | tf_op jit(solution)/shard_map/ppermute | solution.py:378
  84.5 18.8 %copy-start.1 = (bf16[32,1792]{1,0:T(8,128)(2,1)S(1)}, bf16[32,1792]{1,0:T(8,128)(2,1)}, u32[]{:S(2)}) copy-start(bf16[32,1792]{1,0:T(8,128)(2,1)} %param.17) | copy-start | bytes 344068
  85.0 1.9 %collective-permute-start.18 = (bf16[32,4096]{1,0:T(8,128)(2,1)S(1)}, bf16[32,4096]{1,0:T(8,128)(2,1)S(1)}, u32[]{:S(2)}, u32[]{:S(2)}) collective-permute-start(bf16[32,4096]{1,0:T(8,128)(2,1)S(1)} %pad_maximum_fusion.4), channel_id=1, source_target_pairs={{0,1},{1,0},{2,3},{3,2},{4,5},{5,4},{6,7},{7,6},{8,9},{9,8},{10,11... | collective-permute-start | bytes 786440 | tf_op jit(solution)/shard_map/ppermute | solution.py:378
  85.5 1.4 %collective-permute-start.19 = (bf16[16,512]{1,0:T(8,128)(2,1)S(1)}, bf16[16,512]{1,0:T(8,128)(2,1)S(1)}, u32[]{:S(2)}, u32[]{:S(2)}) collective-permute-start(bf16[16,512]{1,0:T(8,128)(2,1)S(1)} %get-tuple-element.182), channel_id=1, source_target_pairs={{0,1},{1,0},{2,3},{3,2},{4,5},{5,4},{6,7},{7,6},{8,9},{9,8},{10,11... | collective-permute-start | bytes 49160 | tf_op jit(solution)/shard_map/ppermute | solution.py:378
  87.0 7.0 %collective-permute-start.22 = (bf16[8,4096]{1,0:T(8,128)(2,1)S(1)}, bf16[8,4096]{1,0:T(8,128)(2,1)S(1)}, u32[]{:S(2)}, u32[]{:S(2)}) collective-permute-start(bf16[8,4096]{1,0:T(8,128)(2,1)S(1)} %get-tuple-element.169), channel_id=1, source_target_pairs={{0,18},{1,19},{2,16},{3,17},{4,22},{5,23},{6,20},{7,21},{8,26},{9,... | collective-permute-start | bytes 196616 | tf_op jit(solution)/shard_map/ppermute | solution.py:383
  88.7 5.3 %collective-permute-start.21 = (bf16[8,4096]{1,0:T(8,128)(2,1)S(1)}, bf16[8,4096]{1,0:T(8,128)(2,1)S(1)}, u32[]{:S(2)}, u32[]{:S(2)}) collective-permute-start(bf16[8,4096]{1,0:T(8,128)(2,1)S(1)} %get-tuple-element.170), channel_id=1, source_target_pairs={{0,16},{1,17},{2,18},{3,19},{4,20},{5,21},{6,22},{7,23},{8,24},{9,... | collective-permute-start | bytes 196616 | tf_op jit(solution)/shard_map/ppermute | solution.py:383
  89.9 4.5 %collective-permute-start.20 = (bf16[8,5120]{1,0:T(8,128)(2,1)S(1)}, bf16[8,5120]{1,0:T(8,128)(2,1)S(1)}, u32[]{:S(2)}, u32[]{:S(2)}) collective-permute-start(bf16[8,5120]{1,0:T(8,128)(2,1)S(1)} %pad_maximum_fusion.9), channel_id=1, source_target_pairs={{0,2},{1,3},{2,0},{3,1},{4,6},{5,7},{6,4},{7,5},{8,10},{9,11},{10,... | collective-permute-start | bytes 245768 | tf_op jit(solution)/shard_map/ppermute | solution.py:378
  94.6 6.8 %collective-permute-start.25 = (bf16[2,10240]{1,0:T(2,128)(2,1)S(1)}, bf16[2,10240]{1,0:T(2,128)(2,1)S(1)}, u32[]{:S(2)}, u32[]{:S(2)}) collective-permute-start(bf16[2,10240]{1,0:T(2,128)(2,1)S(1)} %get-tuple-element.172), channel_id=1, source_target_pairs={{0,12},{1,13},{2,14},{3,15},{4,8},{5,9},{6,10},{7,11},{8,4},{9,5},... | collective-permute-start | bytes 122888 | tf_op jit(solution)/shard_map/ppermute | solution.py:378
  97.3 4.9 %collective-permute-start.24 = (bf16[2,10240]{1,0:T(2,128)(2,1)S(1)}, bf16[2,10240]{1,0:T(2,128)(2,1)S(1)}, u32[]{:S(2)}, u32[]{:S(2)}) collective-permute-start(bf16[2,10240]{1,0:T(2,128)(2,1)S(1)} %get-tuple-element.173), channel_id=1, source_target_pairs={{0,8},{1,9},{2,10},{3,11},{4,12},{5,13},{6,14},{7,15},{8,0},{9,1},... | collective-permute-start | bytes 122888 | tf_op jit(solution)/shard_map/ppermute | solution.py:378
  97.7 4.5 %collective-permute-start.23 = (bf16[2,10240]{1,0:T(2,128)(2,1)S(1)}, bf16[2,10240]{1,0:T(2,128)(2,1)S(1)}, u32[]{:S(2)}, u32[]{:S(2)}) collective-permute-start(bf16[2,10240]{1,0:T(2,128)(2,1)S(1)} %get-tuple-element.174), channel_id=1, source_target_pairs={{0,4},{1,5},{2,6},{3,7},{4,0},{5,1},{6,2},{7,3},{8,12},{9,13},{10,... | collective-permute-start | bytes 122888 | tf_op jit(solution)/shard_map/ppermute | solution.py:378

commit v12 on v11

--- a/solution.py
+++ b/solution.py
@@ -151,6 +151,71 @@
         ),
         name="forward_products",
     )(side, x, pltpu.with_memory_space_constraint(weight, pltpu.HBM))
+
+
+def ahead_kernel(side_ref, w_ref, out_ref, again_ref, sem):
+    pieces = sem.shape[0]
+    depth = out_ref.shape[0] // pieces
+    base = side_ref[0] * out_ref.shape[0]
+    again_ref[0] = side_ref[0]
+    copies = [
+        pltpu.make_async_copy(
+            w_ref.at[
+                pl.ds(pl.multiple_of(base + k * depth, depth), depth), pl.ds(0, out_ref.shape[1])
+            ],
+            out_ref.at[pl.ds(k * depth, depth)],
+            sem.at[k],
+        )
+        for k in range(pieces)
+    ]
+    for copy in copies:
+        copy.start()
+    for copy in copies:
+        copy.wait()
+
+
+def columns_ahead(side, weight, count, pieces=8):
+    depth = weight.shape[0] // 2
+    smem = pl.BlockSpec(memory_space=pltpu.SMEM)
+    return pl.pallas_call(
+        ahead_kernel,
+        in_specs=[smem, pl.BlockSpec(memory_space=pltpu.HBM)],
+        out_specs=[pl.BlockSpec(memory_space=pl.ANY), smem],
+        out_shape=[
+            pltpu.VMEM((depth, count), weight.dtype),
+            jax.ShapeDtypeStruct((1,), jnp.int32),
+        ],
+        scratch_shapes=[pltpu.SemaphoreType.DMA((pieces,))],
+        compiler_params=pltpu.CompilerParams(vmem_limit_bytes=2 << 20),
+        cost_estimate=pl.CostEstimate(
+            flops=0, bytes_accessed=3 * depth * count, transcendentals=0
+        ),
+        name="columns_ahead",
+    )(side, pltpu.with_memory_space_constraint(weight, pltpu.HBM))
+
+
+def product_kernel(x_ref, w_ref, keep_ref, send_ref):
+    half = keep_ref.shape[0]
+    total = jnp.dot(x_ref[...], w_ref[...], preferred_element_type=F32)
+    keep_ref[...] = total[:half]
+    send_ref[...] = total[half:].astype(send_ref.dtype)
+
+
+def product_ahead(x, w):
+    rows, depth = x.shape
+    count = w.shape[1]
+    vmem = pl.BlockSpec(memory_space=pltpu.VMEM)
+    return pl.pallas_call(
+        product_kernel,
+        in_specs=[vmem] * 2,
+        out_specs=[vmem] * 2,
+        out_shape=[jax.ShapeDtypeStruct((rows // 2, count), kind) for kind in (F32, BF16)],
+        compiler_params=pltpu.CompilerParams(vmem_limit_bytes=8 << 20),
+        cost_estimate=pl.CostEstimate(
+            flops=2 * rows * count * depth, bytes_accessed=depth * count, transcendentals=0
+        ),
+        name="product_ahead",
+    )(x, w)
 
 
 def narrow_kernel(g_ref, u_ref, g16_ref, u16_ref):
@@ -426,7 +491,11 @@
     line = jnp.concatenate([line, along_tensor(line, 8)], axis=0)
     mine = lax.dynamic_slice_in_dim(line, group * half, half, 1)
     other = lax.dynamic_slice_in_dim(line, half - group * half, half, 1)
+    side, mine, other = in_order(side, mine, other)
     parts = [along_tensor(mine, X), across_groups(other), across_groups(other, X)]
+    cut = ff * 4 // 7
+    w, side = columns_ahead(side, gate_weight, cut)
+    side, *parts = in_order(side, *parts)
     x = jnp.stack(
         [jnp.concatenate([mine, parts[0]], axis=0), jnp.concatenate([parts[1], parts[2]], axis=0)]
     )
@@ -451,13 +520,11 @@
 
     blocks = lax.dynamic_slice_in_dim(x, (t % per_half) * feat_rows, feat_rows, 1)
     swapped = across_groups(blocks[rows:])
-    cut = ff * 4 // 7
-
     def forward(weight, late):
         first, count = (cut, ff - cut) if late else (0, cut)
         return forward_products(side, x, weight, first, count)
 
-    keep_0, send_0 = forward(gate_weight, False)
+    keep_0, send_0 = product_ahead(x, w)
     swapped, x, keep_0, send_0 = in_order(swapped, x, keep_0, send_0)
     own_cols = jnp.where(t // per_half == group, blocks[:rows], swapped)
     part = jnp.concatenate(

time: 104 us -> 112 us (1.077)
  local copies, waits for them, and re-layouts: 0.91 us -> 7.6 us
  Pallas kernels: 51.2 us -> 56.7 us
  waiting for transfers between devices: 12.3 us -> 9.93 us
    unnamed x7 -> x13, local copies, waits for them, and re-layouts: 0.1 us -> 6.79 us
    pallas_call x0 -> x2, Pallas kernels: none -> 5.72 us  [the longest x1 4.14 us: columns_ahead(): pl.pallas_call(ahead_kernel, in_specs=[smem, pl.BlockSpec(memory_space=pl...]
    ppermute x8, waiting for transfers between devices: 5.01 us -> 2.15 us  [across_groups(): lax.ppermute(value, both, [(i, i ^ (N | mask)) for i in range(2 * N)])]
    pallas_call x4 -> x3, Pallas kernels: 14.8 us -> 12.6 us  [forward_products(): pl.pallas_call(functools.partial(forward_kernel, first), in_specs=[pl.Blo...]
    pallas_call x3, Pallas kernels: 16.3 us -> 18.2 us  [backward_products(): pl.pallas_call(functools.partial(backward_kernel, first), in_specs=[pl.Bl...]
  transfers between devices with their start and end apart: 26 -> 26, of which waited for: 12 -> 8; matrix products, arithmetic and copies ran while one was open for 2% -> 1% of each run, Pallas kernels for 46% -> 47%
where the time goes in v12:
time: 112 us
  Pallas kernels  56.7 us (51%)
  starting transfers between devices  30.6 us (27%)
  waiting for transfers between devices  9.93 us (9%)
  local copies, waits for them, and re-layouts  7.6 us (7%)
  other arithmetic  4.05 us (4%)
  matrix products  1.75 us (2%)
  between operations  1.43 us (1%)
    ppermute x18, starting transfers between devices, along_tensor(): return lax.ppermute(value, 'tensor', [(i, i ^ mask) for i in range(N)])  21.3 us
    pallas_call x3, Pallas kernels, backward_products(): pl.pallas_call(functools.partial(backward_kernel, first), in_specs=[pl.Bl...  18.2 us
    pallas_call x3, Pallas kernels, forward_products(): pl.pallas_call(functools.partial(forward_kernel, first), in_specs=[pl.Blo...  12.6 us
    ppermute x8, starting transfers between devices, across_groups(): lax.ppermute(value, both, [(i, i ^ (N | mask)) for i in range(2 * N)])  9.31 us
    pallas_call x3, Pallas kernels, outer_products(): pl.pallas_call(functools.partial(outer_kernel, len(pairs)), in_specs=[pl....  9.08 us
    pallas_call x2, Pallas kernels, hidden_gradients(): pl.pallas_call(functools.partial(hidden_kernel, first, step), in_specs=[v...  8.72 us
    ppermute x18, waiting for transfers between devices, along_tensor(): return lax.ppermute(value, 'tensor', [(i, i ^ mask) for i in range(N)])  7.78 us
    unnamed x13, local copies, waits for them, and re-layouts  6.79 us
  transfers between devices with their start and end apart: 26, of which 8 were waited for; matrix products, arithmetic and copies ran while one was open for 1% of the time, Pallas kernels for 47%

profile of v12, /device:TPU:0, one launch (start us, length us, event | category | flops | bytes accessed | tf_op | source)
XLA Modules:
  0.0 112.1 jit_solution(13982531143585103005)
XLA Ops:
  0.6 3.1 %collective-permute-start = (bf16[2,8192]{1,0:T(2,128)(2,1)}, bf16[2,8192]{1,0:T(2,128)(2,1)S(1)}, u32[]{:S(2)}, u32[]{:S(2)}) collective-permute-start(bf16[2,8192]{1,0:T(2,128)(2,1)} %param.9), channel_id=1, source_target_pairs={{0,4},{1,5},{2,6},{3,7},{4,0},{5,1},{6,2},{7,3},{8,12},{9,13},{10,... | collective-permute-start | bytes 98312 | tf_op jit(solution)/shard_map/ppermute | solution.py:443
  3.7 2.3 %narrow.1 = (bf16[512,1024]{1,0:T(8,128)(2,1)S(1)}, bf16[512,1024]{1,0:T(8,128)(2,1)S(1)}) custom-call(f32[512,1024]{1,0:T(8,128)} %g_ref.1, f32[512,1024]{1,0:T(8,128)} %u_ref.1), custom_call_target="tpu_custom_call" | custom-call | bytes 6291456 | tf_op jit(solution)/shard_map/narrow/pallas_call | solution.py:229
  6.0 0.8 pad_maximum_fusion.10
  6.9 2.9 %collective-permute-start.1 = (bf16[4,8192]{1,0:T(4,128)(2,1)S(1)}, bf16[4,8192]{1,0:T(4,128)(2,1)S(1)}, u32[]{:S(2)}, u32[]{:S(2)}) collective-permute-start(bf16[4,8192]{1,0:T(4,128)(2,1)S(1)} %pad_maximum_fusion.10), channel_id=1, source_target_pairs={{0,8},{1,9},{2,10},{3,11},{4,12},{5,13},{6,14},{7,15},{8,0},{9,1},... | collective-permute-start | bytes 196616 | tf_op jit(solution)/shard_map/ppermute | solution.py:443
  9.8 2.3 %collective-permute-done.1 = bf16[4,8192]{1,0:T(4,128)(2,1)S(1)} collective-permute-done((bf16[4,8192]{1,0:T(4,128)(2,1)S(1)}, bf16[4,8192]{1,0:T(4,128)(2,1)S(1)}, u32[]{:S(2)}, u32[]{:S(2)}) %collective-permute-start.1) | collective-permute-done | bytes 65568 | tf_op jit(solution)/shard_map/ppermute | solution.py:443
  12.1 0.9 pad_maximum_fusion.6
  13.0 1.8 %collective-permute-start.2 = (bf16[8,4096]{1,0:T(8,128)(2,1)S(1)}, bf16[8,4096]{1,0:T(8,128)(2,1)S(1)}, u32[]{:S(2)}, u32[]{:S(2)}) collective-permute-start(bf16[8,4096]{1,0:T(8,128)(2,1)S(1)} %get-tuple-element.97), channel_id=1, source_target_pairs={{0,2},{1,3},{2,0},{3,1},{4,6},{5,7},{6,4},{7,5},{8,10},{9,11},{10,... | collective-permute-start | bytes 196616 | tf_op jit(solution)/shard_map/ppermute | solution.py:443
  14.8 1.5 %collective-permute-start.4 = (bf16[8,4096]{1,0:T(8,128)(2,1)S(1)}, bf16[8,4096]{1,0:T(8,128)(2,1)S(1)}, u32[]{:S(2)}, u32[]{:S(2)}) collective-permute-start(bf16[8,4096]{1,0:T(8,128)(2,1)S(1)} %get-tuple-element.100), channel_id=1, source_target_pairs={{0,18},{1,19},{2,16},{3,17},{4,22},{5,23},{6,20},{7,21},{8,26},{9,... | collective-permute-start | bytes 196616 | tf_op jit(solution)/shard_map/ppermute | solution.py:448
  16.6 4.1 %columns_ahead.1 = (bf16[4096,1024]{1,0:T(8,128)(2,1)S(1)}, s32[1]{0:T(128)}) custom-call(s32[1]{0:T(128)} %bitcast.side_ref, bf16[8192,1792]{1,0:T(8,128)(2,1)} %wg_ref.5), custom_call_target="tpu_custom_call" | custom-call | bytes 12582912 | tf_op jit(solution)/shard_map/columns_ahead/pallas_call | solution.py:180
  20.7 3.3 %copy-done.2 = bf16[4096,1024]{1,0:T(8,128)(2,1)} copy-done((bf16[4096,1024]{1,0:T(8,128)(2,1)}, bf16[4096,1024]{1,0:T(8,128)(2,1)S(1)}, u32[]{:S(2)}) %copy-start.2) | copy-done | bytes 8388632
  24.4 1.3 %collective-permute-done.5 = bf16[2,16,4096]{2,1,0:T(8,128)(2,1)S(1)} collective-permute-done((bf16[2,16,4096]{2,1,0:T(8,128)(2,1)S(1)}, bf16[2,16,4096]{2,1,0:T(8,128)(2,1)S(1)}, u32[]{:S(2)}, u32[]{:S(2)}) %collective-permute-start.5) | collective-permute-done | bytes 262176 | tf_op jit(solution)/shard_map/ppermute | solution.py:443
  25.8 1.7 %collective-permute-start.6 = (bf16[32,512]{1,0:T(8,128)(2,1)S(1)}, bf16[32,512]{1,0:T(8,128)(2,1)S(1)}, u32[]{:S(2)}, u32[]{:S(2)}) collective-permute-start(bf16[32,512]{1,0:T(8,128)(2,1)S(1)} %dynamic-slice.1), channel_id=1, source_target_pairs={{0,16},{1,17},{2,18},{3,19},{4,20},{5,21},{6,22},{7,23},{8,24},{9,... | collective-permute-start | bytes 98312 | tf_op jit(solution)/shard_map/ppermute | solution.py:448
  27.5 3.4 %copy-done.3 = bf16[4096,1024]{1,0:T(8,128)(2,1)S(1)} copy-done((bf16[4096,1024]{1,0:T(8,128)(2,1)S(1)}, bf16[4096,1024]{1,0:T(8,128)(2,1)}, u32[]{:S(2)}) %copy-start.3) | copy-done | bytes 8388632
  30.8 1.6 %product_ahead.1 = (f32[32,1024]{1,0:T(8,128)S(1)}, bf16[32,1024]{1,0:T(8,128)(2,1)S(1)}) custom-call(bf16[64,4096]{1,0:T(8,128)(2,1)S(1)} %bitcast.64, bf16[4096,1024]{1,0:T(8,128)(2,1)S(1)} %copy-done.3), custom_call_target="tpu_custom_call" | custom-call | flops 536870912 | bytes 4194304 | tf_op jit(solution)/shard_map/product_ahead/pallas_call | solution.py:208
  33.6 0.9 collective-permute-done.7
  34.6 1.5 %collective-permute-start.8 = (f32[32,128]{1,0:T(8,128)S(1)}, f32[32,128]{1,0:T(8,128)S(1)}, u32[]{:S(2)}, u32[]{:S(2)}) collective-permute-start(f32[32,128]{1,0:T(8,128)S(1)} %maximum_add_fusion.1), channel_id=1, source_target_pairs={{0,2},{1,3},{2,0},{3,1},{4,6},{5,7},{6,4},{7,5},{8,10},{9,11},{10,... | collective-permute-start | bytes 49160 | tf_op jit(solution)/shard_map/ppermute | solution.py:443
  36.1 4.7 %forward_products.3 = (f32[32,1024]{1,0:T(8,128)S(1)}, bf16[32,1024]{1,0:T(8,128)(2,1)S(1)}) custom-call(s32[1]{0:T(128)} %get-tuple-element.113.side_ref, bf16[64,4096]{1,0:T(8,128)(2,1)S(1)} %bitcast.66, bf16[8192,1792]{1,0:T(8,128)(2,1)} %wu_ref.5), custom_call_target="tpu_custom_call" | custom-call | flops 536870912 | bytes 12582912 | tf_op jit(solution)/shard_map/forward_products/pallas_call | solution.py:135
  40.8 1.6 %collective-permute-start.9 = (f32[32,128]{1,0:T(8,128)S(1)}, f32[32,128]{1,0:T(8,128)S(1)}, u32[]{:S(2)}, u32[]{:S(2)}) collective-permute-start(f32[32,128]{1,0:T(8,128)S(1)} %maximum_add_fusion.2), channel_id=1, source_target_pairs={{0,4},{1,5},{2,6},{3,7},{4,0},{5,1},{6,2},{7,3},{8,12},{9,13},{10,... | collective-permute-start | bytes 49160 | tf_op jit(solution)/shard_map/ppermute | solution.py:443
  42.4 0.7 collective-permute-start.10
  43.1 4.0 %forward_products.4 = (f32[32,768]{1,0:T(8,128)S(1)}, bf16[32,768]{1,0:T(8,128)(2,1)S(1)}) custom-call(s32[1]{0:T(128)} %get-tuple-element.113.side_ref, bf16[64,4096]{1,0:T(8,128)(2,1)S(1)} %bitcast.67, bf16[8192,1792]{1,0:T(8,128)(2,1)} %wg_ref.5), custom_call_target="tpu_custom_call" | custom-call | flops 402653184 | bytes 9437184 | tf_op jit(solution)/shard_map/forward_products/pallas_call | solution.py:135
  47.5 3.2 %collective-permute-start.11 = (f32[32,128]{1,0:T(8,128)S(1)}, f32[32,128]{1,0:T(8,128)S(1)}, u32[]{:S(2)}, u32[]{:S(2)}) collective-permute-start(f32[32,128]{1,0:T(8,128)S(1)} %add.222), channel_id=1, source_target_pairs={{0,8},{1,9},{2,10},{3,11},{4,12},{5,13},{6,14},{7,15},{8,0},{9,1},... | collective-permute-start | bytes 49160 | tf_op jit(solution)/shard_map/ppermute | solution.py:443
  50.8 4.0 %forward_products.5 = (f32[32,768]{1,0:T(8,128)S(1)}, bf16[32,768]{1,0:T(8,128)(2,1)S(1)}) custom-call(s32[1]{0:T(128)} %get-tuple-element.113.side_ref, bf16[64,4096]{1,0:T(8,128)(2,1)S(1)} %bitcast.68, bf16[8192,1792]{1,0:T(8,128)(2,1)} %wu_ref.5), custom_call_target="tpu_custom_call" | custom-call | flops 402653184 | bytes 9437184 | tf_op jit(solution)/shard_map/forward_products/pallas_call | solution.py:135
  55.2 1.1 %collective-permute-start.12 = (bf16[2,32,768]{2,1,0:T(8,128)(2,1)S(1)}, bf16[2,32,768]{2,1,0:T(8,128)(2,1)S(1)}, u32[]{:S(2)}, u32[]{:S(2)}) collective-permute-start(bf16[2,32,768]{2,1,0:T(8,128)(2,1)S(1)} %pad_maximum_fusion.8), channel_id=1, source_target_pairs={{0,16},{1,17},{2,18},{3,19},{4,20},{5,21},{6,22},{7,23},{8,24},{9,... | collective-permute-start | bytes 294920 | tf_op jit(solution)/shard_map/ppermute | solution.py:448
  56.4 4.7 %hidden_gradients.2 = (bf16[2,32,1024]{2,1,0:T(8,128)(2,1)S(1)}, f32[32,1024]{1,0:T(8,128)S(1)}, f32[32,1024]{1,0:T(8,128)S(1)}) custom-call(bf16[32,1024]{1,0:T(8,128)(2,1)S(1)} %get-tuple-element.233.eug_ref.refs_0_, bf16[32,1024]{1,0:T(8,128)(2,1)S(1)} %get-tuple-element.234.euu_ref.refs_0_, f32[2,32,1024]{2,1,0:T(8,128)S(1)} %pad_maximum_fusion.3.keep_ref, ...), custom_call_target="tpu_custom_call" | custom-call | flops 268435456 | bytes 12582912 | tf_op jit(solution)/shard_map/hidden_gradients/pallas_call | solution.py:304
  61.1 4.0 %hidden_gradients.3 = (bf16[2,32,768]{2,1,0:T(8,128)(2,1)S(1)}, f32[32,1024]{1,0:T(8,128)S(1)}, f32[32,1024]{1,0:T(8,128)S(1)}) custom-call(bf16[32,1024]{1,0:T(8,128)(2,1)S(1)} %get-tuple-element.233.eug_ref.refs_0_, bf16[32,1024]{1,0:T(8,128)(2,1)S(1)} %get-tuple-element.234.euu_ref.refs_0_, f32[2,32,768]{2,1,0:T(8,128)S(1)} %pad_maximum_fusion.5.keep_ref, ...), custom_call_target="tpu_custom_call" | custom-call | flops 201326592 | bytes 9437184 | tf_op jit(solution)/shard_map/hidden_gradients/pallas_call | solution.py:304
  65.5 1.0 collective-permute-start.13
  66.6 3.4 %outer_products.3 = f32[1024,1792]{1,0:T(8,128)} custom-call(bf16[32,1024]{1,0:T(8,128)(2,1)S(1)} %get-tuple-element.233.eug_ref.refs_0_, bf16[32,1792]{1,0:T(8,128)(2,1)S(1)} %slice_bitcast_fusion.3.refs_1_), custom_call_target="tpu_custom_call" | custom-call | flops 117440512 | bytes 7340032 | tf_op jit(solution)/shard_map/outer_products/pallas_call | solution.py:419
  70.0 1.8 %collective-permute-done.13 = bf16[2,32,1792]{2,1,0:T(8,128)(2,1)S(1)} collective-permute-done((bf16[2,32,1792]{2,1,0:T(8,128)(2,1)S(1)}, bf16[2,32,1792]{2,1,0:T(8,128)(2,1)S(1)}, u32[]{:S(2)}, u32[]{:S(2)}) %collective-permute-start.13) | collective-permute-done | bytes 229408 | tf_op jit(solution)/shard_map/ppermute | solution.py:448
  71.9 0.6 collective-permute-start.15
  72.5 3.9 %backward_products.3 = (f32[32,512]{1,0:T(8,128)S(1)}, bf16[32,512]{1,0:T(8,128)(2,1)S(1)}) custom-call(s32[1]{0:T(128)} %get-tuple-element.113.side_ref, bf16[64,1792]{1,0:T(8,128)(2,1)S(1)} %get-tuple-element.156.dg_ref, bf16[64,1792]{1,0:T(8,128)(2,1)S(1)} %get-tuple-element.157.du_ref, bf16[8192,1792]{1,0:T(8,128)(2,1)} %wg_ref.5, bf16[8192,1792]{1,0:T(8,128)(2,1)} %wu_ref.5), custom_call_target="tpu_custom_call" | custom-call | flops 234881024 | bytes 5505024 | tf_op jit(solution)/shard_map/backward_products/pallas_call | solution.py:372
  76.4 0.4 collective-permute-start.16
  76.8 3.9 %backward_products.4 = (f32[32,512]{1,0:T(8,128)S(1)}, bf16[32,512]{1,0:T(8,128)(2,1)S(1)}) custom-call(s32[1]{0:T(128)} %get-tuple-element.113.side_ref, bf16[64,1792]{1,0:T(8,128)(2,1)S(1)} %get-tuple-element.156.dg_ref, bf16[64,1792]{1,0:T(8,128)(2,1)S(1)} %get-tuple-element.157.du_ref, bf16[8192,1792]{1,0:T(8,128)(2,1)} %wg_ref.5, bf16[8192,1792]{1,0:T(8,128)(2,1)} %wu_ref.5), custom_call_target="tpu_custom_call" | custom-call | flops 234881024 | bytes 5505024 | tf_op jit(solution)/shard_map/backward_products/pallas_call | solution.py:372
  80.8 0.4 collective-permute-start.17
  81.1 10.4 %backward_products.5 = (f32[32,3072]{1,0:T(8,128)S(1)}, bf16[32,3072]{1,0:T(8,128)(2,1)S(1)}) custom-call(s32[1]{0:T(128)} %get-tuple-element.113.side_ref, bf16[64,1792]{1,0:T(8,128)(2,1)S(1)} %get-tuple-element.156.dg_ref, bf16[64,1792]{1,0:T(8,128)(2,1)S(1)} %get-tuple-element.157.du_ref, bf16[8192,1792]{1,0:T(8,128)(2,1)} %wg_ref.5, ...), custom_call_target="tpu_custom_call" | custom-call | flops 1409286144 | bytes 33030144 | tf_op jit(solution)/shard_map/backward_products/pallas_call | solution.py:372
  92.0 0.4 fusion.47
  92.6 0.4 fusion.1
  93.0 0.6 collective-permute-start.19
  93.6 0.8 collective-permute-done.19
  94.5 2.0 %collective-permute-start.22 = (bf16[8,4096]{1,0:T(8,128)(2,1)S(1)}, bf16[8,4096]{1,0:T(8,128)(2,1)S(1)}, u32[]{:S(2)}, u32[]{:S(2)}) collective-permute-start(bf16[8,4096]{1,0:T(8,128)(2,1)S(1)} %get-tuple-element.187), channel_id=1, source_target_pairs={{0,18},{1,19},{2,16},{3,17},{4,22},{5,23},{6,20},{7,21},{8,26},{9,... | collective-permute-start | bytes 196616 | tf_op jit(solution)/shard_map/ppermute | solution.py:448
  96.5 1.0 collective-permute-start.21
  97.5 0.6 collective-permute-start.20
  98.2 3.4 %outer_products.4 = f32[1024,1792]{1,0:T(8,128)} custom-call(bf16[32,1024]{1,0:T(8,128)(2,1)S(1)} %get-tuple-element.234.euu_ref.refs_0_, bf16[32,1792]{1,0:T(8,128)(2,1)S(1)} %slice_bitcast_fusion.2.refs_1_), custom_call_target="tpu_custom_call" | custom-call | flops 117440512 | bytes 7340032 | tf_op jit(solution)/shard_map/outer_products/pallas_call | solution.py:419
  101.6 0.5 collective-permute-done.20
  102.2 3.9 %collective-permute-start.25 = (bf16[2,10240]{1,0:T(2,128)(2,1)S(1)}, bf16[2,10240]{1,0:T(2,128)(2,1)S(1)}, u32[]{:S(2)}, u32[]{:S(2)}) collective-permute-start(bf16[2,10240]{1,0:T(2,128)(2,1)S(1)} %get-tuple-element.190), channel_id=1, source_target_pairs={{0,12},{1,13},{2,14},{3,15},{4,8},{5,9},{6,10},{7,11},{8,4},{9,5},... | collective-permute-start | bytes 122888 | tf_op jit(solution)/shard_map/ppermute | solution.py:443
  106.1 0.6 collective-permute-start.23
  106.8 2.3 %outer_products.5 = (f32[512,1024]{1,0:T(8,128)}, f32[512,1024]{1,0:T(8,128)}) custom-call(bf16[32,512]{1,0:T(8,128)(2,1)S(1)} %dynamic-slice_select_fusion.refs_0_.refs_2_, bf16[32,1024]{1,0:T(8,128)(2,1)S(1)} %get-tuple-element.229.refs_1_, bf16[32,512]{1,0:T(8,128)(2,1)S(1)} %dynamic-slice_select_fusion.refs_0_.refs_2_, ...), custom_call_target="tpu_custom_call" | custom-call | flops 67108864 | bytes 4194304 | tf_op jit(solution)/shard_map/outer_products/pallas_call | solution.py:419
  109.1 1.9 %collective-permute-done.24 = bf16[2,10240]{1,0:T(2,128)(2,1)S(1)} collective-permute-done((bf16[2,10240]{1,0:T(2,128)(2,1)S(1)}, bf16[2,10240]{1,0:T(2,128)(2,1)S(1)}, u32[]{:S(2)}, u32[]{:S(2)}) %collective-permute-start.24) | collective-permute-done | bytes 40992 | tf_op jit(solution)/shard_map/ppermute | solution.py:443
  111.4 0.7 fusion.10
  (118 shorter events, 4.3 us)
Async XLA Ops:
  0.6 32.7 %copy-start = (bf16[32,1792]{1,0:T(8,128)(2,1)S(1)}, bf16[32,1792]{1,0:T(8,128)(2,1)}, u32[]{:S(2)}) copy-start(bf16[32,1792]{1,0:T(8,128)(2,1)} %param.17) | copy-start | bytes 344068
  0.6 5.4 %collective-permute-start = (bf16[2,8192]{1,0:T(2,128)(2,1)}, bf16[2,8192]{1,0:T(2,128)(2,1)S(1)}, u32[]{:S(2)}, u32[]{:S(2)}) collective-permute-start(bf16[2,8192]{1,0:T(2,128)(2,1)} %param.9), channel_id=1, source_target_pairs={{0,4},{1,5},{2,6},{3,7},{4,0},{5,1},{6,2},{7,3},{8,12},{9,13},{10,... | collective-permute-start | bytes 98312 | tf_op jit(solution)/shard_map/ppermute | solution.py:443
  6.9 5.2 %collective-permute-start.1 = (bf16[4,8192]{1,0:T(4,128)(2,1)S(1)}, bf16[4,8192]{1,0:T(4,128)(2,1)S(1)}, u32[]{:S(2)}, u32[]{:S(2)}) collective-permute-start(bf16[4,8192]{1,0:T(4,128)(2,1)S(1)} %pad_maximum_fusion.10), channel_id=1, source_target_pairs={{0,8},{1,9},{2,10},{3,11},{4,12},{5,13},{6,14},{7,15},{8,0},{9,1},... | collective-permute-start | bytes 196616 | tf_op jit(solution)/shard_map/ppermute | solution.py:443
  13.0 11.0 %collective-permute-start.2 = (bf16[8,4096]{1,0:T(8,128)(2,1)S(1)}, bf16[8,4096]{1,0:T(8,128)(2,1)S(1)}, u32[]{:S(2)}, u32[]{:S(2)}) collective-permute-start(bf16[8,4096]{1,0:T(8,128)(2,1)S(1)} %get-tuple-element.97), channel_id=1, source_target_pairs={{0,2},{1,3},{2,0},{3,1},{4,6},{5,7},{6,4},{7,5},{8,10},{9,11},{10,... | collective-permute-start | bytes 196616 | tf_op jit(solution)/shard_map/ppermute | solution.py:443
  14.8 9.2 %collective-permute-start.4 = (bf16[8,4096]{1,0:T(8,128)(2,1)S(1)}, bf16[8,4096]{1,0:T(8,128)(2,1)S(1)}, u32[]{:S(2)}, u32[]{:S(2)}) collective-permute-start(bf16[8,4096]{1,0:T(8,128)(2,1)S(1)} %get-tuple-element.100), channel_id=1, source_target_pairs={{0,18},{1,19},{2,16},{3,17},{4,22},{5,23},{6,20},{7,21},{8,26},{9,... | collective-permute-start | bytes 196616 | tf_op jit(solution)/shard_map/ppermute | solution.py:448
  16.3 7.7 %collective-permute-start.3 = (bf16[8,4096]{1,0:T(8,128)(2,1)S(1)}, bf16[8,4096]{1,0:T(8,128)(2,1)S(1)}, u32[]{:S(2)}, u32[]{:S(2)}) collective-permute-start(bf16[8,4096]{1,0:T(8,128)(2,1)S(1)} %get-tuple-element.100), channel_id=1, source_target_pairs={{0,16},{1,17},{2,18},{3,19},{4,20},{5,21},{6,22},{7,23},{8,24},{9,... | collective-permute-start | bytes 196616 | tf_op jit(solution)/shard_map/ppermute | solution.py:448
  16.6 7.7 %copy-start.4 = (s32[32]{0:T(128)S(1)}, s32[32]{0:T(128)}, u32[]{:S(2)}) copy-start(s32[32]{0:T(128)} %param.16) | copy-start | bytes 388
  20.7 3.3 %copy-start.2 = (bf16[4096,1024]{1,0:T(8,128)(2,1)}, bf16[4096,1024]{1,0:T(8,128)(2,1)S(1)}, u32[]{:S(2)}) copy-start(bf16[4096,1024]{1,0:T(8,128)(2,1)S(1)} %get-tuple-element.104.w_ref) | copy-start | bytes 25165828
  24.1 1.6 %collective-permute-start.5 = (bf16[2,16,4096]{2,1,0:T(8,128)(2,1)S(1)}, bf16[2,16,4096]{2,1,0:T(8,128)(2,1)S(1)}, u32[]{:S(2)}, u32[]{:S(2)}) collective-permute-start(bf16[2,16,4096]{2,1,0:T(8,128)(2,1)S(1)} %pad_maximum_fusion.2), channel_id=1, source_target_pairs={{0,1},{1,0},{2,3},{3,2},{4,5},{5,4},{6,7},{7,6},{8,9},{9,8},{10,11... | collective-permute-start | bytes 786440 | tf_op jit(solution)/shard_map/ppermute | solution.py:443
  25.8 6.6 %collective-permute-start.6 = (bf16[32,512]{1,0:T(8,128)(2,1)S(1)}, bf16[32,512]{1,0:T(8,128)(2,1)S(1)}, u32[]{:S(2)}, u32[]{:S(2)}) collective-permute-start(bf16[32,512]{1,0:T(8,128)(2,1)S(1)} %dynamic-slice.1), channel_id=1, source_target_pairs={{0,16},{1,17},{2,18},{3,19},{4,20},{5,21},{6,22},{7,23},{8,24},{9,... | collective-permute-start | bytes 98312 | tf_op jit(solution)/shard_map/ppermute | solution.py:448
  27.4 3.4 %copy-start.3 = (bf16[4096,1024]{1,0:T(8,128)(2,1)S(1)}, bf16[4096,1024]{1,0:T(8,128)(2,1)}, u32[]{:S(2)}) copy-start(bf16[4096,1024]{1,0:T(8,128)(2,1)} %copy-done.2) | copy-start | bytes 25165828
  33.3 1.2 %collective-permute-start.7 = (f32[32,128]{1,0:T(8,128)S(1)}, f32[32,128]{1,0:T(8,128)S(1)}, u32[]{:S(2)}, u32[]{:S(2)}) collective-permute-start(f32[32,128]{1,0:T(8,128)S(1)} %pad_maximum_fusion.17), channel_id=1, source_target_pairs={{0,1},{1,0},{2,3},{3,2},{4,5},{5,4},{6,7},{7,6},{8,9},{9,8},{10,11... | collective-permute-start | bytes 49160 | tf_op jit(solution)/shard_map/ppermute | solution.py:443
  34.6 6.2 %collective-permute-start.8 = (f32[32,128]{1,0:T(8,128)S(1)}, f32[32,128]{1,0:T(8,128)S(1)}, u32[]{:S(2)}, u32[]{:S(2)}) collective-permute-start(f32[32,128]{1,0:T(8,128)S(1)} %maximum_add_fusion.1), channel_id=1, source_target_pairs={{0,2},{1,3},{2,0},{3,1},{4,6},{5,7},{6,4},{7,5},{8,10},{9,11},{10,... | collective-permute-start | bytes 49160 | tf_op jit(solution)/shard_map/ppermute | solution.py:443
  40.8 6.4 %collective-permute-start.9 = (f32[32,128]{1,0:T(8,128)S(1)}, f32[32,128]{1,0:T(8,128)S(1)}, u32[]{:S(2)}, u32[]{:S(2)}) collective-permute-start(f32[32,128]{1,0:T(8,128)S(1)} %maximum_add_fusion.2), channel_id=1, source_target_pairs={{0,4},{1,5},{2,6},{3,7},{4,0},{5,1},{6,2},{7,3},{8,12},{9,13},{10,... | collective-permute-start | bytes 49160 | tf_op jit(solution)/shard_map/ppermute | solution.py:443
  42.4 5.1 %collective-permute-start.10 = (bf16[2,32,1024]{2,1,0:T(8,128)(2,1)S(1)}, bf16[2,32,1024]{2,1,0:T(8,128)(2,1)S(1)}, u32[]{:S(2)}, u32[]{:S(2)}) collective-permute-start(bf16[2,32,1024]{2,1,0:T(8,128)(2,1)S(1)} %pad_maximum_fusion.7), channel_id=1, source_target_pairs={{0,16},{1,17},{2,18},{3,19},{4,20},{5,21},{6,22},{7,23},{8,24},{9,... | collective-permute-start | bytes 393224 | tf_op jit(solution)/shard_map/ppermute | solution.py:448
  47.5 7.2 %collective-permute-start.11 = (f32[32,128]{1,0:T(8,128)S(1)}, f32[32,128]{1,0:T(8,128)S(1)}, u32[]{:S(2)}, u32[]{:S(2)}) collective-permute-start(f32[32,128]{1,0:T(8,128)S(1)} %add.222), channel_id=1, source_target_pairs={{0,8},{1,9},{2,10},{3,11},{4,12},{5,13},{6,14},{7,15},{8,0},{9,1},... | collective-permute-start | bytes 49160 | tf_op jit(solution)/shard_map/ppermute | solution.py:443
  55.2 5.9 %collective-permute-start.12 = (bf16[2,32,768]{2,1,0:T(8,128)(2,1)S(1)}, bf16[2,32,768]{2,1,0:T(8,128)(2,1)S(1)}, u32[]{:S(2)}, u32[]{:S(2)}) collective-permute-start(bf16[2,32,768]{2,1,0:T(8,128)(2,1)S(1)} %pad_maximum_fusion.8), channel_id=1, source_target_pairs={{0,16},{1,17},{2,18},{3,19},{4,20},{5,21},{6,22},{7,23},{8,24},{9,... | collective-permute-start | bytes 294920 | tf_op jit(solution)/shard_map/ppermute | solution.py:448
  65.5 6.3 %collective-permute-start.13 = (bf16[2,32,1792]{2,1,0:T(8,128)(2,1)S(1)}, bf16[2,32,1792]{2,1,0:T(8,128)(2,1)S(1)}, u32[]{:S(2)}, u32[]{:S(2)}) collective-permute-start(bf16[2,32,1792]{2,1,0:T(8,128)(2,1)S(1)} %constant_dynamic-update-slice_fusion), channel_id=1, source_target_pairs={{0,16},{1,17},{2,18},{3,19},{4,20},{5,21},{6,22},{7,23},{8,24},{9,... | collective-permute-start | bytes 688136 | tf_op jit(solution)/shard_map/ppermute | solution.py:448
  66.6 3.4 %collective-permute-start.14 = (f32[32,128]{1,0:T(8,128)S(1)}, f32[32,128]{1,0:T(8,128)S(1)}, u32[]{:S(2)}, u32[]{:S(2)}) collective-permute-start(f32[32,128]{1,0:T(8,128)S(1)} %pad_maximum_fusion.20), channel_id=1, source_target_pairs={{0,1},{1,0},{2,3},{3,2},{4,5},{5,4},{6,7},{7,6},{8,9},{9,8},{10,11... | collective-permute-start | bytes 49160 | tf_op jit(solution)/shard_map/ppermute | solution.py:443
  71.9 4.5 %collective-permute-start.15 = (f32[32,128]{1,0:T(8,128)S(1)}, f32[32,128]{1,0:T(8,128)S(1)}, u32[]{:S(2)}, u32[]{:S(2)}) collective-permute-start(f32[32,128]{1,0:T(8,128)S(1)} %maximum_add_fusion.3), channel_id=1, source_target_pairs={{0,2},{1,3},{2,0},{3,1},{4,6},{5,7},{6,4},{7,5},{8,10},{9,11},{10,... | collective-permute-start | bytes 49160 | tf_op jit(solution)/shard_map/ppermute | solution.py:443
  76.4 4.3 %collective-permute-start.16 = (f32[32,128]{1,0:T(8,128)S(1)}, f32[32,128]{1,0:T(8,128)S(1)}, u32[]{:S(2)}, u32[]{:S(2)}) collective-permute-start(f32[32,128]{1,0:T(8,128)S(1)} %maximum_add_fusion.4), channel_id=1, source_target_pairs={{0,4},{1,5},{2,6},{3,7},{4,0},{5,1},{6,2},{7,3},{8,12},{9,13},{10,... | collective-permute-start | bytes 49160 | tf_op jit(solution)/shard_map/ppermute | solution.py:443
  80.8 10.8 %collective-permute-start.17 = (f32[32,128]{1,0:T(8,128)S(1)}, f32[32,128]{1,0:T(8,128)S(1)}, u32[]{:S(2)}, u32[]{:S(2)}) collective-permute-start(f32[32,128]{1,0:T(8,128)S(1)} %add.244), channel_id=1, source_target_pairs={{0,8},{1,9},{2,10},{3,11},{4,12},{5,13},{6,14},{7,15},{8,0},{9,1},... | collective-permute-start | bytes 49160 | tf_op jit(solution)/shard_map/ppermute | solution.py:443
  92.0 20.0 %copy-start.1 = (bf16[32,1792]{1,0:T(8,128)(2,1)S(1)}, bf16[32,1792]{1,0:T(8,128)(2,1)}, u32[]{:S(2)}) copy-start(bf16[32,1792]{1,0:T(8,128)(2,1)} %param.17) | copy-start | bytes 344068
  92.5 1.9 %collective-permute-start.18 = (bf16[32,4096]{1,0:T(8,128)(2,1)S(1)}, bf16[32,4096]{1,0:T(8,128)(2,1)S(1)}, u32[]{:S(2)}, u32[]{:S(2)}) collective-permute-start(bf16[32,4096]{1,0:T(8,128)(2,1)S(1)} %pad_maximum_fusion.4), channel_id=1, source_target_pairs={{0,1},{1,0},{2,3},{3,2},{4,5},{5,4},{6,7},{7,6},{8,9},{9,8},{10,11... | collective-permute-start | bytes 786440 | tf_op jit(solution)/shard_map/ppermute | solution.py:443
  93.0 1.4 %collective-permute-start.19 = (bf16[16,512]{1,0:T(8,128)(2,1)S(1)}, bf16[16,512]{1,0:T(8,128)(2,1)S(1)}, u32[]{:S(2)}, u32[]{:S(2)}) collective-permute-start(bf16[16,512]{1,0:T(8,128)(2,1)S(1)} %get-tuple-element.200), channel_id=1, source_target_pairs={{0,1},{1,0},{2,3},{3,2},{4,5},{5,4},{6,7},{7,6},{8,9},{9,8},{10,11... | collective-permute-start | bytes 49160 | tf_op jit(solution)/shard_map/ppermute | solution.py:443
  94.5 7.0 %collective-permute-start.22 = (bf16[8,4096]{1,0:T(8,128)(2,1)S(1)}, bf16[8,4096]{1,0:T(8,128)(2,1)S(1)}, u32[]{:S(2)}, u32[]{:S(2)}) collective-permute-start(bf16[8,4096]{1,0:T(8,128)(2,1)S(1)} %get-tuple-element.187), channel_id=1, source_target_pairs={{0,18},{1,19},{2,16},{3,17},{4,22},{5,23},{6,20},{7,21},{8,26},{9,... | collective-permute-start | bytes 196616 | tf_op jit(solution)/shard_map/ppermute | solution.py:448
  96.5 5.0 %collective-permute-start.21 = (bf16[8,4096]{1,0:T(8,128)(2,1)S(1)}, bf16[8,4096]{1,0:T(8,128)(2,1)S(1)}, u32[]{:S(2)}, u32[]{:S(2)}) collective-permute-start(bf16[8,4096]{1,0:T(8,128)(2,1)S(1)} %get-tuple-element.188), channel_id=1, source_target_pairs={{0,16},{1,17},{2,18},{3,19},{4,20},{5,21},{6,22},{7,23},{8,24},{9,... | collective-permute-start | bytes 196616 | tf_op jit(solution)/shard_map/ppermute | solution.py:448
  97.5 4.5 %collective-permute-start.20 = (bf16[8,5120]{1,0:T(8,128)(2,1)S(1)}, bf16[8,5120]{1,0:T(8,128)(2,1)S(1)}, u32[]{:S(2)}, u32[]{:S(2)}) collective-permute-start(bf16[8,5120]{1,0:T(8,128)(2,1)S(1)} %pad_maximum_fusion.9), channel_id=1, source_target_pairs={{0,2},{1,3},{2,0},{3,1},{4,6},{5,7},{6,4},{7,5},{8,10},{9,11},{10,... | collective-permute-start | bytes 245768 | tf_op jit(solution)/shard_map/ppermute | solution.py:443
  102.2 6.9 %collective-permute-start.25 = (bf16[2,10240]{1,0:T(2,128)(2,1)S(1)}, bf16[2,10240]{1,0:T(2,128)(2,1)S(1)}, u32[]{:S(2)}, u32[]{:S(2)}) collective-permute-start(bf16[2,10240]{1,0:T(2,128)(2,1)S(1)} %get-tuple-element.190), channel_id=1, source_target_pairs={{0,12},{1,13},{2,14},{3,15},{4,8},{5,9},{6,10},{7,11},{8,4},{9,5},... | collective-permute-start | bytes 122888 | tf_op jit(solution)/shard_map/ppermute | solution.py:443
  106.1 4.9 %collective-permute-start.24 = (bf16[2,10240]{1,0:T(2,128)(2,1)S(1)}, bf16[2,10240]{1,0:T(2,128)(2,1)S(1)}, u32[]{:S(2)}, u32[]{:S(2)}) collective-permute-start(bf16[2,10240]{1,0:T(2,128)(2,1)S(1)} %get-tuple-element.191), channel_id=1, source_target_pairs={{0,8},{1,9},{2,10},{3,11},{4,12},{5,13},{6,14},{7,15},{8,0},{9,1},... | collective-permute-start | bytes 122888 | tf_op jit(solution)/shard_map/ppermute | solution.py:443
  106.1 4.9 %collective-permute-start.23 = (bf16[2,10240]{1,0:T(2,128)(2,1)S(1)}, bf16[2,10240]{1,0:T(2,128)(2,1)S(1)}, u32[]{:S(2)}, u32[]{:S(2)}) collective-permute-start(bf16[2,10240]{1,0:T(2,128)(2,1)S(1)} %get-tuple-element.192), channel_id=1, source_target_pairs={{0,4},{1,5},{2,6},{3,7},{4,0},{5,1},{6,2},{7,3},{8,12},{9,13},{10,... | collective-permute-start | bytes 122888 | tf_op jit(solution)/shard_map/ppermute | solution.py:443
